TPU v7x, 32 devices: a whole 2x2x4 slice. The times are simulated.
32 devices in a mesh: fsdp: 32 (over z, y, x, core).
Axes of the slice: x: 2, y: 2, z: 4, core: 2. Of those that a mesh axis runs over, the one named last changes fastest.
Arguments:
- tokens: bfloat16 [12544, 768], P('fsdp'), may hold values from -6 to 6
- window_pos: int32 [64], P('fsdp'), may hold values from 0 to 24
- norm1_gain: float32 [768], P('fsdp'), may hold values from 0.5 to 1.5
- norm1_bias: float32 [768], P('fsdp'), may hold values from -4 to 4
- qkv_weight: float32 [768, 2304], P('fsdp'), may hold values from -0.21875 to 0.21875
- qkv_bias: float32 [2304], P('fsdp'), may hold values from -4 to 4
- rel_pos_h: float32 [27, 64], replicated, may hold values from -2 to 2
- rel_pos_w: float32 [27, 64], replicated, may hold values from -2 to 2
- proj_weight: float32 [768, 768], P('fsdp'), may hold values from -0.875 to 0.875
- proj_bias: float32 [768], P('fsdp'), may hold values from -4 to 4
- norm2_gain: float32 [768], P('fsdp'), may hold values from 0.5 to 1.5
- norm2_bias: float32 [768], P('fsdp'), may hold values from -4 to 4
- lin1_weight: float32 [768, 3072], P('fsdp'), may hold values from -0.21875 to 0.21875
- lin1_bias: float32 [3072], P('fsdp'), may hold values from -4 to 4
- lin2_weight: float32 [3072, 768], P('fsdp'), may hold values from -0.15625 to 0.15625
- lin2_bias: float32 [768], P('fsdp'), may hold values from -4 to 4
- out_grad: bfloat16 [12544, 768], P('fsdp'), may hold values from -6 to 6
Outputs:
- output: bfloat16 [12544, 768], P('fsdp')
- tokens_grad: bfloat16 [12544, 768], P('fsdp')
- norm1_gain_grad: float32 [768], P('fsdp')
- norm1_bias_grad: float32 [768], P('fsdp')
- qkv_weight_grad: float32 [768, 2304], P('fsdp')
- qkv_bias_grad: float32 [2304], P('fsdp')
- rel_pos_h_grad: float32 [27, 64], replicated
- rel_pos_w_grad: float32 [27, 64], replicated
- proj_weight_grad: float32 [768, 768], P('fsdp')
- proj_bias_grad: float32 [768], P('fsdp')
- norm2_gain_grad: float32 [768], P('fsdp')
- norm2_bias_grad: float32 [768], P('fsdp')
- lin1_weight_grad: float32 [768, 3072], P('fsdp')
- lin1_bias_grad: float32 [3072], P('fsdp')
- lin2_weight_grad: float32 [3072, 768], P('fsdp')
- lin2_bias_grad: float32 [768], P('fsdp')
Inputs may be any that keep to these rules, and one draw needn't show every extreme that they name: `window_pos`: the place of each window in its image's 5 x 5 grid of windows, row-major.
All inputs are finite; a program needn't handle non-finite values.
Results may differ from a plain program's by a relative error of at most 0.014.
The roundings to bfloat16 on the way count: a program that leaves them out, or rounds other values in their place, can miss the bound.
Values may be sent and summed in bfloat16 or wider, within the bound.
No kernel may reach another device: no remote copies, remote signals or barrier semaphores. Data moves between devices by JAX's collectives and lax.ppermute only.
A program may use at most 192 MiB of HBM per device.

v0:
```python
import jax
import jax.numpy as jnp
from jax import lax
from jax.sharding import PartitionSpec as P

D = 768
HEADS = 12
HEAD_DIM = 64
WIN = 14
MICRO = 2
NWS = 5
EDGE = 8


highest = lax.Precision.HIGHEST
eps_norm = 1e-06


def layer_norm(values, gain_vec, shift_vec):
    row_mean = jnp.mean(values, axis=-1, keepdims=True)
    centred = values - row_mean
    row_var = jnp.mean(centred * centred, axis=-1, keepdims=True)
    return centred * lax.rsqrt(row_var + eps_norm) * gain_vec + shift_vec


def gelu_exact(values):
    return jax.nn.gelu(values, approximate=False)


def slot_mask(window_pos):
    row_win = window_pos // NWS
    col_win = window_pos % NWS
    rows_ok = jnp.where(row_win == NWS - 1, EDGE, WIN)
    cols_ok = jnp.where(col_win == NWS - 1, EDGE, WIN)
    positions = jnp.arange(WIN, dtype=jnp.int32)
    inside = (positions[None, :, None] < rows_ok[:, None, None]) & (
        positions[None, None, :] < cols_ok[:, None, None]
    )
    return inside.reshape(-1, WIN * WIN).astype(jnp.float32)


def spread_onehot():
    positions = jnp.arange(WIN, dtype=jnp.int32)
    offsets = positions[:, None] - positions[None, :] + WIN - 1
    entries = jnp.arange(2 * WIN - 1, dtype=jnp.int32)
    return (offsets[:, :, None] == entries[None, None, :]).astype(jnp.float32)


def attention_scores(queries, keys_all, spread_rows, spread_cols):
    windows = queries.shape[0]
    score_scale = HEAD_DIM ** (-0.5)
    direct = (
        jnp.einsum("wqhc,wkhc->whqk", queries, keys_all, preferred_element_type=jnp.float32)
        * score_scale
    )
    grid_q = queries.reshape(windows, WIN, WIN, HEADS, HEAD_DIM)
    rel_rows = jnp.einsum(
        "wyxhc,ykc->whyxk", grid_q, spread_rows, preferred_element_type=jnp.float32
    )
    rel_cols = jnp.einsum(
        "wyxhc,xkc->whyxk", grid_q, spread_cols, preferred_element_type=jnp.float32
    )
    combined = (
        direct.reshape(windows, HEADS, WIN, WIN, WIN, WIN)
        + rel_rows[..., :, None]
        + rel_cols[..., None, :]
    )
    return combined.reshape(windows, HEADS, WIN * WIN, WIN * WIN)


def forward_micro(token_rows, live, weights, tables):
    (
        gain_one,
        bias_one,
        w_qkv,
        b_qkv,
        w_proj,
        b_proj,
        gain_two,
        bias_two,
        w_up,
        b_up,
        w_down,
        b_down,
    ) = weights
    spread_rows, spread_cols = tables
    windows = live.shape[0]
    length = WIN * WIN
    live_col = live.reshape(-1, 1)
    inputs = token_rows.astype(jnp.float32)
    normed_one = (
        layer_norm(inputs, gain_one.astype(jnp.float32), bias_one.astype(jnp.float32)) * live_col
    ).astype(jnp.bfloat16)
    qkv = jnp.dot(normed_one, w_qkv, preferred_element_type=jnp.float32) + b_qkv.astype(jnp.float32)
    head_split = qkv.astype(jnp.bfloat16).reshape(windows, length, 3, HEADS, HEAD_DIM)
    queries = head_split[:, :, 0]
    keys_all = head_split[:, :, 1]
    values_all = head_split[:, :, 2]
    scores = attention_scores(queries, keys_all, spread_rows, spread_cols)
    row_top = jnp.max(scores, axis=-1, keepdims=True)
    expon = jnp.exp(scores - row_top)
    totals = jnp.sum(expon, axis=-1, keepdims=True)
    attn_probs = (expon / totals).astype(jnp.bfloat16)
    log_norm = row_top + jnp.log(totals)
    mixed_rows = jnp.einsum(
        "whqk,wkhc->wqhc", attn_probs, values_all, preferred_element_type=jnp.float32
    )
    mixed_rows = mixed_rows.reshape(windows * length, D).astype(jnp.bfloat16)
    attn_out = jnp.dot(mixed_rows, w_proj, preferred_element_type=jnp.float32) + b_proj.astype(
        jnp.float32
    )
    residual = inputs + attn_out
    normed_two = layer_norm(
        residual, gain_two.astype(jnp.float32), bias_two.astype(jnp.float32)
    ).astype(jnp.bfloat16)
    hidden = jnp.dot(normed_two, w_up, preferred_element_type=jnp.float32) + b_up.astype(
        jnp.float32
    )
    active = gelu_exact(hidden).astype(jnp.bfloat16)
    branch = jnp.dot(active, w_down, preferred_element_type=jnp.float32) + b_down.astype(
        jnp.float32
    )
    output = ((residual + branch) * live_col).astype(jnp.bfloat16)
    kept_state = (
        inputs,
        normed_one,
        head_split,
        log_norm,
        mixed_rows,
        residual,
        normed_two,
        hidden,
        active,
    )
    return (output, kept_state)


def attention_back(head_split, log_norm, grad_mixed, tables, onehot):
    spread_rows, spread_cols = tables
    windows = head_split.shape[0]
    length = WIN * WIN
    score_scale = HEAD_DIM ** (-0.5)
    queries = head_split[:, :, 0]
    keys_all = head_split[:, :, 1]
    values_all = head_split[:, :, 2]
    scores = attention_scores(queries, keys_all, spread_rows, spread_cols)
    attn_probs = jnp.exp(scores - log_norm)
    probs_low = attn_probs.astype(jnp.bfloat16)
    grad_heads = grad_mixed.reshape(windows, length, HEADS, HEAD_DIM)
    grad_values = jnp.einsum(
        "whqk,wqhc->wkhc", probs_low, grad_heads, preferred_element_type=jnp.float32
    )
    grad_probs = jnp.einsum(
        "wqhc,wkhc->whqk", grad_heads, values_all, preferred_element_type=jnp.float32
    )
    row_dot = jnp.sum(attn_probs * grad_probs, axis=-1, keepdims=True)
    grad_scores = (attn_probs * (grad_probs - row_dot)).astype(jnp.bfloat16)
    grad_queries = (
        jnp.einsum("whqk,wkhc->wqhc", grad_scores, keys_all, preferred_element_type=jnp.float32)
        * score_scale
    )
    grad_keys = (
        jnp.einsum("whqk,wqhc->wkhc", grad_scores, queries, preferred_element_type=jnp.float32)
        * score_scale
    )
    grad_grid = grad_scores.reshape(windows, HEADS, WIN, WIN, WIN, WIN).astype(jnp.float32)
    grad_rel_rows = jnp.sum(grad_grid, axis=5)
    grad_rel_cols = jnp.sum(grad_grid, axis=4)
    rows_table = spread_rows.astype(jnp.float32)
    cols_table = spread_cols.astype(jnp.float32)
    from_rows = jnp.einsum("whyxk,ykc->wyxhc", grad_rel_rows, rows_table, precision=highest)
    from_cols = jnp.einsum("whyxk,xkc->wyxhc", grad_rel_cols, cols_table, precision=highest)
    grad_queries = grad_queries + (from_rows + from_cols).reshape(windows, length, HEADS, HEAD_DIM)
    grid_q = queries.reshape(windows, WIN, WIN, HEADS, HEAD_DIM).astype(jnp.float32)
    spread_grad_rows = jnp.einsum("whyxk,wyxhc->ykc", grad_rel_rows, grid_q, precision=highest)
    spread_grad_cols = jnp.einsum("whyxk,wyxhc->xkc", grad_rel_cols, grid_q, precision=highest)
    table_grad_rows = jnp.einsum("ykr,ykc->rc", onehot, spread_grad_rows, precision=highest)
    table_grad_cols = jnp.einsum("ykr,ykc->rc", onehot, spread_grad_cols, precision=highest)
    grad_qkv = jnp.stack((grad_queries, grad_keys, grad_values), axis=2).reshape(
        windows * length, 3 * D
    )
    return (grad_qkv.astype(jnp.bfloat16), table_grad_rows, table_grad_cols)


def backward_micro(grad_rows, live, kept_state, weights, tables, onehot):
    (
        gain_one,
        bias_one,
        w_qkv,
        b_qkv,
        w_proj,
        b_proj,
        gain_two,
        bias_two,
        w_up,
        b_up,
        w_down,
        b_down,
    ) = weights
    inputs, normed_one, head_split, log_norm, mixed_rows, residual, normed_two, hidden, active = (
        kept_state
    )
    live_col = live.reshape(-1, 1)
    grad_out = grad_rows.astype(jnp.float32) * live_col
    grad_branch = grad_out.astype(jnp.bfloat16)
    grad_w_down = jnp.einsum("nf,nd->fd", active, grad_branch, preferred_element_type=jnp.float32)
    grad_b_down = jnp.sum(grad_branch.astype(jnp.float32), axis=0)
    grad_active = jnp.einsum("nd,fd->nf", grad_branch, w_down, preferred_element_type=jnp.float32)
    gelu_out, gelu_back = jax.vjp(gelu_exact, hidden)
    grad_hidden = gelu_back(grad_active)[0].astype(jnp.bfloat16)
    grad_w_up = jnp.einsum("nd,nf->df", normed_two, grad_hidden, preferred_element_type=jnp.float32)
    grad_b_up = jnp.sum(grad_hidden.astype(jnp.float32), axis=0)
    grad_normed_two = jnp.einsum("nf,df->nd", grad_hidden, w_up, preferred_element_type=jnp.float32)
    norm_out, norm_two_back = jax.vjp(
        layer_norm, residual, gain_two.astype(jnp.float32), bias_two.astype(jnp.float32)
    )
    grad_res_norm, grad_gain_two, grad_bias_two = norm_two_back(grad_normed_two)
    grad_residual = grad_out + grad_res_norm
    grad_attn = grad_residual.astype(jnp.bfloat16)
    grad_w_proj = jnp.einsum("nd,ne->de", mixed_rows, grad_attn, preferred_element_type=jnp.float32)
    grad_b_proj = jnp.sum(grad_attn.astype(jnp.float32), axis=0)
    grad_mixed = jnp.einsum(
        "ne,de->nd", grad_attn, w_proj, preferred_element_type=jnp.float32
    ).astype(jnp.bfloat16)
    grad_qkv, table_grad_rows, table_grad_cols = attention_back(
        head_split, log_norm, grad_mixed, tables, onehot
    )
    grad_w_qkv = jnp.einsum("nd,ne->de", normed_one, grad_qkv, preferred_element_type=jnp.float32)
    grad_b_qkv = jnp.sum(grad_qkv.astype(jnp.float32), axis=0)
    grad_normed_one = (
        jnp.einsum("ne,de->nd", grad_qkv, w_qkv, preferred_element_type=jnp.float32) * live_col
    )
    norm_first, norm_one_back = jax.vjp(
        layer_norm, inputs, gain_one.astype(jnp.float32), bias_one.astype(jnp.float32)
    )
    grad_in_norm, grad_gain_one, grad_bias_one = norm_one_back(grad_normed_one)
    tokens_grad = (grad_in_norm + grad_residual).astype(jnp.bfloat16)
    weight_grads = (
        grad_gain_one,
        grad_bias_one,
        grad_w_qkv,
        grad_b_qkv,
        grad_w_proj,
        grad_b_proj,
        grad_gain_two,
        grad_bias_two,
        grad_w_up,
        grad_b_up,
        grad_w_down,
        grad_b_down,
    )
    return (tokens_grad, weight_grads, (table_grad_rows, table_grad_cols))


def per_device(
    tokens,
    window_pos,
    norm1_gain,
    norm1_bias,
    qkv_weight,
    qkv_bias,
    rel_pos_h,
    rel_pos_w,
    proj_weight,
    proj_bias,
    norm2_gain,
    norm2_bias,
    lin1_weight,
    lin1_bias,
    lin2_weight,
    lin2_bias,
    out_grad,
):
    masters = (
        norm1_gain,
        norm1_bias,
        qkv_weight,
        qkv_bias,
        proj_weight,
        proj_bias,
        norm2_gain,
        norm2_bias,
        lin1_weight,
        lin1_bias,
        lin2_weight,
        lin2_bias,
    )
    shards = tuple((piece.astype(jnp.bfloat16) for piece in masters))
    onehot = spread_onehot()
    spread_rows = jnp.einsum(
        "ykr,rc->ykc", onehot, rel_pos_h.astype(jnp.bfloat16).astype(jnp.float32), precision=highest
    ).astype(jnp.bfloat16)
    spread_cols = jnp.einsum(
        "ykr,rc->ykc", onehot, rel_pos_w.astype(jnp.bfloat16).astype(jnp.float32), precision=highest
    ).astype(jnp.bfloat16)
    tables = (spread_rows, spread_cols)
    live_all = slot_mask(window_pos)
    length = WIN * WIN
    per_micro = window_pos.shape[0] // MICRO
    outputs = []
    input_grads = []
    grad_totals = None
    owned = None
    table_totals = None
    for micro_step in range(MICRO):
        first_win = micro_step * per_micro
        token_rows = tokens[first_win * length : (first_win + per_micro) * length]
        grad_rows = out_grad[first_win * length : (first_win + per_micro) * length]
        live = live_all[first_win : first_win + per_micro]
        forward_weights = (
            lax.all_gather(shards[0], "fsdp", axis=0, tiled=True),
            lax.all_gather(shards[1], "fsdp", axis=0, tiled=True),
            lax.all_gather(shards[2], "fsdp", axis=0, tiled=True),
            lax.all_gather(shards[3], "fsdp", axis=0, tiled=True),
            lax.all_gather(shards[4], "fsdp", axis=0, tiled=True),
            lax.all_gather(shards[5], "fsdp", axis=0, tiled=True),
            lax.all_gather(shards[6], "fsdp", axis=0, tiled=True),
            lax.all_gather(shards[7], "fsdp", axis=0, tiled=True),
            lax.all_gather(shards[8], "fsdp", axis=0, tiled=True),
            lax.all_gather(shards[9], "fsdp", axis=0, tiled=True),
            lax.all_gather(shards[10], "fsdp", axis=0, tiled=True),
            lax.all_gather(shards[11], "fsdp", axis=0, tiled=True),
        )
        output_rows, kept_state = forward_micro(token_rows, live, forward_weights, tables)
        tokens_grad, weight_grads, table_grads = backward_micro(
            grad_rows, live, kept_state, forward_weights, tables, onehot
        )
        outputs.append(output_rows)
        input_grads.append(tokens_grad)
        table_totals = (
            table_grads
            if table_totals is None
            else jax.tree.map(jnp.add, table_totals, table_grads)
        )
        grad_totals = (
            weight_grads
            if grad_totals is None
            else jax.tree.map(jnp.add, grad_totals, weight_grads)
        )
    owned = (
        lax.psum_scatter(grad_totals[0], "fsdp", scatter_dimension=0, tiled=True),
        lax.psum_scatter(grad_totals[1], "fsdp", scatter_dimension=0, tiled=True),
        lax.psum_scatter(grad_totals[2], "fsdp", scatter_dimension=0, tiled=True),
        lax.psum_scatter(grad_totals[3], "fsdp", scatter_dimension=0, tiled=True),
        lax.psum_scatter(grad_totals[4], "fsdp", scatter_dimension=0, tiled=True),
        lax.psum_scatter(grad_totals[5], "fsdp", scatter_dimension=0, tiled=True),
        lax.psum_scatter(grad_totals[6], "fsdp", scatter_dimension=0, tiled=True),
        lax.psum_scatter(grad_totals[7], "fsdp", scatter_dimension=0, tiled=True),
        lax.psum_scatter(grad_totals[8], "fsdp", scatter_dimension=0, tiled=True),
        lax.psum_scatter(grad_totals[9], "fsdp", scatter_dimension=0, tiled=True),
        lax.psum_scatter(grad_totals[10], "fsdp", scatter_dimension=0, tiled=True),
        lax.psum_scatter(grad_totals[11], "fsdp", scatter_dimension=0, tiled=True),
    )
    table_rows_sum, table_cols_sum = lax.psum((table_totals[0], table_totals[1]), "fsdp")
    return (
        jnp.concatenate(outputs, axis=0),
        jnp.concatenate(input_grads, axis=0),
        owned[0],
        owned[1],
        owned[2],
        owned[3],
        table_rows_sum,
        table_cols_sum,
        owned[4],
        owned[5],
        owned[6],
        owned[7],
        owned[8],
        owned[9],
        owned[10],
        owned[11],
    )


def solution(mesh):
    placed = (
        P("fsdp", None),
        P("fsdp"),
        P("fsdp"),
        P("fsdp"),
        P("fsdp", None),
        P("fsdp"),
        P(),
        P(),
        P("fsdp", None),
        P("fsdp"),
        P("fsdp"),
        P("fsdp"),
        P("fsdp", None),
        P("fsdp"),
        P("fsdp", None),
        P("fsdp"),
        P("fsdp", None),
    )
    return jax.shard_map(
        per_device,
        mesh=mesh,
        in_specs=placed,
        out_specs=(
            P("fsdp", None),
            P("fsdp", None),
            P("fsdp"),
            P("fsdp"),
            P("fsdp", None),
            P("fsdp"),
            P(),
            P(),
            P("fsdp", None),
            P("fsdp"),
            P("fsdp"),
            P("fsdp"),
            P("fsdp", None),
            P("fsdp"),
            P("fsdp", None),
            P("fsdp"),
        ),
        check_vma=False,
    )
```

profile of v0, /device:TPU:0, one launch (start us, length us, event | category | flops | bytes accessed | tf_op | source)
XLA Modules:
  0.0 921.0 jit_solution(4616276428180889288)
XLA Ops:
  20.9 43.4 %all-reduce.17 = (bf16[2304]{0:T(1024)(128)(2,1)S(1)}, bf16[768]{0:T(1024)(128)(2,1)S(1)}, bf16[768]{0:T(1024)(128)(2,1)S(1)}, bf16[768]{0:T(1024)(128)(2,1)S(1)...) all-reduce(bf16[2304]{0:T(1024)(128)(2,1)S(1)} %dynamic-update-slic, ...), channel_id=1, replica_groups=mesh['fsdp'=32] {'fsdp'}, use_global_device_ids=true, to_apply=%add.2 | all-reduce | flops 9984 | bytes 39936
  69.5 5.6 all-gather.5.cloned.1.call-done
  75.1 3.0 fusion.1
  82.1 2.3 copy.111
  86.8 8.1 add.415
  94.9 12.8 %add.416 = f32[12,196,196]{1,2,0:T(8,128)} reshape(f32[12,14,14,14,14]{2,1,4,3,0:T(8,128)} %add.415) | data formatting | bytes 3687936 | tf_op jit(solution)/shard_map/add | solution.py:64
  107.7 9.0 add.419
  116.6 13.0 %add.420 = f32[12,196,196]{1,2,0:T(8,128)} reshape(f32[12,14,14,14,14]{2,1,4,3,0:T(8,128)} %add.419) | data formatting | bytes 3687936 | tf_op jit(solution)/shard_map/add | solution.py:64
  129.6 3.4 fusion.138
  139.8 57.5 %all-gather.9.cloned.1.call-done = bf16[768,3072]{1,0:T(8,128)(2,1)} async-done(((bf16[24,3072]{1,0:T(8,128)(2,1)}), bf16[768,3072]{1,0:T(8,128)(2,1)}) %all-gather.9.cloned.1.call-update) | async-done | bytes 4718608 | tf_op jit(solution)/shard_map/all_gather | solution.py:319
  197.3 9.8 %multiply_convert_fusion.2 = (bf16[196,3072]{1,0:T(8,128)(2,1)}, f32[196,3072]{1,0:T(8,128)}, f32[196,3072]{1,0:T(8,128)}) fusion(f32[3072]{0:T(1024)} %convert_element_type.347, bf16[768,3072]{1,0:T(8,128)(2,1)} %all-gather.9.cloned.1.call-done, f32[196,768]{1,0:T(8,128)} %copy-done.24, f32[196]{0:T(256)} %fusion.103, f32[196]{0:T(256)S(1)} %broadcast_multiply_fusion, ...), kind=kOutput, calls=%fused_computation.23 | convolution fusion | flops 965336064 | bytes 11361824 | tf_op jit(solution)/shard_map/dot_general | solution.py:116
  207.2 56.0 %all-gather.11.cloned.1.call-done = bf16[3072,768]{1,0:T(8,128)(2,1)} async-done(((bf16[96,768]{1,0:T(8,128)(2,1)}), bf16[3072,768]{1,0:T(8,128)(2,1)}) %all-gather.11.cloned.1.call-update) | async-done | bytes 4718608 | tf_op jit(solution)/shard_map/all_gather | solution.py:321
  263.2 6.7 convert_reduce_fusion
  269.8 2.3 multiply_reduce_fusion.2
  283.0 11.7 %reshape.698 = f32[1,12,14,14,14,14]{5,4,3,2,1,0:T(8,128)} reshape(f32[12,196,196]{2,1,0:T(8,128)S(1)} %copy.125) | data formatting | bytes 3687936 | tf_op jit(solution)/shard_map/convert_element_type | solution.py:166
  294.8 11.1 %fusion.128 = (f32[12,14,14,14]{3,2,1,0:T(8,128)}, f32[12,14,14,14]{3,2,1,0:T(8,128)}) fusion(f32[1,12,14,14,14,14]{5,4,3,2,1,0:T(8,128)} %reshape.698), kind=kLoop, calls=%fused_computation.253 | loop fusion | flops 856128 | bytes 2107392 | tf_op jit(solution)/shard_map/reduce_sum | solution.py:167
  305.9 2.5 copy.142
  317.8 2.9 fusion.129
  324.1 2.8 convolution_bitcast_fusion.4
  327.0 2.8 convolution_bitcast_fusion.5
  329.8 3.7 copy.104
  334.3 8.1 add.393
  342.3 12.8 %add.394 = f32[12,196,196]{1,2,0:T(8,128)} reshape(f32[12,14,14,14,14]{2,1,4,3,0:T(8,128)} %add.393) | data formatting | bytes 3687936 | tf_op jit(solution)/shard_map/add | solution.py:64
  355.1 9.0 add.397
  364.1 12.7 %add.398 = f32[12,196,196]{1,2,0:T(8,128)} reshape(f32[12,14,14,14,14]{2,1,4,3,0:T(8,128)} %add.397) | data formatting | bytes 3687936 | tf_op jit(solution)/shard_map/add | solution.py:64
  376.7 3.5 fusion.140
  383.9 9.0 multiply_convert_fusion.3
  392.8 2.7 convert_reduce_fusion.1
  395.5 2.4 multiply_reduce_fusion.3
  403.4 3.8 convolution_add_fusion.7
  410.6 3.1 copy.115
  413.6 12.7 %reshape.697 = f32[1,12,14,14,14,14]{5,4,3,2,1,0:T(8,128)} reshape(f32[12,196,196]{2,1,0:T(8,128)} %copy.115) | data formatting | bytes 3687936 | tf_op jit(solution)/shard_map/convert_element_type | solution.py:166
  426.4 11.0 %fusion.127 = (f32[12,14,14,14]{3,2,1,0:T(8,128)}, f32[12,14,14,14]{3,2,1,0:T(8,128)}) fusion(f32[1,12,14,14,14,14]{5,4,3,2,1,0:T(8,128)} %reshape.697), kind=kLoop, calls=%fused_computation.252 | loop fusion | flops 856128 | bytes 2107392 | tf_op jit(solution)/shard_map/reduce_sum | solution.py:167
  437.4 3.6 copy.139
  441.0 2.7 fusion.142
  447.4 3.6 copy.120
  457.0 4.3 convolution_add_fusion
  462.4 3.0 fusion.121
  465.5 5.3 convolution_add_fusion.2
  471.8 2.9 fusion.108
  474.7 5.3 convolution_add_fusion.1
  483.3 3.9 fusion.130
  496.8 42.1 %all-reduce.16 = (f32[768]{0:T(1024)S(1)}, f32[768]{0:T(1024)S(1)}, f32[2304]{0:T(1024)S(1)}, f32[27,64]{1,0:T(8,128)}, f32[27,64]{1,0:T(8,128)}, /*index=5*/f32...) all-reduce(f32[768]{0:T(1024)} %add.439, ...), channel_id=2, replica_groups=mesh['fsdp'=32] {'fsdp'}, use_global_device_ids=true, to_apply=%region_28.29.clone | all-reduce | flops 13440 | bytes 107520
  543.6 3.8 fusion.40
  547.5 3.8 fusion.41
  553.5 77.0 %reduce-scatter.5.cloned.1.call-done = f32[24,2304]{1,0:T(8,128)} async-done(((f32[768,2304]{1,0:T(8,128)}), f32[24,2304]{1,0:T(8,128)}) %reduce-scatter.5.cloned.1.call-update) | async-done | bytes 221200 | tf_op jit(solution)/shard_map/reduce_scatter | solution.py:343
  630.5 141.5 %reduce-scatter.9.cloned.1.call-done = f32[24,3072]{1,0:T(8,128)} async-done(((f32[768,3072]{1,0:T(8,128)}), f32[24,3072]{1,0:T(8,128)}) %reduce-scatter.9.cloned.1.call-update) | async-done | bytes 294928 | tf_op jit(solution)/shard_map/reduce_scatter | solution.py:349
  772.0 142.0 %reduce-scatter.11.cloned.1.call-done = f32[96,768]{1,0:T(8,128)} async-done(((f32[3072,768]{1,0:T(8,128)}), f32[96,768]{1,0:T(8,128)}) %reduce-scatter.11.cloned.1.call-update) | async-done | bytes 294928 | tf_op jit(solution)/shard_map/reduce_scatter | solution.py:351
  (436 shorter events, 99.3 us)
Async XLA Ops:
  7.2 61.8 %copy-start.5 = (bf16[392,768]{1,0:T(8,128)(2,1)S(1)}, bf16[392,768]{1,0:T(8,128)(2,1)}, u32[]{:S(2)}) copy-start(bf16[392,768]{1,0:T(8,128)(2,1)} %param.17) | copy-start | bytes 1806340
  7.2 67.9 %all-gather.5.cloned.1.call-start = ((), (), s32[]{:S(2)}) async-start(), calls=%async_computation.4 | async-start | bytes 3649536 | tf_op jit(solution)/shard_map/all_gather | solution.py:313
  8.9 126.7 %all-gather.7.cloned.1.call-start = ((), (), s32[]{:S(2)}) async-start(), calls=%async_computation.5 | async-start | bytes 1216512 | tf_op jit(solution)/shard_map/all_gather | solution.py:315
  10.5 186.8 %all-gather.9.cloned.1.call-start = ((), (), s32[]{:S(2)}) async-start(), calls=%async_computation.6 | async-start | bytes 4866048 | tf_op jit(solution)/shard_map/all_gather | solution.py:319
  12.2 250.9 %all-gather.11.cloned.1.call-start = ((), (), s32[]{:S(2)}) async-start(), calls=%async_computation.7 | async-start | bytes 4866048 | tf_op jit(solution)/shard_map/all_gather | solution.py:321
  13.9 539.5 %reduce-scatter.7.cloned.1.call-start = ((), (), s32[]{:S(2)}) async-start(), calls=%async_computation.9 | async-start | bytes 2433024 | tf_op jit(solution)/shard_map/reduce_scatter | solution.py:345
  64.9 13.2 %copy-start.103 = (f32[2304]{0:T(1024)}, f32[2304]{0:T(1024)S(1)}, u32[]{:S(2)}) copy-start(f32[2304]{0:T(1024)S(1)} %convert_element_type.326) | copy-start | bytes 27652
  67.1 11.0 %copy-start.71 = (f32[196]{0:T(256)}, f32[196]{0:T(256)S(1)}, u32[]{:S(2)}) copy-start(f32[196]{0:T(256)S(1)} %mul.426) | copy-start | bytes 2356
  67.1 11.0 %copy-start.62 = (s32[14,14]{0,1:T(8,128)}, s32[14,14]{0,1:T(8,128)S(1)}, u32[]{:S(2)}) copy-start(s32[14,14]{0,1:T(8,128)S(1)} %subtract_add_fusion) | copy-start | bytes 2356
  68.1 12.2 %copy-start.53 = (bf16[14,14,64,1]{2,1,3,0:T(8,128)(2,1)}, bf16[14,14,64,1]{2,1,3,0:T(8,128)(2,1)S(1)}, u32[]{:S(2)}) copy-start(bf16[14,14,64,1]{2,1,3,0:T(8,128)(2,1)S(1)} %fusion.43) | copy-start | bytes 75268
  69.0 257.9 %copy-start.51 = (bf16[14,14,64,1]{2,1,3,0:T(8,128)(2,1)}, bf16[14,14,64,1]{2,1,3,0:T(8,128)(2,1)S(1)}, u32[]{:S(2)}) copy-start(bf16[14,14,64,1]{2,1,3,0:T(8,128)(2,1)S(1)} %fusion.42) | copy-start | bytes 75268
  69.2 9.0 copy-start.91
  69.5 8.7 copy-start.117
  69.5 8.7 copy-start.113
  69.5 248.3 %copy-start.84 = (f32[196]{0:T(256)}, f32[196]{0:T(256)S(1)}, u32[]{:S(2)}) copy-start(f32[196]{0:T(256)S(1)} %get-tuple-element.107) | copy-start | bytes 2356
  80.3 5.7 copy-start.3
  94.9 12.8 %copy-start.38 = (f32[12,14,14,14]{2,1,3,0:T(8,128)S(1)}, f32[12,14,14,14]{2,1,3,0:T(8,128)}, u32[]{:S(2)}) copy-start(f32[12,14,14,14]{2,1,3,0:T(8,128)} %copy.111) | copy-start | bytes 395140
  135.6 71.6 %copy-start.61 = (bf16[12,64,196]{2,1,0:T(8,128)(2,1)}, bf16[12,64,196]{2,1,0:T(8,128)(2,1)S(1)}, u32[]{:S(2)}) copy-start(bf16[12,64,196]{2,1,0:T(8,128)(2,1)S(1)} %convolution_convert_fusion) | copy-start | bytes 903172
  137.7 134.5 %copy-start.77 = (f32[196]{0:T(256)}, f32[196]{0:T(256)S(1)}, u32[]{:S(2)}) copy-start(f32[196]{0:T(256)S(1)} %broadcast_multiply_fusion) | copy-start | bytes 2356
  139.8 123.3 %copy-start.72 = (f32[196]{0:T(256)S(1)}, f32[196]{0:T(256)}, u32[]{:S(2)}) copy-start(f32[196]{0:T(256)} %copy-done.71) | copy-start | bytes 2356
  263.1 6.7 copy-start.25
  263.1 6.7 copy-start.87
  263.1 6.7 copy-start.130
  272.5 5.2 copy-start.111
  342.3 12.8 %copy-start.39 = (f32[12,14,14,14]{2,1,3,0:T(8,128)S(1)}, f32[12,14,14,14]{2,1,3,0:T(8,128)}, u32[]{:S(2)}) copy-start(f32[12,14,14,14]{2,1,3,0:T(8,128)} %copy.104) | copy-start | bytes 395140
  376.7 18.8 %slice-start.2 = ((s8[4718592]{0:T(1024)(128)(4,1)}), s8[4194304]{0:T(1024)(128)(4,1)S(1)}, s32[]{:S(2)}) async-start(s8[4718592]{0:T(1024)(128)(4,1)} %bitcast.280), calls=%async_computation.14 | async-start | bytes 8388608
  381.2 11.6 %slice-start = ((s8[4718592]{0:T(1024)(128)(4,1)}), s8[4194304]{0:T(1024)(128)(4,1)S(1)}, s32[]{:S(2)}) async-start(s8[4718592]{0:T(1024)(128)(4,1)} %bitcast.278), calls=%async_computation.12 | async-start | bytes 8388608
  383.5 14.3 %copy-start.21 = (f32[196,768]{1,0:T(8,128)}, f32[196,768]{1,0:T(8,128)S(1)}, u32[]{:S(2)}) copy-start(f32[196,768]{1,0:T(8,128)S(1)} %get-tuple-element.94) | copy-start | bytes 1806340
  383.6 14.3 %copy-start.79 = (f32[196]{0:T(256)}, f32[196]{0:T(256)S(1)}, u32[]{:S(2)}) copy-start(f32[196]{0:T(256)S(1)} %broadcast_multiply_fusion.2) | copy-start | bytes 2356
  383.8 14.1 %copy-start.89 = (f32[196]{0:T(256)}, f32[196]{0:T(256)S(1)}, u32[]{:S(2)}) copy-start(f32[196]{0:T(256)S(1)} %fusion.101) | copy-start | bytes 2356
  383.9 9.0 copy-start.29
  383.9 9.0 slice-start.1
  383.9 11.7 %slice-start.3 = ((s8[4718592]{0:T(1024)(128)(4,1)}), s8[524288]{0:T(1024)(128)(4,1)S(1)}, s32[]{:S(2)}) async-start(s8[4718592]{0:T(1024)(128)(4,1)} %bitcast.280), calls=%async_computation.15 | async-start | bytes 1048576
  407.2 223.3 %reduce-scatter.5.cloned.1.call-start = ((), (), s32[]{:S(2)}) async-start(), calls=%async_computation.8 | async-start | bytes 7299072 | tf_op jit(solution)/shard_map/reduce_scatter | solution.py:343
  461.4 310.6 %reduce-scatter.9.cloned.1.call-start = ((), (), s32[]{:S(2)}) async-start(), calls=%async_computation.10 | async-start | bytes 9732096 | tf_op jit(solution)/shard_map/reduce_scatter | solution.py:349
  470.8 443.2 %reduce-scatter.11.cloned.1.call-start = ((), (), s32[]{:S(2)}) async-start(), calls=%async_computation.11 | async-start | bytes 9732096 | tf_op jit(solution)/shard_map/reduce_scatter | solution.py:351
  483.3 4.6 copy-start.31
  483.3 4.6 copy-start.36
  483.3 4.6 copy-start.60
  483.3 4.6 copy-start.83
  493.0 50.6 %copy-start.27 = (f32[196,768]{1,0:T(8,128)S(1)}, f32[196,768]{1,0:T(8,128)}, u32[]{:S(2)}) copy-start(f32[196,768]{1,0:T(8,128)} %copy-done.24) | copy-start | bytes 1806340
  493.0 50.6 %copy-start.43 = (bf16[196,3072]{1,0:T(8,128)(2,1)S(1)}, bf16[196,3072]{1,0:T(8,128)(2,1)}, u32[]{:S(2)}) copy-start(bf16[196,3072]{1,0:T(8,128)(2,1)} %get-tuple-element.73) | copy-start | bytes 3612676
  547.4 4.7 copy-start.119
  547.4 4.7 copy-start.32
  547.4 4.7 copy-start.34
  547.4 4.7 copy-start.47
  547.4 4.7 copy-start.108
  547.5 4.7 copy-start.110
  (96 other events, 224.4 us)
Sparse Core Ops, SparseCore 0:
  11.5 63.5 all-gather.4
  78.5 52.6 all-gather.6
  134.7 62.5 all-gather.8
  200.7 62.4 all-gather.10
  407.4 97.8 reduce-scatter.6
  512.3 118.1 reduce-scatter.4
  637.0 134.9 reduce-scatter.8
  779.4 134.4 reduce-scatter.10
where the time goes:
time: 925 us; the launch traced here: 921 us
  waiting for transfers between devices  480 us (52%)
  local copies, waits for them, and re-layouts  157 us (17%)
  matrix products  130 us (14%)
  blocking collectives  85.5 us (9%)
  other arithmetic  51.6 us (6%)
  between operations  16 us (2%)
    reduce_scatter x1, waiting for transfers between devices, per_device(): lax.psum_scatter(grad_totals[10], 'fsdp', scatter_dimension=0, tiled=True)  142 us
    reduce_scatter x1, waiting for transfers between devices, per_device(): lax.psum_scatter(grad_totals[8], 'fsdp', scatter_dimension=0, tiled=True)  141 us
    add x12, local copies, waits for them, and re-layouts, attention_scores(): direct.reshape(windows, HEADS, WIN, WIN, WIN, WIN) + rel_rows[..., :, None]  92.8 us
    unnamed x2, blocking collectives  85.5 us
    reduce_scatter x1, waiting for transfers between devices, per_device(): lax.psum_scatter(grad_totals[2], 'fsdp', scatter_dimension=0, tiled=True)  77 us
    all_gather x1, waiting for transfers between devices, per_device(): lax.all_gather(shards[8], 'fsdp', axis=0, tiled=True)  57.5 us
    all_gather x1, waiting for transfers between devices, per_device(): lax.all_gather(shards[10], 'fsdp', axis=0, tiled=True)  56 us
    convert_element_type x4, local copies, waits for them, and re-layouts, attention_back(): grad_scores.reshape(windows, HEADS, WIN, WIN, WIN, WIN).astype(jnp.float32)  29.2 us
  transfers between devices with their start and end apart: 8, of which 6 were waited for; matrix products, arithmetic and copies ran while one was open for 20% of the time, Pallas kernels for 0%

commit v1 on v0

v1 whole, which is shorter than its diff:
```python
import jax
import jax.numpy as jnp
import numpy as np
from jax import lax
from jax.experimental import pallas as pl
from jax.experimental.pallas import tpu as pltpu
from jax.sharding import PartitionSpec as P

D = 768
HEADS = 12
HEAD_DIM = 64
FF = 3072
WIN = 14
NWS = 5
EDGE = 8
LENGTH = WIN * WIN
PAIRS = HEADS // 2
BLOCK = 200
SCALE = HEAD_DIM ** (-0.5)
EPS = 1e-06
ONE_LANE = 60
BF = jnp.bfloat16
F32 = jnp.float32


def window_constants():
    onehot = np.zeros((2, BLOCK, 128), np.float32)
    shift = np.zeros((2, BLOCK, 128), np.int32)
    for win in range(2):
        for row in range(BLOCK):
            slot = row - 4 * win
            if not 0 <= slot < LENGTH:
                onehot[win, row, ONE_LANE] = onehot[win, row, 64 + ONE_LANE] = -1e30
                continue
            y, x = divmod(slot, WIN)
            for base in (0, 64):
                for lane in (y, WIN + y, 32 + x, 32 + WIN + x):
                    onehot[win, row, base + lane] = 1.0
                shift[win, row, base : base + 32] = WIN - 1 - y
                shift[win, row, base + 32 : base + 64] = WIN - 1 - x
    return onehot, shift


def table_lanes(rel_pos_h, rel_pos_w):
    flip = jnp.concatenate(
        (
            jnp.pad(rel_pos_h[::-1].T, ((0, 0), (0, 5))),
            jnp.pad(rel_pos_w[::-1].T, ((0, 0), (0, 5))),
        ),
        axis=1,
    ).astype(BF)
    nothing = jnp.zeros_like(flip)
    return jnp.concatenate(
        (jnp.concatenate((nothing, flip), axis=1), jnp.concatenate((flip, nothing), axis=1)), axis=0
    )


def table_grads(lanes_grad):
    folded = lanes_grad[64:, :64] + lanes_grad[:64, 64:]
    count = 2 * WIN - 1
    return folded[:count][::-1], folded[32 : 32 + count][::-1]


def dot_nn(a, b):
    return jnp.dot(a, b, preferred_element_type=F32)


def dot_nt(a, b):
    return lax.dot_general(a, b, (((1,), (1,)), ((), ())), preferred_element_type=F32)


def dot_tn(a, b):
    return lax.dot_general(a, b, (((0,), (0,)), ((), ())), preferred_element_type=F32)


def lane_facts():
    lane = lax.broadcasted_iota(jnp.int32, (BLOCK, 128), 1)
    row = lax.broadcasted_iota(jnp.int32, (BLOCK, 128), 0)
    return lane, row, lane < 64, (lane & 31) < WIN


def row_valid(row, win):
    return row < LENGTH if win == 0 else row >= BLOCK - LENGTH


def merge_windows(first, second):
    return jnp.concatenate((first[:192], first[192:] + second[:8], second[8:]), axis=0)


def attn_fwd_kernel(q_ref, k_ref, v_ref, table_ref, onehot_ref, shift_ref, mixed_ref, probs_ref):
    lane, row, low_half, rel_lanes = lane_facts()
    one_lane = (lane & 63) == ONE_LANE
    mixed = []
    for win in range(2):
        rows = pl.ds(192 * win, BLOCK)
        q = q_ref[rows, :]
        k = k_ref[rows, :].astype(F32)
        v = v_ref[rows, :]
        rel = dot_nn(q, table_ref[...])
        shift = shift_ref[win]
        for bit in range(4):
            rel = jnp.where((shift & (1 << bit)) != 0, pltpu.roll(rel, 128 - (1 << bit), 1), rel)
        rel = jnp.where(rel_lanes, rel, 0.0)
        rel_top = rel.astype(BF).astype(F32)
        extra = rel_top + pltpu.roll(rel - rel_top, WIN, 1)
        extra = jnp.where(one_lane, 1.0, extra)
        scaled = q.astype(F32) * SCALE
        onehot = onehot_ref[win].astype(F32)
        halves = []
        for head in range(2):
            own = low_half if head == 0 else jnp.logical_not(low_half)
            left = jnp.where(own, scaled, extra).astype(BF)
            right = jnp.where(own, k, onehot).astype(BF)
            scores = dot_nt(left, right)
            expon = jnp.exp(scores - jnp.max(scores, axis=-1, keepdims=True))
            probs = expon * (1.0 / jnp.sum(expon, axis=-1, keepdims=True))
            probs_ref[0, 2 * win + head] = probs
            halves.append(dot_nn(probs.astype(BF), v))
        both = jnp.where(low_half, halves[0], halves[1])
        mixed.append(jnp.where(row_valid(row, win), both, 0.0))
    mixed_ref[...] = merge_windows(*mixed).astype(BF)


def attn_bwd_kernel(
    q_ref,
    k_ref,
    v_ref,
    grad_ref,
    probs_ref,
    table_ref,
    onehot_ref,
    shift_ref,
    grad_qkv_ref,
    table_grad_ref,
):
    pair = pl.program_id(0)
    lane, row, low_half, rel_lanes = lane_facts()

    @pl.when(pair == 0)
    def _():
        table_grad_ref[...] = jnp.zeros_like(table_grad_ref)

    parts = ([], [], [])
    table_total = jnp.zeros((128, 128), F32)
    for win in range(2):
        rows = pl.ds(192 * win, BLOCK)
        q = q_ref[rows, :]
        k = k_ref[rows, :].astype(F32)
        v = v_ref[rows, :]
        grad = jnp.where(row_valid(row, win), grad_ref[rows, :].astype(F32), 0.0)
        grad_low = grad.astype(BF)
        onehot = onehot_ref[win].astype(F32)
        by_query, by_key, by_value = [], [], []
        for head in range(2):
            own = low_half if head == 0 else jnp.logical_not(low_half)
            right = jnp.where(own, k, onehot).astype(BF)
            probs = probs_ref[0, 2 * win + head]
            grad_probs = dot_nt(jnp.where(own, grad, 0.0).astype(BF), v)
            row_dot = jnp.sum(probs * grad_probs, axis=-1, keepdims=True)
            grad_scores = (probs * (grad_probs - row_dot)).astype(BF)
            by_value.append(dot_tn(probs.astype(BF), grad_low))
            by_query.append(dot_nn(grad_scores, right))
            by_key.append(dot_tn(grad_scores, q))
        rel = jnp.where(rel_lanes, jnp.where(low_half, by_query[1], by_query[0]), 0.0)
        shift = shift_ref[win]
        for bit in range(4):
            rel = jnp.where((shift & (1 << bit)) != 0, pltpu.roll(rel, 1 << bit, 1), rel)
        rel_top = rel.astype(BF)
        rel_rest = (rel - rel_top.astype(F32)).astype(BF)
        table = table_ref[...]
        from_rel = dot_nt(rel_top, table) + dot_nt(rel_rest, table)
        table_total += dot_tn(rel_top, q) + dot_tn(rel_rest, q)
        parts[0].append(jnp.where(low_half, by_query[0], by_query[1]) * SCALE + from_rel)
        parts[1].append(jnp.where(low_half, by_key[0], by_key[1]) * SCALE)
        parts[2].append(jnp.where(low_half, by_value[0], by_value[1]))
    for block in range(3):
        at = pl.multiple_of(block * D + pair * 128, 128)
        grad_qkv_ref[:, pl.ds(at, 128)] = merge_windows(*parts[block]).astype(BF)
    table_grad_ref[...] += table_total


def attention_specs(rows):
    column = lambda block: pl.BlockSpec((rows, 128), lambda pair: (0, block * PAIRS + pair))
    whole = lambda *shape: pl.BlockSpec(shape, lambda pair: (0,) * len(shape))
    return (
        [column(0), column(1), column(2)],
        [whole(128, 128), whole(2, BLOCK, 128), whole(2, BLOCK, 128)],
        pl.BlockSpec((1, 4, BLOCK, BLOCK), lambda pair: (pair, 0, 0, 0)),
        whole,
    )


def attention(qkv, table, onehot, shift):
    rows = qkv.shape[0]
    columns, constants, probs_spec, _ = attention_specs(rows)
    return pl.pallas_call(
        attn_fwd_kernel,
        grid=(PAIRS,),
        in_specs=columns + constants,
        out_specs=[pl.BlockSpec((rows, 128), lambda pair: (0, pair)), probs_spec],
        out_shape=[
            jax.ShapeDtypeStruct((rows, D), BF),
            jax.ShapeDtypeStruct((PAIRS, 4, BLOCK, BLOCK), F32),
        ],
        compiler_params=pltpu.CompilerParams(vmem_limit_bytes=32 * 1024 * 1024),
        name="attention",
    )(qkv, qkv, qkv, table, onehot, shift)


def attention_back(qkv, grad_mixed, probs, table, onehot, shift):
    rows = qkv.shape[0]
    columns, constants, probs_spec, whole = attention_specs(rows)
    return pl.pallas_call(
        attn_bwd_kernel,
        grid=(PAIRS,),
        in_specs=columns + [pl.BlockSpec((rows, 128), lambda pair: (0, pair)), probs_spec] + constants,
        out_specs=[whole(rows, 3 * D), whole(128, 128)],
        out_shape=[
            jax.ShapeDtypeStruct((rows, 3 * D), BF),
            jax.ShapeDtypeStruct((128, 128), F32),
        ],
        compiler_params=pltpu.CompilerParams(vmem_limit_bytes=32 * 1024 * 1024),
        name="attention_back",
    )(qkv, qkv, qkv, grad_mixed, probs, table, onehot, shift)


def slot_mask(window_pos):
    row_win = window_pos // NWS
    col_win = window_pos % NWS
    rows_ok = jnp.where(row_win == NWS - 1, EDGE, WIN)
    cols_ok = jnp.where(col_win == NWS - 1, EDGE, WIN)
    positions = jnp.arange(WIN, dtype=jnp.int32)
    inside = (positions[None, :, None] < rows_ok[:, None, None]) & (
        positions[None, None, :] < cols_ok[:, None, None]
    )
    return inside.reshape(-1, 1).astype(F32)


def normalise(values):
    centred = values - jnp.mean(values, axis=-1, keepdims=True)
    rstd = lax.rsqrt(jnp.mean(centred * centred, axis=-1, keepdims=True) + EPS)
    return centred * rstd, rstd


def normalise_back(grad, hat, rstd, gain):
    grad_hat = grad * gain
    return rstd * (
        grad_hat
        - jnp.mean(grad_hat, axis=-1, keepdims=True)
        - hat * jnp.mean(grad_hat * hat, axis=-1, keepdims=True)
    )


def normal_cdf(values):
    return 0.5 * (1.0 + lax.erf(values * np.float32(np.sqrt(0.5))))


def normal_pdf(values):
    return np.float32(1.0 / np.sqrt(2.0 * np.pi)) * jnp.exp(-0.5 * values * values)


def gather(shard):
    return lax.all_gather(shard, "fsdp", axis=0, tiled=True)


def scatter_sum(partial):
    return lax.psum_scatter(partial, "fsdp", scatter_dimension=0, tiled=True)


def per_device(
    tokens,
    window_pos,
    norm1_gain,
    norm1_bias,
    qkv_weight,
    qkv_bias,
    rel_pos_h,
    rel_pos_w,
    proj_weight,
    proj_bias,
    norm2_gain,
    norm2_bias,
    lin1_weight,
    lin1_bias,
    lin2_weight,
    lin2_bias,
    out_grad,
):
    vectors = (
        norm1_gain,
        norm1_bias,
        qkv_bias,
        proj_bias,
        norm2_gain,
        norm2_bias,
        lin1_bias,
        lin2_bias,
    )
    sizes = [v.shape[0] for v in vectors]
    count = sum(sizes)
    shard_rows = qkv_weight.shape[0]
    packed = jnp.pad(
        jnp.concatenate(vectors).astype(BF), (0, shard_rows * 128 - count)
    ).reshape(shard_rows, 128)
    chunk_one = gather(
        jnp.concatenate((qkv_weight.astype(BF), proj_weight.astype(BF), packed), axis=1)
    )
    w_qkv = chunk_one[:, : 3 * D]
    w_proj = chunk_one[:, 3 * D : 4 * D]
    small = chunk_one[:, 4 * D :].reshape(-1, shard_rows * 128)[:, :count].astype(F32)
    edges = np.cumsum([0] + sizes)
    gain_one, bias_one, b_qkv, b_proj, gain_two, bias_two, b_up, b_down = (
        small[:, lo:hi].reshape(-1) for lo, hi in zip(edges[:-1], edges[1:])
    )
    w_up = gather(lin1_weight.astype(BF))
    w_down = gather(lin2_weight.astype(BF))

    onehot, shift = window_constants()
    onehot = jnp.asarray(onehot, BF)
    shift = jnp.asarray(shift)
    table = table_lanes(rel_pos_h, rel_pos_w)
    live = slot_mask(window_pos)

    inputs = tokens.astype(F32)
    hat_one, rstd_one = normalise(inputs)
    normed_one = ((hat_one * gain_one + bias_one) * live).astype(BF)
    qkv = (dot_nn(normed_one, w_qkv) + b_qkv).astype(BF)
    mixed, probs = attention(qkv, table, onehot, shift)
    residual = inputs + dot_nn(mixed, w_proj) + b_proj
    hat_two, rstd_two = normalise(residual)
    normed_two = (hat_two * gain_two + bias_two).astype(BF)
    hidden = dot_nn(normed_two, w_up) + b_up
    cdf = normal_cdf(hidden)
    active = (hidden * cdf).astype(BF)
    slope = cdf + hidden * normal_pdf(hidden)
    grad_out = out_grad.astype(F32) * live
    grad_branch = grad_out.astype(BF)
    grad_w_down = dot_tn(active, grad_branch).astype(BF)
    own_down = scatter_sum(grad_w_down)
    output = ((residual + dot_nn(active, w_down) + b_down) * live).astype(BF)

    grad_hidden = (dot_nt(grad_branch, w_down) * slope).astype(BF)
    grad_w_up = dot_tn(normed_two, grad_hidden).astype(BF)
    own_up = scatter_sum(grad_w_up)
    grad_normed_two = dot_nt(grad_hidden, w_up)
    grad_residual = grad_out + normalise_back(grad_normed_two, hat_two, rstd_two, gain_two)
    grad_attn = grad_residual.astype(BF)
    grad_w_proj = dot_tn(mixed, grad_attn).astype(BF)
    grad_mixed = dot_nt(grad_attn, w_proj).astype(BF)
    grad_qkv, lanes_grad = attention_back(qkv, grad_mixed, probs, table, onehot, shift)
    grad_w_qkv = dot_tn(normed_one, grad_qkv).astype(BF)
    own_attn = scatter_sum(jnp.concatenate((grad_w_qkv, grad_w_proj), axis=1))
    grad_normed_one = dot_nt(grad_qkv, w_qkv) * live
    tokens_grad = (
        grad_residual + normalise_back(grad_normed_one, hat_one, rstd_one, gain_one)
    ).astype(BF)

    totals = (
        jnp.sum(grad_normed_one * hat_one, axis=0),
        jnp.sum(grad_normed_one, axis=0),
        jnp.sum(grad_qkv.astype(F32), axis=0),
        jnp.sum(grad_attn.astype(F32), axis=0),
        jnp.sum(grad_normed_two * hat_two, axis=0),
        jnp.sum(grad_normed_two, axis=0),
        jnp.sum(grad_hidden.astype(F32), axis=0),
        jnp.sum(grad_branch.astype(F32), axis=0),
    )
    small_total = lax.psum(jnp.concatenate(totals + (lanes_grad.reshape(-1),)), "fsdp")
    me = lax.axis_index("fsdp")
    owned, at = [], 0
    for size, total in zip(sizes, totals):
        owned.append(lax.dynamic_slice(small_total, (at + me * size,), (size,)))
        at += total.shape[0]
    table_h, table_w = table_grads(small_total[at:].reshape(128, 128))

    return (
        output,
        tokens_grad,
        owned[0],
        owned[1],
        own_attn[:, : 3 * D].astype(F32),
        owned[2],
        table_h,
        table_w,
        own_attn[:, 3 * D :].astype(F32),
        owned[3],
        owned[4],
        owned[5],
        own_up.astype(F32),
        owned[6],
        own_down.astype(F32),
        owned[7],
    )


def solution(mesh):
    rows = P("fsdp", None)
    line = P("fsdp")
    return jax.shard_map(
        per_device,
        mesh=mesh,
        in_specs=(
            rows,
            line,
            line,
            line,
            rows,
            line,
            P(),
            P(),
            rows,
            line,
            line,
            line,
            rows,
            line,
            rows,
            line,
            rows,
        ),
        out_specs=(
            rows,
            rows,
            line,
            line,
            rows,
            line,
            P(),
            P(),
            rows,
            line,
            line,
            line,
            rows,
            line,
            rows,
            line,
        ),
        check_vma=False,
    )
```

time: 925 us -> 714 us (0.77)
  local copies, waits for them, and re-layouts: 157 us -> 18.3 us
  waiting for transfers between devices: 480 us -> 580 us
  blocking collectives: 85.5 us -> 0 us
  matrix products: 130 us -> 49.1 us
  other arithmetic: 51.6 us -> 22.7 us
  Pallas kernels: 0 us -> 27.8 us
    add x15 -> x6, local copies, waits for them, and re-layouts: 96.3 us -> 0.47 us  [the longest x1 0.08 us: per_device(): qkv = (dot_nn(normed_one, w_qkv) + b_qkv).astype(BF)]
    psum x0 -> x1, waiting for transfers between devices: none -> 88.6 us  [per_device(): lax.psum(jnp.concatenate(totals + (lanes_grad.reshape(-1),)), 'fsdp')]
    unnamed x2 -> x0, blocking collectives: 85.5 us -> none
    dot_general x54 -> x12, matrix products: 130 us -> 49.1 us  [the longest x4 17.6 us: dot_tn(): lax.dot_general(a, b, (((0,), (0,)), ((), ())), preferred_element_type=F32)]
    all_gather x4 -> x3, waiting for transfers between devices: 119 us -> 165 us  [gather(): return lax.all_gather(shard, 'fsdp', axis=0, tiled=True)]
    reduce_scatter x4 -> x3, waiting for transfers between devices: 361 us -> 326 us  [scatter_sum(): return lax.psum_scatter(partial, 'fsdp', scatter_dimension=0, tiled=True)]
    convert_element_type x8 -> x1, local copies, waits for them, and re-layouts: 33.1 us -> 0.1 us  [slot_mask(): return inside.reshape(-1, 1).astype(F32)]
    pallas_call x0 -> x2, Pallas kernels: none -> 27.8 us  [the longest x1 15.2 us: attention_back(): pl.pallas_call(attn_bwd_kernel, grid=(PAIRS,), in_specs=columns + [pl.Blo...]
  transfers between devices with their start and end apart: 8 -> 7, of which waited for: 6 -> 7; matrix products, arithmetic and copies ran while one was open for 20% -> 8% of each run, Pallas kernels for 0% -> 2%
where the time goes in v1:
time: 714 us; the launch traced here: 713 us
  waiting for transfers between devices  580 us (81%)
  matrix products  49.1 us (7%)
  Pallas kernels  27.8 us (4%)
  other arithmetic  22.7 us (3%)
  local copies, waits for them, and re-layouts  18.3 us (3%)
  between operations  14.7 us (2%)
    reduce_scatter x3, waiting for transfers between devices, scatter_sum(): return lax.psum_scatter(partial, 'fsdp', scatter_dimension=0, tiled=True)  326 us
    all_gather x3, waiting for transfers between devices, gather(): return lax.all_gather(shard, 'fsdp', axis=0, tiled=True)  165 us
    psum x1, waiting for transfers between devices, per_device(): lax.psum(jnp.concatenate(totals + (lanes_grad.reshape(-1),)), 'fsdp')  88.6 us
    dot_general x4, matrix products, dot_tn(): lax.dot_general(a, b, (((0,), (0,)), ((), ())), preferred_element_type=F32)  17.6 us
    dot_general x4, matrix products, dot_nn(): return jnp.dot(a, b, preferred_element_type=F32)  17.6 us
    pallas_call x1, Pallas kernels, attention_back(): pl.pallas_call(attn_bwd_kernel, grid=(PAIRS,), in_specs=columns + [pl.Blo...  15.2 us
  transfers between devices with their start and end apart: 7, of which 7 were waited for; matrix products, arithmetic and copies ran while one was open for 8% of the time, Pallas kernels for 2%

profile of v1, /device:TPU:0, one launch (start us, length us, event | category | flops | bytes accessed | tf_op | source)
XLA Modules:
  0.0 712.9 jit_solution(5495309698572029397)
XLA Ops:
  7.3 1.0 convert_element_type.106
  8.3 0.9 convert_element_type.107
  9.2 0.7 convert.37
  9.9 0.7 convert.38
  10.5 0.7 convert.39
  11.2 0.7 convert.40
  11.8 0.7 convert.41
  14.6 0.7 pad_maximum_fusion.1
  15.3 1.6 convert_element_type.114
  17.1 0.7 convert_element_type.116
  19.2 63.3 %all-gather.4.cloned.1.call-done = bf16[768,3200]{1,0:T(8,128)(2,1)} async-done(((bf16[24,3200]{1,0:T(8,128)(2,1)}), bf16[768,3200]{1,0:T(8,128)(2,1)}) %all-gather.4.cloned.1.call-update) | async-done | bytes 4915216 | tf_op jit(solution)/shard_map/all_gather | solution.py:263
  82.5 0.9 slice.87
  84.4 3.8 fusion.6.q_ref.k_ref.v_ref
  88.2 12.7 %attention.1 = (bf16[392,768]{1,0:T(8,128)(2,1)S(1)}, f32[6,4,200,200]{3,2,1,0:T(8,128)S(1)}) custom-call(bf16[392,2304]{1,0:T(8,128)(2,1)S(1)} %fusion.6.q_ref.k_ref.v_ref, bf16[392,2304]{1,0:T(8,128)(2,1)S(1)} %fusion.6.q_ref.k_ref.v_ref, bf16[392,2304]{1,0:T(8,128)(2,1)S(1)} %fusion.6.q_ref.k_ref.v_ref, bf16[128,128]{1,0:T(8,128)(2,1)S(1)} %fusion.38.table_ref, ...), custom_call_target="tpu_custom_call" | custom-call | tf_op jit(solution)/shard_map/attention/pallas_call | solution.py:196
  100.9 2.2 copy-done
  103.2 2.0 fusion.52
  105.2 1.0 copy-done.9
  106.6 41.8 %all-gather.6.cloned.1.call-done = bf16[768,3072]{1,0:T(8,128)(2,1)} async-done(((bf16[24,3072]{1,0:T(8,128)(2,1)}), bf16[768,3072]{1,0:T(8,128)(2,1)}) %all-gather.6.cloned.1.call-update) | async-done | bytes 4718608 | tf_op jit(solution)/shard_map/all_gather | solution.py:263
  148.4 6.4 multiply_convert_fusion
  154.8 59.5 %all-gather.8.cloned.1.call-done = bf16[3072,768]{1,0:T(8,128)(2,1)} async-done(((bf16[96,768]{1,0:T(8,128)(2,1)}), bf16[3072,768]{1,0:T(8,128)(2,1)}) %all-gather.8.cloned.1.call-update) | async-done | bytes 4718608 | tf_op jit(solution)/shard_map/all_gather | solution.py:263
  214.4 6.2 convert_reduce_fusion
  220.7 2.5 multiply_reduce_fusion
  223.8 2.4 convolution_convert_fusion.4.grad_ref
  226.2 2.4 copy-done.1
  228.6 15.2 %attention_back.1 = (bf16[392,2304]{1,0:T(8,128)(2,1)S(1)}, f32[128,128]{1,0:T(8,128)S(1)}) custom-call(bf16[392,2304]{1,0:T(8,128)(2,1)S(1)} %fusion.6.q_ref.k_ref.v_ref, bf16[392,2304]{1,0:T(8,128)(2,1)S(1)} %fusion.6.q_ref.k_ref.v_ref, bf16[392,2304]{1,0:T(8,128)(2,1)S(1)} %fusion.6.q_ref.k_ref.v_ref, ...), custom_call_target="tpu_custom_call" | custom-call | tf_op jit(solution)/shard_map/attention_back/pallas_call | solution.py:213
  244.1 2.9 fusion.31
  247.9 6.3 convolution_convert_fusion.1
  254.2 2.2 convolution_convert_fusion.3
  256.4 2.3 convolution_convert_fusion.2
  258.8 2.8 pad_maximum_fusion
  261.9 0.7 copy-done.15
  262.7 6.8 convolution_convert_fusion
  269.6 1.1 copy-done.7
  271.1 1.3 fusion.30
  272.4 1.0 copy-done.23
  273.4 5.3 fusion.22
  278.7 88.6 %all-reduce.7.cloned.1.call-done = f32[26368]{0:T(1024)} async-done(((f32[26368]{0:T(1024)}), f32[26368]{0:T(1024)}) %all-reduce.7.cloned.1.call-update) | async-done | bytes 105488 | tf_op jit(solution)/shard_map/psum | solution.py:368
  367.3 0.9 slice_bitcast_fusion
  369.5 1.3 dynamic_slice.26
  370.8 1.3 dynamic_slice.30
  372.0 1.4 fusion.49
  373.4 107.1 %reduce-scatter.6.cloned.1.call-done = bf16[24,3072]{1,0:T(8,128)(2,1)} async-done(((bf16[768,3072]{1,0:T(8,128)(2,1)}), bf16[24,3072]{1,0:T(8,128)(2,1)}) %reduce-scatter.6.cloned.1.call-update) | async-done | bytes 147472 | tf_op jit(solution)/shard_map/reduce_scatter | solution.py:267
  480.5 1.6 convert_element_type.133
  482.1 110.7 %reduce-scatter.4.cloned.1.call-done = bf16[24,3072]{1,0:T(8,128)(2,1)} async-done(((bf16[768,3072]{1,0:T(8,128)(2,1)}), bf16[24,3072]{1,0:T(8,128)(2,1)}) %reduce-scatter.4.cloned.1.call-update) | async-done | bytes 147472 | tf_op jit(solution)/shard_map/reduce_scatter | solution.py:267
  592.8 1.4 slice_convert_fusion.1
  594.2 1.6 slice_convert_fusion
  595.8 108.5 %reduce-scatter.8.cloned.1.call-done = bf16[96,768]{1,0:T(8,128)(2,1)} async-done(((bf16[3072,768]{1,0:T(8,128)(2,1)}), bf16[96,768]{1,0:T(8,128)(2,1)}) %reduce-scatter.8.cloned.1.call-update) | async-done | bytes 147472 | tf_op jit(solution)/shard_map/reduce_scatter | solution.py:267
  704.4 1.6 convert_element_type.135
  (116 shorter events, 8.7 us)
Async XLA Ops:
  7.2 9.9 %copy-start.16 = (f32[96,768]{1,0:T(8,128)S(1)}, f32[96,768]{1,0:T(8,128)}, u32[]{:S(2)}) copy-start(f32[96,768]{1,0:T(8,128)} %param.33) | copy-start | bytes 884740
  7.2 10.6 %copy-start.21 = (s32[2]{0:T(128)S(1)}, s32[2]{0:T(128)}, u32[]{:S(2)}) copy-start(s32[2]{0:T(128)} %param.20) | copy-start | bytes 28
  7.2 10.9 %copy-start.18 = (f32[27,64]{1,0:T(8,128)S(1)}, f32[27,64]{1,0:T(8,128)}, u32[]{:S(2)}) copy-start(f32[27,64]{1,0:T(8,128)} %param.26) | copy-start | bytes 20740
  7.2 11.1 %copy-start.19 = (f32[27,64]{1,0:T(8,128)S(1)}, f32[27,64]{1,0:T(8,128)}, u32[]{:S(2)}) copy-start(f32[27,64]{1,0:T(8,128)} %param.25) | copy-start | bytes 20740
  7.2 11.4 %copy-start.8 = (bf16[392,768]{1,0:T(8,128)(2,1)S(1)}, bf16[392,768]{1,0:T(8,128)(2,1)}, u32[]{:S(2)}) copy-start(bf16[392,768]{1,0:T(8,128)(2,1)} %param.19) | copy-start | bytes 1806340
  7.2 75.3 %all-gather.4.cloned.1.call-start = ((), (), s32[]{:S(2)}) async-start(), calls=%async_computation.3 | async-start | bytes 5068800 | tf_op jit(solution)/shard_map/all_gather | solution.py:263
  15.3 133.1 %all-gather.6.cloned.1.call-start = ((), (), s32[]{:S(2)}) async-start(), calls=%async_computation.4 | async-start | bytes 4866048 | tf_op jit(solution)/shard_map/all_gather | solution.py:263
  17.0 197.4 %all-gather.8.cloned.1.call-start = ((), (), s32[]{:S(2)}) async-start(), calls=%async_computation.5 | async-start | bytes 4866048 | tf_op jit(solution)/shard_map/all_gather | solution.py:263
  17.8 349.5 %all-reduce.7.cloned.1.call-start = ((), (), s32[]{:S(2)}) async-start(), calls=%async_computation.6 | async-start | bytes 212992 | tf_op jit(solution)/shard_map/psum | solution.py:368
  84.4 3.8 copy-start.4
  84.4 3.8 copy-start.5
  100.9 2.3 copy-start
  105.2 1.1 copy-start.9
  214.4 6.2 copy-start.10
  214.4 6.2 copy-start.20
  214.4 29.7 %slice-start = ((s8[4915200]{0:T(1024)(128)(4,1)}), s8[4194304]{0:T(1024)(128)(4,1)S(1)}, s32[]{:S(2)}) async-start(s8[4915200]{0:T(1024)(128)(4,1)} %bitcast.24), calls=%async_computation.10 | async-start | bytes 8388608
  220.6 2.6 copy-start.22
  220.6 2.6 copy-start.14
  220.6 23.5 %slice-start.1 = ((s8[4915200]{0:T(1024)(128)(4,1)}), s8[720896]{0:T(1024)(128)(4,1)S(1)}, s32[]{:S(2)}) async-start(s8[4915200]{0:T(1024)(128)(4,1)} %bitcast.24), calls=%async_computation.11 | async-start | bytes 1441792
  223.8 2.4 copy-start.6
  226.2 2.4 copy-start.1
  243.8 3.2 copy-start.2
  244.1 3.7 copy-start.11
  247.1 0.6 copy-start.17
  247.8 232.7 %reduce-scatter.6.cloned.1.call-start = ((), (), s32[]{:S(2)}) async-start(), calls=%async_computation.8 | async-start | bytes 4866048 | tf_op jit(solution)/shard_map/reduce_scatter | solution.py:267
  254.1 2.3 copy-start.3
  254.1 338.7 %reduce-scatter.4.cloned.1.call-start = ((), (), s32[]{:S(2)}) async-start(), calls=%async_computation.7 | async-start | bytes 4866048 | tf_op jit(solution)/shard_map/reduce_scatter | solution.py:267
  261.6 1.1 copy-start.15
  261.6 442.8 %reduce-scatter.8.cloned.1.call-start = ((), (), s32[]{:S(2)}) async-start(), calls=%async_computation.9 | async-start | bytes 4866048 | tf_op jit(solution)/shard_map/reduce_scatter | solution.py:267
  269.4 1.3 copy-start.7
  269.4 1.6 copy-start.13
  271.1 1.3 copy-start.12
  271.1 2.3 copy-start.23
Sparse Core Ops, SparseCore 0:
  15.4 67.0 all-gather.3
  86.0 62.3 all-gather.5
  151.9 62.4 all-gather.7
  247.9 119.3 all-reduce.6
  372.6 107.8 reduce-scatter.5
  486.7 106.0 reduce-scatter.3
  598.3 106.0 reduce-scatter.7

commit v2 on v1

v2 whole, which is shorter than its diff:
```python
import functools

import jax
import jax.numpy as jnp
import numpy as np
from jax import lax
from jax.experimental import pallas as pl
from jax.experimental.pallas import tpu as pltpu
from jax.sharding import PartitionSpec as P

D = 768
HEADS = 12
HEAD_DIM = 64
FF = 3072
WIN = 14
NWS = 5
EDGE = 8
LENGTH = WIN * WIN
PAIRS = HEADS // 2
BLOCK = 200
SCALE = HEAD_DIM ** (-0.5)
EPS = 1e-06
LANES = 256
BF = jnp.bfloat16
F32 = jnp.float32


def window_constants():
    onehot = np.zeros((2, BLOCK, 128), np.float32)
    shift = np.zeros((2, 16, LANES), np.int32)
    for win in range(2):
        for row in range(BLOCK):
            slot = row - 4 * win
            if not 0 <= slot < LENGTH:
                onehot[win, row, 63] = onehot[win, row, 127] = -1e30
                continue
            y, x = divmod(slot, WIN)
            for base in (0, 64):
                for lane in (y, 16 + y, 32 + x, 48 + x):
                    onehot[win, row, base + lane] = 1.0
            shift[win, :8, row] = WIN - 1 - y
            shift[win, 8:, row] = WIN - 1 - x
    return onehot, shift


def table_lanes(rel_pos_h, rel_pos_w):
    flip = jnp.concatenate(
        (
            jnp.pad(rel_pos_h[::-1], ((0, 5), (0, 0))),
            jnp.pad(rel_pos_w[::-1], ((0, 5), (0, 0))),
        ),
        axis=0,
    ).astype(BF) * BF(1.0 / SCALE)
    nothing = jnp.zeros_like(flip)
    return jnp.concatenate(
        (jnp.concatenate((nothing, flip), axis=1), jnp.concatenate((flip, nothing), axis=1)), axis=0
    )


def table_grads(lanes_grad):
    folded = (lanes_grad[64:, :64] + lanes_grad[:64, 64:]) * np.float32(1.0 / SCALE)
    count = 2 * WIN - 1
    return folded[:count][::-1], folded[32 : 32 + count][::-1]


def dot_nn(a, b):
    return jnp.dot(a, b, preferred_element_type=F32)


def dot_nt(a, b):
    return lax.dot_general(a, b, (((1,), (1,)), ((), ())), preferred_element_type=F32)


def dot_tn(a, b):
    return lax.dot_general(a, b, (((0,), (0,)), ((), ())), preferred_element_type=F32)


def low_half():
    return lax.broadcasted_iota(jnp.int32, (BLOCK, 128), 1) < 64


def row_valid(win):
    row = lax.broadcasted_iota(jnp.int32, (BLOCK, 128), 0)
    return row < LENGTH if win == 0 else row >= BLOCK - LENGTH


def merge_windows(first, second):
    return jnp.concatenate((first[:192], first[192:] + second[:8], second[8:]), axis=0)


def pad_rows(values):
    return jnp.concatenate((values, jnp.zeros((LANES - BLOCK, 128), F32)), axis=0)


def bit_masks(shift, rows):
    shift = jnp.broadcast_to(shift[:1], (rows, LANES))
    return [(shift & (1 << bit)) != 0 for bit in range(4)]


def skew(values, masks):
    values = jnp.where(masks[3], values[8:], values[:24])
    values = jnp.where(masks[2], pltpu.roll(values, 20, 0), values)
    values = jnp.where(masks[1], pltpu.roll(values, 22, 0), values)[:16]
    return jnp.where(masks[0][:16], pltpu.roll(values, 15, 0), values)


def unskew(values, masks):
    nothing = jnp.zeros((8, LANES), F32)
    values = jnp.concatenate((values, nothing), axis=0)
    for bit in range(3):
        values = jnp.where(masks[bit], pltpu.roll(values, 1 << bit, 0), values)
    return jnp.concatenate(
        (
            jnp.where(masks[3][:8], 0.0, values[:8]),
            jnp.where(masks[3][:16], values[:16], values[8:]),
            jnp.where(masks[3][:8], values[16:], 0.0),
        ),
        axis=0,
    )


def attn_fwd_kernel(q_ref, k_ref, v_ref, table_ref, onehot_ref, shift_ref, mixed_ref, probs_ref):
    low = low_half()
    last = lax.broadcasted_iota(jnp.int32, (16, LANES), 0) == 15
    mixed = []
    for win in range(2):
        rows = pl.ds(192 * win, BLOCK)
        queries = pad_rows(q_ref[rows, :].astype(F32) * SCALE).T
        k = k_ref[rows, :].astype(F32)
        v = v_ref[rows, :]
        rel = dot_nn(table_ref[...], queries.astype(BF))
        onehot = onehot_ref[win].astype(F32)
        by_row = bit_masks(shift_ref[win, :8], 24)
        by_col = bit_masks(shift_ref[win, 8:], 24)
        halves = []
        for head in range(2):
            base = 64 if head == 0 else 0
            from_row = skew(rel[base : base + 32], by_row)
            from_col = skew(rel[base + 32 : base + 64], by_col)
            row_top = from_row.astype(BF).astype(F32)
            col_top = from_col.astype(BF).astype(F32)
            extra = (row_top, from_row - row_top, col_top, jnp.where(last, 1.0, from_col - col_top))
            if head == 0:
                left = jnp.concatenate((queries[:64],) + extra, axis=0).astype(BF)
                right = jnp.where(low, k, onehot).astype(BF)
            else:
                left = jnp.concatenate(extra + (queries[64:],), axis=0).astype(BF)
                right = jnp.where(low, onehot, k).astype(BF)
            scores = dot_nn(right, left)
            expon = jnp.exp(scores - jnp.max(scores, axis=0, keepdims=True))
            probs = expon * (1.0 / jnp.sum(expon, axis=0, keepdims=True))
            probs_ref[0, 2 * win + head] = probs
            halves.append(dot_tn(v, probs.astype(BF)))
        both = jnp.concatenate((halves[0][:HEAD_DIM], halves[1][HEAD_DIM:]), axis=0).T[:BLOCK]
        mixed.append(jnp.where(row_valid(win), both, 0.0))
    mixed_ref[...] = merge_windows(*mixed).astype(BF)


def attn_bwd_kernel(
    q_ref,
    k_ref,
    v_ref,
    grad_ref,
    probs_ref,
    table_ref,
    onehot_ref,
    shift_ref,
    grad_qkv_ref,
    table_grad_ref,
):
    pair = pl.program_id(0)
    low = low_half()

    @pl.when(pair == 0)
    def _():
        table_grad_ref[...] = jnp.zeros_like(table_grad_ref)

    parts = ([], [], [])
    table_total = jnp.zeros((128, 128), F32)
    for win in range(2):
        rows = pl.ds(192 * win, BLOCK)
        q = pad_rows(q_ref[rows, :].astype(F32) * SCALE).astype(BF)
        k = k_ref[rows, :].astype(F32)
        v = v_ref[rows, :]
        grad = pad_rows(jnp.where(row_valid(win), grad_ref[rows, :].astype(F32), 0.0))
        grad_low = grad.astype(BF)
        wide_low = lax.broadcasted_iota(jnp.int32, (LANES, 128), 1) < 64
        onehot = onehot_ref[win].astype(F32)
        by_row = bit_masks(shift_ref[win, :8], 24)
        by_col = bit_masks(shift_ref[win, 8:], 24)
        by_query, by_key, by_value, rel = [], [], [], []
        for head in range(2):
            if head == 0:
                right = jnp.where(low, k, onehot).astype(BF)
                grad_own = jnp.where(wide_low, grad, 0.0).astype(BF)
            else:
                right = jnp.where(low, onehot, k).astype(BF)
                grad_own = jnp.where(wide_low, 0.0, grad).astype(BF)
            probs = probs_ref[0, 2 * win + head]
            grad_probs = dot_nt(v, grad_own)
            row_dot = jnp.sum(probs * grad_probs, axis=0, keepdims=True)
            grad_scores = (probs * (grad_probs - row_dot)).astype(BF)
            by_value.append(dot_nn(probs.astype(BF), grad_low))
            by_key.append(dot_nn(grad_scores, q))
            back = dot_tn(right, grad_scores)
            own, base = (back[:64], 64) if head == 0 else (back[64:], 0)
            by_query.append(own)
            rel.append(unskew(back[base : base + 16], by_row))
            rel.append(unskew(back[base + 32 : base + 48], by_col))
        rel = jnp.concatenate((rel[2], rel[3], rel[0], rel[1]), axis=0)
        rel_top = rel.astype(BF)
        rel_rest = (rel - rel_top.astype(F32)).astype(BF)
        table = table_ref[...]
        from_rel = dot_tn(table, rel_top) + dot_tn(table, rel_rest)
        table_total += dot_nn(rel_top, q) + dot_nn(rel_rest, q)
        parts[0].append((jnp.concatenate(by_query, axis=0) + from_rel).T[:BLOCK] * SCALE)
        parts[1].append(jnp.where(low, by_key[0], by_key[1]))
        parts[2].append(jnp.where(low, by_value[0], by_value[1]))
    for block in range(3):
        at = pl.multiple_of(block * D + pair * 128, 128)
        grad_qkv_ref[:, pl.ds(at, 128)] = merge_windows(*parts[block]).astype(BF)
    table_grad_ref[...] += table_total


def attention_specs(rows):
    column = lambda block: pl.BlockSpec((rows, 128), lambda pair: (0, block * PAIRS + pair))
    whole = lambda *shape: pl.BlockSpec(shape, lambda pair: (0,) * len(shape))
    return (
        [column(0), column(1), column(2)],
        [whole(128, 128), whole(2, BLOCK, 128), whole(2, 16, LANES)],
        pl.BlockSpec((1, 4, BLOCK, LANES), lambda pair: (pair, 0, 0, 0)),
        whole,
    )


def attention(qkv, table, onehot, shift):
    rows = qkv.shape[0]
    columns, constants, probs_spec, _ = attention_specs(rows)
    return pl.pallas_call(
        attn_fwd_kernel,
        grid=(PAIRS,),
        in_specs=columns + constants,
        out_specs=[pl.BlockSpec((rows, 128), lambda pair: (0, pair)), probs_spec],
        out_shape=[
            jax.ShapeDtypeStruct((rows, D), BF),
            jax.ShapeDtypeStruct((PAIRS, 4, BLOCK, LANES), F32),
        ],
        compiler_params=pltpu.CompilerParams(vmem_limit_bytes=32 * 1024 * 1024),
        name="attention",
    )(qkv, qkv, qkv, table, onehot, shift)


def attention_back(qkv, grad_mixed, probs, table, onehot, shift):
    rows = qkv.shape[0]
    columns, constants, probs_spec, whole = attention_specs(rows)
    return pl.pallas_call(
        attn_bwd_kernel,
        grid=(PAIRS,),
        in_specs=columns + [pl.BlockSpec((rows, 128), lambda pair: (0, pair)), probs_spec] + constants,
        out_specs=[whole(rows, 3 * D), whole(128, 128)],
        out_shape=[
            jax.ShapeDtypeStruct((rows, 3 * D), BF),
            jax.ShapeDtypeStruct((128, 128), F32),
        ],
        compiler_params=pltpu.CompilerParams(vmem_limit_bytes=32 * 1024 * 1024),
        name="attention_back",
    )(qkv, qkv, qkv, grad_mixed, probs, table, onehot, shift)


def slot_mask(window_pos):
    row_win = window_pos // NWS
    col_win = window_pos % NWS
    rows_ok = jnp.where(row_win == NWS - 1, EDGE, WIN)
    cols_ok = jnp.where(col_win == NWS - 1, EDGE, WIN)
    positions = jnp.arange(WIN, dtype=jnp.int32)
    inside = (positions[None, :, None] < rows_ok[:, None, None]) & (
        positions[None, None, :] < cols_ok[:, None, None]
    )
    return inside.reshape(-1, 1).astype(F32)


def normalise(values):
    centred = values - jnp.mean(values, axis=-1, keepdims=True)
    rstd = lax.rsqrt(jnp.mean(centred * centred, axis=-1, keepdims=True) + EPS)
    return centred * rstd, rstd


def normalise_back(grad, hat, rstd, gain):
    grad_hat = grad * gain
    return rstd * (
        grad_hat
        - jnp.mean(grad_hat, axis=-1, keepdims=True)
        - hat * jnp.mean(grad_hat * hat, axis=-1, keepdims=True)
    )


def normal_cdf(values):
    return 0.5 * (1.0 + lax.erf(values * np.float32(np.sqrt(0.5))))


def normal_pdf(values):
    return np.float32(1.0 / np.sqrt(2.0 * np.pi)) * jnp.exp(-0.5 * values * values)


def hop(array, mask, count):
    return lax.ppermute(array, "fsdp", [(i, i ^ mask) for i in range(count)])


def hop_plan(count):
    far = count // 4
    return (far, 2 * far, 3 * far), [1 << bit for bit in range(1, far.bit_length() - 1)]


def gather_pieces(shard, count):
    far, middle = hop_plan(count)
    received = [hop(shard, mask, count) for mask in far]
    stacks = (
        [jnp.stack((shard, received[0])), [0, far[0]], middle],
        [jnp.stack((received[1], received[2])), [far[1], far[2]], middle[::-1]],
    )
    pieces = []
    for stack, owners, masks in stacks:
        for mask in masks[:-1]:
            stack = jnp.concatenate((stack, hop(stack, mask, count)), axis=0)
            owners = owners + [owner ^ mask for owner in owners]
        pieces.append((stack, owners))
        pieces.append((hop(stack, masks[-1], count), [owner ^ masks[-1] for owner in owners]))
    other = [(hop(stack, 1, count), [owner ^ 1 for owner in owners]) for stack, owners in pieces]
    return pieces + other


def place_kernel(owners, columns, me_ref, *refs):
    stacks, outs, sem = refs[: len(owners)], refs[len(owners) : -1], refs[-1]
    copies = []
    for stack, stack_owners in zip(stacks, owners):
        for index, mask in enumerate(stack_owners):
            owner = jnp.bitwise_xor(me_ref[0], mask)
            for out, (lo, hi) in zip(outs, columns):
                copies.append(
                    pltpu.make_async_copy(
                        stack.at[index, :, lo:hi], out.at[owner], sem.at[len(copies)]
                    )
                )
                copies[-1].start()
    for copy in copies:
        copy.wait()


def place(pieces, widths, me, count):
    edges = np.cumsum([0] + list(widths))
    columns = tuple(zip(edges[:-1].tolist(), edges[1:].tolist()))
    stacks = [stack for stack, _ in pieces]
    rows = stacks[0].shape[1]
    outs = pl.pallas_call(
        functools.partial(place_kernel, tuple(tuple(o) for _, o in pieces), columns),
        in_specs=[pl.BlockSpec(memory_space=pltpu.SMEM)]
        + [pl.BlockSpec(memory_space=pl.ANY)] * len(stacks),
        out_specs=[pl.BlockSpec(memory_space=pltpu.VMEM)] * len(widths),
        out_shape=[jax.ShapeDtypeStruct((count, rows, width), BF) for width in widths],
        scratch_shapes=[pltpu.SemaphoreType.DMA((count * len(widths),))],
        compiler_params=pltpu.CompilerParams(vmem_limit_bytes=16 * 1024 * 1024),
        name="place",
    )(me.reshape(1), *stacks)
    return [out.reshape(count * rows, width) for out, width in zip(outs, widths)]


def sum_order(count):
    far, middle = hop_plan(count)
    order = []
    for masks, last in ((middle, (0, far[0])), (middle[::-1], (far[1], far[2]))):
        block = list(last)
        for mask in masks[::-1]:
            block = block + [owner ^ mask for owner in block]
        order += block
    return order + [owner ^ 1 for owner in order]


def order_matrix(me, count, rows):
    masks = np.repeat(np.array(sum_order(count), np.int32), rows)
    wanted = jnp.bitwise_xor(me, masks) * rows + np.tile(np.arange(rows, dtype=np.int32), count)
    features = lax.broadcasted_iota(jnp.int32, (count * rows, count * rows), 0)
    return (features == wanted[None, :]).astype(BF)


def pick_kernel(masks, me_ref, stack, kept, sent, sem):
    half = len(masks) // 2
    copies = []
    for index, mask in enumerate(masks):
        owner = jnp.bitwise_xor(me_ref[0], mask)
        out = kept if index < half else sent
        copies.append(
            pltpu.make_async_copy(stack.at[owner], out.at[index % half], sem.at[index])
        )
        copies[-1].start()
    for copy in copies:
        copy.wait()


def pick(array, me, count):
    stack = array.reshape(count, -1, array.shape[-1])
    half = jax.ShapeDtypeStruct((count // 2,) + stack.shape[1:], BF)
    return pl.pallas_call(
        functools.partial(pick_kernel, tuple(sum_order(count))),
        in_specs=[
            pl.BlockSpec(memory_space=pltpu.SMEM),
            pl.BlockSpec(memory_space=pl.ANY),
        ],
        out_specs=[pl.BlockSpec(memory_space=pltpu.VMEM)] * 2,
        out_shape=[half, half],
        scratch_shapes=[pltpu.SemaphoreType.DMA((count,))],
        compiler_params=pltpu.CompilerParams(vmem_limit_bytes=16 * 1024 * 1024),
        name="pick",
    )(me.reshape(1), stack)


def add_low(left, right):
    return (left.astype(F32) + right.astype(F32)).astype(BF)


def scatter_sum(kept, sent, count):
    far, middle = hop_plan(count)
    blocks = count // 2
    kept = kept.reshape(blocks, -1, kept.shape[-1])
    arrived = hop(sent.reshape(kept.shape), 1, count)
    half = blocks // 2
    ends = []
    for at, masks in ((0, middle), (half, middle[::-1])):
        here, there, size = kept[at : at + half], arrived[at : at + half], half
        for mask in masks:
            size //= 2
            away = hop(add_low(here[size:], there[size:]), mask, count)
            here, there = add_low(here[:size], there[:size]), away
        ends.append((here, there))
    (near, near_in), (back, back_in) = ends
    total = near[0].astype(F32) + near_in[0].astype(F32)
    sends = (
        add_low(near[1], near_in[1]),
        add_low(back[0], back_in[0]),
        add_low(back[1], back_in[1]),
    )
    for block, mask in zip(sends, far):
        total = total + hop(block, mask, count).astype(F32)
    return total


def sum_everywhere(vector, count):
    mask = 1
    while mask < count:
        vector = vector + hop(vector, mask, count)
        mask *= 2
    return vector


def per_device(
    tokens,
    window_pos,
    norm1_gain,
    norm1_bias,
    qkv_weight,
    qkv_bias,
    rel_pos_h,
    rel_pos_w,
    proj_weight,
    proj_bias,
    norm2_gain,
    norm2_bias,
    lin1_weight,
    lin1_bias,
    lin2_weight,
    lin2_bias,
    out_grad,
):
    vectors = (
        norm1_gain,
        norm1_bias,
        qkv_bias,
        proj_bias,
        norm2_gain,
        norm2_bias,
        lin1_bias,
        lin2_bias,
    )
    sizes = [v.shape[0] for v in vectors]
    used = sum(sizes)
    shard_rows = qkv_weight.shape[0]
    packed = jnp.pad(
        jnp.concatenate(vectors).astype(BF), (0, shard_rows * 128 - used)
    ).reshape(shard_rows, 128)
    count = lax.axis_size("fsdp")
    me = lax.axis_index("fsdp")
    first = jnp.concatenate((qkv_weight.astype(BF), proj_weight.astype(BF), packed), axis=1)
    w_qkv, w_proj, small = place(gather_pieces(first, count), (3 * D, D, 128), me, count)
    (w_up,) = place(gather_pieces(lin1_weight.astype(BF), count), (FF,), me, count)
    w_down = lax.all_gather(lin2_weight.astype(BF), "fsdp", axis=0, tiled=True)
    small = small.reshape(count, shard_rows * 128)[:, :used].astype(F32)
    edges = np.cumsum([0] + sizes)
    gain_one, bias_one, b_qkv, b_proj, gain_two, bias_two, b_up, b_down = (
        small[:, lo:hi].reshape(-1) for lo, hi in zip(edges[:-1], edges[1:])
    )
    order = order_matrix(me, count, shard_rows)

    onehot, shift = window_constants()
    onehot = jnp.asarray(onehot, BF)
    shift = jnp.asarray(shift)
    table = table_lanes(rel_pos_h, rel_pos_w)
    live = slot_mask(window_pos)

    inputs = tokens.astype(F32)
    hat_one, rstd_one = normalise(inputs)
    normed_one = ((hat_one * gain_one + bias_one) * live).astype(BF)
    qkv = (dot_nn(normed_one, w_qkv) + b_qkv).astype(BF)
    mixed, probs = attention(qkv, table, onehot, shift)
    residual = inputs + dot_nn(mixed, w_proj) + b_proj
    hat_two, rstd_two = normalise(residual)
    normed_two = (hat_two * gain_two + bias_two).astype(BF)
    hidden = dot_nn(normed_two, w_up) + b_up
    cdf = normal_cdf(hidden)
    active = (hidden * cdf).astype(BF)
    slope = cdf + hidden * normal_pdf(hidden)
    grad_out = out_grad.astype(F32) * live
    grad_branch = grad_out.astype(BF)
    grad_w_down = dot_tn(active, grad_branch).astype(BF)
    own_down = scatter_sum(*pick(grad_w_down, me, count), count)
    output = ((residual + dot_nn(active, w_down) + b_down) * live).astype(BF)

    grad_hidden = (dot_nt(grad_branch, w_down) * slope).astype(BF)
    ordered = dot_nn(normed_two, order).astype(BF)
    kept = dot_tn(ordered[:, : D // 2], grad_hidden).astype(BF)
    sent = dot_tn(ordered[:, D // 2 :], grad_hidden).astype(BF)
    kept, sent, grad_hidden = lax.optimization_barrier((kept, sent, grad_hidden))
    own_up = scatter_sum(kept, sent, count)
    grad_normed_two = dot_nt(grad_hidden, w_up)
    grad_residual = grad_out + normalise_back(grad_normed_two, hat_two, rstd_two, gain_two)
    grad_attn = grad_residual.astype(BF)
    ordered = dot_nn(mixed, order).astype(BF)
    kept = dot_tn(ordered[:, : D // 2], grad_attn).astype(BF)
    sent = dot_tn(ordered[:, D // 2 :], grad_attn).astype(BF)
    kept, sent, grad_attn = lax.optimization_barrier((kept, sent, grad_attn))
    own_proj = scatter_sum(kept, sent, count)
    grad_mixed = dot_nt(grad_attn, w_proj).astype(BF)
    grad_qkv, lanes_grad = attention_back(qkv, grad_mixed, probs, table, onehot, shift)
    ordered = dot_nn(normed_one, order).astype(BF)
    kept = dot_tn(ordered[:, : D // 2], grad_qkv).astype(BF)
    sent = dot_tn(ordered[:, D // 2 :], grad_qkv).astype(BF)
    kept, sent, grad_qkv = lax.optimization_barrier((kept, sent, grad_qkv))
    own_qkv = scatter_sum(kept, sent, count)
    grad_normed_one = dot_nt(grad_qkv, w_qkv) * live
    tokens_grad = (
        grad_residual + normalise_back(grad_normed_one, hat_one, rstd_one, gain_one)
    ).astype(BF)

    totals = (
        jnp.sum(grad_normed_one * hat_one, axis=0),
        jnp.sum(grad_normed_one, axis=0),
        jnp.sum(grad_qkv.astype(F32), axis=0),
        jnp.sum(grad_attn.astype(F32), axis=0),
        jnp.sum(grad_normed_two * hat_two, axis=0),
        jnp.sum(grad_normed_two, axis=0),
        jnp.sum(grad_hidden.astype(F32), axis=0),
        jnp.sum(grad_branch.astype(F32), axis=0),
    )
    by_owner = jnp.concatenate([total.reshape(count, -1) for total in totals], axis=1).reshape(-1)
    table_h, table_w = table_grads(lanes_grad)
    small_total = sum_everywhere(
        jnp.concatenate((by_owner, table_h.reshape(-1), table_w.reshape(-1))), count
    )
    own_small = lax.dynamic_slice(small_total, (me * used,), (used,))
    owned = [own_small[lo:hi] for lo, hi in zip(edges[:-1], edges[1:])]
    table_h, table_w = small_total[count * used :].reshape(2, 2 * WIN - 1, HEAD_DIM)

    return (
        output,
        tokens_grad,
        owned[0],
        owned[1],
        own_qkv,
        owned[2],
        table_h,
        table_w,
        own_proj,
        owned[3],
        owned[4],
        owned[5],
        own_up,
        owned[6],
        own_down.astype(F32),
        owned[7],
    )


def solution(mesh):
    rows = P("fsdp", None)
    line = P("fsdp")
    return jax.shard_map(
        per_device,
        mesh=mesh,
        in_specs=(
            rows,
            line,
            line,
            line,
            rows,
            line,
            P(),
            P(),
            rows,
            line,
            line,
            line,
            rows,
            line,
            rows,
            line,
            rows,
        ),
        out_specs=(
            rows,
            rows,
            line,
            line,
            rows,
            line,
            P(),
            P(),
            rows,
            line,
            line,
            line,
            rows,
            line,
            rows,
            line,
        ),
        check_vma=False,
    )
```

time: 714 us -> 351 us (0.49)
  waiting for transfers between devices: 580 us -> 125 us
  starting transfers between devices: 0.55 us -> 66.1 us
  other arithmetic: 22.7 us -> 34.7 us
    reduce_scatter x3 -> x0, waiting for transfers between devices: 326 us -> none  [scatter_sum(): return lax.psum_scatter(partial, 'fsdp', scatter_dimension=0, tiled=True)]
    all_gather x3 -> x1, waiting for transfers between devices: 165 us -> 0.01 us  [per_device(): w_down = lax.all_gather(lin2_weight.astype(BF), 'fsdp', axis=0, tiled=True)]
    ppermute x0 -> x59, waiting for transfers between devices: none -> 125 us  [hop(): return lax.ppermute(array, 'fsdp', [(i, i ^ mask) for i in range(count)])]
    psum x1 -> x0, waiting for transfers between devices: 88.6 us -> none  [per_device(): lax.psum(jnp.concatenate(totals + (lanes_grad.reshape(-1),)), 'fsdp')]
    ppermute x0 -> x59, starting transfers between devices: none -> 66.1 us  [hop(): return lax.ppermute(array, 'fsdp', [(i, i ^ mask) for i in range(count)])]
    pallas_call x0 -> x3, Pallas kernels: none -> 14.7 us  [the longest x2 8.16 us: place(): pl.pallas_call(functools.partial(place_kernel, tuple((tuple(o) for _, o i...]
    convert_element_type x7 -> x24, other arithmetic: 8.61 us -> 16.9 us  [the longest x20 13.7 us: add_low(): return (left.astype(F32) + right.astype(F32)).astype(BF)]
    dot_general x4 -> x7, matrix products: 17.6 us -> 22.5 us  [dot_nn(): return jnp.dot(a, b, preferred_element_type=F32)]
  transfers between devices with their start and end apart: 7 -> 60, of which waited for: 7 -> 28; matrix products, arithmetic and copies ran while one was open for 8% -> 17% of each run, Pallas kernels for 2% -> 7%
where the time goes in v2:
time: 351 us; the launch traced here: 347 us
  waiting for transfers between devices  125 us (36%)
  starting transfers between devices  66.1 us (19%)
  matrix products  53.2 us (15%)
  other arithmetic  34.7 us (10%)
  Pallas kernels  34.2 us (10%)
  local copies, waits for them, and re-layouts  18.7 us (5%)
  between operations  15.4 us (4%)
    ppermute x59, waiting for transfers between devices, hop(): return lax.ppermute(array, 'fsdp', [(i, i ^ mask) for i in range(count)])  125 us
    ppermute x59, starting transfers between devices, hop(): return lax.ppermute(array, 'fsdp', [(i, i ^ mask) for i in range(count)])  66.1 us
    dot_general x7, matrix products, dot_nn(): return jnp.dot(a, b, preferred_element_type=F32)  22.5 us
    dot_general x7, matrix products, dot_tn(): lax.dot_general(a, b, (((0,), (0,)), ((), ())), preferred_element_type=F32)  16.4 us
    dot_general x4, matrix products, dot_nt(): lax.dot_general(a, b, (((1,), (1,)), ((), ())), preferred_element_type=F32)  14.3 us
    convert_element_type x20, other arithmetic, add_low(): return (left.astype(F32) + right.astype(F32)).astype(BF)  13.7 us
    pallas_call x1, Pallas kernels, attention_back(): pl.pallas_call(attn_bwd_kernel, grid=(PAIRS,), in_specs=columns + [pl.Blo...  11 us
    unnamed x87, local copies, waits for them, and re-layouts  10.1 us
  transfers between devices with their start and end apart: 60, of which 28 were waited for; matrix products, arithmetic and copies ran while one was open for 17% of the time, Pallas kernels for 7%

profile of v2, /device:TPU:0, one launch (start us, length us, event | category | flops | bytes accessed | tf_op | source)
XLA Modules:
  0.0 346.8 jit_solution(10747082867498605114)
XLA Ops:
  14.6 3.1 collective-permute-start
  17.7 2.5 collective-permute-start.4
  23.1 2.5 collective-permute-start.15
  26.4 5.4 %collective-permute-done.11 = bf16[24,3072]{1,0:T(8,128)(2,1)S(1)} collective-permute-done((bf16[24,3072]{1,0:T(8,128)(2,1)S(1)}, bf16[24,3072]{1,0:T(8,128)(2,1)S(1)}, u32[]{:S(2)}, u32[]{:S(2)}) %collective-permute-start.11) | collective-permute-done | bytes 147488 | tf_op jit(solution)/shard_map/ppermute | solution.py:306
  31.8 3.6 %collective-permute-start.14 = (bf16[24,3072]{1,0:T(8,128)(2,1)S(1)}, bf16[24,3072]{1,0:T(8,128)(2,1)S(1)}, u32[]{:S(2)}, u32[]{:S(2)}) collective-permute-start(bf16[24,3072]{1,0:T(8,128)(2,1)S(1)} %convert_element_type.681), channel_id=1, source_target_pairs={{0,16},{1,17},{2,18},{3,19},{4,20},{5,21},{6,22},{7,23},{8,24},{9,... | collective-permute-start | bytes 442376 | tf_op jit(solution)/shard_map/ppermute | solution.py:306
  35.4 2.7 collective-permute-done.15
  39.5 10.1 %collective-permute-done.14 = bf16[24,3072]{1,0:T(8,128)(2,1)S(1)} collective-permute-done((bf16[24,3072]{1,0:T(8,128)(2,1)S(1)}, bf16[24,3072]{1,0:T(8,128)(2,1)S(1)}, u32[]{:S(2)}, u32[]{:S(2)}) %collective-permute-start.14) | collective-permute-done | bytes 147488 | tf_op jit(solution)/shard_map/ppermute | solution.py:306
  55.2 6.6 %collective-permute-done.16 = bf16[2,24,3072]{2,1,0:T(8,128)(2,1)S(1)} collective-permute-done((bf16[2,24,3072]{2,1,0:T(8,128)(2,1)S(1)}, bf16[2,24,3072]{2,1,0:T(8,128)(2,1)S(1)}, u32[]{:S(2)}, u32[]{:S(2)}) %collective-permute-start.16) | collective-permute-done | bytes 294944 | tf_op jit(solution)/shard_map/ppermute | solution.py:306
  65.7 2.7 collective-permute-done.5
  70.0 15.4 %collective-permute-done.13.refs_1_ = bf16[4,24,3072]{2,1,0:T(8,128)(2,1)S(1)} collective-permute-done((bf16[4,24,3072]{2,1,0:T(8,128)(2,1)S(1)}, bf16[4,24,3072]{2,1,0:T(8,128)(2,1)S(1)}, u32[]{:S(2)}, u32[]{:S(2)}) %collective-permute-start.13) | collective-permute-done | bytes 589856 | tf_op jit(solution)/shard_map/ppermute | solution.py:306
  89.7 10.9 %collective-permute-done.2.refs_1_ = bf16[4,24,3200]{2,1,0:T(8,128)(2,1)S(1)} collective-permute-done((bf16[4,24,3200]{2,1,0:T(8,128)(2,1)S(1)}, bf16[4,24,3200]{2,1,0:T(8,128)(2,1)S(1)}, u32[]{:S(2)}, u32[]{:S(2)}) %collective-permute-start.2) | collective-permute-done | bytes 614432 | tf_op jit(solution)/shard_map/ppermute | solution.py:306
  105.9 4.5 %place.3 = bf16[32,24,3072]{2,1,0:T(8,128)(2,1)S(1)} custom-call(s32[1]{0:T(128)} %bitcast.me_ref, bf16[4,24,3072]{2,1,0:T(8,128)(2,1)S(1)} %pad_maximum_fusion.2.refs_0_, bf16[4,24,3072]{2,1,0:T(8,128)(2,1)S(1)} %copy-done.3, bf16[4,24,3072]{2,1,0:T(8,128)(2,1)S(1)} %pad_maximum_fusion.3.refs_2_, bf16[4,24,3072]{2,1,0:T(8,128)(2,1)} %collective-permute-done.17.refs_3_, ...), custom_call_target="tpu_custom_call" | custom-call | tf_op jit(solution)/shard_map/place/pallas_call | solution.py:354
  112.5 3.7 %place.2 = (bf16[32,24,2304]{2,1,0:T(8,128)(2,1)S(1)}, bf16[32,24,768]{2,1,0:T(8,128)(2,1)S(1)}, bf16[32,24,128]{2,1,0:T(8,128)(2,1)S(1)}) custom-call(s32[1]{0:T(128)} %bitcast.me_ref, bf16[4,24,3200]{2,1,0:T(8,128)(2,1)S(1)} %pad_maximum_fusion.refs_0_, bf16[4,24,3200]{2,1,0:T(8,128)(2,1)S(1)} %collective-permute-done.2.refs_1_, ...), custom_call_target="tpu_custom_call" | custom-call | tf_op jit(solution)/shard_map/place/pallas_call | solution.py:354
  119.9 4.0 %fusion.6.q_ref.k_ref.v_ref = bf16[392,2304]{1,0:T(8,128)(2,1)S(1)} fusion(bf16[768,2304]{1,0:T(8,128)(2,1)} %bitcast.123, f32[2304]{0:T(1024)S(1)} %add.347, bf16[392,768]{1,0:T(8,128)(2,1)} %param.21, f32[392]{0:T(512)S(1)} %reshape.357, f32[768]{0:T(1024)S(1)} %add.343, f32[768]{0:T(1024)S(1)} %mul.180, f32[392]{0:T(512)S(1)} %add_rsqrt_fusion.1, ...), kind=kOutput, calls=%fused_computation.12 | convolution fusion | flops 1391179776 | bytes 5967456 | tf_op jit(solution)/shard_map/dot_general | solution.py:67
  124.0 8.5 %attention.1 = (bf16[392,768]{1,0:T(8,128)(2,1)S(1)}, f32[6,4,200,256]{3,2,1,0:T(8,128)S(1)}) custom-call(bf16[392,2304]{1,0:T(8,128)(2,1)S(1)} %fusion.6.q_ref.k_ref.v_ref, bf16[392,2304]{1,0:T(8,128)(2,1)S(1)} %fusion.6.q_ref.k_ref.v_ref, bf16[392,2304]{1,0:T(8,128)(2,1)S(1)} %fusion.6.q_ref.k_ref.v_ref, bf16[128,128]{1,0:T(8,128)(2,1)S(1)} %fusion.77.table_ref, ...), custom_call_target="tpu_custom_call" | custom-call | tf_op jit(solution)/shard_map/attention/pallas_call | solution.py:239
  132.5 2.2 copy-done
  135.8 5.9 %multiply_convert_fusion = (bf16[392,3072]{1,0:T(8,128)(2,1)S(1)}, f32[392,3072]{1,0:T(8,128)}) fusion(f32[3072]{0:T(1024)S(1)} %add.358, bf16[768,3072]{1,0:T(8,128)(2,1)} %bitcast.119, f32[392,768]{1,0:T(8,128)S(1)} %get-tuple-element.136, f32[768]{0:T(1024)S(1)} %add.355, f32[768]{0:T(1024)S(1)} %mul.190, f32[392]{0:T(512)S(1)} %add_rsqrt_fusion, ...), kind=kOutput, calls=%fused_computation.9 | convolution fusion | flops 1858418688 | bytes 13169728 | tf_op jit(solution)/shard_map/dot_general | solution.py:67
  141.8 3.2 convolution_convert_fusion
  145.0 6.6 %pick.1 = (bf16[16,96,768]{2,1,0:T(8,128)(2,1)S(1)}, bf16[16,96,768]{2,1,0:T(8,128)(2,1)S(1)}) custom-call(s32[1]{0:T(128)} %bitcast.me_ref, bf16[32,96,768]{2,1,0:T(8,128)(2,1)S(1)} %bitcast.121), custom_call_target="tpu_custom_call" | custom-call | tf_op jit(solution)/shard_map/pick/pallas_call | solution.py:402
  152.0 4.2 %collective-permute-done.51 = bf16[16,96,768]{2,1,0:T(8,128)(2,1)S(1)} collective-permute-done((bf16[16,96,768]{2,1,0:T(8,128)(2,1)S(1)}, bf16[16,96,768]{2,1,0:T(8,128)(2,1)S(1)}, u32[]{:S(2)}, u32[]{:S(2)}) %collective-permute-start.51) | collective-permute-done | bytes 2359328 | tf_op jit(solution)/shard_map/ppermute | solution.py:306
  160.8 3.1 fusion.20
  163.8 10.1 %collective-permute-done.55 = bf16[4,96,768]{2,1,0:T(8,128)(2,1)} collective-permute-done((bf16[4,96,768]{2,1,0:T(8,128)(2,1)}, bf16[4,96,768]{2,1,0:T(8,128)(2,1)}, u32[]{:S(2)}, u32[]{:S(2)}) %collective-permute-start.55) | collective-permute-done | bytes 589856 | tf_op jit(solution)/shard_map/ppermute | solution.py:306
  182.4 2.2 collective-permute-done.56
  185.7 2.3 collective-permute-start.58
  189.0 2.3 collective-permute-start.54
  194.4 5.5 %collective-permute-done.57 = bf16[96,768]{1,0:T(8,128)(2,1)S(1)} collective-permute-done((bf16[96,768]{1,0:T(8,128)(2,1)S(1)}, bf16[96,768]{1,0:T(8,128)(2,1)S(1)}, u32[]{:S(2)}, u32[]{:S(2)}) %collective-permute-start.57) | collective-permute-done | bytes 147488 | tf_op jit(solution)/shard_map/ppermute | solution.py:306
  201.6 6.0 %fusion.5 = bf16[392,3072]{1,0:T(8,128)(2,1)S(1)} fusion(bf16[3072,768]{1,0:T(8,128)(2,1)} %all-gather.2.cloned.1.call-done, f32[392,3072]{1,0:T(8,128)} %get-tuple-element.138, f32[3072]{0:T(1024)S(1)} %add.358, bf16[392,768]{1,0:T(8,128)(2,1)} %param.37, f32[392]{0:T(512)S(1)} %reshape.357), kind=kOutput, calls=%fused_computation.7 | convolution fusion | flops 1863837696 | bytes 12559904 | tf_op jit(solution)/shard_map/dot_general | solution.py:71
  207.6 2.9 convolution_convert_fusion.4
  210.5 2.9 convolution_convert_fusion.3
  213.4 4.9 %multiply_reduce_fusion = (f32[768]{0:T(1024)S(1)}, f32[392]{0:T(512)S(1)}, f32[392]{0:T(512)S(1)}, f32[768]{0:T(1024)S(1)}, f32[392,768]{1,0:T(8,128)S(1)}) fusion(f32[392,768]{1,0:T(8,128)S(1)} %copy-done.17, f32[392]{0:T(512)S(1)} %add_rsqrt_fusion, f32[392]{0:T(512)S(1)} %broadcast_multiply_fusion.4, f32[768]{0:T(1024)S(1)} %mul.190, ...), kind=kOutput, calls=%fused_computation.54 | convolution fusion | flops 1852395264 | bytes 9550976 | tf_op jit(solution)/shard_map/dot_general | solution.py:71
  223.3 11.0 %attention_back.1 = (bf16[392,2304]{1,0:T(8,128)(2,1)S(1)}, f32[128,128]{1,0:T(8,128)S(1)}) custom-call(bf16[392,2304]{1,0:T(8,128)(2,1)S(1)} %fusion.6.q_ref.k_ref.v_ref, bf16[392,2304]{1,0:T(8,128)(2,1)S(1)} %fusion.6.q_ref.k_ref.v_ref, bf16[392,2304]{1,0:T(8,128)(2,1)S(1)} %fusion.6.q_ref.k_ref.v_ref, ...), custom_call_target="tpu_custom_call" | custom-call | tf_op jit(solution)/shard_map/attention_back/pallas_call | solution.py:256
  234.3 2.4 convolution_convert_fusion.2
  236.7 2.3 convolution_convert_fusion.1
  239.1 2.8 fusion.31
  246.5 5.4 %fusion.19 = bf16[392,768]{1,0:T(8,128)(2,1)} fusion(f32[392,768]{1,0:T(8,128)S(1)} %copy-done.18, bf16[392,3072]{1,0:T(8,128)(2,1)S(1)} %copy-done.40, bf16[3072,768]{1,0:T(8,128)(2,1)} %all-gather.2.cloned.1.call-done, f32[768]{0:T(1024)S(1)} %add.364, f32[392]{0:T(512)S(1)} %reshape.357), kind=kOutput, calls=%fused_computation.36 | convolution fusion | flops 1850892288 | bytes 8938016 | tf_op jit(solution)/shard_map/dot_general | solution.py:67
  254.2 2.5 collective-permute-done.23
  258.0 3.0 collective-permute-done.24
  262.3 2.9 collective-permute-done.25
  265.3 5.5 %collective-permute-done.26 = f32[13440]{0:T(1024)S(1)} collective-permute-done((f32[13440]{0:T(1024)S(1)}, f32[13440]{0:T(1024)S(1)}, u32[]{:S(2)}, u32[]{:S(2)}) %collective-permute-start.26) | collective-permute-done | bytes 53792 | tf_op jit(solution)/shard_map/ppermute | solution.py:306
  274.3 2.7 collective-permute-done.39
  283.9 2.2 collective-permute-start.38
  298.8 5.9 %collective-permute-done.28 = bf16[4,24,2304]{2,1,0:T(8,128)(2,1)S(1)} collective-permute-done((bf16[4,24,2304]{2,1,0:T(8,128)(2,1)}, bf16[4,24,2304]{2,1,0:T(8,128)(2,1)S(1)}, u32[]{:S(2)}, u32[]{:S(2)}) %collective-permute-start.28) | collective-permute-done | bytes 442400 | tf_op jit(solution)/shard_map/ppermute | solution.py:306
  305.9 2.5 fusion.37
  312.2 2.8 collective-permute-start.30
  315.0 6.5 %collective-permute-done.47 = bf16[4,24,3072]{2,1,0:T(8,128)(2,1)S(1)} collective-permute-done((bf16[4,24,3072]{2,1,0:T(8,128)(2,1)S(1)}, bf16[4,24,3072]{2,1,0:T(8,128)(2,1)S(1)}, u32[]{:S(2)}, u32[]{:S(2)}) %collective-permute-start.47) | collective-permute-done | bytes 589856 | tf_op jit(solution)/shard_map/ppermute | solution.py:306
  323.9 4.6 %collective-permute-done.48 = bf16[2,24,3072]{2,1,0:T(8,128)(2,1)S(1)} collective-permute-done((bf16[2,24,3072]{2,1,0:T(8,128)(2,1)S(1)}, bf16[2,24,3072]{2,1,0:T(8,128)(2,1)S(1)}, u32[]{:S(2)}, u32[]{:S(2)}) %collective-permute-start.48) | collective-permute-done | bytes 294944 | tf_op jit(solution)/shard_map/ppermute | solution.py:306
  330.2 2.9 collective-permute-start.46
  335.7 3.0 collective-permute-done.49
  (301 shorter events, 110.5 us)
Async XLA Ops:
  7.2 194.4 %all-gather.2.cloned.1.call-start = ((), (), s32[]{:S(2)}) async-start(), calls=%async_computation | async-start | bytes 4866048 | tf_op jit(solution)/shard_map/all_gather | solution.py:494
  14.6 36.7 %collective-permute-start = (bf16[24,3200]{1,0:T(8,128)(2,1)S(1)}, bf16[24,3200]{1,0:T(8,128)(2,1)S(1)}, u32[]{:S(2)}, u32[]{:S(2)}) collective-permute-start(bf16[24,3200]{1,0:T(8,128)(2,1)S(1)} %get-tuple-element.114), channel_id=1, source_target_pairs={{0,8},{1,9},{2,10},{3,11},{4,12},{5,13},{6,14},{7,15},{8,0},{9,1},... | collective-permute-start | bytes 460808 | tf_op jit(solution)/shard_map/ppermute | solution.py:306
  17.7 35.2 %collective-permute-start.4 = (bf16[24,3200]{1,0:T(8,128)(2,1)S(1)}, bf16[24,3200]{1,0:T(8,128)(2,1)S(1)}, u32[]{:S(2)}, u32[]{:S(2)}) collective-permute-start(bf16[24,3200]{1,0:T(8,128)(2,1)S(1)} %get-tuple-element.114), channel_id=1, source_target_pairs={{0,24},{1,25},{2,26},{3,27},{4,28},{5,29},{6,30},{7,31},{8,16},{9,... | collective-permute-start | bytes 460808 | tf_op jit(solution)/shard_map/ppermute | solution.py:306
  20.1 32.8 %collective-permute-start.3 = (bf16[24,3200]{1,0:T(8,128)(2,1)S(1)}, bf16[24,3200]{1,0:T(8,128)(2,1)S(1)}, u32[]{:S(2)}, u32[]{:S(2)}) collective-permute-start(bf16[24,3200]{1,0:T(8,128)(2,1)S(1)} %get-tuple-element.114), channel_id=1, source_target_pairs={{0,16},{1,17},{2,18},{3,19},{4,20},{5,21},{6,22},{7,23},{8,24},{9,... | collective-permute-start | bytes 460808 | tf_op jit(solution)/shard_map/ppermute | solution.py:306
  21.2 10.5 %collective-permute-start.11 = (bf16[24,3072]{1,0:T(8,128)(2,1)S(1)}, bf16[24,3072]{1,0:T(8,128)(2,1)S(1)}, u32[]{:S(2)}, u32[]{:S(2)}) collective-permute-start(bf16[24,3072]{1,0:T(8,128)(2,1)S(1)} %convert_element_type.681), channel_id=1, source_target_pairs={{0,8},{1,9},{2,10},{3,11},{4,12},{5,13},{6,14},{7,15},{8,0},{9,1},... | collective-permute-start | bytes 442376 | tf_op jit(solution)/shard_map/ppermute | solution.py:306
  23.1 14.9 %collective-permute-start.15 = (bf16[24,3072]{1,0:T(8,128)(2,1)S(1)}, bf16[24,3072]{1,0:T(8,128)(2,1)S(1)}, u32[]{:S(2)}, u32[]{:S(2)}) collective-permute-start(bf16[24,3072]{1,0:T(8,128)(2,1)S(1)} %convert_element_type.681), channel_id=1, source_target_pairs={{0,24},{1,25},{2,26},{3,27},{4,28},{5,29},{6,30},{7,31},{8,16},{9,... | collective-permute-start | bytes 442376 | tf_op jit(solution)/shard_map/ppermute | solution.py:306
  31.8 17.9 %collective-permute-start.14 = (bf16[24,3072]{1,0:T(8,128)(2,1)S(1)}, bf16[24,3072]{1,0:T(8,128)(2,1)S(1)}, u32[]{:S(2)}, u32[]{:S(2)}) collective-permute-start(bf16[24,3072]{1,0:T(8,128)(2,1)S(1)} %convert_element_type.681), channel_id=1, source_target_pairs={{0,16},{1,17},{2,18},{3,19},{4,20},{5,21},{6,22},{7,23},{8,24},{9,... | collective-permute-start | bytes 442376 | tf_op jit(solution)/shard_map/ppermute | solution.py:306
  38.0 15.5 %collective-permute-start.12 = (bf16[2,24,3072]{2,1,0:T(8,128)(2,1)S(1)}, bf16[2,24,3072]{2,1,0:T(8,128)(2,1)S(1)}, u32[]{:S(2)}, u32[]{:S(2)}) collective-permute-start(bf16[2,24,3072]{2,1,0:T(8,128)(2,1)S(1)} %pad_maximum_fusion.6), channel_id=1, source_target_pairs={{0,2},{1,3},{2,0},{3,1},{4,6},{5,7},{6,4},{7,5},{8,10},{9,11},{10,... | collective-permute-start | bytes 884744 | tf_op jit(solution)/shard_map/ppermute | solution.py:306
  49.7 12.1 %collective-permute-start.16 = (bf16[2,24,3072]{2,1,0:T(8,128)(2,1)S(1)}, bf16[2,24,3072]{2,1,0:T(8,128)(2,1)S(1)}, u32[]{:S(2)}, u32[]{:S(2)}) collective-permute-start(bf16[2,24,3072]{2,1,0:T(8,128)(2,1)S(1)} %pad_maximum_fusion.7), channel_id=1, source_target_pairs={{0,4},{1,5},{2,6},{3,7},{4,0},{5,1},{6,2},{7,3},{8,12},{9,13},{10,... | collective-permute-start | bytes 884744 | tf_op jit(solution)/shard_map/ppermute | solution.py:306
  51.4 14.3 %collective-permute-start.1 = (bf16[2,24,3200]{2,1,0:T(8,128)(2,1)S(1)}, bf16[2,24,3200]{2,1,0:T(8,128)(2,1)S(1)}, u32[]{:S(2)}, u32[]{:S(2)}) collective-permute-start(bf16[2,24,3200]{2,1,0:T(8,128)(2,1)S(1)} %pad_maximum_fusion.4), channel_id=1, source_target_pairs={{0,2},{1,3},{2,0},{3,1},{4,6},{5,7},{6,4},{7,5},{8,10},{9,11},{10,... | collective-permute-start | bytes 921608 | tf_op jit(solution)/shard_map/ppermute | solution.py:306
  53.0 15.4 %collective-permute-start.5 = (bf16[2,24,3200]{2,1,0:T(8,128)(2,1)S(1)}, bf16[2,24,3200]{2,1,0:T(8,128)(2,1)S(1)}, u32[]{:S(2)}, u32[]{:S(2)}) collective-permute-start(bf16[2,24,3200]{2,1,0:T(8,128)(2,1)S(1)} %pad_maximum_fusion.5), channel_id=1, source_target_pairs={{0,4},{1,5},{2,6},{3,7},{4,0},{5,1},{6,2},{7,3},{8,12},{9,13},{10,... | collective-permute-start | bytes 921608 | tf_op jit(solution)/shard_map/ppermute | solution.py:306
  53.6 31.9 %collective-permute-start.13 = (bf16[4,24,3072]{2,1,0:T(8,128)(2,1)S(1)}, bf16[4,24,3072]{2,1,0:T(8,128)(2,1)S(1)}, u32[]{:S(2)}, u32[]{:S(2)}) collective-permute-start(bf16[4,24,3072]{2,1,0:T(8,128)(2,1)S(1)} %pad_maximum_fusion.2.refs_0_), channel_id=1, source_target_pairs={{0,4},{1,5},{2,6},{3,7},{4,0},{5,1},{6,2},{7,3},{8,12},{9,13},{10,... | collective-permute-start | bytes 1769480 | tf_op jit(solution)/shard_map/ppermute | solution.py:306
  55.2 33.9 %collective-permute-start.18 = (bf16[4,24,3072]{2,1,0:T(8,128)(2,1)S(1)}, bf16[4,24,3072]{2,1,0:T(8,128)(2,1)}, u32[]{:S(2)}, u32[]{:S(2)}) collective-permute-start(bf16[4,24,3072]{2,1,0:T(8,128)(2,1)S(1)} %pad_maximum_fusion.2.refs_0_), channel_id=1, source_target_pairs={{0,1},{1,0},{2,3},{3,2},{4,5},{5,4},{6,7},{7,6},{8,9},{9,8},{10,11... | collective-permute-start | bytes 1769480 | tf_op jit(solution)/shard_map/ppermute | solution.py:306
  61.9 25.8 %collective-permute-start.17 = (bf16[4,24,3072]{2,1,0:T(8,128)(2,1)S(1)}, bf16[4,24,3072]{2,1,0:T(8,128)(2,1)}, u32[]{:S(2)}, u32[]{:S(2)}) collective-permute-start(bf16[4,24,3072]{2,1,0:T(8,128)(2,1)S(1)} %pad_maximum_fusion.3.refs_2_), channel_id=1, source_target_pairs={{0,2},{1,3},{2,0},{3,1},{4,6},{5,7},{6,4},{7,5},{8,10},{9,11},{10,... | collective-permute-start | bytes 1769480 | tf_op jit(solution)/shard_map/ppermute | solution.py:306
  65.6 24.0 %collective-permute-start.20 = (bf16[4,24,3072]{2,1,0:T(8,128)(2,1)S(1)}, bf16[4,24,3072]{2,1,0:T(8,128)(2,1)}, u32[]{:S(2)}, u32[]{:S(2)}) collective-permute-start(bf16[4,24,3072]{2,1,0:T(8,128)(2,1)S(1)} %pad_maximum_fusion.3.refs_2_), channel_id=1, source_target_pairs={{0,1},{1,0},{2,3},{3,2},{4,5},{5,4},{6,7},{7,6},{8,9},{9,8},{10,11... | collective-permute-start | bytes 1769480 | tf_op jit(solution)/shard_map/ppermute | solution.py:306
  68.4 32.1 %collective-permute-start.2 = (bf16[4,24,3200]{2,1,0:T(8,128)(2,1)S(1)}, bf16[4,24,3200]{2,1,0:T(8,128)(2,1)S(1)}, u32[]{:S(2)}, u32[]{:S(2)}) collective-permute-start(bf16[4,24,3200]{2,1,0:T(8,128)(2,1)S(1)} %pad_maximum_fusion.refs_0_), channel_id=1, source_target_pairs={{0,4},{1,5},{2,6},{3,7},{4,0},{5,1},{6,2},{7,3},{8,12},{9,13},{10,... | collective-permute-start | bytes 1843208 | tf_op jit(solution)/shard_map/ppermute | solution.py:306
  86.3 14.3 %collective-permute-start.6 = (bf16[4,24,3200]{2,1,0:T(8,128)(2,1)S(1)}, bf16[4,24,3200]{2,1,0:T(8,128)(2,1)}, u32[]{:S(2)}, u32[]{:S(2)}) collective-permute-start(bf16[4,24,3200]{2,1,0:T(8,128)(2,1)S(1)} %pad_maximum_fusion.1.refs_2_), channel_id=1, source_target_pairs={{0,2},{1,3},{2,0},{3,1},{4,6},{5,7},{6,4},{7,5},{8,10},{9,11},{10,... | collective-permute-start | bytes 1843208 | tf_op jit(solution)/shard_map/ppermute | solution.py:306
  87.7 13.6 %collective-permute-start.19 = (bf16[4,24,3072]{2,1,0:T(8,128)(2,1)}, bf16[4,24,3072]{2,1,0:T(8,128)(2,1)}, u32[]{:S(2)}, u32[]{:S(2)}) collective-permute-start(bf16[4,24,3072]{2,1,0:T(8,128)(2,1)} %copy-done.2), channel_id=1, source_target_pairs={{0,1},{1,0},{2,3},{3,2},{4,5},{5,4},{6,7},{7,6},{8,9},{9,8},{10,11... | collective-permute-start | bytes 1769480 | tf_op jit(solution)/shard_map/ppermute | solution.py:306
  89.1 23.4 %collective-permute-start.7 = (bf16[4,24,3200]{2,1,0:T(8,128)(2,1)S(1)}, bf16[4,24,3200]{2,1,0:T(8,128)(2,1)}, u32[]{:S(2)}, u32[]{:S(2)}) collective-permute-start(bf16[4,24,3200]{2,1,0:T(8,128)(2,1)S(1)} %pad_maximum_fusion.refs_0_), channel_id=1, source_target_pairs={{0,1},{1,0},{2,3},{3,2},{4,5},{5,4},{6,7},{7,6},{8,9},{9,8},{10,11... | collective-permute-start | bytes 1843208 | tf_op jit(solution)/shard_map/ppermute | solution.py:306
  89.6 22.9 %collective-permute-start.9 = (bf16[4,24,3200]{2,1,0:T(8,128)(2,1)S(1)}, bf16[4,24,3200]{2,1,0:T(8,128)(2,1)}, u32[]{:S(2)}, u32[]{:S(2)}) collective-permute-start(bf16[4,24,3200]{2,1,0:T(8,128)(2,1)S(1)} %pad_maximum_fusion.1.refs_2_), channel_id=1, source_target_pairs={{0,1},{1,0},{2,3},{3,2},{4,5},{5,4},{6,7},{7,6},{8,9},{9,8},{10,11... | collective-permute-start | bytes 1843208 | tf_op jit(solution)/shard_map/ppermute | solution.py:306
  100.6 11.9 %collective-permute-start.8 = (bf16[4,24,3200]{2,1,0:T(8,128)(2,1)S(1)}, bf16[4,24,3200]{2,1,0:T(8,128)(2,1)}, u32[]{:S(2)}, u32[]{:S(2)}) collective-permute-start(bf16[4,24,3200]{2,1,0:T(8,128)(2,1)S(1)} %collective-permute-done.2.refs_1_), channel_id=1, source_target_pairs={{0,1},{1,0},{2,3},{3,2},{4,5},{5,4},{6,7},{7,6},{8,9},{9,8},{10,11... | collective-permute-start | bytes 1843208 | tf_op jit(solution)/shard_map/ppermute | solution.py:306
  100.6 11.9 %collective-permute-start.10 = (bf16[4,24,3200]{2,1,0:T(8,128)(2,1)}, bf16[4,24,3200]{2,1,0:T(8,128)(2,1)}, u32[]{:S(2)}, u32[]{:S(2)}) collective-permute-start(bf16[4,24,3200]{2,1,0:T(8,128)(2,1)} %collective-permute-done.6.refs_3_), channel_id=1, source_target_pairs={{0,1},{1,0},{2,3},{3,2},{4,5},{5,4},{6,7},{7,6},{8,9},{9,8},{10,11... | collective-permute-start | bytes 1843208 | tf_op jit(solution)/shard_map/ppermute | solution.py:306
  158.0 15.9 %collective-permute-start.55 = (bf16[4,96,768]{2,1,0:T(8,128)(2,1)}, bf16[4,96,768]{2,1,0:T(8,128)(2,1)}, u32[]{:S(2)}, u32[]{:S(2)}) collective-permute-start(bf16[4,96,768]{2,1,0:T(8,128)(2,1)} %get-tuple-element.63), channel_id=1, source_target_pairs={{0,4},{1,5},{2,6},{3,7},{4,0},{5,1},{6,2},{7,3},{8,12},{9,13},{10,... | collective-permute-start | bytes 1769480 | tf_op jit(solution)/shard_map/ppermute | solution.py:306
  159.3 18.1 %collective-permute-start.52 = (bf16[4,96,768]{2,1,0:T(8,128)(2,1)}, bf16[4,96,768]{2,1,0:T(8,128)(2,1)}, u32[]{:S(2)}, u32[]{:S(2)}) collective-permute-start(bf16[4,96,768]{2,1,0:T(8,128)(2,1)} %get-tuple-element.65), channel_id=1, source_target_pairs={{0,2},{1,3},{2,0},{3,1},{4,6},{5,7},{6,4},{7,5},{8,10},{9,11},{10,... | collective-permute-start | bytes 1769480 | tf_op jit(solution)/shard_map/ppermute | solution.py:306
  175.9 8.8 %collective-permute-start.56 = (bf16[2,96,768]{2,1,0:T(8,128)(2,1)}, bf16[2,96,768]{2,1,0:T(8,128)(2,1)}, u32[]{:S(2)}, u32[]{:S(2)}) collective-permute-start(bf16[2,96,768]{2,1,0:T(8,128)(2,1)} %get-tuple-element.85), channel_id=1, source_target_pairs={{0,2},{1,3},{2,0},{3,1},{4,6},{5,7},{6,4},{7,5},{8,10},{9,11},{10,... | collective-permute-start | bytes 884744 | tf_op jit(solution)/shard_map/ppermute | solution.py:306
  179.4 8.6 %collective-permute-start.53 = (bf16[2,96,768]{2,1,0:T(8,128)(2,1)}, bf16[2,96,768]{2,1,0:T(8,128)(2,1)}, u32[]{:S(2)}, u32[]{:S(2)}) collective-permute-start(bf16[2,96,768]{2,1,0:T(8,128)(2,1)} %get-tuple-element.83), channel_id=1, source_target_pairs={{0,4},{1,5},{2,6},{3,7},{4,0},{5,1},{6,2},{7,3},{8,12},{9,13},{10,... | collective-permute-start | bytes 884744 | tf_op jit(solution)/shard_map/ppermute | solution.py:306
  185.7 8.6 %collective-permute-start.58 = (bf16[96,768]{1,0:T(8,128)(2,1)S(1)}, bf16[96,768]{1,0:T(8,128)(2,1)S(1)}, u32[]{:S(2)}, u32[]{:S(2)}) collective-permute-start(bf16[96,768]{1,0:T(8,128)(2,1)S(1)} %get-tuple-element.96), channel_id=1, source_target_pairs={{0,24},{1,25},{2,26},{3,27},{4,28},{5,29},{6,30},{7,31},{8,16},{9,... | collective-permute-start | bytes 442376 | tf_op jit(solution)/shard_map/ppermute | solution.py:306
  188.0 11.9 %collective-permute-start.57 = (bf16[96,768]{1,0:T(8,128)(2,1)S(1)}, bf16[96,768]{1,0:T(8,128)(2,1)S(1)}, u32[]{:S(2)}, u32[]{:S(2)}) collective-permute-start(bf16[96,768]{1,0:T(8,128)(2,1)S(1)} %get-tuple-element.95), channel_id=1, source_target_pairs={{0,16},{1,17},{2,18},{3,19},{4,20},{5,21},{6,22},{7,23},{8,24},{9,... | collective-permute-start | bytes 442376 | tf_op jit(solution)/shard_map/ppermute | solution.py:306
  189.0 10.9 %collective-permute-start.54 = (bf16[96,768]{1,0:T(8,128)(2,1)S(1)}, bf16[96,768]{1,0:T(8,128)(2,1)S(1)}, u32[]{:S(2)}, u32[]{:S(2)}) collective-permute-start(bf16[96,768]{1,0:T(8,128)(2,1)S(1)} %fusion.64), channel_id=1, source_target_pairs={{0,8},{1,9},{2,10},{3,11},{4,12},{5,13},{6,14},{7,15},{8,0},{9,1},... | collective-permute-start | bytes 442376 | tf_op jit(solution)/shard_map/ppermute | solution.py:306
  244.0 8.4 %collective-permute-start.22 = (f32[13440]{0:T(1024)S(1)}, f32[13440]{0:T(1024)S(1)}, u32[]{:S(2)}, u32[]{:S(2)}) collective-permute-start(f32[13440]{0:T(1024)S(1)} %concatenate.53), channel_id=1, source_target_pairs={{0,1},{1,0},{2,3},{3,2},{4,5},{5,4},{6,7},{7,6},{8,9},{9,8},{10,11... | collective-permute-start | bytes 161288 | tf_op jit(solution)/shard_map/ppermute | solution.py:306
  251.9 34.2 %collective-permute-start.27 = (bf16[16,24,2304]{2,1,0:T(8,128)(2,1)S(1)}, bf16[16,24,2304]{2,1,0:T(8,128)(2,1)S(1)}, u32[]{:S(2)}, u32[]{:S(2)}) collective-permute-start(bf16[16,24,2304]{2,1,0:T(8,128)(2,1)S(1)} %bitcast.152), channel_id=1, source_target_pairs={{0,1},{1,0},{2,3},{3,2},{4,5},{5,4},{6,7},{7,6},{8,9},{9,8},{10,11... | collective-permute-start | bytes 5308424 | tf_op jit(solution)/shard_map/ppermute | solution.py:306
  251.9 19.0 %collective-permute-start.35 = (bf16[16,24,768]{2,1,0:T(8,128)(2,1)S(1)}, bf16[16,24,768]{2,1,0:T(8,128)(2,1)S(1)}, u32[]{:S(2)}, u32[]{:S(2)}) collective-permute-start(bf16[16,24,768]{2,1,0:T(8,128)(2,1)S(1)} %bitcast.153), channel_id=1, source_target_pairs={{0,1},{1,0},{2,3},{3,2},{4,5},{5,4},{6,7},{7,6},{8,9},{9,8},{10,11... | collective-permute-start | bytes 1769480 | tf_op jit(solution)/shard_map/ppermute | solution.py:306
  258.0 48.0 %collective-permute-start.43 = (bf16[16,24,3072]{2,1,0:T(8,128)(2,1)}, bf16[16,24,3072]{2,1,0:T(8,128)(2,1)}, u32[]{:S(2)}, u32[]{:S(2)}) collective-permute-start(bf16[16,24,3072]{2,1,0:T(8,128)(2,1)} %bitcast.32), channel_id=1, source_target_pairs={{0,1},{1,0},{2,3},{3,2},{4,5},{5,4},{6,7},{7,6},{8,9},{9,8},{10,11... | collective-permute-start | bytes 7077896 | tf_op jit(solution)/shard_map/ppermute | solution.py:306
  281.5 10.8 %collective-permute-start.42 = (bf16[24,768]{1,0:T(8,128)(2,1)S(1)}, bf16[24,768]{1,0:T(8,128)(2,1)}, u32[]{:S(2)}, u32[]{:S(2)}) collective-permute-start(bf16[24,768]{1,0:T(8,128)(2,1)S(1)} %get-tuple-element.116), channel_id=1, source_target_pairs={{0,24},{1,25},{2,26},{3,27},{4,28},{5,29},{6,30},{7,31},{8,16},{9,... | collective-permute-start | bytes 110600 | tf_op jit(solution)/shard_map/ppermute | solution.py:306
  282.7 9.7 %collective-permute-start.41 = (bf16[24,768]{1,0:T(8,128)(2,1)S(1)}, bf16[24,768]{1,0:T(8,128)(2,1)}, u32[]{:S(2)}, u32[]{:S(2)}) collective-permute-start(bf16[24,768]{1,0:T(8,128)(2,1)S(1)} %get-tuple-element.115), channel_id=1, source_target_pairs={{0,16},{1,17},{2,18},{3,19},{4,20},{5,21},{6,22},{7,23},{8,24},{9,... | collective-permute-start | bytes 110600 | tf_op jit(solution)/shard_map/ppermute | solution.py:306
  283.9 8.5 %collective-permute-start.38 = (bf16[24,768]{1,0:T(8,128)(2,1)S(1)}, bf16[24,768]{1,0:T(8,128)(2,1)S(1)}, u32[]{:S(2)}, u32[]{:S(2)}) collective-permute-start(bf16[24,768]{1,0:T(8,128)(2,1)S(1)} %fusion.74), channel_id=1, source_target_pairs={{0,8},{1,9},{2,10},{3,11},{4,12},{5,13},{6,14},{7,15},{8,0},{9,1},... | collective-permute-start | bytes 110600 | tf_op jit(solution)/shard_map/ppermute | solution.py:306
  287.5 8.6 %collective-permute-start.31 = (bf16[4,24,2304]{2,1,0:T(8,128)(2,1)}, bf16[4,24,2304]{2,1,0:T(8,128)(2,1)}, u32[]{:S(2)}, u32[]{:S(2)}) collective-permute-start(bf16[4,24,2304]{2,1,0:T(8,128)(2,1)} %get-tuple-element.75), channel_id=1, source_target_pairs={{0,4},{1,5},{2,6},{3,7},{4,0},{5,1},{6,2},{7,3},{8,12},{9,13},{10,... | collective-permute-start | bytes 1327112 | tf_op jit(solution)/shard_map/ppermute | solution.py:306
  293.8 10.9 %collective-permute-start.28 = (bf16[4,24,2304]{2,1,0:T(8,128)(2,1)}, bf16[4,24,2304]{2,1,0:T(8,128)(2,1)S(1)}, u32[]{:S(2)}, u32[]{:S(2)}) collective-permute-start(bf16[4,24,2304]{2,1,0:T(8,128)(2,1)} %get-tuple-element.77), channel_id=1, source_target_pairs={{0,2},{1,3},{2,0},{3,1},{4,6},{5,7},{6,4},{7,5},{8,10},{9,11},{10,... | collective-permute-start | bytes 1327112 | tf_op jit(solution)/shard_map/ppermute | solution.py:306
  297.2 13.2 %collective-permute-start.32 = (bf16[2,24,2304]{2,1,0:T(8,128)(2,1)S(1)}, bf16[2,24,2304]{2,1,0:T(8,128)(2,1)S(1)}, u32[]{:S(2)}, u32[]{:S(2)}) collective-permute-start(bf16[2,24,2304]{2,1,0:T(8,128)(2,1)S(1)} %get-tuple-element.93), channel_id=1, source_target_pairs={{0,2},{1,3},{2,0},{3,1},{4,6},{5,7},{6,4},{7,5},{8,10},{9,11},{10,... | collective-permute-start | bytes 663560 | tf_op jit(solution)/shard_map/ppermute | solution.py:306
  304.8 7.4 %collective-permute-start.29 = (bf16[2,24,2304]{2,1,0:T(8,128)(2,1)S(1)}, bf16[2,24,2304]{2,1,0:T(8,128)(2,1)S(1)}, u32[]{:S(2)}, u32[]{:S(2)}) collective-permute-start(bf16[2,24,2304]{2,1,0:T(8,128)(2,1)S(1)} %get-tuple-element.91), channel_id=1, source_target_pairs={{0,4},{1,5},{2,6},{3,7},{4,0},{5,1},{6,2},{7,3},{8,12},{9,13},{10,... | collective-permute-start | bytes 663560 | tf_op jit(solution)/shard_map/ppermute | solution.py:306
  308.4 13.1 %collective-permute-start.47 = (bf16[4,24,3072]{2,1,0:T(8,128)(2,1)S(1)}, bf16[4,24,3072]{2,1,0:T(8,128)(2,1)S(1)}, u32[]{:S(2)}, u32[]{:S(2)}) collective-permute-start(bf16[4,24,3072]{2,1,0:T(8,128)(2,1)S(1)} %get-tuple-element.67), channel_id=1, source_target_pairs={{0,4},{1,5},{2,6},{3,7},{4,0},{5,1},{6,2},{7,3},{8,12},{9,13},{10,... | collective-permute-start | bytes 1769480 | tf_op jit(solution)/shard_map/ppermute | solution.py:306
  309.5 13.8 %collective-permute-start.44 = (bf16[4,24,3072]{2,1,0:T(8,128)(2,1)S(1)}, bf16[4,24,3072]{2,1,0:T(8,128)(2,1)S(1)}, u32[]{:S(2)}, u32[]{:S(2)}) collective-permute-start(bf16[4,24,3072]{2,1,0:T(8,128)(2,1)S(1)} %get-tuple-element.69), channel_id=1, source_target_pairs={{0,2},{1,3},{2,0},{3,1},{4,6},{5,7},{6,4},{7,5},{8,10},{9,11},{10,... | collective-permute-start | bytes 1769480 | tf_op jit(solution)/shard_map/ppermute | solution.py:306
  310.5 19.7 %collective-permute-start.34 = (bf16[24,2304]{1,0:T(8,128)(2,1)S(1)}, bf16[24,2304]{1,0:T(8,128)(2,1)S(1)}, u32[]{:S(2)}, u32[]{:S(2)}) collective-permute-start(bf16[24,2304]{1,0:T(8,128)(2,1)S(1)} %get-tuple-element.108), channel_id=1, source_target_pairs={{0,24},{1,25},{2,26},{3,27},{4,28},{5,29},{6,30},{7,31},{8,16},{9,... | collective-permute-start | bytes 331784 | tf_op jit(solution)/shard_map/ppermute | solution.py:306
  312.2 20.9 %collective-permute-start.33 = (bf16[24,2304]{1,0:T(8,128)(2,1)S(1)}, bf16[24,2304]{1,0:T(8,128)(2,1)S(1)}, u32[]{:S(2)}, u32[]{:S(2)}) collective-permute-start(bf16[24,2304]{1,0:T(8,128)(2,1)S(1)} %get-tuple-element.107), channel_id=1, source_target_pairs={{0,16},{1,17},{2,18},{3,19},{4,20},{5,21},{6,22},{7,23},{8,24},{9,... | collective-permute-start | bytes 331784 | tf_op jit(solution)/shard_map/ppermute | solution.py:306
  312.2 20.9 %collective-permute-start.30 = (bf16[24,2304]{1,0:T(8,128)(2,1)S(1)}, bf16[24,2304]{1,0:T(8,128)(2,1)S(1)}, u32[]{:S(2)}, u32[]{:S(2)}) collective-permute-start(bf16[24,2304]{1,0:T(8,128)(2,1)S(1)} %fusion.67), channel_id=1, source_target_pairs={{0,8},{1,9},{2,10},{3,11},{4,12},{5,13},{6,14},{7,15},{8,0},{9,1},... | collective-permute-start | bytes 331784 | tf_op jit(solution)/shard_map/ppermute | solution.py:306
  328.5 7.2 %collective-permute-start.50 = (bf16[24,3072]{1,0:T(8,128)(2,1)S(1)}, bf16[24,3072]{1,0:T(8,128)(2,1)S(1)}, u32[]{:S(2)}, u32[]{:S(2)}) collective-permute-start(bf16[24,3072]{1,0:T(8,128)(2,1)S(1)} %get-tuple-element.98), channel_id=1, source_target_pairs={{0,24},{1,25},{2,26},{3,27},{4,28},{5,29},{6,30},{7,31},{8,16},{9,... | collective-permute-start | bytes 442376 | tf_op jit(solution)/shard_map/ppermute | solution.py:306
  330.2 8.5 %collective-permute-start.49 = (bf16[24,3072]{1,0:T(8,128)(2,1)S(1)}, bf16[24,3072]{1,0:T(8,128)(2,1)S(1)}, u32[]{:S(2)}, u32[]{:S(2)}) collective-permute-start(bf16[24,3072]{1,0:T(8,128)(2,1)S(1)} %get-tuple-element.97), channel_id=1, source_target_pairs={{0,16},{1,17},{2,18},{3,19},{4,20},{5,21},{6,22},{7,23},{8,24},{9,... | collective-permute-start | bytes 442376 | tf_op jit(solution)/shard_map/ppermute | solution.py:306
  330.2 8.5 %collective-permute-start.46 = (bf16[24,3072]{1,0:T(8,128)(2,1)S(1)}, bf16[24,3072]{1,0:T(8,128)(2,1)S(1)}, u32[]{:S(2)}, u32[]{:S(2)}) collective-permute-start(bf16[24,3072]{1,0:T(8,128)(2,1)S(1)} %fusion.61), channel_id=1, source_target_pairs={{0,8},{1,9},{2,10},{3,11},{4,12},{5,13},{6,14},{7,15},{8,0},{9,1},... | collective-permute-start | bytes 442376 | tf_op jit(solution)/shard_map/ppermute | solution.py:306
  (55 other events, 385.2 us)
Sparse Core Ops, SparseCore 0:
  26.4 78.1 all-gather.1

commit v3 on v2

--- a/solution.py
+++ b/solution.py
@@ -16,10 +16,13 @@
 NWS = 5
 EDGE = 8
 LENGTH = WIN * WIN
-PAIRS = HEADS // 2
+GROUPS = 2
+PAIRS = HEADS // 2 // GROUPS
+GROUP = PAIRS * 128
 BLOCK = 200
 SCALE = HEAD_DIM ** (-0.5)
 EPS = 1e-06
+QUICK = pl.CostEstimate(flops=1, bytes_accessed=1, transcendentals=0)
 LANES = 256
 BF = jnp.bfloat16
 F32 = jnp.float32
@@ -36,18 +39,19 @@
                 continue
             y, x = divmod(slot, WIN)
             for base in (0, 64):
-                for lane in (y, 16 + y, 32 + x, 48 + x):
-                    onehot[win, row, base + lane] = 1.0
-            shift[win, :8, row] = WIN - 1 - y
-            shift[win, 8:, row] = WIN - 1 - x
+                for lane in (0, 16):
+                    onehot[win, row, base + lane + WIN - 1 - y] = 1.0
+                    onehot[win, row, base + 32 + lane + WIN - 1 - x] = 1.0
+            shift[win, :8, row] = y
+            shift[win, 8:, row] = x
     return onehot, shift
 
 
 def table_lanes(rel_pos_h, rel_pos_w):
     flip = jnp.concatenate(
         (
-            jnp.pad(rel_pos_h[::-1], ((0, 5), (0, 0))),
-            jnp.pad(rel_pos_w[::-1], ((0, 5), (0, 0))),
+            jnp.pad(rel_pos_h, ((0, 5), (0, 0))),
+            jnp.pad(rel_pos_w, ((0, 5), (0, 0))),
         ),
         axis=0,
     ).astype(BF) * BF(1.0 / SCALE)
@@ -55,12 +59,6 @@
     return jnp.concatenate(
         (jnp.concatenate((nothing, flip), axis=1), jnp.concatenate((flip, nothing), axis=1)), axis=0
     )
-
-
-def table_grads(lanes_grad):
-    folded = (lanes_grad[64:, :64] + lanes_grad[:64, 64:]) * np.float32(1.0 / SCALE)
-    count = 2 * WIN - 1
-    return folded[:count][::-1], folded[32 : 32 + count][::-1]
 
 
 def dot_nn(a, b):
@@ -217,7 +215,7 @@
         parts[1].append(jnp.where(low, by_key[0], by_key[1]))
         parts[2].append(jnp.where(low, by_value[0], by_value[1]))
     for block in range(3):
-        at = pl.multiple_of(block * D + pair * 128, 128)
+        at = pl.multiple_of(block * GROUP + pair * 128, 128)
         grad_qkv_ref[:, pl.ds(at, 128)] = merge_windows(*parts[block]).astype(BF)
     table_grad_ref[...] += table_total
 
@@ -242,9 +240,10 @@
         in_specs=columns + constants,
         out_specs=[pl.BlockSpec((rows, 128), lambda pair: (0, pair)), probs_spec],
         out_shape=[
-            jax.ShapeDtypeStruct((rows, D), BF),
+            jax.ShapeDtypeStruct((rows, GROUP), BF),
             jax.ShapeDtypeStruct((PAIRS, 4, BLOCK, LANES), F32),
         ],
+        cost_estimate=QUICK,
         compiler_params=pltpu.CompilerParams(vmem_limit_bytes=32 * 1024 * 1024),
         name="attention",
     )(qkv, qkv, qkv, table, onehot, shift)
@@ -257,11 +256,12 @@
         attn_bwd_kernel,
         grid=(PAIRS,),
         in_specs=columns + [pl.BlockSpec((rows, 128), lambda pair: (0, pair)), probs_spec] + constants,
-        out_specs=[whole(rows, 3 * D), whole(128, 128)],
+        out_specs=[whole(rows, 3 * GROUP), whole(128, 128)],
         out_shape=[
-            jax.ShapeDtypeStruct((rows, 3 * D), BF),
+            jax.ShapeDtypeStruct((rows, 3 * GROUP), BF),
             jax.ShapeDtypeStruct((128, 128), F32),
         ],
+        cost_estimate=QUICK,
         compiler_params=pltpu.CompilerParams(vmem_limit_bytes=32 * 1024 * 1024),
         name="attention_back",
     )(qkv, qkv, qkv, grad_mixed, probs, table, onehot, shift)
@@ -302,31 +302,556 @@
     return np.float32(1.0 / np.sqrt(2.0 * np.pi)) * jnp.exp(-0.5 * values * values)
 
 
+def copy_rows(pieces, columns, out, to, sems):
+    rows = pieces[0].shape[0]
+    lo, width = columns
+    return [
+        pltpu.make_async_copy(
+            piece.at[:, pl.ds(lo, width)],
+            out.at[index * rows : (index + 1) * rows, pl.ds(to, width)],
+            sems.at[index],
+        )
+        for index, piece in enumerate(pieces)
+    ]
+
+
+def start_all(copies):
+    for copy in copies:
+        copy.start()
+
+
+def wait_all(copies):
+    for copy in copies:
+        copy.wait()
+
+
+def front_kernel(tokens_ref, live_ref, order_ref, rows_ref, b_qkv_ref, *rest):
+    pieces, (normed_ref, one_ref, two_ref, weight, sem) = rest[:PIECES], rest[PIECES:]
+    copies = [copy_rows(pieces, (block * D, D), weight, block * D, sem.at[block]) for block in range(3)]
+    for block in copies:
+        start_all(block)
+    unit, _ = normalise(tokens_ref[...].astype(F32))
+    normed = ((unit * rows_ref[0:1, :] + rows_ref[1:2, :]) * live_ref[...]).astype(BF)
+    normed = dot_nn(normed, order_ref[...]).astype(BF)
+    normed_ref[...] = normed
+    for block in range(3):
+        wait_all(copies[block])
+        at = block * D
+        values = (dot_nn(normed, weight[:, at : at + D]) + b_qkv_ref[:, at : at + D]).astype(BF)
+        one_ref[:, block * GROUP : (block + 1) * GROUP] = values[:, :GROUP]
+        two_ref[:, block * GROUP : (block + 1) * GROUP] = values[:, GROUP:]
+
+
+PIECES = 8
+HBM = pl.BlockSpec(memory_space=pl.ANY)
+VMEM = pl.BlockSpec(memory_space=pltpu.VMEM)
+SMEM = pl.BlockSpec(memory_space=pltpu.SMEM)
+
+
+def front(tokens, live, order, vectors, b_qkv, pieces):
+    rows = tokens.shape[0]
+    return pl.pallas_call(
+        front_kernel,
+        in_specs=[VMEM] * 5 + [HBM] * PIECES,
+        out_specs=[VMEM] * 3,
+        out_shape=[struct((rows, D), BF)] + [struct((rows, 3 * GROUP), BF)] * GROUPS,
+        scratch_shapes=[pltpu.VMEM((D, 3 * D), BF), pltpu.SemaphoreType.DMA((3, PIECES))],
+        cost_estimate=QUICK,
+        compiler_params=pltpu.CompilerParams(vmem_limit_bytes=32 * 1024 * 1024),
+        name="front",
+    )(tokens, live, order, vectors, b_qkv, *in_hbm(pieces))
+
+
+def proj_kernel(tokens_ref, one_ref, two_ref, order_ref, rows_ref, *rest):
+    pieces, (residual_ref, normed_ref, turned_ref, mixed_ref, w_proj, sem) = rest[:PIECES], rest[PIECES:]
+    b_proj, gain, bias = (rows_ref[i : i + 1, :] for i in range(3))
+    copies = copy_rows(pieces, (0, D), w_proj, 0, sem)
+    start_all(copies)
+    mixed = dot_nn(one_ref[...], order_ref[:GROUP, :]) + dot_nn(two_ref[...], order_ref[GROUP:, :])
+    mixed = mixed.astype(BF)
+    mixed_ref[...] = mixed
+    wait_all(copies)
+    values = tokens_ref[...].astype(F32) + dot_nn(mixed, w_proj[...]) + b_proj
+    residual_ref[...] = values
+    low = (normalise(values)[0] * gain + bias).astype(BF)
+    low = dot_nn(low, order_ref[...])
+    normed_ref[...] = low.astype(BF)
+    turned_ref[...] = low.T.astype(BF)
+
+
+def mlp_kernel(split_rows, owners, place_ref, me_ref, *rest):
+    normed_ref, turned_ref, residual_ref, mixed_ref, live_ref, out_grad_ref, *rest = rest
+    order_ref, rows_ref, b_up_ref, *rest = rest
+    up_pieces, rest = rest[:PIECES], rest[PIECES:]
+    down_pieces, rest = rest[: len(owners)], rest[len(owners) :]
+    output_ref, grad_residual_ref, grad_one_ref, grad_two_ref, kept_ref, sent_ref, *rest = rest
+    kept_proj_ref, sent_proj_ref, sums_ref, grad_b_ref, *rest = rest
+    if split_rows:
+        kept_down_ref, sent_down_ref, *rest = rest
+    else:
+        grad_down_ref, *rest = rest
+    branch, total, grad_normed, w_up, w_down, w_proj, staged, sem, up_sem, down_sem = rest
+    step = pl.program_id(0)
+    last = STEPS - 1
+    half = D // 2
+
+    def up_copies(index):
+        return copy_rows(up_pieces, (D + index * TILE, TILE), w_up, index * TILE, up_sem.at[index])
+
+    def proj_copies():
+        return copy_rows(up_pieces, (0, D), w_proj, 0, up_sem.at[STEPS])
+
+    def down_copies():
+        copies = []
+        for piece, masks in zip(down_pieces, owners):
+            rows = piece.shape[0] // len(masks)
+            for index, mask in enumerate(masks):
+                to = jnp.bitwise_xor(me_ref[0], mask) * rows
+                copies.append(
+                    pltpu.make_async_copy(
+                        piece.at[index * rows : (index + 1) * rows],
+                        w_down.at[pl.ds(pl.multiple_of(to, rows), rows)],
+                        down_sem.at[len(copies)],
+                    )
+                )
+        return copies
+
+    @pl.when(step == 0)
+    def _():
+        start_all(up_copies(0))
+        copies = down_copies()
+        start_all(copies)
+        for index in range(1, STEPS):
+            start_all(up_copies(index))
+        start_all(proj_copies())
+        branch[...] = (out_grad_ref[...].astype(F32) * live_ref[...]).astype(BF)
+        total[...] = jnp.zeros_like(total)
+        grad_normed[...] = jnp.zeros_like(grad_normed)
+        wait_all(copies)
+
+    wait_all(up_copies(step))
+    at = pl.multiple_of(step * TILE, TILE)
+    weight = w_down[pl.ds(at, TILE), :]
+    weight_up = w_up[:, pl.ds(at, TILE)]
+    hidden = dot_nn(normed_ref[...], weight_up) + b_up_ref[...]
+    grad_active = dot_nt(branch[...], weight)
+    cdf = normal_cdf(hidden)
+    active = (hidden * cdf).astype(BF)
+    grad_hidden = (grad_active * (cdf + hidden * normal_pdf(hidden))).astype(BF)
+    grad_down = dot_tn(active, branch[...]).astype(BF)
+    total[...] += dot_nn(active, weight)
+    sent_ref[...] = dot_nn(turned_ref[half:, :], grad_hidden).astype(BF)
+    kept_ref[...] = dot_nn(turned_ref[:half, :], grad_hidden).astype(BF)
+    grad_normed[...] += dot_nt(grad_hidden, weight_up)
+    grad_b_ref[...] = jnp.sum(grad_hidden.astype(F32), axis=0, keepdims=True)
+    if split_rows:
+        slot = lax.rem(step, 2)
+        blocks = staged.shape[1]
+
+        def copy(slot, block, out, to):
+            return pltpu.make_async_copy(staged.at[slot, block], out.at[to], sem.at[slot, block])
+
+        @pl.when(step >= 2)
+        def _():
+            for block in range(blocks):
+                copy(slot, block, kept_down_ref, 0).wait()
+
+        staged[slot] = grad_down.reshape(blocks, split_rows, D)
+        places = kept_down_ref.shape[0]
+        for block in range(blocks):
+            to = place_ref[step * blocks + block]
+
+            @pl.when(to < places)
+            def _():
+                copy(slot, block, kept_down_ref, to).start()
+
+            @pl.when(to >= places)
+            def _():
+                copy(slot, block, sent_down_ref, to - places).start()
+
+    else:
+        grad_down_ref[...] = grad_down
+
+    @pl.when(step == last)
+    def _():
+        wait_all(proj_copies())
+        gain, b_down = rows_ref[1:2, :], rows_ref[3:4, :]
+        live = live_ref[...]
+        residual = residual_ref[...]
+        output_ref[...] = ((residual + total[...] + b_down) * live).astype(BF)
+        grad = natural_order(grad_normed[...], order_ref[...])
+        unit, rstd = normalise(residual)
+        grad_residual = out_grad_ref[...].astype(F32) * live + normalise_back(
+            grad, unit, rstd, gain
+        )
+        grad_residual_ref[...] = grad_residual
+        grad_attn = grad_residual.astype(BF)
+        grad_mixed = dot_nt(grad_attn, w_proj[...]).astype(BF)
+        grad_mixed = dot_nt(grad_mixed, order_ref[...]).astype(BF)
+        grad_one_ref[...] = grad_mixed[:, :GROUP]
+        grad_two_ref[...] = grad_mixed[:, GROUP:]
+        sent_proj_ref[...] = dot_tn(mixed_ref[:, half:], grad_attn).astype(BF)
+        kept_proj_ref[...] = dot_tn(mixed_ref[:, :half], grad_attn).astype(BF)
+        sums_ref[0:1, :] = jnp.sum(grad_attn.astype(F32), axis=0, keepdims=True)
+        sums_ref[1:2, :] = jnp.sum(grad * unit, axis=0, keepdims=True)
+        sums_ref[2:3, :] = jnp.sum(grad, axis=0, keepdims=True)
+        sums_ref[3:4, :] = jnp.sum(branch[...].astype(F32), axis=0, keepdims=True)
+        sums_ref[4:, :] = jnp.zeros((4, D), F32)
+        if split_rows:
+            for last_slot in range(2):
+                for block in range(staged.shape[1]):
+                    pltpu.make_async_copy(
+                        staged.at[last_slot, block], kept_down_ref.at[0], sem.at[last_slot, block]
+                    ).wait()
+
+
+def natural_order(values, order):
+    top = values.astype(BF)
+    rest = (values - top.astype(F32)).astype(BF)
+    return dot_nt(top, order) + dot_nt(rest, order)
+
+
+TILE = 768
+STEPS = FF // TILE
+
+
+def whole(*shape):
+    return pl.BlockSpec(shape, lambda step: (0,) * len(shape))
+
+
+def struct(shape, dtype):
+    return jax.ShapeDtypeStruct(shape, dtype)
+
+
+def in_hbm(arrays):
+    return [pltpu.with_memory_space_constraint(array, pltpu.HBM) for array in arrays]
+
+
+def project(tokens, mixed, order, vectors, pieces):
+    rows = tokens.shape[0]
+    return pl.pallas_call(
+        proj_kernel,
+        in_specs=[VMEM] * 5 + [HBM] * PIECES,
+        out_specs=[VMEM] * 4,
+        out_shape=[
+            struct((rows, D), F32),
+            struct((rows, D), BF),
+            struct((D, rows), BF),
+            struct((rows, D), BF),
+        ],
+        scratch_shapes=[pltpu.VMEM((D, D), BF), pltpu.SemaphoreType.DMA((PIECES,))],
+        cost_estimate=QUICK,
+        compiler_params=pltpu.CompilerParams(vmem_limit_bytes=24 * 1024 * 1024),
+        name="project",
+    )(tokens, *mixed, order, vectors, *in_hbm(pieces))
+
+
+def mlp(
+    me, count, normed, turned, residual, mixed, live, out_grad, order, vectors, b_up, up_pieces, down_pieces
+):
+    rows = residual.shape[0]
+    block_rows = FF // count
+    split_rows = block_rows if block_rows % 16 == 0 else 0
+    column = lambda height: pl.BlockSpec((height, TILE), lambda step: (0, step))
+    inverse = np.argsort(np.array(sum_order(count)))
+    places = jnp.take(jnp.asarray(inverse, jnp.int32), jnp.bitwise_xor(me, np.arange(count)))
+    if split_rows:
+        owners = tuple(tuple(masks) for _, masks in down_pieces)
+        down_pieces = [stack.reshape(-1, D) for stack, _ in down_pieces]
+        half = struct((count // 2, block_rows, D), BF)
+        grad_specs, grad_shapes = [HBM] * 2, [half, half]
+        staged = (2, TILE // block_rows, block_rows, D)
+    else:
+        down_pieces = place(down_pieces, ((0, 0, D, 0),), (D,), me, count)
+        owners, me_down = ((0,),), jnp.zeros_like(me)
+        grad_specs = [pl.BlockSpec((TILE, D), lambda step: (step, 0))]
+        grad_shapes = [struct((FF, D), BF)]
+        staged = (2, 1, 16, 128)
+    wide, turn, square = (rows, D), (D, rows), (D, D)
+    results = pl.pallas_call(
+        functools.partial(mlp_kernel, split_rows, owners),
+        grid=(STEPS,),
+        in_specs=[
+            SMEM,
+            SMEM,
+            whole(*wide),
+            whole(*turn),
+            whole(*wide),
+            whole(*wide),
+            whole(rows, 1),
+            whole(*wide),
+            whole(*square),
+            whole(4, D),
+            column(1),
+        ]
+        + [HBM] * (PIECES + len(down_pieces)),
+        out_specs=[
+            whole(*wide),
+            whole(*wide),
+            whole(rows, GROUP),
+            whole(rows, GROUP),
+            column(D // 2),
+            column(D // 2),
+            whole(D // 2, D),
+            whole(D // 2, D),
+            whole(8, D),
+            column(1),
+        ]
+        + grad_specs,
+        out_shape=[
+            struct(wide, BF),
+            struct(wide, F32),
+            struct((rows, GROUP), BF),
+            struct((rows, GROUP), BF),
+            struct((D // 2, FF), BF),
+            struct((D // 2, FF), BF),
+            struct((D // 2, D), BF),
+            struct((D // 2, D), BF),
+            struct((8, D), F32),
+            struct((1, FF), F32),
+        ]
+        + grad_shapes,
+        scratch_shapes=[
+            pltpu.VMEM(wide, BF),
+            pltpu.VMEM(wide, F32),
+            pltpu.VMEM(wide, F32),
+            pltpu.VMEM((D, FF), BF),
+            pltpu.VMEM((FF, D), BF),
+            pltpu.VMEM(square, BF),
+            pltpu.VMEM(staged, BF),
+            pltpu.SemaphoreType.DMA(staged[:2]),
+            pltpu.SemaphoreType.DMA((1 + STEPS, PIECES)),
+            pltpu.SemaphoreType.DMA((sum(map(len, owners)),)),
+        ],
+        cost_estimate=QUICK,
+        compiler_params=pltpu.CompilerParams(vmem_limit_bytes=48 * 1024 * 1024),
+        name="mlp",
+    )(
+        places,
+        (me if split_rows else me_down).reshape(1),
+        normed,
+        turned,
+        residual,
+        mixed,
+        live,
+        out_grad,
+        order,
+        vectors,
+        b_up,
+        *in_hbm(up_pieces),
+        *in_hbm(down_pieces),
+    )
+    down = results[10:] if split_rows else pick(results[10], me, count)
+    return tuple(results[:10]) + (tuple(down),)
+
+
+def first_norm_kernel(
+    grad_one_ref,
+    grad_two_ref,
+    tokens_ref,
+    live_ref,
+    gain_ref,
+    order_ref,
+    grad_residual_ref,
+    mlp_sums_ref,
+    grad_b_ref,
+    tables_one_ref,
+    tables_two_ref,
+    *rest,
+):
+    pieces, (tokens_grad_ref, sums_ref, total, columns, weight, sem) = rest[:PIECES], rest[PIECES:]
+    step = pl.program_id(0)
+
+    def copies(index):
+        group, block = index // 3, lax.rem(index, 3)
+        return copy_rows(
+            pieces,
+            (pl.multiple_of(block * D + group * GROUP, 128), GROUP),
+            weight,
+            pl.multiple_of(index * GROUP, 128),
+            sem.at[index],
+        )
+
+    @pl.when(step == 0)
+    def _():
+        for index in range(6):
+            start_all(copies(jnp.int32(index)))
+        total[...] = jnp.zeros_like(total)
+
+    wait_all(copies(step))
+    for group, grad_ref in ((0, grad_one_ref), (1, grad_two_ref)):
+
+        @pl.when(step // 3 == group)
+        def _():
+            grad = grad_ref[...]
+            at = pl.multiple_of(step * GROUP, 128)
+            total[...] += dot_nt(grad, weight[:, pl.ds(at, GROUP)])
+            columns[pl.ds(step, 1), :] = jnp.sum(grad.astype(F32), axis=0, keepdims=True)
+
+    @pl.when(step == 5)
+    def _():
+        unit, rstd = normalise(tokens_ref[...].astype(F32))
+        grad = natural_order(total[...], order_ref[...]) * live_ref[...]
+        tokens_grad_ref[...] = (
+            grad_residual_ref[...] + normalise_back(grad, unit, rstd, gain_ref[...])
+        ).astype(BF)
+        qkv = [
+            columns[group * 3 + block : group * 3 + block + 1, :]
+            for block in range(3)
+            for group in range(GROUPS)
+        ]
+        vectors = [
+            [jnp.sum(grad * unit, axis=0, keepdims=True)],
+            [jnp.sum(grad, axis=0, keepdims=True)],
+            qkv,
+            [mlp_sums_ref[0:1, :]],
+            [mlp_sums_ref[1:2, :]],
+            [mlp_sums_ref[2:3, :]],
+            [grad_b_ref[...]],
+            [mlp_sums_ref[3:4, :]],
+        ]
+        at = 0
+        for vector in vectors:
+            for piece in vector:
+                for lane in range(0, piece.shape[1], 128):
+                    sums_ref[at : at + 1, :] = piece[:, lane : lane + 128]
+                    at += 1
+        sums_ref[at:TABLE_ROW, :] = jnp.zeros((TABLE_ROW - at, 128), F32)
+        tables = (tables_one_ref[...] + tables_two_ref[...]) * (1.0 / SCALE)
+        low = lax.broadcasted_iota(jnp.int32, (32, 128), 1) < 64
+        sums_ref[TABLE_ROW:, :] = jnp.where(
+            low,
+            tables[64:96] + pltpu.roll(tables[:32], 64, 1),
+            pltpu.roll(tables[96:], 64, 1) + tables[32:64],
+        )
+
+
+TABLE_ROW = 80
+SUM_ROWS = TABLE_ROW + 32
+
+
+def first_norm_back(grads, pieces, tokens, live, gain, order, grad_residual, sums, b_up, tables):
+    rows = tokens.shape[0]
+    first = lambda height: pl.BlockSpec((height, GROUP), lambda step: (0, jnp.minimum(step, 2)))
+    second = lambda height: pl.BlockSpec((height, GROUP), lambda step: (0, jnp.maximum(step, 3) - 3))
+    return pl.pallas_call(
+        first_norm_kernel,
+        grid=(6,),
+        in_specs=[
+            first(rows),
+            second(rows),
+            whole(rows, D),
+            whole(rows, 1),
+            whole(1, D),
+            whole(D, D),
+            whole(rows, D),
+            whole(8, D),
+            whole(1, FF),
+            whole(128, 128),
+            whole(128, 128),
+        ]
+        + [HBM] * PIECES,
+        out_specs=[whole(rows, D), whole(SUM_ROWS, 128)],
+        out_shape=[struct((rows, D), BF), struct((SUM_ROWS, 128), F32)],
+        scratch_shapes=[
+            pltpu.VMEM((rows, D), F32),
+            pltpu.VMEM((8, GROUP), F32),
+            pltpu.VMEM((D, 3 * D), BF),
+            pltpu.SemaphoreType.DMA((6, PIECES)),
+        ],
+        cost_estimate=QUICK,
+        compiler_params=pltpu.CompilerParams(vmem_limit_bytes=32 * 1024 * 1024),
+        name="first_norm_back",
+    )(*grads, tokens, live, gain, order, grad_residual, sums, b_up, *tables, *in_hbm(pieces))
+
+
+def own_kernel(sizes, me_ref, sums_ref, *refs):
+    outs, (table_h_ref, table_w_ref) = refs[:-2], refs[-2:]
+    lane = lax.broadcasted_iota(jnp.int32, (1, 128), 1)
+    row = 0
+    for size, whole_size, out in zip(sizes, WHOLE_SIZES, outs):
+        start = me_ref[0] * size
+        at, shift = row + start // 128, lax.rem(start, 128)
+        here = pltpu.roll(sums_ref[pl.ds(at, 1), :], lax.rem(128 - shift, 128), 1)
+        there = pltpu.roll(sums_ref[pl.ds(at + 1, 1), :], lax.rem(128 - shift, 128), 1)
+        out[...] = jnp.where(lane + shift < 128, here, there)[:, :size]
+        row += whole_size // 128
+    count = 2 * WIN - 1
+    table_h_ref[...] = sums_ref[TABLE_ROW : TABLE_ROW + count, :HEAD_DIM]
+    table_w_ref[...] = pltpu.roll(sums_ref[TABLE_ROW:, :], 64, 1)[:count, :HEAD_DIM]
+
+
+WHOLE_SIZES = (D, D, 3 * D, D, D, D, FF, D)
+
+
+def own_small(sums, me, sizes):
+    table = struct((2 * WIN - 1, HEAD_DIM), F32)
+    return pl.pallas_call(
+        functools.partial(own_kernel, tuple(sizes)),
+        in_specs=[
+            pl.BlockSpec(memory_space=pltpu.SMEM),
+            pl.BlockSpec(memory_space=pltpu.VMEM),
+        ],
+        out_specs=[pl.BlockSpec(memory_space=pltpu.VMEM)] * (len(sizes) + 2),
+        out_shape=[struct((1, size), F32) for size in sizes] + [table, table],
+        name="own_small",
+    )(me.reshape(1), sums)
+
+
 def hop(array, mask, count):
     return lax.ppermute(array, "fsdp", [(i, i ^ mask) for i in range(count)])
 
 
 def hop_plan(count):
     far = count // 4
-    return (far, 2 * far, 3 * far), [1 << bit for bit in range(1, far.bit_length() - 1)]
-
-
-def gather_pieces(shard, count):
-    far, middle = hop_plan(count)
-    received = [hop(shard, mask, count) for mask in far]
-    stacks = (
-        [jnp.stack((shard, received[0])), [0, far[0]], middle],
-        [jnp.stack((received[1], received[2])), [far[1], far[2]], middle[::-1]],
-    )
-    pieces = []
-    for stack, owners, masks in stacks:
-        for mask in masks[:-1]:
-            stack = jnp.concatenate((stack, hop(stack, mask, count)), axis=0)
-            owners = owners + [owner ^ mask for owner in owners]
-        pieces.append((stack, owners))
-        pieces.append((hop(stack, masks[-1], count), [owner ^ masks[-1] for owner in owners]))
-    other = [(hop(stack, 1, count), [owner ^ 1 for owner in owners]) for stack, owners in pieces]
-    return pieces + other
+    return 2 * far, far, [1 << bit for bit in range(1, far.bit_length() - 1)]
+
+
+def after(values, deps):
+    if not deps:
+        return list(values)
+    return list(lax.optimization_barrier(tuple(values) + tuple(deps))[: len(values)])
+
+
+def gather_stages(shard, count, pieces):
+    farthest, far, middle = hop_plan(count)
+    deps = yield
+    (shard,) = after([shard], deps)
+    got = hop(shard, farthest, count)
+    deps = yield [shard]
+    (got,) = after([got], deps)
+    near = jnp.stack((shard, got))
+    got = hop(near, far, count)
+    deps = yield [near]
+    (got,) = after([got], deps)
+    stacks = [near, got]
+    owners = [[0, farthest], [far, far ^ farthest]]
+    for masks in zip(middle, middle[::-1]):
+        got = [hop(stack, mask, count) for stack, mask in zip(stacks, masks)]
+        deps = yield stacks
+        if masks[0] != middle[-1]:
+            got = after(got, deps)
+            stacks = [jnp.concatenate(pair, axis=0) for pair in zip(stacks, got)]
+            owners = [own + [o ^ m for o in own] for own, m in zip(owners, masks)]
+    other = [hop(stack, 1, count) for stack in stacks]
+    deps = yield stacks
+    got = after(got, deps)
+    late = [hop(stack, 1, count) for stack in got]
+    for core, sides in ((0, (stacks, got)), (1, (other, late))):
+        for stack, arrived, own, mask in zip(*sides, owners, masks):
+            own = [o ^ core for o in own]
+            pieces += [(stack, own), (arrived, [o ^ mask for o in own])]
+    yield got
+
+
+def start(stages):
+    next(stages)
+    return stages
+
+
+def finish(stages):
+    for _ in stages:
+        pass
 
 
 def place_kernel(owners, columns, me_ref, *refs):
@@ -335,10 +860,12 @@
     for stack, stack_owners in zip(stacks, owners):
         for index, mask in enumerate(stack_owners):
             owner = jnp.bitwise_xor(me_ref[0], mask)
-            for out, (lo, hi) in zip(outs, columns):
+            for out, lo, hi, to in columns:
                 copies.append(
                     pltpu.make_async_copy(
-                        stack.at[index, :, lo:hi], out.at[owner], sem.at[len(copies)]
+                        stack.at[index, :, lo:hi],
+                        outs[out].at[owner, :, to : to + hi - lo],
+                        sem.at[len(copies)],
                     )
                 )
                 copies[-1].start()
@@ -346,9 +873,7 @@
         copy.wait()
 
 
-def place(pieces, widths, me, count):
-    edges = np.cumsum([0] + list(widths))
-    columns = tuple(zip(edges[:-1].tolist(), edges[1:].tolist()))
+def place(pieces, columns, widths, me, count):
     stacks = [stack for stack, _ in pieces]
     rows = stacks[0].shape[1]
     outs = pl.pallas_call(
@@ -357,7 +882,8 @@
         + [pl.BlockSpec(memory_space=pl.ANY)] * len(stacks),
         out_specs=[pl.BlockSpec(memory_space=pltpu.VMEM)] * len(widths),
         out_shape=[jax.ShapeDtypeStruct((count, rows, width), BF) for width in widths],
-        scratch_shapes=[pltpu.SemaphoreType.DMA((count * len(widths),))],
+        scratch_shapes=[pltpu.SemaphoreType.DMA((count * len(columns),))],
+        cost_estimate=QUICK,
         compiler_params=pltpu.CompilerParams(vmem_limit_bytes=16 * 1024 * 1024),
         name="place",
     )(me.reshape(1), *stacks)
@@ -365,11 +891,10 @@
 
 
 def sum_order(count):
-    far, middle = hop_plan(count)
+    farthest, far, middle = hop_plan(count)
     order = []
-    for masks, last in ((middle, (0, far[0])), (middle[::-1], (far[1], far[2]))):
-        block = list(last)
-        for mask in masks[::-1]:
+    for masks, block in ((middle, [0, farthest]), (middle[::-1], [far, far ^ farthest])):
+        for mask in masks:
             block = block + [owner ^ mask for owner in block]
         order += block
     return order + [owner ^ 1 for owner in order]
@@ -408,6 +933,7 @@
         out_specs=[pl.BlockSpec(memory_space=pltpu.VMEM)] * 2,
         out_shape=[half, half],
         scratch_shapes=[pltpu.SemaphoreType.DMA((count,))],
+        cost_estimate=QUICK,
         compiler_params=pltpu.CompilerParams(vmem_limit_bytes=16 * 1024 * 1024),
         name="pick",
     )(me.reshape(1), stack)
@@ -417,38 +943,61 @@
     return (left.astype(F32) + right.astype(F32)).astype(BF)
 
 
-def scatter_sum(kept, sent, count):
-    far, middle = hop_plan(count)
+def scatter_stages(parts, count, result):
+    farthest, far, middle = hop_plan(count)
     blocks = count // 2
-    kept = kept.reshape(blocks, -1, kept.shape[-1])
-    arrived = hop(sent.reshape(kept.shape), 1, count)
     half = blocks // 2
-    ends = []
-    for at, masks in ((0, middle), (half, middle[::-1])):
-        here, there, size = kept[at : at + half], arrived[at : at + half], half
-        for mask in masks:
-            size //= 2
-            away = hop(add_low(here[size:], there[size:]), mask, count)
-            here, there = add_low(here[:size], there[:size]), away
-        ends.append((here, there))
-    (near, near_in), (back, back_in) = ends
-    total = near[0].astype(F32) + near_in[0].astype(F32)
-    sends = (
-        add_low(near[1], near_in[1]),
-        add_low(back[0], back_in[0]),
-        add_low(back[1], back_in[1]),
-    )
-    for block, mask in zip(sends, far):
-        total = total + hop(block, mask, count).astype(F32)
-    return total
-
-
-def sum_everywhere(vector, count):
+    shaped = [
+        [side.reshape(blocks, -1, side.shape[-1]) for side in part] for part in parts
+    ]
+    deps = yield
+    sent = after([sent for _, sent in shaped], deps)
+    arrived = [hop(side, 1, count) for side in sent]
+    deps = yield sent
+    arrived = after(arrived, deps)
+    pairs = [(kept, got) for (kept, _), got in zip(shaped, arrived)]
+
+    def added(pairs, lo, hi):
+        sums = [add_low(kept[lo:hi], got[lo:hi]) for kept, got in pairs]
+        return sums[0] if len(sums) == 1 else jnp.concatenate(sums, axis=-1)
+
+    sides = [(pairs, 0), (pairs, half)]
+    size = half
+    for masks in zip(middle[::-1], middle):
+        size //= 2
+        sends = [added(p, at + size, at + 2 * size) for p, at in sides]
+        got = [hop(send, mask, count) for send, mask in zip(sends, masks)]
+        kept = [added(p, at, at + size) for p, at in sides]
+        deps = yield sends
+        got = after(got, deps)
+        sides = [([pair], 0) for pair in zip(kept, got)]
+    (near, _), (back, _) = sides
+    send = added(back, 0, 2)
+    got = hop(send, far, count)
+    kept = added(near, 0, 2)
+    deps = yield [send]
+    (got,) = after([got], deps)
+    send = add_low(kept[1], got[1])
+    arrived = hop(send, farthest, count)
+    deps = yield [send]
+    (arrived,) = after([arrived], deps)
+    total = kept[0].astype(F32) + got[0].astype(F32) + arrived.astype(F32)
+    result.append(total)
+    yield [total]
+
+
+def sum_stages(array, count, result):
     mask = 1
+    deps = yield
     while mask < count:
-        vector = vector + hop(vector, mask, count)
+        (array,) = after([array], deps)
+        got = hop(array, mask, count)
+        deps = yield [array]
+        (got,) = after([got], deps)
+        array = array + got
         mask *= 2
-    return vector
+    result.append(array)
+    yield [array]
 
 
 def per_device(
@@ -483,90 +1032,167 @@
     sizes = [v.shape[0] for v in vectors]
     used = sum(sizes)
     shard_rows = qkv_weight.shape[0]
-    packed = jnp.pad(
-        jnp.concatenate(vectors).astype(BF), (0, shard_rows * 128 - used)
-    ).reshape(shard_rows, 128)
     count = lax.axis_size("fsdp")
     me = lax.axis_index("fsdp")
-    first = jnp.concatenate((qkv_weight.astype(BF), proj_weight.astype(BF), packed), axis=1)
-    w_qkv, w_proj, small = place(gather_pieces(first, count), (3 * D, D, 128), me, count)
-    (w_up,) = place(gather_pieces(lin1_weight.astype(BF), count), (FF,), me, count)
-    w_down = lax.all_gather(lin2_weight.astype(BF), "fsdp", axis=0, tiled=True)
+
+    packed = lax.optimization_barrier(jnp.concatenate(vectors))
+    packed = jnp.pad(packed, (0, shard_rows * 128 - used)).reshape(shard_rows, 128)
+    first_pieces, second_pieces, third_pieces = [], [], []
+    first = start(
+        gather_stages(jnp.concatenate((qkv_weight, packed), axis=1).astype(BF), count, first_pieces)
+    )
+    second = start(
+        gather_stages(
+            jnp.concatenate((proj_weight, lin1_weight), axis=1).astype(BF), count, second_pieces
+        )
+    )
+    third = start(gather_stages(lin2_weight.astype(BF), count, third_pieces))
+    middle = len(hop_plan(count)[2])
+    first.send(None)
+    sent = first.send(None)
+    second.send(sent)
+    for _ in range(middle):
+        sent = first.send(sent)
+        sent = second.send(sent)
+    sent = first.send(sent)
+    sent = sent + third.send(sent)
+    sent = first.send(sent)
+    sent = sent + third.send(sent)
+
+    (small,) = place(
+        [(stack[:, :, 3 * D :], own) for stack, own in first_pieces], ((0, 0, 128, 0),), (128,), me, count
+    )
     small = small.reshape(count, shard_rows * 128)[:, :used].astype(F32)
     edges = np.cumsum([0] + sizes)
     gain_one, bias_one, b_qkv, b_proj, gain_two, bias_two, b_up, b_down = (
         small[:, lo:hi].reshape(-1) for lo, hi in zip(edges[:-1], edges[1:])
     )
+    flat = lambda pieces: [stack.reshape(-1, stack.shape[-1]) for stack, _ in pieces]
+    first_pieces = flat(first_pieces)
     order = order_matrix(me, count, shard_rows)
-
     onehot, shift = window_constants()
     onehot = jnp.asarray(onehot, BF)
     shift = jnp.asarray(shift)
     table = table_lanes(rel_pos_h, rel_pos_w)
     live = slot_mask(window_pos)
 
-    inputs = tokens.astype(F32)
-    hat_one, rstd_one = normalise(inputs)
-    normed_one = ((hat_one * gain_one + bias_one) * live).astype(BF)
-    qkv = (dot_nn(normed_one, w_qkv) + b_qkv).astype(BF)
-    mixed, probs = attention(qkv, table, onehot, shift)
-    residual = inputs + dot_nn(mixed, w_proj) + b_proj
-    hat_two, rstd_two = normalise(residual)
-    normed_two = (hat_two * gain_two + bias_two).astype(BF)
-    hidden = dot_nn(normed_two, w_up) + b_up
-    cdf = normal_cdf(hidden)
-    active = (hidden * cdf).astype(BF)
-    slope = cdf + hidden * normal_pdf(hidden)
-    grad_out = out_grad.astype(F32) * live
-    grad_branch = grad_out.astype(BF)
-    grad_w_down = dot_tn(active, grad_branch).astype(BF)
-    own_down = scatter_sum(*pick(grad_w_down, me, count), count)
-    output = ((residual + dot_nn(active, w_down) + b_down) * live).astype(BF)
-
-    grad_hidden = (dot_nt(grad_branch, w_down) * slope).astype(BF)
-    ordered = dot_nn(normed_two, order).astype(BF)
-    kept = dot_tn(ordered[:, : D // 2], grad_hidden).astype(BF)
-    sent = dot_tn(ordered[:, D // 2 :], grad_hidden).astype(BF)
-    kept, sent, grad_hidden = lax.optimization_barrier((kept, sent, grad_hidden))
-    own_up = scatter_sum(kept, sent, count)
-    grad_normed_two = dot_nt(grad_hidden, w_up)
-    grad_residual = grad_out + normalise_back(grad_normed_two, hat_two, rstd_two, gain_two)
-    grad_attn = grad_residual.astype(BF)
-    ordered = dot_nn(mixed, order).astype(BF)
-    kept = dot_tn(ordered[:, : D // 2], grad_attn).astype(BF)
-    sent = dot_tn(ordered[:, D // 2 :], grad_attn).astype(BF)
-    kept, sent, grad_attn = lax.optimization_barrier((kept, sent, grad_attn))
-    own_proj = scatter_sum(kept, sent, count)
-    grad_mixed = dot_nt(grad_attn, w_proj).astype(BF)
-    grad_qkv, lanes_grad = attention_back(qkv, grad_mixed, probs, table, onehot, shift)
-    ordered = dot_nn(normed_one, order).astype(BF)
-    kept = dot_tn(ordered[:, : D // 2], grad_qkv).astype(BF)
-    sent = dot_tn(ordered[:, D // 2 :], grad_qkv).astype(BF)
-    kept, sent, grad_qkv = lax.optimization_barrier((kept, sent, grad_qkv))
-    own_qkv = scatter_sum(kept, sent, count)
-    grad_normed_one = dot_nt(grad_qkv, w_qkv) * live
-    tokens_grad = (
-        grad_residual + normalise_back(grad_normed_one, hat_one, rstd_one, gain_one)
-    ).astype(BF)
-
-    totals = (
-        jnp.sum(grad_normed_one * hat_one, axis=0),
-        jnp.sum(grad_normed_one, axis=0),
-        jnp.sum(grad_qkv.astype(F32), axis=0),
-        jnp.sum(grad_attn.astype(F32), axis=0),
-        jnp.sum(grad_normed_two * hat_two, axis=0),
-        jnp.sum(grad_normed_two, axis=0),
-        jnp.sum(grad_hidden.astype(F32), axis=0),
-        jnp.sum(grad_branch.astype(F32), axis=0),
-    )
-    by_owner = jnp.concatenate([total.reshape(count, -1) for total in totals], axis=1).reshape(-1)
-    table_h, table_w = table_grads(lanes_grad)
-    small_total = sum_everywhere(
-        jnp.concatenate((by_owner, table_h.reshape(-1), table_w.reshape(-1))), count
-    )
-    own_small = lax.dynamic_slice(small_total, (me * used,), (used,))
-    owned = [own_small[lo:hi] for lo, hi in zip(edges[:-1], edges[1:])]
-    table_h, table_w = small_total[count * used :].reshape(2, 2 * WIN - 1, HEAD_DIM)
+    ordered_one, *qkv = front(
+        tokens, live, order, jnp.stack((gain_one, bias_one)), b_qkv.reshape(1, -1), first_pieces
+    )
+    sent = second.send(sent + [ordered_one])
+    sent = sent + third.send(sent)
+    (qkv[0],) = after([qkv[0]], sent)
+    attended = [attention(qkv[0], table, onehot, shift)]
+    sent = second.send([attended[0][0]])
+    sent = sent + third.send(sent)
+    (qkv[1],) = after([qkv[1]], sent)
+    attended.append(attention(qkv[1], table, onehot, shift))
+    sent = third.send([attended[1][0]])
+    finish(second)
+    second_pieces = flat(second_pieces)
+    mixed = [m for m, _ in attended]
+    (mixed[0],) = after([mixed[0]], sent)
+    vectors = jnp.stack((b_proj, gain_two, bias_two, b_down))
+    residual, normed_two, turned_two, ordered_mixed = project(
+        tokens, mixed, order, vectors, second_pieces
+    )
+    third.send([residual])
+    finish(third)
+
+    own_down, own_up, own_first, own_second, all_small = [], [], [], [], []
+    (
+        output,
+        grad_residual,
+        grad_one,
+        grad_two,
+        kept_up,
+        sent_up,
+        kept_proj,
+        sent_proj,
+        mlp_sums,
+        grad_b_up,
+        down_parts,
+    ) = mlp(
+        me,
+        count,
+        normed_two,
+        turned_two,
+        residual,
+        ordered_mixed,
+        live,
+        out_grad,
+        order,
+        vectors,
+        b_up.reshape(1, FF),
+        second_pieces,
+        third_pieces,
+    )
+    down = start(scatter_stages([down_parts], count, own_down))
+    up = start(scatter_stages([(kept_up, sent_up)], count, own_up))
+    sent = down.send(None)
+    sent = sent + up.send(sent)
+    (grad_one,) = after([grad_one], sent)
+    back = [attention_back(qkv[0], grad_one, attended[0][1], table, onehot, shift)]
+    sent = down.send([back[0][0]])
+
+    def qkv_part(grad_qkv):
+        sent = dot_tn(ordered_one[:, D // 2 :], grad_qkv).astype(BF)
+        return dot_tn(ordered_one[:, : D // 2], grad_qkv).astype(BF), sent
+
+    first_sum = start(
+        scatter_stages([qkv_part(back[0][0]), (kept_proj, sent_proj)], count, own_first)
+    )
+    sent = sent + first_sum.send(sent)
+    (grad_two,) = after([grad_two], sent)
+    back.append(attention_back(qkv[1], grad_two, attended[1][1], table, onehot, shift))
+    sent = up.send([back[1][0]])
+    second_sum = start(scatter_stages([qkv_part(back[1][0])], count, own_second))
+    sent = sent + second_sum.send(sent)
+    (grad_qkv,) = after([back[1][0]], sent)
+    tokens_grad, small_sums = first_norm_back(
+        (back[0][0], grad_qkv),
+        first_pieces,
+        tokens,
+        live,
+        gain_one.reshape(1, D),
+        order,
+        grad_residual,
+        mlp_sums,
+        grad_b_up,
+        (back[0][1], back[1][1]),
+    )
+    sent = down.send([small_sums])
+    small_stages = start(sum_stages(small_sums, count, all_small))
+    sent = small_stages.send(sent)
+    sent = first_sum.send(sent)
+    sent = down.send(sent)
+    sent = small_stages.send(sent)
+    sent = up.send(sent)
+    sent = down.send(sent)
+    sent = second_sum.send(sent)
+    sent = small_stages.send(sent)
+    sent = up.send(sent)
+    sent = first_sum.send(sent)
+    sent = small_stages.send(sent)
+    sent = up.send(sent)
+    sent = second_sum.send(sent)
+    sent = first_sum.send(sent)
+    sent = small_stages.send(sent)
+    sent = second_sum.send(sent)
+    sent = first_sum.send(sent)
+    sent = second_sum.send(sent)
+    for stages in (down, up, first_sum, second_sum, small_stages):
+        finish(stages)
+    own_qkv = jnp.stack(
+        [
+            own.reshape(shard_rows, 3, GROUP)
+            for own in (own_first[0][:, : 3 * GROUP], own_second[0])
+        ],
+        axis=2,
+    ).reshape(shard_rows, 3 * D)
+    own_proj = own_first[0][:, 3 * GROUP :]
+    *owned, table_h, table_w = own_small(all_small[0], me, sizes)
+    owned = [vector.reshape(-1) for vector in owned]
 
     return (
         output,
@@ -581,9 +1207,9 @@
         owned[3],
         owned[4],
         owned[5],
-        own_up,
+        own_up[0],
         owned[6],
-        own_down.astype(F32),
+        own_down[0],
         owned[7],
     )
 

time: 351 us -> 262 us (0.75)
  matrix products: 53.2 us -> 2.82 us
  waiting for transfers between devices: 125 us -> 84.5 us
  Pallas kernels: 34.2 us -> 64 us
  other arithmetic: 34.7 us -> 13.8 us
  between operations: 15.4 us -> 1.73 us
  local copies, waits for them, and re-layouts: 18.7 us -> 28.3 us
    ppermute x59 -> x64, waiting for transfers between devices: 125 us -> 84.5 us  [hop(): return lax.ppermute(array, 'fsdp', [(i, i ^ mask) for i in range(count)])]
    pallas_call x1 -> x5, Pallas kernels: 6.55 us -> 44.2 us  [the longest x1 26.7 us: mlp(): pl.pallas_call(functools.partial(mlp_kernel, split_rows, owners), grid=(S...]
    dot_general x11 -> x0, matrix products: 36.8 us -> none  [the longest x7 22.5 us: dot_nn(): return jnp.dot(a, b, preferred_element_type=F32)]
    dot_general x7 -> x4, matrix products: 16.4 us -> 2.82 us  [dot_tn(): lax.dot_general(a, b, (((0,), (0,)), ((), ())), preferred_element_type=F32)]
    convert_element_type x20 -> x25, other arithmetic: 13.7 us -> 3.35 us  [add_low(): return (left.astype(F32) + right.astype(F32)).astype(BF)]
    unnamed x87 -> x104, local copies, waits for them, and re-layouts: 10.1 us -> 17.9 us
    pallas_call x2 -> x1, Pallas kernels: 8.16 us -> 0.63 us  [place(): pl.pallas_call(functools.partial(place_kernel, tuple((tuple(o) for _, o i...]
    convert_element_type x6 -> x2, other arithmetic: 6.36 us -> 0.43 us  [the longest x1 0.41 us: order_matrix(): return (features == wanted[None, :]).astype(BF)]
  transfers between devices with their start and end apart: 60 -> 64, of which waited for: 28 -> 20; matrix products, arithmetic and copies ran while one was open for 17% -> 10% of each run, Pallas kernels for 7% -> 14%
where the time goes in v3:
time: 262 us; the launch traced here: 261 us
  waiting for transfers between devices  84.5 us (32%)
  starting transfers between devices  65.7 us (25%)
  Pallas kernels  64 us (24%)
  local copies, waits for them, and re-layouts  28.3 us (11%)
  other arithmetic  13.8 us (5%)
  matrix products  2.82 us (1%)
    ppermute x64, waiting for transfers between devices, hop(): return lax.ppermute(array, 'fsdp', [(i, i ^ mask) for i in range(count)])  84.5 us
    ppermute x64, starting transfers between devices, hop(): return lax.ppermute(array, 'fsdp', [(i, i ^ mask) for i in range(count)])  65.7 us
    pallas_call x1, Pallas kernels, mlp(): pl.pallas_call(functools.partial(mlp_kernel, split_rows, owners), grid=(S...  26.7 us
    unnamed x104, local copies, waits for them, and re-layouts  17.9 us
    pallas_call x2, Pallas kernels, attention_back(): pl.pallas_call(attn_bwd_kernel, grid=(PAIRS,), in_specs=columns + [pl.Blo...  10.7 us
    pallas_call x2, Pallas kernels, attention(): pl.pallas_call(attn_fwd_kernel, grid=(PAIRS,), in_specs=columns + constan...  8.54 us
    pallas_call x1, Pallas kernels, first_norm_back(): pl.pallas_call(first_norm_kernel, grid=(6,), in_specs=[first(rows), secon...  7.87 us
  transfers between devices with their start and end apart: 64, of which 20 were waited for; matrix products, arithmetic and copies ran while one was open for 10% of the time, Pallas kernels for 14%

profile of v3, /device:TPU:0, one launch (start us, length us, event | category | flops | bytes accessed | tf_op | source)
XLA Modules:
  0.0 260.9 jit_solution(6490472450293529636)
XLA Ops:
  2.6 4.1 %collective-permute-start = (bf16[24,2432]{1,0:T(8,128)(2,1)S(1)}, bf16[24,2432]{1,0:T(8,128)(2,1)S(1)}, u32[]{:S(2)}, u32[]{:S(2)}) collective-permute-start(bf16[24,2432]{1,0:T(8,128)(2,1)S(1)} %pad_maximum_fusion.12), channel_id=1, source_target_pairs={{0,16},{1,17},{2,18},{3,19},{4,20},{5,21},{6,22},{7,23},{8,24},{9,... | collective-permute-start | bytes 350216 | tf_op jit(solution)/shard_map/ppermute | solution.py:802
  8.6 3.8 %collective-permute-done = bf16[24,2432]{1,0:T(8,128)(2,1)S(1)} collective-permute-done((bf16[24,2432]{1,0:T(8,128)(2,1)S(1)}, bf16[24,2432]{1,0:T(8,128)(2,1)S(1)}, u32[]{:S(2)}, u32[]{:S(2)}) %collective-permute-start) | collective-permute-done | bytes 116768 | tf_op jit(solution)/shard_map/ppermute | solution.py:802
  13.2 3.4 %collective-permute-start.4 = (bf16[24,3840]{1,0:T(8,128)(2,1)S(1)}, bf16[24,3840]{1,0:T(8,128)(2,1)S(1)}, u32[]{:S(2)}, u32[]{:S(2)}) collective-permute-start(bf16[24,3840]{1,0:T(8,128)(2,1)S(1)} %pad_maximum_fusion.11), channel_id=1, source_target_pairs={{0,16},{1,17},{2,18},{3,19},{4,20},{5,21},{6,22},{7,23},{8,24},{9,... | collective-permute-start | bytes 552968 | tf_op jit(solution)/shard_map/ppermute | solution.py:802
  17.0 1.6 collective-permute-start.1
  18.5 4.8 %collective-permute-done.2 = bf16[2,24,2432]{2,1,0:T(8,128)(2,1)S(1)} collective-permute-done((bf16[2,24,2432]{2,1,0:T(8,128)(2,1)S(1)}, bf16[2,24,2432]{2,1,0:T(8,128)(2,1)S(1)}, u32[]{:S(2)}, u32[]{:S(2)}) %collective-permute-start.2) | collective-permute-done | bytes 233504 | tf_op jit(solution)/shard_map/ppermute | solution.py:802
  25.4 4.0 %collective-permute-done.3 = bf16[2,24,2432]{2,1,0:T(8,128)(2,1)S(1)} collective-permute-done((bf16[2,24,2432]{2,1,0:T(8,128)(2,1)S(1)}, bf16[2,24,2432]{2,1,0:T(8,128)(2,1)S(1)}, u32[]{:S(2)}, u32[]{:S(2)}) %collective-permute-start.3) | collective-permute-done | bytes 233504 | tf_op jit(solution)/shard_map/ppermute | solution.py:802
  30.8 2.2 collective-permute-start.5
  33.9 7.0 %collective-permute-done.12 = bf16[2,24,3840]{2,1,0:T(8,128)(2,1)} collective-permute-done((bf16[2,24,3840]{2,1,0:T(8,128)(2,1)}, bf16[2,24,3840]{2,1,0:T(8,128)(2,1)}, u32[]{:S(2)}, u32[]{:S(2)}) %collective-permute-start.12) | collective-permute-done | bytes 368672 | tf_op jit(solution)/shard_map/ppermute | solution.py:802
  40.9 3.6 %collective-permute-start.14 = (bf16[96,768]{1,0:T(8,128)(2,1)S(1)}, bf16[96,768]{1,0:T(8,128)(2,1)S(1)}, u32[]{:S(2)}, u32[]{:S(2)}) collective-permute-start(bf16[96,768]{1,0:T(8,128)(2,1)S(1)} %convert_element_type.588), channel_id=1, source_target_pairs={{0,16},{1,17},{2,18},{3,19},{4,20},{5,21},{6,22},{7,23},{8,24},{9,... | collective-permute-start | bytes 442376 | tf_op jit(solution)/shard_map/ppermute | solution.py:802
  45.1 1.8 constant_dynamic-update-slice_fusion.3
  47.6 1.6 collective-permute-done.14
  56.3 4.6 %front.1 = (bf16[392,768]{1,0:T(8,128)(2,1)S(1)}, bf16[392,1152]{1,0:T(8,128)(2,1)S(1)}, bf16[392,1152]{1,0:T(8,128)(2,1)S(1)}) custom-call(bf16[392,768]{1,0:T(8,128)(2,1)S(1)} %copy-done, f32[392,1]{1,0:T(8,128)S(1)} %reshape.409.live_ref.rest_4_, bf16[768,768]{1,0:T(8,128)(2,1)S(1)} %fusion.order_ref.rest_6_, f32[2,768]{1,0:T(2,128)S(1)} %pad_maximum_fusion.14.rows_ref, ...), custom_call_target="tpu_custom_call" | custom-call | flops 1 | bytes 1 | tf_op jit(solution)/shard_map/front/pallas_call | solution.py:353
  62.3 1.5 collective-permute-start.19
  63.8 1.9 pad_maximum_fusion
  65.8 1.6 collective-permute-start.18
  68.7 5.4 %collective-permute-done.15 = bf16[2,96,768]{2,1,0:T(8,128)(2,1)S(1)} collective-permute-done((bf16[2,96,768]{2,1,0:T(8,128)(2,1)S(1)}, bf16[2,96,768]{2,1,0:T(8,128)(2,1)S(1)}, u32[]{:S(2)}, u32[]{:S(2)}) %collective-permute-start.15) | collective-permute-done | bytes 294944 | tf_op jit(solution)/shard_map/ppermute | solution.py:802
  75.3 9.7 %collective-permute-done.16 = bf16[2,96,768]{2,1,0:T(8,128)(2,1)S(1)} collective-permute-done((bf16[2,96,768]{2,1,0:T(8,128)(2,1)S(1)}, bf16[2,96,768]{2,1,0:T(8,128)(2,1)S(1)}, u32[]{:S(2)}, u32[]{:S(2)}) %collective-permute-start.16) | collective-permute-done | bytes 294944 | tf_op jit(solution)/shard_map/ppermute | solution.py:802
  85.0 3.4 %collective-permute-done.17 = bf16[2,96,768]{2,1,0:T(8,128)(2,1)S(1)} collective-permute-done((bf16[2,96,768]{2,1,0:T(8,128)(2,1)S(1)}, bf16[2,96,768]{2,1,0:T(8,128)(2,1)S(1)}, u32[]{:S(2)}, u32[]{:S(2)}) %collective-permute-start.17) | collective-permute-done | bytes 294944 | tf_op jit(solution)/shard_map/ppermute | solution.py:802
  91.2 1.5 collective-permute-start.24
  92.9 4.3 %attention.2 = (bf16[392,384]{1,0:T(8,128)(2,1)S(1)}, f32[3,4,200,256]{3,2,1,0:T(8,128)S(1)}) custom-call(bf16[392,1152]{1,0:T(8,128)(2,1)S(1)} %get-tuple-element.131.q_ref.k_ref.v_ref, bf16[392,1152]{1,0:T(8,128)(2,1)S(1)} %get-tuple-element.131.q_ref.k_ref.v_ref, bf16[392,1152]{1,0:T(8,128)(2,1)S(1)} %get-tuple-element.131.q_ref.k_ref.v_ref, ...), custom_call_target="tpu_custom_call" | custom-call | flops 1 | bytes 1 | tf_op jit(solution)/shard_map/attention/pallas_call | solution.py:237
  99.8 4.3 %attention.3 = (bf16[392,384]{1,0:T(8,128)(2,1)S(1)}, f32[3,4,200,256]{3,2,1,0:T(8,128)S(1)}) custom-call(bf16[392,1152]{1,0:T(8,128)(2,1)S(1)} %get-tuple-element.137.q_ref.k_ref.v_ref, bf16[392,1152]{1,0:T(8,128)(2,1)S(1)} %get-tuple-element.137.q_ref.k_ref.v_ref, bf16[392,1152]{1,0:T(8,128)(2,1)S(1)} %get-tuple-element.137.q_ref.k_ref.v_ref, ...), custom_call_target="tpu_custom_call" | custom-call | flops 1 | bytes 1 | tf_op jit(solution)/shard_map/attention/pallas_call | solution.py:237
  104.7 3.5 %project.1 = (f32[392,768]{1,0:T(8,128)S(1)}, bf16[392,768]{1,0:T(8,128)(2,1)S(1)}, bf16[768,392]{1,0:T(8,128)(2,1)S(1)}, bf16[392,768]{1,0:T(8,128)(2,1)S(1)}) custom-call(bf16[392,768]{1,0:T(8,128)(2,1)S(1)} %copy-done.1, bf16[392,384]{1,0:T(8,128)(2,1)S(1)} %copy-done.19, bf16[392,384]{1,0:T(8,128)(2,1)S(1)} %get-tuple-element.138.two_ref, ...), custom_call_target="tpu_custom_call" | custom-call | flops 1 | bytes 1 | tf_op jit(solution)/shard_map/project/pallas_call | solution.py:532
  119.4 26.7 %mlp.1 = (bf16[392,768]{1,0:T(8,128)(2,1)}, f32[392,768]{1,0:T(8,128)}, bf16[392,384]{1,0:T(8,128)(2,1)S(1)}, bf16[392,384]{1,0:T(8,128)(2,1)S(1)}, bf16[384,307...) custom-call(s32[32]{0:T(128)S(1)} %and_select_fusion.2.place_ref, ...), custom_call_target="tpu_custom_call" | custom-call | flops 1 | bytes 1 | tf_op jit(solution)/shard_map/mlp/pallas_call | solution.py:571
  146.6 5.3 %attention_back.2 = (bf16[392,1152]{1,0:T(8,128)(2,1)S(1)}, f32[128,128]{1,0:T(8,128)S(1)}) custom-call(bf16[392,1152]{1,0:T(8,128)(2,1)S(1)} %get-tuple-element.131.q_ref.k_ref.v_ref, bf16[392,1152]{1,0:T(8,128)(2,1)S(1)} %get-tuple-element.131.q_ref.k_ref.v_ref, bf16[392,1152]{1,0:T(8,128)(2,1)S(1)} %get-tuple-element.131.q_ref.k_ref.v_ref, ...), custom_call_target="tpu_custom_call" | custom-call | flops 1 | bytes 1 | tf_op jit(solution)/shard_map/attention_back/pallas_call | solution.py:255
  154.6 1.5 copy-done.28
  156.8 1.6 collective-permute-start.33
  159.5 5.3 %attention_back.3 = (bf16[392,1152]{1,0:T(8,128)(2,1)S(1)}, f32[128,128]{1,0:T(8,128)S(1)}) custom-call(bf16[392,1152]{1,0:T(8,128)(2,1)S(1)} %get-tuple-element.137.q_ref.k_ref.v_ref, bf16[392,1152]{1,0:T(8,128)(2,1)S(1)} %get-tuple-element.137.q_ref.k_ref.v_ref, bf16[392,1152]{1,0:T(8,128)(2,1)S(1)} %get-tuple-element.137.q_ref.k_ref.v_ref, ...), custom_call_target="tpu_custom_call" | custom-call | flops 1 | bytes 1 | tf_op jit(solution)/shard_map/attention_back/pallas_call | solution.py:255
  168.5 7.9 %first_norm_back.1 = (bf16[392,768]{1,0:T(8,128)(2,1)}, f32[112,128]{1,0:T(8,128)S(1)}) custom-call(bf16[392,1152]{1,0:T(8,128)(2,1)S(1)} %get-tuple-element.152.grad_one_ref, bf16[392,1152]{1,0:T(8,128)(2,1)S(1)} %get-tuple-element.165.grad_two_ref, bf16[392,768]{1,0:T(8,128)(2,1)S(1)} %copy-done.2, f32[392,1]{1,0:T(8,128)S(1)} %reshape.409.live_ref.rest_4_, ...), custom_call_target="tpu_custom_call" | custom-call | flops 1 | bytes 1 | tf_op jit(solution)/shard_map/first_norm_back/pallas_call | solution.py:737
  178.8 1.5 collective-permute-start.35
  180.7 17.1 %collective-permute-done.36 = bf16[2,96,768]{2,1,0:T(8,128)(2,1)S(1)} collective-permute-done((bf16[2,96,768]{2,1,0:T(8,128)(2,1)S(1)}, bf16[2,96,768]{2,1,0:T(8,128)(2,1)S(1)}, u32[]{:S(2)}, u32[]{:S(2)}) %collective-permute-start.36) | collective-permute-done | bytes 294944 | tf_op jit(solution)/shard_map/ppermute | solution.py:802
  200.6 1.5 collective-permute-start.39
  203.5 4.9 %collective-permute-done.41 = bf16[2,96,768]{2,1,0:T(8,128)(2,1)S(1)} collective-permute-done((bf16[2,96,768]{2,1,0:T(8,128)(2,1)S(1)}, bf16[2,96,768]{2,1,0:T(8,128)(2,1)S(1)}, u32[]{:S(2)}, u32[]{:S(2)}) %collective-permute-start.41) | collective-permute-done | bytes 294944 | tf_op jit(solution)/shard_map/ppermute | solution.py:802
  208.4 1.5 collective-permute-start.47
  211.3 3.8 %collective-permute-done.48 = bf16[2,24,3072]{2,1,0:T(8,128)(2,1)S(1)} collective-permute-done((bf16[2,24,3072]{2,1,0:T(8,128)(2,1)S(1)}, bf16[2,24,3072]{2,1,0:T(8,128)(2,1)S(1)}, u32[]{:S(2)}, u32[]{:S(2)}) %collective-permute-start.48) | collective-permute-done | bytes 294944 | tf_op jit(solution)/shard_map/ppermute | solution.py:802
  215.1 1.5 collective-permute-start.53
  216.6 1.8 collective-permute-done.47
  220.7 5.6 %collective-permute-done.46 = bf16[4,24,1920]{2,1,0:T(8,128)(2,1)S(1)} collective-permute-done((bf16[4,24,1920]{2,1,0:T(8,128)(2,1)S(1)}, bf16[4,24,1920]{2,1,0:T(8,128)(2,1)S(1)}, u32[]{:S(2)}, u32[]{:S(2)}) %collective-permute-start.46) | collective-permute-done | bytes 368672 | tf_op jit(solution)/shard_map/ppermute | solution.py:802
  228.7 1.5 collective-permute-start.50
  231.1 2.6 collective-permute-done.54
  233.6 2.0 collective-permute-start.49
  235.7 1.8 collective-permute-start.62
  238.3 1.5 collective-permute-start.57
  240.0 1.9 collective-permute-start.55
  242.0 3.3 %collective-permute-done.55 = f32[112,128]{1,0:T(8,128)S(1)} collective-permute-done((f32[112,128]{1,0:T(8,128)S(1)}, f32[112,128]{1,0:T(8,128)S(1)}, u32[]{:S(2)}, u32[]{:S(2)}) %collective-permute-start.55) | collective-permute-done | bytes 57376 | tf_op jit(solution)/shard_map/ppermute | solution.py:802
  245.9 1.5 own_small.1
  247.5 4.2 %collective-permute-start.60 = (bf16[2,24,1152]{2,1,0:T(8,128)(2,1)S(1)}, bf16[2,24,1152]{2,1,0:T(8,128)(2,1)S(1)}, u32[]{:S(2)}, u32[]{:S(2)}) collective-permute-start(bf16[2,24,1152]{2,1,0:T(8,128)(2,1)S(1)} %add_convert_fusion.26), channel_id=1, source_target_pairs={{0,8},{1,9},{2,10},{3,11},{4,12},{5,13},{6,14},{7,15},{8,0},{9,1},... | collective-permute-start | bytes 331784 | tf_op jit(solution)/shard_map/ppermute | solution.py:802
  253.0 1.5 collective-permute-done.60
  255.6 2.9 %collective-permute-done.59 = bf16[24,1920]{1,0:T(8,128)(2,1)S(1)} collective-permute-done((bf16[24,1920]{1,0:T(8,128)(2,1)S(1)}, bf16[24,1920]{1,0:T(8,128)(2,1)S(1)}, u32[]{:S(2)}, u32[]{:S(2)}) %collective-permute-start.59) | collective-permute-done | bytes 92192 | tf_op jit(solution)/shard_map/ppermute | solution.py:802
  (299 shorter events, 67.5 us)
Async XLA Ops:
  2.6 9.8 %collective-permute-start = (bf16[24,2432]{1,0:T(8,128)(2,1)S(1)}, bf16[24,2432]{1,0:T(8,128)(2,1)S(1)}, u32[]{:S(2)}, u32[]{:S(2)}) collective-permute-start(bf16[24,2432]{1,0:T(8,128)(2,1)S(1)} %pad_maximum_fusion.12), channel_id=1, source_target_pairs={{0,16},{1,17},{2,18},{3,19},{4,20},{5,21},{6,22},{7,23},{8,24},{9,... | collective-permute-start | bytes 350216 | tf_op jit(solution)/shard_map/ppermute | solution.py:802
  12.4 10.9 %collective-permute-start.2 = (bf16[2,24,2432]{2,1,0:T(8,128)(2,1)S(1)}, bf16[2,24,2432]{2,1,0:T(8,128)(2,1)S(1)}, u32[]{:S(2)}, u32[]{:S(2)}) collective-permute-start(bf16[2,24,2432]{2,1,0:T(8,128)(2,1)S(1)} %pad_maximum_fusion.8), channel_id=1, source_target_pairs={{0,8},{1,9},{2,10},{3,11},{4,12},{5,13},{6,14},{7,15},{8,0},{9,1},... | collective-permute-start | bytes 700424 | tf_op jit(solution)/shard_map/ppermute | solution.py:802
  13.2 11.4 %collective-permute-start.4 = (bf16[24,3840]{1,0:T(8,128)(2,1)S(1)}, bf16[24,3840]{1,0:T(8,128)(2,1)S(1)}, u32[]{:S(2)}, u32[]{:S(2)}) collective-permute-start(bf16[24,3840]{1,0:T(8,128)(2,1)S(1)} %pad_maximum_fusion.11), channel_id=1, source_target_pairs={{0,16},{1,17},{2,18},{3,19},{4,20},{5,21},{6,22},{7,23},{8,24},{9,... | collective-permute-start | bytes 552968 | tf_op jit(solution)/shard_map/ppermute | solution.py:802
  29.4 15.0 %collective-permute-start.6 = (bf16[4,24,2432]{2,1,0:T(8,128)(2,1)S(1)}, bf16[4,24,2432]{2,1,0:T(8,128)(2,1)S(1)}, u32[]{:S(2)}, u32[]{:S(2)}) collective-permute-start(bf16[4,24,2432]{2,1,0:T(8,128)(2,1)S(1)} %constant_dynamic-update-slice_fusion), channel_id=1, source_target_pairs={{0,2},{1,3},{2,0},{3,1},{4,6},{5,7},{6,4},{7,5},{8,10},{9,11},{10,... | collective-permute-start | bytes 1400840 | tf_op jit(solution)/shard_map/ppermute | solution.py:802
  30.8 13.7 %collective-permute-start.5 = (bf16[4,24,2432]{2,1,0:T(8,128)(2,1)S(1)}, bf16[4,24,2432]{2,1,0:T(8,128)(2,1)}, u32[]{:S(2)}, u32[]{:S(2)}) collective-permute-start(bf16[4,24,2432]{2,1,0:T(8,128)(2,1)S(1)} %pad_maximum_fusion.2), channel_id=1, source_target_pairs={{0,4},{1,5},{2,6},{3,7},{4,0},{5,1},{6,2},{7,3},{8,12},{9,13},{10,... | collective-permute-start | bytes 1400840 | tf_op jit(solution)/shard_map/ppermute | solution.py:802
  33.1 16.6 %collective-permute-start.9 = (bf16[4,24,2432]{2,1,0:T(8,128)(2,1)S(1)}, bf16[4,24,2432]{2,1,0:T(8,128)(2,1)}, u32[]{:S(2)}, u32[]{:S(2)}) collective-permute-start(bf16[4,24,2432]{2,1,0:T(8,128)(2,1)S(1)} %constant_dynamic-update-slice_fusion), channel_id=1, source_target_pairs={{0,1},{1,0},{2,3},{3,2},{4,5},{5,4},{6,7},{7,6},{8,9},{9,8},{10,11... | collective-permute-start | bytes 1400840 | tf_op jit(solution)/shard_map/ppermute | solution.py:802
  33.2 17.8 %collective-permute-start.7 = (bf16[4,24,2432]{2,1,0:T(8,128)(2,1)S(1)}, bf16[4,24,2432]{2,1,0:T(8,128)(2,1)}, u32[]{:S(2)}, u32[]{:S(2)}) collective-permute-start(bf16[4,24,2432]{2,1,0:T(8,128)(2,1)S(1)} %pad_maximum_fusion.2), channel_id=1, source_target_pairs={{0,1},{1,0},{2,3},{3,2},{4,5},{5,4},{6,7},{7,6},{8,9},{9,8},{10,11... | collective-permute-start | bytes 1400840 | tf_op jit(solution)/shard_map/ppermute | solution.py:802
  49.2 11.8 %collective-permute-start.11 = (bf16[2,24,3840]{2,1,0:T(8,128)(2,1)}, bf16[2,24,3840]{2,1,0:T(8,128)(2,1)}, u32[]{:S(2)}, u32[]{:S(2)}) collective-permute-start(bf16[2,24,3840]{2,1,0:T(8,128)(2,1)} %pad_maximum_fusion.3), channel_id=1, source_target_pairs={{0,2},{1,3},{2,0},{3,1},{4,6},{5,7},{6,4},{7,5},{8,10},{9,11},{10,... | collective-permute-start | bytes 1105928 | tf_op jit(solution)/shard_map/ppermute | solution.py:802
  49.7 11.2 %collective-permute-start.13 = (bf16[2,24,3840]{2,1,0:T(8,128)(2,1)}, bf16[2,24,3840]{2,1,0:T(8,128)(2,1)}, u32[]{:S(2)}, u32[]{:S(2)}) collective-permute-start(bf16[2,24,3840]{2,1,0:T(8,128)(2,1)} %collective-permute-done.12), channel_id=1, source_target_pairs={{0,4},{1,5},{2,6},{3,7},{4,0},{5,1},{6,2},{7,3},{8,12},{9,13},{10,... | collective-permute-start | bytes 1105928 | tf_op jit(solution)/shard_map/ppermute | solution.py:802
  62.3 26.2 %collective-permute-start.19 = (bf16[4,24,3840]{2,1,0:T(8,128)(2,1)S(1)}, bf16[4,24,3840]{2,1,0:T(8,128)(2,1)}, u32[]{:S(2)}, u32[]{:S(2)}) collective-permute-start(bf16[4,24,3840]{2,1,0:T(8,128)(2,1)S(1)} %constant_dynamic-update-slice_fusion.2), channel_id=1, source_target_pairs={{0,2},{1,3},{2,0},{3,1},{4,6},{5,7},{6,4},{7,5},{8,10},{9,11},{10,... | collective-permute-start | bytes 2211848 | tf_op jit(solution)/shard_map/ppermute | solution.py:802
  65.8 22.7 %collective-permute-start.18 = (bf16[4,24,3840]{2,1,0:T(8,128)(2,1)}, bf16[4,24,3840]{2,1,0:T(8,128)(2,1)}, u32[]{:S(2)}, u32[]{:S(2)}) collective-permute-start(bf16[4,24,3840]{2,1,0:T(8,128)(2,1)} %pad_maximum_fusion), channel_id=1, source_target_pairs={{0,4},{1,5},{2,6},{3,7},{4,0},{5,1},{6,2},{7,3},{8,12},{9,13},{10,... | collective-permute-start | bytes 2211848 | tf_op jit(solution)/shard_map/ppermute | solution.py:802
  68.2 23.1 %collective-permute-start.22 = (bf16[4,24,3840]{2,1,0:T(8,128)(2,1)S(1)}, bf16[4,24,3840]{2,1,0:T(8,128)(2,1)S(1)}, u32[]{:S(2)}, u32[]{:S(2)}) collective-permute-start(bf16[4,24,3840]{2,1,0:T(8,128)(2,1)S(1)} %constant_dynamic-update-slice_fusion.2), channel_id=1, source_target_pairs={{0,1},{1,0},{2,3},{3,2},{4,5},{5,4},{6,7},{7,6},{8,9},{9,8},{10,11... | collective-permute-start | bytes 2211848 | tf_op jit(solution)/shard_map/ppermute | solution.py:802
  68.2 16.9 %collective-permute-start.16 = (bf16[2,96,768]{2,1,0:T(8,128)(2,1)S(1)}, bf16[2,96,768]{2,1,0:T(8,128)(2,1)S(1)}, u32[]{:S(2)}, u32[]{:S(2)}) collective-permute-start(bf16[2,96,768]{2,1,0:T(8,128)(2,1)S(1)} %copy-done.42), channel_id=1, source_target_pairs={{0,2},{1,3},{2,0},{3,1},{4,6},{5,7},{6,4},{7,5},{8,10},{9,11},{10,... | collective-permute-start | bytes 884744 | tf_op jit(solution)/shard_map/ppermute | solution.py:802
  74.1 14.4 %collective-permute-start.17 = (bf16[2,96,768]{2,1,0:T(8,128)(2,1)S(1)}, bf16[2,96,768]{2,1,0:T(8,128)(2,1)S(1)}, u32[]{:S(2)}, u32[]{:S(2)}) collective-permute-start(bf16[2,96,768]{2,1,0:T(8,128)(2,1)S(1)} %collective-permute-done.15), channel_id=1, source_target_pairs={{0,4},{1,5},{2,6},{3,7},{4,0},{5,1},{6,2},{7,3},{8,12},{9,13},{10,... | collective-permute-start | bytes 884744 | tf_op jit(solution)/shard_map/ppermute | solution.py:802
  85.0 19.1 %collective-permute-start.20 = (bf16[4,24,3840]{2,1,0:T(8,128)(2,1)}, bf16[4,24,3840]{2,1,0:T(8,128)(2,1)}, u32[]{:S(2)}, u32[]{:S(2)}) collective-permute-start(bf16[4,24,3840]{2,1,0:T(8,128)(2,1)} %pad_maximum_fusion), channel_id=1, source_target_pairs={{0,1},{1,0},{2,3},{3,2},{4,5},{5,4},{6,7},{7,6},{8,9},{9,8},{10,11... | collective-permute-start | bytes 2211848 | tf_op jit(solution)/shard_map/ppermute | solution.py:802
  88.5 15.7 %collective-permute-start.23 = (bf16[4,24,3840]{2,1,0:T(8,128)(2,1)}, bf16[4,24,3840]{2,1,0:T(8,128)(2,1)}, u32[]{:S(2)}, u32[]{:S(2)}) collective-permute-start(bf16[4,24,3840]{2,1,0:T(8,128)(2,1)} %collective-permute-done.19), channel_id=1, source_target_pairs={{0,1},{1,0},{2,3},{3,2},{4,5},{5,4},{6,7},{7,6},{8,9},{9,8},{10,11... | collective-permute-start | bytes 2211848 | tf_op jit(solution)/shard_map/ppermute | solution.py:802
  88.5 16.2 %collective-permute-start.21 = (bf16[4,24,3840]{2,1,0:T(8,128)(2,1)}, bf16[4,24,3840]{2,1,0:T(8,128)(2,1)}, u32[]{:S(2)}, u32[]{:S(2)}) collective-permute-start(bf16[4,24,3840]{2,1,0:T(8,128)(2,1)} %collective-permute-done.18), channel_id=1, source_target_pairs={{0,1},{1,0},{2,3},{3,2},{4,5},{5,4},{6,7},{7,6},{8,9},{9,8},{10,11... | collective-permute-start | bytes 2211848 | tf_op jit(solution)/shard_map/ppermute | solution.py:802
  89.7 22.1 %collective-permute-start.25 = (bf16[4,96,768]{2,1,0:T(8,128)(2,1)}, bf16[4,96,768]{2,1,0:T(8,128)(2,1)}, u32[]{:S(2)}, u32[]{:S(2)}) collective-permute-start(bf16[4,96,768]{2,1,0:T(8,128)(2,1)} %constant_dynamic-update-slice_fusion.4), channel_id=1, source_target_pairs={{0,2},{1,3},{2,0},{3,1},{4,6},{5,7},{6,4},{7,5},{8,10},{9,11},{10,... | collective-permute-start | bytes 1769480 | tf_op jit(solution)/shard_map/ppermute | solution.py:802
  91.2 20.6 %collective-permute-start.24 = (bf16[4,96,768]{2,1,0:T(8,128)(2,1)}, bf16[4,96,768]{2,1,0:T(8,128)(2,1)}, u32[]{:S(2)}, u32[]{:S(2)}) collective-permute-start(bf16[4,96,768]{2,1,0:T(8,128)(2,1)} %pad_maximum_fusion.1), channel_id=1, source_target_pairs={{0,4},{1,5},{2,6},{3,7},{4,0},{5,1},{6,2},{7,3},{8,12},{9,13},{10,... | collective-permute-start | bytes 1769480 | tf_op jit(solution)/shard_map/ppermute | solution.py:802
  104.1 9.9 %collective-permute-start.28 = (bf16[4,96,768]{2,1,0:T(8,128)(2,1)}, bf16[4,96,768]{2,1,0:T(8,128)(2,1)}, u32[]{:S(2)}, u32[]{:S(2)}) collective-permute-start(bf16[4,96,768]{2,1,0:T(8,128)(2,1)} %constant_dynamic-update-slice_fusion.4), channel_id=1, source_target_pairs={{0,1},{1,0},{2,3},{3,2},{4,5},{5,4},{6,7},{7,6},{8,9},{9,8},{10,11... | collective-permute-start | bytes 1769480 | tf_op jit(solution)/shard_map/ppermute | solution.py:802
  104.2 9.8 %collective-permute-start.26 = (bf16[4,96,768]{2,1,0:T(8,128)(2,1)}, bf16[4,96,768]{2,1,0:T(8,128)(2,1)}, u32[]{:S(2)}, u32[]{:S(2)}) collective-permute-start(bf16[4,96,768]{2,1,0:T(8,128)(2,1)} %pad_maximum_fusion.1), channel_id=1, source_target_pairs={{0,1},{1,0},{2,3},{3,2},{4,5},{5,4},{6,7},{7,6},{8,9},{9,8},{10,11... | collective-permute-start | bytes 1769480 | tf_op jit(solution)/shard_map/ppermute | solution.py:802
  146.1 8.5 %collective-permute-start.30 = (bf16[16,96,768]{2,1,0:T(8,128)(2,1)}, bf16[16,96,768]{2,1,0:T(8,128)(2,1)S(1)}, u32[]{:S(2)}, u32[]{:S(2)}) collective-permute-start(bf16[16,96,768]{2,1,0:T(8,128)(2,1)} %get-tuple-element.147), channel_id=1, source_target_pairs={{0,1},{1,0},{2,3},{3,2},{4,5},{5,4},{6,7},{7,6},{8,9},{9,8},{10,11... | collective-permute-start | bytes 7077896 | tf_op jit(solution)/shard_map/ppermute | solution.py:802
  146.3 19.3 %collective-permute-start.31 = (bf16[16,24,3072]{2,1,0:T(8,128)(2,1)}, bf16[16,24,3072]{2,1,0:T(8,128)(2,1)S(1)}, u32[]{:S(2)}, u32[]{:S(2)}) collective-permute-start(bf16[16,24,3072]{2,1,0:T(8,128)(2,1)} %bitcast.147), channel_id=1, source_target_pairs={{0,1},{1,0},{2,3},{3,2},{4,5},{5,4},{6,7},{7,6},{8,9},{9,8},{10,11... | collective-permute-start | bytes 7077896 | tf_op jit(solution)/shard_map/ppermute | solution.py:802
  156.8 19.7 %collective-permute-start.33 = (bf16[4,96,768]{2,1,0:T(8,128)(2,1)S(1)}, bf16[4,96,768]{2,1,0:T(8,128)(2,1)S(1)}, u32[]{:S(2)}, u32[]{:S(2)}) collective-permute-start(bf16[4,96,768]{2,1,0:T(8,128)(2,1)S(1)} %get-tuple-element.218), channel_id=1, source_target_pairs={{0,2},{1,3},{2,0},{3,1},{4,6},{5,7},{6,4},{7,5},{8,10},{9,11},{10,... | collective-permute-start | bytes 1769480 | tf_op jit(solution)/shard_map/ppermute | solution.py:802
  158.3 19.5 %collective-permute-start.32 = (bf16[4,96,768]{2,1,0:T(8,128)(2,1)S(1)}, bf16[4,96,768]{2,1,0:T(8,128)(2,1)S(1)}, u32[]{:S(2)}, u32[]{:S(2)}) collective-permute-start(bf16[4,96,768]{2,1,0:T(8,128)(2,1)S(1)} %get-tuple-element.219), channel_id=1, source_target_pairs={{0,4},{1,5},{2,6},{3,7},{4,0},{5,1},{6,2},{7,3},{8,12},{9,13},{10,... | collective-permute-start | bytes 1769480 | tf_op jit(solution)/shard_map/ppermute | solution.py:802
  159.0 19.0 %collective-permute-start.38 = (bf16[16,24,768]{2,1,0:T(8,128)(2,1)S(1)}, bf16[16,24,768]{2,1,0:T(8,128)(2,1)S(1)}, u32[]{:S(2)}, u32[]{:S(2)}) collective-permute-start(bf16[16,24,768]{2,1,0:T(8,128)(2,1)S(1)} %bitcast.105), channel_id=1, source_target_pairs={{0,1},{1,0},{2,3},{3,2},{4,5},{5,4},{6,7},{7,6},{8,9},{9,8},{10,11... | collective-permute-start | bytes 1769480 | tf_op jit(solution)/shard_map/ppermute | solution.py:802
  159.0 19.7 %collective-permute-start.37 = (bf16[16,24,1152]{2,1,0:T(8,128)(2,1)S(1)}, bf16[16,24,1152]{2,1,0:T(8,128)(2,1)S(1)}, u32[]{:S(2)}, u32[]{:S(2)}) collective-permute-start(bf16[16,24,1152]{2,1,0:T(8,128)(2,1)S(1)} %bitcast.149), channel_id=1, source_target_pairs={{0,1},{1,0},{2,3},{3,2},{4,5},{5,4},{6,7},{7,6},{8,9},{9,8},{10,11... | collective-permute-start | bytes 2654216 | tf_op jit(solution)/shard_map/ppermute | solution.py:802
  166.4 34.2 %collective-permute-start.43 = (bf16[4,24,3072]{2,1,0:T(8,128)(2,1)S(1)}, bf16[4,24,3072]{2,1,0:T(8,128)(2,1)S(1)}, u32[]{:S(2)}, u32[]{:S(2)}) collective-permute-start(bf16[4,24,3072]{2,1,0:T(8,128)(2,1)S(1)} %get-tuple-element.222), channel_id=1, source_target_pairs={{0,2},{1,3},{2,0},{3,1},{4,6},{5,7},{6,4},{7,5},{8,10},{9,11},{10,... | collective-permute-start | bytes 1769480 | tf_op jit(solution)/shard_map/ppermute | solution.py:802
  176.4 25.7 %collective-permute-start.42 = (bf16[4,24,3072]{2,1,0:T(8,128)(2,1)S(1)}, bf16[4,24,3072]{2,1,0:T(8,128)(2,1)S(1)}, u32[]{:S(2)}, u32[]{:S(2)}) collective-permute-start(bf16[4,24,3072]{2,1,0:T(8,128)(2,1)S(1)} %get-tuple-element.223), channel_id=1, source_target_pairs={{0,4},{1,5},{2,6},{3,7},{4,0},{5,1},{6,2},{7,3},{8,12},{9,13},{10,... | collective-permute-start | bytes 1769480 | tf_op jit(solution)/shard_map/ppermute | solution.py:802
  177.8 32.2 %collective-permute-start.40 = (bf16[16,24,1152]{2,1,0:T(8,128)(2,1)S(1)}, bf16[16,24,1152]{2,1,0:T(8,128)(2,1)S(1)}, u32[]{:S(2)}, u32[]{:S(2)}) collective-permute-start(bf16[16,24,1152]{2,1,0:T(8,128)(2,1)S(1)} %bitcast.148), channel_id=1, source_target_pairs={{0,1},{1,0},{2,3},{3,2},{4,5},{5,4},{6,7},{7,6},{8,9},{9,8},{10,11... | collective-permute-start | bytes 2654216 | tf_op jit(solution)/shard_map/ppermute | solution.py:802
  178.0 19.8 %collective-permute-start.36 = (bf16[2,96,768]{2,1,0:T(8,128)(2,1)S(1)}, bf16[2,96,768]{2,1,0:T(8,128)(2,1)S(1)}, u32[]{:S(2)}, u32[]{:S(2)}) collective-permute-start(bf16[2,96,768]{2,1,0:T(8,128)(2,1)S(1)} %add_convert_fusion.14), channel_id=1, source_target_pairs={{0,4},{1,5},{2,6},{3,7},{4,0},{5,1},{6,2},{7,3},{8,12},{9,13},{10,... | collective-permute-start | bytes 884744 | tf_op jit(solution)/shard_map/ppermute | solution.py:802
  178.8 19.0 %collective-permute-start.35 = (bf16[2,96,768]{2,1,0:T(8,128)(2,1)S(1)}, bf16[2,96,768]{2,1,0:T(8,128)(2,1)S(1)}, u32[]{:S(2)}, u32[]{:S(2)}) collective-permute-start(bf16[2,96,768]{2,1,0:T(8,128)(2,1)S(1)} %add_convert_fusion.15), channel_id=1, source_target_pairs={{0,2},{1,3},{2,0},{3,1},{4,6},{5,7},{6,4},{7,5},{8,10},{9,11},{10,... | collective-permute-start | bytes 884744 | tf_op jit(solution)/shard_map/ppermute | solution.py:802
  197.8 21.8 %collective-permute-start.45 = (bf16[4,24,1920]{2,1,0:T(8,128)(2,1)S(1)}, bf16[4,24,1920]{2,1,0:T(8,128)(2,1)S(1)}, u32[]{:S(2)}, u32[]{:S(2)}) collective-permute-start(bf16[4,24,1920]{2,1,0:T(8,128)(2,1)S(1)} %pad_maximum_fusion.4), channel_id=1, source_target_pairs={{0,4},{1,5},{2,6},{3,7},{4,0},{5,1},{6,2},{7,3},{8,12},{9,13},{10,... | collective-permute-start | bytes 1105928 | tf_op jit(solution)/shard_map/ppermute | solution.py:802
  199.2 9.2 %collective-permute-start.41 = (bf16[2,96,768]{2,1,0:T(8,128)(2,1)S(1)}, bf16[2,96,768]{2,1,0:T(8,128)(2,1)S(1)}, u32[]{:S(2)}, u32[]{:S(2)}) collective-permute-start(bf16[2,96,768]{2,1,0:T(8,128)(2,1)S(1)} %add_convert_fusion.12), channel_id=1, source_target_pairs={{0,8},{1,9},{2,10},{3,11},{4,12},{5,13},{6,14},{7,15},{8,0},{9,1},... | collective-permute-start | bytes 884744 | tf_op jit(solution)/shard_map/ppermute | solution.py:802
  200.6 10.2 %collective-permute-start.39 = (f32[112,128]{1,0:T(8,128)S(1)}, f32[112,128]{1,0:T(8,128)S(1)}, u32[]{:S(2)}, u32[]{:S(2)}) collective-permute-start(f32[112,128]{1,0:T(8,128)S(1)} %add.245), channel_id=1, source_target_pairs={{0,2},{1,3},{2,0},{3,1},{4,6},{5,7},{6,4},{7,5},{8,10},{9,11},{10,... | collective-permute-start | bytes 172040 | tf_op jit(solution)/shard_map/ppermute | solution.py:802
  202.2 12.9 %collective-permute-start.48 = (bf16[2,24,3072]{2,1,0:T(8,128)(2,1)S(1)}, bf16[2,24,3072]{2,1,0:T(8,128)(2,1)S(1)}, u32[]{:S(2)}, u32[]{:S(2)}) collective-permute-start(bf16[2,24,3072]{2,1,0:T(8,128)(2,1)S(1)} %add_convert_fusion.8), channel_id=1, source_target_pairs={{0,4},{1,5},{2,6},{3,7},{4,0},{5,1},{6,2},{7,3},{8,12},{9,13},{10,... | collective-permute-start | bytes 884744 | tf_op jit(solution)/shard_map/ppermute | solution.py:802
  208.4 9.9 %collective-permute-start.47 = (bf16[2,24,3072]{2,1,0:T(8,128)(2,1)S(1)}, bf16[2,24,3072]{2,1,0:T(8,128)(2,1)S(1)}, u32[]{:S(2)}, u32[]{:S(2)}) collective-permute-start(bf16[2,24,3072]{2,1,0:T(8,128)(2,1)S(1)} %add_convert_fusion.9), channel_id=1, source_target_pairs={{0,2},{1,3},{2,0},{3,1},{4,6},{5,7},{6,4},{7,5},{8,10},{9,11},{10,... | collective-permute-start | bytes 884744 | tf_op jit(solution)/shard_map/ppermute | solution.py:802
  210.0 16.3 %collective-permute-start.46 = (bf16[4,24,1920]{2,1,0:T(8,128)(2,1)S(1)}, bf16[4,24,1920]{2,1,0:T(8,128)(2,1)S(1)}, u32[]{:S(2)}, u32[]{:S(2)}) collective-permute-start(bf16[4,24,1920]{2,1,0:T(8,128)(2,1)S(1)} %pad_maximum_fusion.5), channel_id=1, source_target_pairs={{0,2},{1,3},{2,0},{3,1},{4,6},{5,7},{6,4},{7,5},{8,10},{9,11},{10,... | collective-permute-start | bytes 1105928 | tf_op jit(solution)/shard_map/ppermute | solution.py:802
  210.8 17.9 %collective-permute-start.63 = (bf16[96,768]{1,0:T(8,128)(2,1)S(1)}, bf16[96,768]{1,0:T(8,128)(2,1)S(1)}, u32[]{:S(2)}, u32[]{:S(2)}) collective-permute-start(bf16[96,768]{1,0:T(8,128)(2,1)S(1)} %fusion.23), channel_id=1, source_target_pairs={{0,16},{1,17},{2,18},{3,19},{4,20},{5,21},{6,22},{7,23},{8,24},{9,... | collective-permute-start | bytes 442376 | tf_op jit(solution)/shard_map/ppermute | solution.py:802
  215.1 20.5 %collective-permute-start.53 = (bf16[4,24,1152]{2,1,0:T(8,128)(2,1)S(1)}, bf16[4,24,1152]{2,1,0:T(8,128)(2,1)S(1)}, u32[]{:S(2)}, u32[]{:S(2)}) collective-permute-start(bf16[4,24,1152]{2,1,0:T(8,128)(2,1)S(1)} %get-tuple-element.230), channel_id=1, source_target_pairs={{0,2},{1,3},{2,0},{3,1},{4,6},{5,7},{6,4},{7,5},{8,10},{9,11},{10,... | collective-permute-start | bytes 663560 | tf_op jit(solution)/shard_map/ppermute | solution.py:802
  218.4 9.3 %collective-permute-start.44 = (f32[112,128]{1,0:T(8,128)S(1)}, f32[112,128]{1,0:T(8,128)S(1)}, u32[]{:S(2)}, u32[]{:S(2)}) collective-permute-start(f32[112,128]{1,0:T(8,128)S(1)} %add.255), channel_id=1, source_target_pairs={{0,4},{1,5},{2,6},{3,7},{4,0},{5,1},{6,2},{7,3},{8,12},{9,13},{10,... | collective-permute-start | bytes 172040 | tf_op jit(solution)/shard_map/ppermute | solution.py:802
  219.6 17.9 %collective-permute-start.52 = (bf16[4,24,1152]{2,1,0:T(8,128)(2,1)S(1)}, bf16[4,24,1152]{2,1,0:T(8,128)(2,1)S(1)}, u32[]{:S(2)}, u32[]{:S(2)}) collective-permute-start(bf16[4,24,1152]{2,1,0:T(8,128)(2,1)S(1)} %get-tuple-element.231), channel_id=1, source_target_pairs={{0,4},{1,5},{2,6},{3,7},{4,0},{5,1},{6,2},{7,3},{8,12},{9,13},{10,... | collective-permute-start | bytes 663560 | tf_op jit(solution)/shard_map/ppermute | solution.py:802
  227.7 10.6 %collective-permute-start.51 = (bf16[2,24,1920]{2,1,0:T(8,128)(2,1)S(1)}, bf16[2,24,1920]{2,1,0:T(8,128)(2,1)S(1)}, u32[]{:S(2)}, u32[]{:S(2)}) collective-permute-start(bf16[2,24,1920]{2,1,0:T(8,128)(2,1)S(1)} %add_convert_fusion.20), channel_id=1, source_target_pairs={{0,4},{1,5},{2,6},{3,7},{4,0},{5,1},{6,2},{7,3},{8,12},{9,13},{10,... | collective-permute-start | bytes 552968 | tf_op jit(solution)/shard_map/ppermute | solution.py:802
  228.7 11.1 %collective-permute-start.50 = (bf16[2,24,1920]{2,1,0:T(8,128)(2,1)S(1)}, bf16[2,24,1920]{2,1,0:T(8,128)(2,1)S(1)}, u32[]{:S(2)}, u32[]{:S(2)}) collective-permute-start(bf16[2,24,1920]{2,1,0:T(8,128)(2,1)S(1)} %add_convert_fusion.21), channel_id=1, source_target_pairs={{0,2},{1,3},{2,0},{3,1},{4,6},{5,7},{6,4},{7,5},{8,10},{9,11},{10,... | collective-permute-start | bytes 552968 | tf_op jit(solution)/shard_map/ppermute | solution.py:802
  235.7 16.1 %collective-permute-start.62 = (bf16[24,3072]{1,0:T(8,128)(2,1)S(1)}, bf16[24,3072]{1,0:T(8,128)(2,1)S(1)}, u32[]{:S(2)}, u32[]{:S(2)}) collective-permute-start(bf16[24,3072]{1,0:T(8,128)(2,1)S(1)} %fusion.24), channel_id=1, source_target_pairs={{0,16},{1,17},{2,18},{3,19},{4,20},{5,21},{6,22},{7,23},{8,24},{9,... | collective-permute-start | bytes 442376 | tf_op jit(solution)/shard_map/ppermute | solution.py:802
  237.5 9.9 %collective-permute-start.58 = (bf16[2,24,1152]{2,1,0:T(8,128)(2,1)S(1)}, bf16[2,24,1152]{2,1,0:T(8,128)(2,1)S(1)}, u32[]{:S(2)}, u32[]{:S(2)}) collective-permute-start(bf16[2,24,1152]{2,1,0:T(8,128)(2,1)S(1)} %add_convert_fusion.28), channel_id=1, source_target_pairs={{0,4},{1,5},{2,6},{3,7},{4,0},{5,1},{6,2},{7,3},{8,12},{9,13},{10,... | collective-permute-start | bytes 331784 | tf_op jit(solution)/shard_map/ppermute | solution.py:802
  238.3 9.2 %collective-permute-start.57 = (bf16[2,24,1152]{2,1,0:T(8,128)(2,1)S(1)}, bf16[2,24,1152]{2,1,0:T(8,128)(2,1)S(1)}, u32[]{:S(2)}, u32[]{:S(2)}) collective-permute-start(bf16[2,24,1152]{2,1,0:T(8,128)(2,1)S(1)} %add_convert_fusion.29), channel_id=1, source_target_pairs={{0,2},{1,3},{2,0},{3,1},{4,6},{5,7},{6,4},{7,5},{8,10},{9,11},{10,... | collective-permute-start | bytes 331784 | tf_op jit(solution)/shard_map/ppermute | solution.py:802
  239.9 12.6 %collective-permute-start.56 = (bf16[2,24,1920]{2,1,0:T(8,128)(2,1)S(1)}, bf16[2,24,1920]{2,1,0:T(8,128)(2,1)S(1)}, u32[]{:S(2)}, u32[]{:S(2)}) collective-permute-start(bf16[2,24,1920]{2,1,0:T(8,128)(2,1)S(1)} %add_convert_fusion.18), channel_id=1, source_target_pairs={{0,8},{1,9},{2,10},{3,11},{4,12},{5,13},{6,14},{7,15},{8,0},{9,1},... | collective-permute-start | bytes 552968 | tf_op jit(solution)/shard_map/ppermute | solution.py:802
  (66 other events, 517.2 us)

commit v4 on v3

--- a/solution.py
+++ b/solution.py
@@ -16,13 +16,14 @@
 NWS = 5
 EDGE = 8
 LENGTH = WIN * WIN
-GROUPS = 2
-PAIRS = HEADS // 2 // GROUPS
-GROUP = PAIRS * 128
+PAIRS = HEADS // 2
 BLOCK = 200
 SCALE = HEAD_DIM ** (-0.5)
 EPS = 1e-06
+ATTENTION_VMEM = 60 * 1024 * 1024
+KERNEL_VMEM = 60 * 1024 * 1024
 QUICK = pl.CostEstimate(flops=1, bytes_accessed=1, transcendentals=0)
+LONG = pl.CostEstimate(flops=100_000_000_000, bytes_accessed=1, transcendentals=0)
 LANES = 256
 BF = jnp.bfloat16
 F32 = jnp.float32
@@ -215,7 +216,7 @@
         parts[1].append(jnp.where(low, by_key[0], by_key[1]))
         parts[2].append(jnp.where(low, by_value[0], by_value[1]))
     for block in range(3):
-        at = pl.multiple_of(block * GROUP + pair * 128, 128)
+        at = pl.multiple_of(block * D + pair * 128, 128)
         grad_qkv_ref[:, pl.ds(at, 128)] = merge_windows(*parts[block]).astype(BF)
     table_grad_ref[...] += table_total
 
@@ -240,11 +241,11 @@
         in_specs=columns + constants,
         out_specs=[pl.BlockSpec((rows, 128), lambda pair: (0, pair)), probs_spec],
         out_shape=[
-            jax.ShapeDtypeStruct((rows, GROUP), BF),
+            jax.ShapeDtypeStruct((rows, D), BF),
             jax.ShapeDtypeStruct((PAIRS, 4, BLOCK, LANES), F32),
         ],
         cost_estimate=QUICK,
-        compiler_params=pltpu.CompilerParams(vmem_limit_bytes=32 * 1024 * 1024),
+        compiler_params=pltpu.CompilerParams(vmem_limit_bytes=ATTENTION_VMEM),
         name="attention",
     )(qkv, qkv, qkv, table, onehot, shift)
 
@@ -255,14 +256,15 @@
     return pl.pallas_call(
         attn_bwd_kernel,
         grid=(PAIRS,),
-        in_specs=columns + [pl.BlockSpec((rows, 128), lambda pair: (0, pair)), probs_spec] + constants,
-        out_specs=[whole(rows, 3 * GROUP), whole(128, 128)],
+        in_specs=columns + [pl.BlockSpec((rows, 128), lambda pair: (0, pair)), probs_spec]
+        + constants,
+        out_specs=[whole(rows, 3 * D), whole(128, 128)],
         out_shape=[
-            jax.ShapeDtypeStruct((rows, 3 * GROUP), BF),
+            jax.ShapeDtypeStruct((rows, 3 * D), BF),
             jax.ShapeDtypeStruct((128, 128), F32),
         ],
         cost_estimate=QUICK,
-        compiler_params=pltpu.CompilerParams(vmem_limit_bytes=32 * 1024 * 1024),
+        compiler_params=pltpu.CompilerParams(vmem_limit_bytes=ATTENTION_VMEM),
         name="attention_back",
     )(qkv, qkv, qkv, grad_mixed, probs, table, onehot, shift)
 
@@ -326,23 +328,23 @@
 
 
 def front_kernel(tokens_ref, live_ref, order_ref, rows_ref, b_qkv_ref, *rest):
-    pieces, (normed_ref, one_ref, two_ref, weight, sem) = rest[:PIECES], rest[PIECES:]
+    pieces, (turned_ref, qkv_ref, weight, sem) = rest[:PIECES], rest[PIECES:]
     copies = [copy_rows(pieces, (block * D, D), weight, block * D, sem.at[block]) for block in range(3)]
     for block in copies:
         start_all(block)
     unit, _ = normalise(tokens_ref[...].astype(F32))
     normed = ((unit * rows_ref[0:1, :] + rows_ref[1:2, :]) * live_ref[...]).astype(BF)
-    normed = dot_nn(normed, order_ref[...]).astype(BF)
-    normed_ref[...] = normed
+    turned = dot_nn(normed, order_ref[...])
+    normed = turned.astype(BF)
+    turned_ref[...] = turned.T.astype(BF)
     for block in range(3):
         wait_all(copies[block])
         at = block * D
-        values = (dot_nn(normed, weight[:, at : at + D]) + b_qkv_ref[:, at : at + D]).astype(BF)
-        one_ref[:, block * GROUP : (block + 1) * GROUP] = values[:, :GROUP]
-        two_ref[:, block * GROUP : (block + 1) * GROUP] = values[:, GROUP:]
-
-
-PIECES = 8
+        values = dot_nn(normed, weight[:, at : at + D]) + b_qkv_ref[:, at : at + D]
+        qkv_ref[:, at : at + D] = values.astype(BF)
+
+
+PIECES = 2
 HBM = pl.BlockSpec(memory_space=pl.ANY)
 VMEM = pl.BlockSpec(memory_space=pltpu.VMEM)
 SMEM = pl.BlockSpec(memory_space=pltpu.SMEM)
@@ -353,22 +355,21 @@
     return pl.pallas_call(
         front_kernel,
         in_specs=[VMEM] * 5 + [HBM] * PIECES,
-        out_specs=[VMEM] * 3,
-        out_shape=[struct((rows, D), BF)] + [struct((rows, 3 * GROUP), BF)] * GROUPS,
+        out_specs=[VMEM] * 2,
+        out_shape=[struct((D, rows), BF), struct((rows, 3 * D), BF)],
         scratch_shapes=[pltpu.VMEM((D, 3 * D), BF), pltpu.SemaphoreType.DMA((3, PIECES))],
         cost_estimate=QUICK,
-        compiler_params=pltpu.CompilerParams(vmem_limit_bytes=32 * 1024 * 1024),
+        compiler_params=pltpu.CompilerParams(vmem_limit_bytes=KERNEL_VMEM),
         name="front",
-    )(tokens, live, order, vectors, b_qkv, *in_hbm(pieces))
-
-
-def proj_kernel(tokens_ref, one_ref, two_ref, order_ref, rows_ref, *rest):
+    )(tokens, live, order, vectors, b_qkv, *pieces)
+
+
+def proj_kernel(tokens_ref, values_ref, order_ref, rows_ref, *rest):
     pieces, (residual_ref, normed_ref, turned_ref, mixed_ref, w_proj, sem) = rest[:PIECES], rest[PIECES:]
     b_proj, gain, bias = (rows_ref[i : i + 1, :] for i in range(3))
-    copies = copy_rows(pieces, (0, D), w_proj, 0, sem)
+    copies = copy_rows(pieces, (3 * D, D), w_proj, 0, sem)
     start_all(copies)
-    mixed = dot_nn(one_ref[...], order_ref[:GROUP, :]) + dot_nn(two_ref[...], order_ref[GROUP:, :])
-    mixed = mixed.astype(BF)
+    mixed = dot_nn(values_ref[...], order_ref[...]).astype(BF)
     mixed_ref[...] = mixed
     wait_all(copies)
     values = tokens_ref[...].astype(F32) + dot_nn(mixed, w_proj[...]) + b_proj
@@ -379,130 +380,134 @@
     turned_ref[...] = low.T.astype(BF)
 
 
+def down_copies(pieces, owners, me_ref, weight, sems):
+    copies = []
+    for piece, masks in zip(pieces, owners):
+        rows = piece.shape[0] // len(masks)
+        for index, mask in enumerate(masks):
+            to = jnp.bitwise_xor(me_ref[0], mask) * rows
+            copies.append(
+                pltpu.make_async_copy(
+                    piece.at[index * rows : (index + 1) * rows],
+                    weight.at[pl.ds(pl.multiple_of(to, rows), rows)],
+                    sems.at[len(copies)],
+                )
+            )
+    return copies
+
+
 def mlp_kernel(split_rows, owners, place_ref, me_ref, *rest):
-    normed_ref, turned_ref, residual_ref, mixed_ref, live_ref, out_grad_ref, *rest = rest
-    order_ref, rows_ref, b_up_ref, *rest = rest
+    normed_ref, turned_ref, live_ref, out_grad_ref, residual_ref, rows_ref, b_up_ref, *rest = rest
     up_pieces, rest = rest[:PIECES], rest[PIECES:]
     down_pieces, rest = rest[: len(owners)], rest[len(owners) :]
-    output_ref, grad_residual_ref, grad_one_ref, grad_two_ref, kept_ref, sent_ref, *rest = rest
-    kept_proj_ref, sent_proj_ref, sums_ref, grad_b_ref, *rest = rest
+    output_ref, grad_normed_ref, kept_ref, sent_ref, grad_b_ref, *rest = rest
     if split_rows:
         kept_down_ref, sent_down_ref, *rest = rest
     else:
         grad_down_ref, *rest = rest
-    branch, total, grad_normed, w_up, w_down, w_proj, staged, sem, up_sem, down_sem = rest
+    branch, total, w_up, w_down, staged, sem, up_sem, down_sem = rest
     step = pl.program_id(0)
-    last = STEPS - 1
     half = D // 2
 
     def up_copies(index):
-        return copy_rows(up_pieces, (D + index * TILE, TILE), w_up, index * TILE, up_sem.at[index])
-
-    def proj_copies():
-        return copy_rows(up_pieces, (0, D), w_proj, 0, up_sem.at[STEPS])
-
-    def down_copies():
-        copies = []
-        for piece, masks in zip(down_pieces, owners):
-            rows = piece.shape[0] // len(masks)
-            for index, mask in enumerate(masks):
-                to = jnp.bitwise_xor(me_ref[0], mask) * rows
-                copies.append(
-                    pltpu.make_async_copy(
-                        piece.at[index * rows : (index + 1) * rows],
-                        w_down.at[pl.ds(pl.multiple_of(to, rows), rows)],
-                        down_sem.at[len(copies)],
-                    )
-                )
-        return copies
+        return copy_rows(up_pieces, (index * TILE, TILE), w_up, index * TILE, up_sem.at[index])
 
     @pl.when(step == 0)
     def _():
         start_all(up_copies(0))
-        copies = down_copies()
-        start_all(copies)
+        start_all(down_copies(down_pieces, owners, me_ref, w_down, down_sem))
         for index in range(1, STEPS):
             start_all(up_copies(index))
-        start_all(proj_copies())
         branch[...] = (out_grad_ref[...].astype(F32) * live_ref[...]).astype(BF)
-        total[...] = jnp.zeros_like(total)
-        grad_normed[...] = jnp.zeros_like(grad_normed)
-        wait_all(copies)
+        grad_normed_ref[...] = jnp.zeros_like(grad_normed_ref)
+        total[...] = residual_ref[...] + rows_ref[3:4, :]
 
     wait_all(up_copies(step))
     at = pl.multiple_of(step * TILE, TILE)
-    weight = w_down[pl.ds(at, TILE), :]
     weight_up = w_up[:, pl.ds(at, TILE)]
     hidden = dot_nn(normed_ref[...], weight_up) + b_up_ref[...]
-    grad_active = dot_nt(branch[...], weight)
     cdf = normal_cdf(hidden)
     active = (hidden * cdf).astype(BF)
-    grad_hidden = (grad_active * (cdf + hidden * normal_pdf(hidden))).astype(BF)
+    slope = cdf + hidden * normal_pdf(hidden)
     grad_down = dot_tn(active, branch[...]).astype(BF)
-    total[...] += dot_nn(active, weight)
+
+    @pl.when(step == 0)
+    def _():
+        wait_all(down_copies(down_pieces, owners, me_ref, w_down, down_sem))
+
+    weight_down = w_down[pl.ds(at, TILE), :]
+    grad_active = dot_nt(branch[...], weight_down)
+    total[...] += dot_nn(active, weight_down)
+    grad_hidden = (grad_active * slope).astype(BF)
     sent_ref[...] = dot_nn(turned_ref[half:, :], grad_hidden).astype(BF)
     kept_ref[...] = dot_nn(turned_ref[:half, :], grad_hidden).astype(BF)
-    grad_normed[...] += dot_nt(grad_hidden, weight_up)
+    grad_normed_ref[...] += dot_nt(grad_hidden, weight_up)
     grad_b_ref[...] = jnp.sum(grad_hidden.astype(F32), axis=0, keepdims=True)
-    if split_rows:
-        slot = lax.rem(step, 2)
-        blocks = staged.shape[1]
-
-        def copy(slot, block, out, to):
-            return pltpu.make_async_copy(staged.at[slot, block], out.at[to], sem.at[slot, block])
-
-        @pl.when(step >= 2)
+
+    @pl.when(step == STEPS - 1)
+    def _():
+        output_ref[...] = (total[...] * live_ref[...]).astype(BF)
+
+    if not split_rows:
+        grad_down_ref[...] = grad_down
+        return
+
+    slot = lax.rem(step, 2)
+    blocks = staged.shape[1]
+
+    def copy(slot, block, out, to):
+        return pltpu.make_async_copy(staged.at[slot, block], out.at[to], sem.at[slot, block])
+
+    @pl.when(step >= 2)
+    def _():
+        for block in range(blocks):
+            copy(slot, block, kept_down_ref, 0).wait()
+
+    staged[slot] = grad_down.reshape(blocks, split_rows, D)
+    places = kept_down_ref.shape[0]
+    for block in range(blocks):
+        to = place_ref[step * blocks + block]
+
+        @pl.when(to < places)
         def _():
+            copy(slot, block, kept_down_ref, to).start()
+
+        @pl.when(to >= places)
+        def _():
+            copy(slot, block, sent_down_ref, to - places).start()
+
+    @pl.when(step == STEPS - 1)
+    def _():
+        for last_slot in range(2):
             for block in range(blocks):
-                copy(slot, block, kept_down_ref, 0).wait()
-
-        staged[slot] = grad_down.reshape(blocks, split_rows, D)
-        places = kept_down_ref.shape[0]
-        for block in range(blocks):
-            to = place_ref[step * blocks + block]
-
-            @pl.when(to < places)
-            def _():
-                copy(slot, block, kept_down_ref, to).start()
-
-            @pl.when(to >= places)
-            def _():
-                copy(slot, block, sent_down_ref, to - places).start()
-
-    else:
-        grad_down_ref[...] = grad_down
-
-    @pl.when(step == last)
-    def _():
-        wait_all(proj_copies())
-        gain, b_down = rows_ref[1:2, :], rows_ref[3:4, :]
-        live = live_ref[...]
-        residual = residual_ref[...]
-        output_ref[...] = ((residual + total[...] + b_down) * live).astype(BF)
-        grad = natural_order(grad_normed[...], order_ref[...])
-        unit, rstd = normalise(residual)
-        grad_residual = out_grad_ref[...].astype(F32) * live + normalise_back(
-            grad, unit, rstd, gain
-        )
-        grad_residual_ref[...] = grad_residual
-        grad_attn = grad_residual.astype(BF)
-        grad_mixed = dot_nt(grad_attn, w_proj[...]).astype(BF)
-        grad_mixed = dot_nt(grad_mixed, order_ref[...]).astype(BF)
-        grad_one_ref[...] = grad_mixed[:, :GROUP]
-        grad_two_ref[...] = grad_mixed[:, GROUP:]
-        sent_proj_ref[...] = dot_tn(mixed_ref[:, half:], grad_attn).astype(BF)
-        kept_proj_ref[...] = dot_tn(mixed_ref[:, :half], grad_attn).astype(BF)
-        sums_ref[0:1, :] = jnp.sum(grad_attn.astype(F32), axis=0, keepdims=True)
-        sums_ref[1:2, :] = jnp.sum(grad * unit, axis=0, keepdims=True)
-        sums_ref[2:3, :] = jnp.sum(grad, axis=0, keepdims=True)
-        sums_ref[3:4, :] = jnp.sum(branch[...].astype(F32), axis=0, keepdims=True)
-        sums_ref[4:, :] = jnp.zeros((4, D), F32)
-        if split_rows:
-            for last_slot in range(2):
-                for block in range(staged.shape[1]):
-                    pltpu.make_async_copy(
-                        staged.at[last_slot, block], kept_down_ref.at[0], sem.at[last_slot, block]
-                    ).wait()
+                copy(last_slot, block, kept_down_ref, 0).wait()
+
+
+def second_norm_kernel(
+    grad_normed_ref, residual_ref, mixed_ref, live_ref, out_grad_ref, order_ref, rows_ref, *rest
+):
+    pieces, rest = rest[:PIECES], rest[PIECES:]
+    grad_residual_ref, grad_mixed_ref, *rest = rest
+    kept_proj_ref, sent_proj_ref, sums_ref, w_proj, sem = rest
+    half = D // 2
+    copies = copy_rows(pieces, (3 * D, D), w_proj, 0, sem)
+    start_all(copies)
+    grad = natural_order(grad_normed_ref[...], order_ref[...])
+    unit, rstd = normalise(residual_ref[...])
+    grad_out = out_grad_ref[...].astype(F32) * live_ref[...]
+    grad_residual = grad_out + normalise_back(grad, unit, rstd, rows_ref[1:2, :])
+    grad_residual_ref[...] = grad_residual
+    grad_attn = grad_residual.astype(BF)
+    wait_all(copies)
+    grad_mixed = dot_nt(grad_attn, w_proj[...]).astype(BF)
+    grad_mixed_ref[...] = dot_nt(grad_mixed, order_ref[...]).astype(BF)
+    sent_proj_ref[...] = dot_tn(mixed_ref[:, half:], grad_attn).astype(BF)
+    kept_proj_ref[...] = dot_tn(mixed_ref[:, :half], grad_attn).astype(BF)
+    sums_ref[0:1, :] = jnp.sum(grad_attn.astype(F32), axis=0, keepdims=True)
+    sums_ref[1:2, :] = jnp.sum(grad * unit, axis=0, keepdims=True)
+    sums_ref[2:3, :] = jnp.sum(grad, axis=0, keepdims=True)
+    sums_ref[3:4, :] = jnp.sum(grad_out.astype(BF).astype(F32), axis=0, keepdims=True)
+    sums_ref[4:, :] = jnp.zeros((4, D), F32)
 
 
 def natural_order(values, order):
@@ -523,15 +528,11 @@
     return jax.ShapeDtypeStruct(shape, dtype)
 
 
-def in_hbm(arrays):
-    return [pltpu.with_memory_space_constraint(array, pltpu.HBM) for array in arrays]
-
-
 def project(tokens, mixed, order, vectors, pieces):
     rows = tokens.shape[0]
     return pl.pallas_call(
         proj_kernel,
-        in_specs=[VMEM] * 5 + [HBM] * PIECES,
+        in_specs=[VMEM] * 4 + [HBM] * PIECES,
         out_specs=[VMEM] * 4,
         out_shape=[
             struct((rows, D), F32),
@@ -541,113 +542,234 @@
         ],
         scratch_shapes=[pltpu.VMEM((D, D), BF), pltpu.SemaphoreType.DMA((PIECES,))],
         cost_estimate=QUICK,
-        compiler_params=pltpu.CompilerParams(vmem_limit_bytes=24 * 1024 * 1024),
+        compiler_params=pltpu.CompilerParams(vmem_limit_bytes=KERNEL_VMEM),
         name="project",
-    )(tokens, *mixed, order, vectors, *in_hbm(pieces))
+    )(tokens, mixed, order, vectors, *pieces)
+
+
+def placed_down(pieces, me, count):
+    if FF // count % 16:
+        return place(pieces, ((0, 0, D, 0),), (D,), me, count), ((0,),), jnp.zeros((1,), jnp.int32)
+    owners = tuple(tuple(masks) for _, masks in pieces)
+    return [stack.reshape(-1, D) for stack, _ in pieces], owners, me.reshape(1)
 
 
 def mlp(
-    me, count, normed, turned, residual, mixed, live, out_grad, order, vectors, b_up, up_pieces, down_pieces
+    me, count, places, normed, turned, live, out_grad, residual, vectors, b_up, up_pieces, down
 ):
-    rows = residual.shape[0]
+    rows = normed.shape[0]
     block_rows = FF // count
     split_rows = block_rows if block_rows % 16 == 0 else 0
+    down_pieces, owners, me_down = down
     column = lambda height: pl.BlockSpec((height, TILE), lambda step: (0, step))
-    inverse = np.argsort(np.array(sum_order(count)))
-    places = jnp.take(jnp.asarray(inverse, jnp.int32), jnp.bitwise_xor(me, np.arange(count)))
     if split_rows:
-        owners = tuple(tuple(masks) for _, masks in down_pieces)
-        down_pieces = [stack.reshape(-1, D) for stack, _ in down_pieces]
         half = struct((count // 2, block_rows, D), BF)
         grad_specs, grad_shapes = [HBM] * 2, [half, half]
         staged = (2, TILE // block_rows, block_rows, D)
     else:
-        down_pieces = place(down_pieces, ((0, 0, D, 0),), (D,), me, count)
-        owners, me_down = ((0,),), jnp.zeros_like(me)
         grad_specs = [pl.BlockSpec((TILE, D), lambda step: (step, 0))]
         grad_shapes = [struct((FF, D), BF)]
         staged = (2, 1, 16, 128)
-    wide, turn, square = (rows, D), (D, rows), (D, D)
+    wide = (rows, D)
     results = pl.pallas_call(
         functools.partial(mlp_kernel, split_rows, owners),
         grid=(STEPS,),
-        in_specs=[
-            SMEM,
-            SMEM,
-            whole(*wide),
-            whole(*turn),
-            whole(*wide),
-            whole(*wide),
-            whole(rows, 1),
-            whole(*wide),
-            whole(*square),
-            whole(4, D),
-            column(1),
-        ]
-        + [HBM] * (PIECES + len(down_pieces)),
-        out_specs=[
-            whole(*wide),
-            whole(*wide),
-            whole(rows, GROUP),
-            whole(rows, GROUP),
-            column(D // 2),
-            column(D // 2),
-            whole(D // 2, D),
-            whole(D // 2, D),
-            whole(8, D),
-            column(1),
-        ]
+        in_specs=[SMEM, SMEM, whole(*wide), whole(D, rows), whole(rows, 1)]
+        + [whole(*wide), whole(*wide), whole(4, D), column(1)]
+        + [HBM] * (len(up_pieces) + len(down_pieces)),
+        out_specs=[whole(*wide), whole(*wide), column(D // 2), column(D // 2), column(1)]
         + grad_specs,
         out_shape=[
             struct(wide, BF),
             struct(wide, F32),
-            struct((rows, GROUP), BF),
-            struct((rows, GROUP), BF),
             struct((D // 2, FF), BF),
             struct((D // 2, FF), BF),
-            struct((D // 2, D), BF),
-            struct((D // 2, D), BF),
-            struct((8, D), F32),
             struct((1, FF), F32),
         ]
         + grad_shapes,
         scratch_shapes=[
             pltpu.VMEM(wide, BF),
             pltpu.VMEM(wide, F32),
-            pltpu.VMEM(wide, F32),
             pltpu.VMEM((D, FF), BF),
             pltpu.VMEM((FF, D), BF),
-            pltpu.VMEM(square, BF),
             pltpu.VMEM(staged, BF),
             pltpu.SemaphoreType.DMA(staged[:2]),
-            pltpu.SemaphoreType.DMA((1 + STEPS, PIECES)),
+            pltpu.SemaphoreType.DMA((STEPS, PIECES)),
             pltpu.SemaphoreType.DMA((sum(map(len, owners)),)),
         ],
         cost_estimate=QUICK,
-        compiler_params=pltpu.CompilerParams(vmem_limit_bytes=48 * 1024 * 1024),
+        compiler_params=pltpu.CompilerParams(vmem_limit_bytes=KERNEL_VMEM),
         name="mlp",
     )(
         places,
-        (me if split_rows else me_down).reshape(1),
+        me_down,
         normed,
         turned,
-        residual,
-        mixed,
         live,
         out_grad,
-        order,
+        residual,
         vectors,
         b_up,
-        *in_hbm(up_pieces),
-        *in_hbm(down_pieces),
-    )
-    down = results[10:] if split_rows else pick(results[10], me, count)
-    return tuple(results[:10]) + (tuple(down),)
+        *up_pieces,
+        *down_pieces,
+    )
+    parts = results[5:] if split_rows else pick(results[5], me, count)
+    return tuple(results[:5]) + (tuple(parts),)
+
+
+def second_norm_back(grad_normed, residual, mixed, live, out_grad, order, vectors, pieces):
+    rows = residual.shape[0]
+    return pl.pallas_call(
+        second_norm_kernel,
+        in_specs=[VMEM] * 7 + [HBM] * PIECES,
+        out_specs=[VMEM] * 5,
+        out_shape=[
+            struct((rows, D), F32),
+            struct((rows, D), BF),
+            struct((D // 2, D), BF),
+            struct((D // 2, D), BF),
+            struct((8, D), F32),
+        ],
+        scratch_shapes=[pltpu.VMEM((D, D), BF), pltpu.SemaphoreType.DMA((PIECES,))],
+        cost_estimate=QUICK,
+        compiler_params=pltpu.CompilerParams(vmem_limit_bytes=KERNEL_VMEM),
+        name="second_norm_back",
+    )(grad_normed, residual, mixed, live, out_grad, order, vectors, *pieces)
+
+
+def marker_kernel(value_ref, out_ref):
+    out_ref[...] = value_ref[...]
+
+
+def marker(value):
+    return pl.pallas_call(
+        marker_kernel,
+        in_specs=[VMEM],
+        out_specs=VMEM,
+        out_shape=struct(value.shape, value.dtype),
+        cost_estimate=LONG,
+        name="marker",
+    )(value)
+
+
+def join_kernel(sizes, *refs):
+    ins, (*outs, sems) = refs[: sum(map(len, sizes))], refs[sum(map(len, sizes)) : -len(sizes)]
+    spaces = refs[-len(sizes) :]
+    inward, outward = [], []
+    ins = list(ins)
+    for out, space, parts in zip(outs, spaces, sizes):
+        at = 0
+        for size in parts:
+            number = len(inward)
+            to = pl.ds(at, size)
+            inward.append(pltpu.make_async_copy(ins.pop(0), space.at[to], sems.at[0, number]))
+            outward.append(pltpu.make_async_copy(space.at[to], out.at[to], sems.at[1, number]))
+            inward[-1].start()
+            at += size
+    for first, second in zip(inward, outward):
+        first.wait()
+        second.start()
+    wait_all(outward)
+
+
+def join(groups):
+    arrays = [array for group in groups for array in group]
+    sizes = tuple(tuple(array.shape[0] for array in group) for group in groups)
+    shapes = [(sum(parts),) + group[0].shape[1:] for parts, group in zip(sizes, groups)]
+    results = pl.pallas_call(
+        functools.partial(join_kernel, sizes),
+        in_specs=[HBM] * len(arrays),
+        out_specs=[HBM] * len(groups),
+        out_shape=[struct(shape, BF) for shape in shapes],
+        scratch_shapes=[pltpu.SemaphoreType.DMA((2, len(arrays)))]
+        + [pltpu.VMEM(shape, BF) for shape in shapes],
+        cost_estimate=QUICK,
+        compiler_params=pltpu.CompilerParams(vmem_limit_bytes=KERNEL_VMEM),
+        name="join",
+    )(*arrays)
+    return list(results)
+
+
+def weight_kernel(turned_ref, grad_ref, kept_ref, sent_ref):
+    half = D // 2
+    sent_ref[...] = dot_nn(turned_ref[half:, :], grad_ref[...]).astype(BF)
+    kept_ref[...] = dot_nn(turned_ref[:half, :], grad_ref[...]).astype(BF)
+
+
+def weight_grad(turned, grad):
+    rows, width = grad.shape
+    column = lambda height: pl.BlockSpec((height, D), lambda step: (0, step))
+    return pl.pallas_call(
+        weight_kernel,
+        grid=(width // D,),
+        in_specs=[whole(D, rows), column(rows)],
+        out_specs=[column(D // 2)] * 2,
+        out_shape=[struct((D // 2, width), BF)] * 2,
+        cost_estimate=QUICK,
+        compiler_params=pltpu.CompilerParams(vmem_limit_bytes=KERNEL_VMEM),
+        name="weight_grad",
+    )(turned, grad)
+
+
+def add_kernel(widths, outputs, *refs):
+    count = sum(map(len, widths)) * 2
+    ins, outs, (in_sem, out_sem, *spaces) = (
+        refs[:count],
+        refs[count : count + len(outputs)],
+        refs[count + len(outputs) :],
+    )
+    firsts = np.cumsum([0] + [len(parts) for parts in widths])
+    loads, stores = [], []
+    for number, ranges in enumerate(outputs):
+        here, below = [], 0
+        for group, lo, hi in ranges:
+            at = 0
+            for part, width in enumerate(widths[group]):
+                for side in range(2):
+                    source = ins[2 * (firsts[group] + part) + side].at[lo:hi]
+                    space = spaces[2 * number + side]
+                    to = space.at[below : below + hi - lo, at : at + width]
+                    sem = in_sem.at[number, len(here)]
+                    here.append(pltpu.make_async_copy(source, to, sem))
+                at += width
+            below += hi - lo
+        start_all(here)
+        loads.append(here)
+    for number in range(len(outputs)):
+        wait_all(loads[number])
+        left, right = spaces[2 * number], spaces[2 * number + 1]
+        left[...] = (left[...].astype(F32) + right[...].astype(F32)).astype(BF)
+        stores.append(pltpu.make_async_copy(left, outs[number], out_sem.at[number]))
+        stores[-1].start()
+    wait_all(stores)
+
+
+def add_ranges(groups, outputs):
+    rows = groups[0][0][0].shape[1]
+    flat = [side.reshape(-1, side.shape[-1]) for group in groups for pair in group for side in pair]
+    widths = tuple(tuple(pair[0].shape[-1] for pair in group) for group in groups)
+    plan = tuple(tuple((g, lo * rows, hi * rows) for g, lo, hi in ranges) for ranges in outputs)
+    shapes = [(sum(hi - lo for _, lo, hi in r), sum(widths[r[0][0]])) for r in plan]
+    most = max(sum(2 * len(widths[g]) for g, _, _ in ranges) for ranges in plan)
+    results = pl.pallas_call(
+        functools.partial(add_kernel, widths, plan),
+        in_specs=[HBM] * len(flat),
+        out_specs=[HBM] * len(plan),
+        out_shape=[struct(shape, BF) for shape in shapes],
+        scratch_shapes=[
+            pltpu.SemaphoreType.DMA((len(plan), most)),
+            pltpu.SemaphoreType.DMA((len(plan),)),
+        ]
+        + [pltpu.VMEM(shape, BF) for shape in shapes for _ in range(2)],
+        cost_estimate=QUICK,
+        compiler_params=pltpu.CompilerParams(vmem_limit_bytes=KERNEL_VMEM),
+        name="add_ranges",
+    )(*flat)
+    return [r.reshape(-1, rows, r.shape[-1]) for r in results]
 
 
 def first_norm_kernel(
-    grad_one_ref,
-    grad_two_ref,
+    grad_ref,
     tokens_ref,
     live_ref,
     gain_ref,
@@ -655,55 +777,38 @@
     grad_residual_ref,
     mlp_sums_ref,
     grad_b_ref,
-    tables_one_ref,
-    tables_two_ref,
+    tables_ref,
     *rest,
 ):
     pieces, (tokens_grad_ref, sums_ref, total, columns, weight, sem) = rest[:PIECES], rest[PIECES:]
     step = pl.program_id(0)
 
     def copies(index):
-        group, block = index // 3, lax.rem(index, 3)
-        return copy_rows(
-            pieces,
-            (pl.multiple_of(block * D + group * GROUP, 128), GROUP),
-            weight,
-            pl.multiple_of(index * GROUP, 128),
-            sem.at[index],
-        )
+        return copy_rows(pieces, (index * D, D), weight, index * D, sem.at[index])
 
     @pl.when(step == 0)
     def _():
-        for index in range(6):
-            start_all(copies(jnp.int32(index)))
+        for index in range(3):
+            start_all(copies(index))
         total[...] = jnp.zeros_like(total)
 
     wait_all(copies(step))
-    for group, grad_ref in ((0, grad_one_ref), (1, grad_two_ref)):
-
-        @pl.when(step // 3 == group)
-        def _():
-            grad = grad_ref[...]
-            at = pl.multiple_of(step * GROUP, 128)
-            total[...] += dot_nt(grad, weight[:, pl.ds(at, GROUP)])
-            columns[pl.ds(step, 1), :] = jnp.sum(grad.astype(F32), axis=0, keepdims=True)
-
-    @pl.when(step == 5)
+    grad_qkv = grad_ref[...]
+    at = pl.multiple_of(step * D, 128)
+    total[...] += dot_nt(grad_qkv, weight[:, pl.ds(at, D)])
+    columns[pl.ds(step, 1), :] = jnp.sum(grad_qkv.astype(F32), axis=0, keepdims=True)
+
+    @pl.when(step == 2)
     def _():
         unit, rstd = normalise(tokens_ref[...].astype(F32))
         grad = natural_order(total[...], order_ref[...]) * live_ref[...]
         tokens_grad_ref[...] = (
             grad_residual_ref[...] + normalise_back(grad, unit, rstd, gain_ref[...])
         ).astype(BF)
-        qkv = [
-            columns[group * 3 + block : group * 3 + block + 1, :]
-            for block in range(3)
-            for group in range(GROUPS)
-        ]
         vectors = [
             [jnp.sum(grad * unit, axis=0, keepdims=True)],
             [jnp.sum(grad, axis=0, keepdims=True)],
-            qkv,
+            [columns[block : block + 1, :] for block in range(3)],
             [mlp_sums_ref[0:1, :]],
             [mlp_sums_ref[1:2, :]],
             [mlp_sums_ref[2:3, :]],
@@ -717,7 +822,7 @@
                     sums_ref[at : at + 1, :] = piece[:, lane : lane + 128]
                     at += 1
         sums_ref[at:TABLE_ROW, :] = jnp.zeros((TABLE_ROW - at, 128), F32)
-        tables = (tables_one_ref[...] + tables_two_ref[...]) * (1.0 / SCALE)
+        tables = tables_ref[...] * (1.0 / SCALE)
         low = lax.broadcasted_iota(jnp.int32, (32, 128), 1) < 64
         sums_ref[TABLE_ROW:, :] = jnp.where(
             low,
@@ -730,16 +835,13 @@
 SUM_ROWS = TABLE_ROW + 32
 
 
-def first_norm_back(grads, pieces, tokens, live, gain, order, grad_residual, sums, b_up, tables):
+def first_norm_back(grad_qkv, pieces, tokens, live, gain, order, grad_residual, sums, b_up, tables):
     rows = tokens.shape[0]
-    first = lambda height: pl.BlockSpec((height, GROUP), lambda step: (0, jnp.minimum(step, 2)))
-    second = lambda height: pl.BlockSpec((height, GROUP), lambda step: (0, jnp.maximum(step, 3) - 3))
     return pl.pallas_call(
         first_norm_kernel,
-        grid=(6,),
+        grid=(3,),
         in_specs=[
-            first(rows),
-            second(rows),
+            pl.BlockSpec((rows, D), lambda step: (0, step)),
             whole(rows, D),
             whole(rows, 1),
             whole(1, D),
@@ -748,21 +850,20 @@
             whole(8, D),
             whole(1, FF),
             whole(128, 128),
-            whole(128, 128),
         ]
         + [HBM] * PIECES,
         out_specs=[whole(rows, D), whole(SUM_ROWS, 128)],
         out_shape=[struct((rows, D), BF), struct((SUM_ROWS, 128), F32)],
         scratch_shapes=[
             pltpu.VMEM((rows, D), F32),
-            pltpu.VMEM((8, GROUP), F32),
+            pltpu.VMEM((8, D), F32),
             pltpu.VMEM((D, 3 * D), BF),
-            pltpu.SemaphoreType.DMA((6, PIECES)),
+            pltpu.SemaphoreType.DMA((3, PIECES)),
         ],
-        cost_estimate=QUICK,
-        compiler_params=pltpu.CompilerParams(vmem_limit_bytes=32 * 1024 * 1024),
+        cost_estimate=LONG,
+        compiler_params=pltpu.CompilerParams(vmem_limit_bytes=KERNEL_VMEM),
         name="first_norm_back",
-    )(*grads, tokens, live, gain, order, grad_residual, sums, b_up, *tables, *in_hbm(pieces))
+    )(grad_qkv, tokens, live, gain, order, grad_residual, sums, b_up, tables, *pieces)
 
 
 def own_kernel(sizes, me_ref, sums_ref, *refs):
@@ -813,7 +914,7 @@
     return list(lax.optimization_barrier(tuple(values) + tuple(deps))[: len(values)])
 
 
-def gather_stages(shard, count, pieces):
+def gather_stages(shard, count, pieces, early=False):
     farthest, far, middle = hop_plan(count)
     deps = yield
     (shard,) = after([shard], deps)
@@ -825,23 +926,18 @@
     deps = yield [near]
     (got,) = after([got], deps)
     stacks = [near, got]
-    owners = [[0, farthest], [far, far ^ farthest]]
     for masks in zip(middle, middle[::-1]):
         got = [hop(stack, mask, count) for stack, mask in zip(stacks, masks)]
         deps = yield stacks
+        got = after(got, deps or stacks)
         if masks[0] != middle[-1]:
-            got = after(got, deps)
-            stacks = [jnp.concatenate(pair, axis=0) for pair in zip(stacks, got)]
-            owners = [own + [o ^ m for o in own] for own, m in zip(owners, masks)]
-    other = [hop(stack, 1, count) for stack in stacks]
-    deps = yield stacks
-    got = after(got, deps)
-    late = [hop(stack, 1, count) for stack in got]
-    for core, sides in ((0, (stacks, got)), (1, (other, late))):
-        for stack, arrived, own, mask in zip(*sides, owners, masks):
-            own = [o ^ core for o in own]
-            pieces += [(stack, own), (arrived, [o ^ mask for o in own])]
-    yield got
+            pairs = list(zip(stacks, got))
+            stacks = [jnp.concatenate(p, axis=0) for p in pairs] if early else join(pairs)
+    (own,) = join([(stacks[0], got[0], stacks[1], got[1])])
+    other = hop(own, 1, count)
+    order = sum_order(count)
+    pieces += [(own, order[: count // 2]), (other, order[count // 2 :])]
+    yield [own]
 
 
 def start(stages):
@@ -884,7 +980,7 @@
         out_shape=[jax.ShapeDtypeStruct((count, rows, width), BF) for width in widths],
         scratch_shapes=[pltpu.SemaphoreType.DMA((count * len(columns),))],
         cost_estimate=QUICK,
-        compiler_params=pltpu.CompilerParams(vmem_limit_bytes=16 * 1024 * 1024),
+        compiler_params=pltpu.CompilerParams(vmem_limit_bytes=KERNEL_VMEM),
         name="place",
     )(me.reshape(1), *stacks)
     return [out.reshape(count * rows, width) for out, width in zip(outs, widths)]
@@ -943,38 +1039,61 @@
     return (left.astype(F32) + right.astype(F32)).astype(BF)
 
 
-def scatter_stages(parts, count, result):
+def scatter_stages(parts, count, result, late=(), direct=False, inbox=None):
     farthest, far, middle = hop_plan(count)
     blocks = count // 2
     half = blocks // 2
-    shaped = [
-        [side.reshape(blocks, -1, side.shape[-1]) for side in part] for part in parts
-    ]
+    shape = lambda side: side.reshape(blocks, -1, side.shape[-1])
+    kept, sent = [shape(k) for k, _ in parts], [shape(s) for _, s in parts]
     deps = yield
-    sent = after([sent for _, sent in shaped], deps)
+    sent = after(sent, deps)
     arrived = [hop(side, 1, count) for side in sent]
     deps = yield sent
     arrived = after(arrived, deps)
-    pairs = [(kept, got) for (kept, _), got in zip(shaped, arrived)]
-
-    def added(pairs, lo, hi):
-        sums = [add_low(kept[lo:hi], got[lo:hi]) for kept, got in pairs]
-        return sums[0] if len(sums) == 1 else jnp.concatenate(sums, axis=-1)
-
-    sides = [(pairs, 0), (pairs, half)]
-    size = half
+    pairs = list(zip(kept, arrived)) + [(shape(k), shape(got)) for k, got in late]
+
+    def added(groups, outputs):
+        rows = groups[0][0][0].shape[1]
+        if all(lo * rows % 16 == 0 and hi * rows % 16 == 0 for o in outputs for _, lo, hi in o):
+            return add_ranges(groups, outputs)
+        return [
+            jnp.concatenate(
+                [
+                    jnp.concatenate([add_low(a[lo:hi], b[lo:hi]) for a, b in groups[g]], axis=-1)
+                    for g, lo, hi in ranges
+                ],
+                axis=0,
+            )
+            for ranges in outputs
+        ]
+
+    groups, size = [pairs], half
     for masks in zip(middle[::-1], middle):
         size //= 2
-        sends = [added(p, at + size, at + 2 * size) for p, at in sides]
+        at = [(0, 0), (0, half)] if len(groups) == 1 else [(0, 0), (1, 0)]
+        *sends, near, back = added(
+            groups,
+            [[(group, lo + size, lo + 2 * size)] for group, lo in at]
+            + [[(group, lo, lo + size)] for group, lo in at],
+        )
         got = [hop(send, mask, count) for send, mask in zip(sends, masks)]
-        kept = [added(p, at, at + size) for p, at in sides]
+        if inbox is not None:
+            inbox[:] = got
         deps = yield sends
         got = after(got, deps)
-        sides = [([pair], 0) for pair in zip(kept, got)]
-    (near, _), (back, _) = sides
-    send = added(back, 0, 2)
+        groups = [[(near, got[0])], [(back, got[1])]]
+    if direct:
+        near, back = (a.astype(F32) + b.astype(F32) for ((a, b),) in groups)
+        sends = [block.astype(BF) for block in (near[1], back[0], back[1])]
+        got = [hop(s, m, count) for s, m in zip(sends, (farthest, far, far ^ farthest))]
+        deps = yield sends
+        got = after(got, deps)
+        total = near[0] + got[0].astype(F32) + got[1].astype(F32) + got[2].astype(F32)
+        result.append(total)
+        yield [total]
+        return
+    send, kept = added(groups, [[(1, 0, 2)], [(0, 0, 2)]])
     got = hop(send, far, count)
-    kept = added(near, 0, 2)
     deps = yield [send]
     (got,) = after([got], deps)
     send = add_low(kept[1], got[1])
@@ -987,15 +1106,14 @@
 
 
 def sum_stages(array, count, result):
-    mask = 1
+    bits = count.bit_length() - 1
     deps = yield
-    while mask < count:
+    for mask in [1 << bit for bit in [0, bits - 2, bits - 1] + list(range(1, bits - 2))]:
         (array,) = after([array], deps)
         got = hop(array, mask, count)
         deps = yield [array]
         (got,) = after([got], deps)
         array = array + got
-        mask *= 2
     result.append(array)
     yield [array]
 
@@ -1037,30 +1155,36 @@
 
     packed = lax.optimization_barrier(jnp.concatenate(vectors))
     packed = jnp.pad(packed, (0, shard_rows * 128 - used)).reshape(shard_rows, 128)
+    middle = len(hop_plan(count)[2])
     first_pieces, second_pieces, third_pieces = [], [], []
     first = start(
-        gather_stages(jnp.concatenate((qkv_weight, packed), axis=1).astype(BF), count, first_pieces)
-    )
-    second = start(
         gather_stages(
-            jnp.concatenate((proj_weight, lin1_weight), axis=1).astype(BF), count, second_pieces
+            jnp.concatenate((qkv_weight, proj_weight, packed), axis=1).astype(BF), count, first_pieces, early=True
         )
     )
+    second = start(gather_stages(lin1_weight.astype(BF), count, second_pieces))
     third = start(gather_stages(lin2_weight.astype(BF), count, third_pieces))
-    middle = len(hop_plan(count)[2])
+    onehot, shift = window_constants()
+    onehot = jnp.asarray(onehot, BF)
+    shift = jnp.asarray(shift)
+    order = order_matrix(me, count, shard_rows)
+    table = table_lanes(rel_pos_h, rel_pos_w)
+    live = slot_mask(window_pos)
+    inverse = np.argsort(np.array(sum_order(count)))
+    places = jnp.take(jnp.asarray(inverse, jnp.int32), jnp.bitwise_xor(me, np.arange(count)))
     first.send(None)
     sent = first.send(None)
+    first.send(None)
     second.send(sent)
-    for _ in range(middle):
-        sent = first.send(sent)
-        sent = second.send(sent)
-    sent = first.send(sent)
-    sent = sent + third.send(sent)
-    sent = first.send(sent)
-    sent = sent + third.send(sent)
+    third.send(sent)
+    for _ in range(middle - 1):
+        sent = first.send(None)
+    sent = second.send(sent) + third.send(sent)
+    sent = second.send(sent) + third.send(sent)
+    first.send(sent + [order, table, live, places])
 
     (small,) = place(
-        [(stack[:, :, 3 * D :], own) for stack, own in first_pieces], ((0, 0, 128, 0),), (128,), me, count
+        first_pieces, ((0, 4 * D, 4 * D + 128, 0),), (128,), me, count
     )
     small = small.reshape(count, shard_rows * 128)[:, :used].astype(F32)
     edges = np.cumsum([0] + sizes)
@@ -1069,88 +1193,67 @@
     )
     flat = lambda pieces: [stack.reshape(-1, stack.shape[-1]) for stack, _ in pieces]
     first_pieces = flat(first_pieces)
-    order = order_matrix(me, count, shard_rows)
-    onehot, shift = window_constants()
-    onehot = jnp.asarray(onehot, BF)
-    shift = jnp.asarray(shift)
-    table = table_lanes(rel_pos_h, rel_pos_w)
-    live = slot_mask(window_pos)
-
-    ordered_one, *qkv = front(
-        tokens, live, order, jnp.stack((gain_one, bias_one)), b_qkv.reshape(1, -1), first_pieces
-    )
-    sent = second.send(sent + [ordered_one])
-    sent = sent + third.send(sent)
-    (qkv[0],) = after([qkv[0]], sent)
-    attended = [attention(qkv[0], table, onehot, shift)]
-    sent = second.send([attended[0][0]])
-    sent = sent + third.send(sent)
-    (qkv[1],) = after([qkv[1]], sent)
-    attended.append(attention(qkv[1], table, onehot, shift))
-    sent = third.send([attended[1][0]])
-    finish(second)
-    second_pieces = flat(second_pieces)
-    mixed = [m for m, _ in attended]
-    (mixed[0],) = after([mixed[0]], sent)
+    (gated_tokens,) = after([tokens], sent)
+    turned_one, qkv = front(
+        gated_tokens, live, order, jnp.stack((gain_one, bias_one)), b_qkv.reshape(1, -1), first_pieces
+    )
+    sent = [turned_one]
+    for _ in range(middle - 1):
+        sent = second.send(sent) + third.send(sent)
+    (qkv,) = after([qkv], sent)
+    mixed, probs = attention(qkv, table, onehot, shift)
+    sent = third.send([mixed])
+    b_up = b_up.reshape(1, FF)
+    (mixed,) = after([mixed], sent + [b_up])
     vectors = jnp.stack((b_proj, gain_two, bias_two, b_down))
     residual, normed_two, turned_two, ordered_mixed = project(
-        tokens, mixed, order, vectors, second_pieces
-    )
-    third.send([residual])
-    finish(third)
-
-    own_down, own_up, own_first, own_second, all_small = [], [], [], [], []
-    (
-        output,
-        grad_residual,
-        grad_one,
-        grad_two,
-        kept_up,
-        sent_up,
-        kept_proj,
-        sent_proj,
-        mlp_sums,
-        grad_b_up,
-        down_parts,
-    ) = mlp(
+        tokens, mixed, order, vectors, first_pieces
+    )
+    second.send([residual])
+
+    own_down, own_up, own_third, all_small = [], [], [], []
+    down_weight = placed_down(third_pieces, me, count)
+    output, grad_normed, kept_up, sent_up, grad_b_up, down_parts = mlp(
         me,
         count,
+        places,
         normed_two,
         turned_two,
-        residual,
-        ordered_mixed,
         live,
         out_grad,
-        order,
+        residual,
         vectors,
-        b_up.reshape(1, FF),
-        second_pieces,
-        third_pieces,
-    )
-    down = start(scatter_stages([down_parts], count, own_down))
-    up = start(scatter_stages([(kept_up, sent_up)], count, own_up))
-    sent = down.send(None)
-    sent = sent + up.send(sent)
-    (grad_one,) = after([grad_one], sent)
-    back = [attention_back(qkv[0], grad_one, attended[0][1], table, onehot, shift)]
-    sent = down.send([back[0][0]])
-
-    def qkv_part(grad_qkv):
-        sent = dot_tn(ordered_one[:, D // 2 :], grad_qkv).astype(BF)
-        return dot_tn(ordered_one[:, : D // 2], grad_qkv).astype(BF), sent
-
-    first_sum = start(
-        scatter_stages([qkv_part(back[0][0]), (kept_proj, sent_proj)], count, own_first)
-    )
-    sent = sent + first_sum.send(sent)
-    (grad_two,) = after([grad_two], sent)
-    back.append(attention_back(qkv[1], grad_two, attended[1][1], table, onehot, shift))
-    sent = up.send([back[1][0]])
-    second_sum = start(scatter_stages([qkv_part(back[1][0])], count, own_second))
-    sent = sent + second_sum.send(sent)
-    (grad_qkv,) = after([back[1][0]], sent)
+        b_up,
+        flat(second_pieces),
+        down_weight,
+    )
+    late, got_up, got_down = [], [], []
+    up = start(scatter_stages([(kept_up, sent_up)], count, own_up, late, inbox=got_up))
+    down = start(scatter_stages([down_parts], count, own_down, inbox=got_down))
+    sent = up.send(None)
+    sent = down.send(sent)
+    (grad_normed,) = after([grad_normed], sent)
+    grad_residual, grad_mixed, kept_proj, sent_proj, mlp_sums = second_norm_back(
+        grad_normed, residual, ordered_mixed, live, out_grad, order, vectors, first_pieces
+    )
+    late.append((kept_proj, hop(sent_proj, 1, count)))
+    sent = up.send([grad_mixed])
+    sent = down.send(sent)
+    (grad_mixed,) = after([grad_mixed], sent)
+    grad_qkv, tables = attention_back(qkv, grad_mixed, probs, table, onehot, shift)
+    sent = [grad_qkv]
+    for _ in range(middle - 1):
+        sent = up.send(sent)
+    (grad_qkv,) = after([grad_qkv], sent)
+    kept_qkv, sent_qkv = weight_grad(turned_one, grad_qkv)
+    third_sum = start(scatter_stages([(kept_qkv, sent_qkv)], count, own_third, direct=True))
+    sent = third_sum.send(None)
+    for _ in range(middle - 1):
+        sent = down.send([kept_qkv] + sent)
+    sent = up.send(sent)
+    (grad_qkv,) = after([grad_qkv], sent)
     tokens_grad, small_sums = first_norm_back(
-        (back[0][0], grad_qkv),
+        grad_qkv,
         first_pieces,
         tokens,
         live,
@@ -1159,38 +1262,27 @@
         grad_residual,
         mlp_sums,
         grad_b_up,
-        (back[0][1], back[1][1]),
-    )
-    sent = down.send([small_sums])
+        tables,
+    )
     small_stages = start(sum_stages(small_sums, count, all_small))
+    sent = third_sum.send([small_sums] + got_down)
     sent = small_stages.send(sent)
-    sent = first_sum.send(sent)
+    sent = down.send(sent)
+    sent = up.send(sent)
+    (gated_tables,) = after([tables], sent)
+    sent = [marker(gated_tables)]
+    sent = small_stages.send(sent)
+    for _ in range(middle - 1):
+        sent = third_sum.send(sent)
+    sent = small_stages.send(sent)
     sent = down.send(sent)
     sent = small_stages.send(sent)
+    sent = third_sum.send(sent)
     sent = up.send(sent)
-    sent = down.send(sent)
-    sent = second_sum.send(sent)
     sent = small_stages.send(sent)
-    sent = up.send(sent)
-    sent = first_sum.send(sent)
-    sent = small_stages.send(sent)
-    sent = up.send(sent)
-    sent = second_sum.send(sent)
-    sent = first_sum.send(sent)
-    sent = small_stages.send(sent)
-    sent = second_sum.send(sent)
-    sent = first_sum.send(sent)
-    sent = second_sum.send(sent)
-    for stages in (down, up, first_sum, second_sum, small_stages):
+    for stages in (down, up, third_sum, small_stages):
         finish(stages)
-    own_qkv = jnp.stack(
-        [
-            own.reshape(shard_rows, 3, GROUP)
-            for own in (own_first[0][:, : 3 * GROUP], own_second[0])
-        ],
-        axis=2,
-    ).reshape(shard_rows, 3 * D)
-    own_proj = own_first[0][:, 3 * GROUP :]
+    own_qkv, own_proj = own_third[0], own_up[0][:, FF:]
     *owned, table_h, table_w = own_small(all_small[0], me, sizes)
     owned = [vector.reshape(-1) for vector in owned]
 
@@ -1207,7 +1299,7 @@
         owned[3],
         owned[4],
         owned[5],
-        own_up[0],
+        own_up[0][:, :FF],
         owned[6],
         own_down[0],
         owned[7],

time: 262 us -> 255 us (0.973)
  Pallas kernels: 64 us -> 120 us
  waiting for transfers between devices: 84.5 us -> 40.5 us
  local copies, waits for them, and re-layouts: 28.3 us -> 19.2 us
  starting transfers between devices: 65.7 us -> 58 us
  matrix products: 2.82 us -> 0 us
    pallas_call x2 -> x17, Pallas kernels: 11.4 us -> 61.3 us  [the longest x8 22.6 us: add_ranges(): pl.pallas_call(functools.partial(add_kernel, widths, plan), in_specs=[HBM...]
    ppermute x64 -> x49, waiting for transfers between devices: 84.5 us -> 40.5 us  [hop(): return lax.ppermute(array, 'fsdp', [(i, i ^ mask) for i in range(count)])]
    ppermute x64 -> x49, starting transfers between devices: 65.7 us -> 58 us  [hop(): return lax.ppermute(array, 'fsdp', [(i, i ^ mask) for i in range(count)])]
    unnamed x104 -> x70, local copies, waits for them, and re-layouts: 17.9 us -> 13.1 us
    convert_element_type x25 -> x2, other arithmetic: 3.35 us -> 0.09 us  [add_low(): return (left.astype(F32) + right.astype(F32)).astype(BF)]
    dot_general x4 -> x0, matrix products: 2.82 us -> none  [dot_tn(): lax.dot_general(a, b, (((0,), (0,)), ((), ())), preferred_element_type=F32)]
    pallas_call x2 -> x1, Pallas kernels: 10.7 us -> 13 us  [attention_back(): pl.pallas_call(attn_bwd_kernel, grid=(PAIRS,), in_specs=columns + [pl.Blo...]
    pallas_call x2 -> x1, Pallas kernels: 8.54 us -> 9.9 us  [attention(): pl.pallas_call(attn_fwd_kernel, grid=(PAIRS,), in_specs=columns + constan...]
  transfers between devices with their start and end apart: 64 -> 49, of which waited for: 20 -> 13; matrix products, arithmetic and copies ran while one was open for 10% -> 7% of each run, Pallas kernels for 14% -> 36%
where the time goes in v4:
time: 255 us; the launch traced here: 254 us
  Pallas kernels  120 us (47%)
  starting transfers between devices  58 us (23%)
  waiting for transfers between devices  40.5 us (16%)
  local copies, waits for them, and re-layouts  19.2 us (8%)
  other arithmetic  14.4 us (6%)
    ppermute x49, starting transfers between devices, hop(): return lax.ppermute(array, 'fsdp', [(i, i ^ mask) for i in range(count)])  58 us
    ppermute x49, waiting for transfers between devices, hop(): return lax.ppermute(array, 'fsdp', [(i, i ^ mask) for i in range(count)])  40.5 us
    pallas_call x1, Pallas kernels, mlp(): pl.pallas_call(functools.partial(mlp_kernel, split_rows, owners), grid=(S...  26.1 us
    pallas_call x8, Pallas kernels, add_ranges(): pl.pallas_call(functools.partial(add_kernel, widths, plan), in_specs=[HBM...  22.6 us
    unnamed x70, local copies, waits for them, and re-layouts  13.1 us
    pallas_call x1, Pallas kernels, attention_back(): pl.pallas_call(attn_bwd_kernel, grid=(PAIRS,), in_specs=columns + [pl.Blo...  13 us
    pallas_call x5, Pallas kernels, join(): pl.pallas_call(functools.partial(join_kernel, sizes), in_specs=[HBM] * le...  11.9 us
    pallas_call x1, Pallas kernels, attention(): pl.pallas_call(attn_fwd_kernel, grid=(PAIRS,), in_specs=columns + constan...  9.9 us
  transfers between devices with their start and end apart: 49, of which 13 were waited for; matrix products, arithmetic and copies ran while one was open for 7% of the time, Pallas kernels for 36%

profile of v4, /device:TPU:0, one launch (start us, length us, event | category | flops | bytes accessed | tf_op | source)
XLA Modules:
  0.0 253.7 jit_solution(14803043714942443668)
XLA Ops:
  3.5 4.1 %collective-permute-start = (bf16[24,3200]{1,0:T(8,128)(2,1)S(1)}, bf16[24,3200]{1,0:T(8,128)(2,1)S(1)}, u32[]{:S(2)}, u32[]{:S(2)}) collective-permute-start(bf16[24,3200]{1,0:T(8,128)(2,1)S(1)} %pad_maximum_fusion.4), channel_id=1, source_target_pairs={{0,16},{1,17},{2,18},{3,19},{4,20},{5,21},{6,22},{7,23},{8,24},{9,... | collective-permute-start | bytes 460808 | tf_op jit(solution)/shard_map/ppermute | solution.py:903
  17.2 3.4 %collective-permute-start.1 = (bf16[24,3072]{1,0:T(8,128)(2,1)S(1)}, bf16[24,3072]{1,0:T(8,128)(2,1)S(1)}, u32[]{:S(2)}, u32[]{:S(2)}) collective-permute-start(bf16[24,3072]{1,0:T(8,128)(2,1)S(1)} %convert_element_type.118), channel_id=1, source_target_pairs={{0,16},{1,17},{2,18},{3,19},{4,20},{5,21},{6,22},{7,23},{8,24},{9,... | collective-permute-start | bytes 442376 | tf_op jit(solution)/shard_map/ppermute | solution.py:903
  20.7 7.8 %collective-permute-done.3 = bf16[2,24,3200]{2,1,0:T(8,128)(2,1)S(1)} collective-permute-done((bf16[2,24,3200]{2,1,0:T(8,128)(2,1)S(1)}, bf16[2,24,3200]{2,1,0:T(8,128)(2,1)S(1)}, u32[]{:S(2)}, u32[]{:S(2)}) %collective-permute-start.3) | collective-permute-done | bytes 307232 | tf_op jit(solution)/shard_map/ppermute | solution.py:903
  29.8 6.2 %collective-permute-done.4 = bf16[2,24,3200]{2,1,0:T(8,128)(2,1)S(1)} collective-permute-done((bf16[2,24,3200]{2,1,0:T(8,128)(2,1)S(1)}, bf16[2,24,3200]{2,1,0:T(8,128)(2,1)S(1)}, u32[]{:S(2)}, u32[]{:S(2)}) %collective-permute-start.4) | collective-permute-done | bytes 307232 | tf_op jit(solution)/shard_map/ppermute | solution.py:903
  36.1 2.0 collective-permute-start.9
  38.1 1.5 collective-permute-start.8
  39.8 2.1 collective-permute-start.7
  44.1 4.3 %collective-permute-done.5.refs_2_ = bf16[2,24,3072]{2,1,0:T(8,128)(2,1)S(1)} collective-permute-done((bf16[2,24,3072]{2,1,0:T(8,128)(2,1)S(1)}, bf16[2,24,3072]{2,1,0:T(8,128)(2,1)S(1)}, u32[]{:S(2)}, u32[]{:S(2)}) %collective-permute-start.5) | collective-permute-done | bytes 294944 | tf_op jit(solution)/shard_map/ppermute | solution.py:903
  48.4 3.3 %collective-permute-done.7.refs_2_ = bf16[2,96,768]{2,1,0:T(8,128)(2,1)} collective-permute-done((bf16[2,96,768]{2,1,0:T(8,128)(2,1)S(1)}, bf16[2,96,768]{2,1,0:T(8,128)(2,1)}, u32[]{:S(2)}, u32[]{:S(2)}) %collective-permute-start.7) | collective-permute-done | bytes 294944 | tf_op jit(solution)/shard_map/ppermute | solution.py:903
  53.3 2.7 %join.5.refs_0_ = bf16[16,24,3200]{2,1,0:T(8,128)(2,1)} custom-call(bf16[4,24,3200]{2,1,0:T(8,128)(2,1)} %copy-done.2, bf16[4,24,3200]{2,1,0:T(8,128)(2,1)} %copy-done.12, bf16[4,24,3200]{2,1,0:T(8,128)(2,1)} %copy-done.6, bf16[4,24,3200]{2,1,0:T(8,128)(2,1)} %copy-done.11), custom_call_target="tpu_custom_call" | custom-call | flops 1 | bytes 1 | tf_op jit(solution)/shard_map/join/pallas_call | solution.py:679
  57.2 1.7 collective-permute-start.13
  62.4 1.9 place.1
  66.9 6.5 %front.1 = (bf16[768,392]{1,0:T(8,128)(2,1)}, bf16[392,2304]{1,0:T(8,128)(2,1)}) custom-call(bf16[392,768]{1,0:T(8,128)(2,1)} %tokens_ref.4, f32[392,1]{1,0:T(8,128)} %copy.39.live_ref.rest_2_, bf16[768,768]{1,0:T(8,128)(2,1)} %fusion.order_ref, f32[2,768]{1,0:T(2,128)} %pad_maximum_fusion.6.rows_ref, f32[1,2304]{1,0:T(1,128)} %reshape_reshape.11.b_qkv_ref, ...), custom_call_target="tpu_custom_call" | custom-call | flops 1 | bytes 1 | tf_op jit(solution)/shard_map/front/pallas_call | solution.py:355
  74.2 2.1 join.7
  77.3 2.0 join.6
  79.3 1.5 collective-permute-start.17
  80.8 1.7 collective-permute-start.18
  82.5 9.9 %attention.1 = (bf16[392,768]{1,0:T(8,128)(2,1)}, f32[6,4,200,256]{3,2,1,0:T(8,128)}) custom-call(bf16[392,2304]{1,0:T(8,128)(2,1)} %get-tuple-element.159.q_ref.k_ref.v_ref, bf16[392,2304]{1,0:T(8,128)(2,1)} %get-tuple-element.159.q_ref.k_ref.v_ref, bf16[392,2304]{1,0:T(8,128)(2,1)} %get-tuple-element.159.q_ref.k_ref.v_ref, ...), custom_call_target="tpu_custom_call" | custom-call | flops 1 | bytes 1 | tf_op jit(solution)/shard_map/attention/pallas_call | solution.py:238
  95.1 2.5 join.8
  97.7 6.0 %project.1 = (f32[392,768]{1,0:T(8,128)}, bf16[392,768]{1,0:T(8,128)(2,1)}, bf16[768,392]{1,0:T(8,128)(2,1)}, bf16[392,768]{1,0:T(8,128)(2,1)}) custom-call(bf16[392,768]{1,0:T(8,128)(2,1)} %tokens_ref.4, bf16[392,768]{1,0:T(8,128)(2,1)} %get-tuple-element.163.values_ref, bf16[768,768]{1,0:T(8,128)(2,1)} %fusion.order_ref, ...), custom_call_target="tpu_custom_call" | custom-call | flops 1 | bytes 1 | tf_op jit(solution)/shard_map/project/pallas_call | solution.py:533
  104.9 2.6 %join.9 = bf16[16,24,3072]{2,1,0:T(8,128)(2,1)} custom-call(bf16[4,24,3072]{2,1,0:T(8,128)(2,1)} %get-tuple-element.153.refs_0_, bf16[4,24,3072]{2,1,0:T(8,128)(2,1)} %copy-done.14, bf16[4,24,3072]{2,1,0:T(8,128)(2,1)} %get-tuple-element.154.refs_2_, bf16[4,24,3072]{2,1,0:T(8,128)(2,1)} %copy-done.16), custom_call_target="tpu_custom_call" | custom-call | flops 1 | bytes 1 | tf_op jit(solution)/shard_map/join/pallas_call | solution.py:679
  108.0 4.5 %collective-permute-done.19 = bf16[16,24,3072]{2,1,0:T(8,128)(2,1)} collective-permute-done((bf16[16,24,3072]{2,1,0:T(8,128)(2,1)}, bf16[16,24,3072]{2,1,0:T(8,128)(2,1)}, u32[]{:S(2)}, u32[]{:S(2)}) %collective-permute-start.19) | collective-permute-done | bytes 2359328 | tf_op jit(solution)/shard_map/ppermute | solution.py:903
  112.5 26.1 %mlp.1 = (bf16[392,768]{1,0:T(8,128)(2,1)}, f32[392,768]{1,0:T(8,128)}, bf16[384,3072]{1,0:T(8,128)(2,1)}, bf16[384,3072]{1,0:T(8,128)(2,1)}, f32[1,3072]{1,0:T(...) custom-call(s32[32]{0:T(128)} %and_select_fusion.2.place_ref, s32[1]{0:T(128)} %bitcast.me_ref, ...), custom_call_target="tpu_custom_call" | custom-call | flops 1 | bytes 1 | tf_op jit(solution)/shard_map/mlp/pallas_call | solution.py:574
  139.2 7.3 %second_norm_back.1 = (f32[392,768]{1,0:T(8,128)}, bf16[392,768]{1,0:T(8,128)(2,1)}, bf16[384,768]{1,0:T(8,128)(2,1)}, bf16[384,768]{1,0:T(8,128)(2,1)}, f32[8,768]{1,0:T(8,128)}) custom-call(f32[392,768]{1,0:T(8,128)} %get-tuple-element.174.grad_normed_ref, f32[392,768]{1,0:T(8,128)} %get-tuple-element.166.rest_4_.residual_ref, ...), custom_call_target="tpu_custom_call" | custom-call | flops 1 | bytes 1 | tf_op jit(solution)/shard_map/second_norm_back/pallas_call | solution.py:622
  146.9 1.9 collective-permute-done.23.refs_3_
  149.6 4.4 %add_ranges.8 = (bf16[96,3840]{1,0:T(8,128)(2,1)}, bf16[96,3840]{1,0:T(8,128)(2,1)}, bf16[96,3840]{1,0:T(8,128)(2,1)}, bf16[96,3840]{1,0:T(8,128)(2,1)}) custom-call(bf16[384,3072]{1,0:T(8,128)(2,1)} %get-tuple-element.178.refs_0_, bf16[384,3072]{1,0:T(8,128)(2,1)} %bitcast.18.refs_1_, bf16[384,768]{1,0:T(8,128)(2,1)} %get-tuple-element.180.refs_2_, ...), custom_call_target="tpu_custom_call" | custom-call | flops 1 | bytes 1 | tf_op jit(solution)/shard_map/add_ranges/pallas_call | solution.py:754
  157.2 3.5 %add_ranges.9 = (bf16[384,768]{1,0:T(8,128)(2,1)}, bf16[384,768]{1,0:T(8,128)(2,1)}, bf16[384,768]{1,0:T(8,128)(2,1)}, bf16[384,768]{1,0:T(8,128)(2,1)}) custom-call(bf16[1536,768]{1,0:T(8,128)(2,1)} %bitcast.102, bf16[1536,768]{1,0:T(8,128)(2,1)} %bitcast.103), custom_call_target="tpu_custom_call" | custom-call | flops 1 | bytes 1 | tf_op jit(solution)/shard_map/add_ranges/pallas_call | solution.py:754
  160.7 1.7 collective-permute-start.29
  163.0 13.0 %attention_back.1 = (bf16[392,2304]{1,0:T(8,128)(2,1)}, f32[128,128]{1,0:T(8,128)}) custom-call(bf16[392,2304]{1,0:T(8,128)(2,1)} %get-tuple-element.159.q_ref.k_ref.v_ref, bf16[392,2304]{1,0:T(8,128)(2,1)} %get-tuple-element.159.q_ref.k_ref.v_ref, bf16[392,2304]{1,0:T(8,128)(2,1)} %get-tuple-element.159.q_ref.k_ref.v_ref, ...), custom_call_target="tpu_custom_call" | custom-call | flops 1 | bytes 1 | tf_op jit(solution)/shard_map/attention_back/pallas_call | solution.py:256
  177.1 2.7 %add_ranges.10 = (bf16[48,3840]{1,0:T(8,128)(2,1)}, bf16[48,3840]{1,0:T(8,128)(2,1)}, bf16[48,3840]{1,0:T(8,128)(2,1)}, bf16[48,3840]{1,0:T(8,128)(2,1)}) custom-call(bf16[96,3840]{1,0:T(8,128)(2,1)} %get-tuple-element.190.refs_0_, bf16[96,3840]{1,0:T(8,128)(2,1)} %bitcast.108, bf16[96,3840]{1,0:T(8,128)(2,1)} %get-tuple-element.192.refs_2_, ...), custom_call_target="tpu_custom_call" | custom-call | flops 1 | bytes 1 | tf_op jit(solution)/shard_map/add_ranges/pallas_call | solution.py:754
  181.7 5.0 %weight_grad.1 = (bf16[384,2304]{1,0:T(8,128)(2,1)}, bf16[384,2304]{1,0:T(8,128)(2,1)}) custom-call(bf16[768,392]{1,0:T(8,128)(2,1)} %get-tuple-element.150.turned_ref, bf16[392,2304]{1,0:T(8,128)(2,1)} %get-tuple-element.210.grad_ref), custom_call_target="tpu_custom_call" | custom-call | flops 1 | bytes 1 | tf_op jit(solution)/shard_map/weight_grad/pallas_call | solution.py:702
  187.5 2.5 add_ranges.11
  194.6 2.2 add_ranges.12
  197.1 8.4 %first_norm_back.1 = (bf16[392,768]{1,0:T(8,128)(2,1)}, f32[112,128]{1,0:T(8,128)}) custom-call(bf16[392,2304]{1,0:T(8,128)(2,1)} %get-tuple-element.210.grad_ref, bf16[392,768]{1,0:T(8,128)(2,1)} %tokens_ref.4, f32[392,1]{1,0:T(8,128)} %copy.39.live_ref.rest_2_, f32[1,768]{1,0:T(1,128)} %copy-done.31, bf16[768,768]{1,0:T(8,128)(2,1)} %fusion.order_ref, ...), custom_call_target="tpu_custom_call" | custom-call | flops 99999997952 | bytes 1 | tf_op jit(solution)/shard_map/first_norm_back/pallas_call | solution.py:840
  206.9 3.0 %add_ranges.13 = (bf16[96,2304]{1,0:T(8,128)(2,1)}, bf16[96,2304]{1,0:T(8,128)(2,1)}, bf16[96,2304]{1,0:T(8,128)(2,1)}, bf16[96,2304]{1,0:T(8,128)(2,1)}) custom-call(bf16[384,2304]{1,0:T(8,128)(2,1)} %get-tuple-element.199.refs_0_, bf16[384,2304]{1,0:T(8,128)(2,1)} %bitcast.105), custom_call_target="tpu_custom_call" | custom-call | flops 1 | bytes 1 | tf_op jit(solution)/shard_map/add_ranges/pallas_call | solution.py:754
  209.9 1.7 collective-permute-start.37
  211.6 2.0 collective-permute-start.36
  213.6 2.1 add_ranges.14
  215.7 1.7 collective-permute-start.39
  217.9 5.3 %collective-permute-start.41 = (bf16[24,3840]{1,0:T(8,128)(2,1)S(1)}, bf16[24,3840]{1,0:T(8,128)(2,1)S(1)}, u32[]{:S(2)}, u32[]{:S(2)}) collective-permute-start(bf16[24,3840]{1,0:T(8,128)(2,1)S(1)} %fusion.3), channel_id=1, source_target_pairs={{0,16},{1,17},{2,18},{3,19},{4,20},{5,21},{6,22},{7,23},{8,24},{9,... | collective-permute-start | bytes 552968 | tf_op jit(solution)/shard_map/ppermute | solution.py:903
  224.1 2.4 add_ranges.15
  227.2 3.3 %collective-permute-done.35 = f32[112,128]{1,0:T(8,128)S(1)} collective-permute-done((f32[112,128]{1,0:T(8,128)S(1)}, f32[112,128]{1,0:T(8,128)S(1)}, u32[]{:S(2)}, u32[]{:S(2)}) %collective-permute-start.35) | collective-permute-done | bytes 57376 | tf_op jit(solution)/shard_map/ppermute | solution.py:903
  230.5 3.1 %collective-permute-start.38 = (f32[112,128]{1,0:T(8,128)S(1)}, f32[112,128]{1,0:T(8,128)S(1)}, u32[]{:S(2)}, u32[]{:S(2)}) collective-permute-start(f32[112,128]{1,0:T(8,128)S(1)} %add.82), channel_id=1, source_target_pairs={{0,16},{1,17},{2,18},{3,19},{4,20},{5,21},{6,22},{7,23},{8,24},{9,... | collective-permute-start | bytes 172040 | tf_op jit(solution)/shard_map/ppermute | solution.py:903
  233.8 4.0 %collective-permute-done.38 = f32[112,128]{1,0:T(8,128)S(1)} collective-permute-done((f32[112,128]{1,0:T(8,128)S(1)}, f32[112,128]{1,0:T(8,128)S(1)}, u32[]{:S(2)}, u32[]{:S(2)}) %collective-permute-start.38) | collective-permute-done | bytes 57376 | tf_op jit(solution)/shard_map/ppermute | solution.py:903
  239.4 1.9 collective-permute-start.45
  241.2 4.7 %collective-permute-start.47 = (bf16[24,2304]{1,0:T(8,128)(2,1)S(1)}, bf16[24,2304]{1,0:T(8,128)(2,1)S(1)}, u32[]{:S(2)}, u32[]{:S(2)}) collective-permute-start(bf16[24,2304]{1,0:T(8,128)(2,1)S(1)} %get-tuple-element.260), channel_id=1, source_target_pairs={{0,24},{1,25},{2,26},{3,27},{4,28},{5,29},{6,30},{7,31},{8,16},{9,... | collective-permute-start | bytes 331784 | tf_op jit(solution)/shard_map/ppermute | solution.py:903
  248.9 1.8 collective-permute-done.44
  251.4 1.5 own_small.1
  (202 shorter events, 55.1 us)
Async XLA Ops:
  3.5 11.4 %collective-permute-start = (bf16[24,3200]{1,0:T(8,128)(2,1)S(1)}, bf16[24,3200]{1,0:T(8,128)(2,1)S(1)}, u32[]{:S(2)}, u32[]{:S(2)}) collective-permute-start(bf16[24,3200]{1,0:T(8,128)(2,1)S(1)} %pad_maximum_fusion.4), channel_id=1, source_target_pairs={{0,16},{1,17},{2,18},{3,19},{4,20},{5,21},{6,22},{7,23},{8,24},{9,... | collective-permute-start | bytes 460808 | tf_op jit(solution)/shard_map/ppermute | solution.py:903
  14.9 13.6 %collective-permute-start.3 = (bf16[2,24,3200]{2,1,0:T(8,128)(2,1)S(1)}, bf16[2,24,3200]{2,1,0:T(8,128)(2,1)S(1)}, u32[]{:S(2)}, u32[]{:S(2)}) collective-permute-start(bf16[2,24,3200]{2,1,0:T(8,128)(2,1)S(1)} %pad_maximum_fusion.1), channel_id=1, source_target_pairs={{0,8},{1,9},{2,10},{3,11},{4,12},{5,13},{6,14},{7,15},{8,0},{9,1},... | collective-permute-start | bytes 921608 | tf_op jit(solution)/shard_map/ppermute | solution.py:903
  15.8 14.0 %collective-permute-start.2 = (bf16[2,24,3200]{2,1,0:T(8,128)(2,1)S(1)}, bf16[2,24,3200]{2,1,0:T(8,128)(2,1)S(1)}, u32[]{:S(2)}, u32[]{:S(2)}) collective-permute-start(bf16[2,24,3200]{2,1,0:T(8,128)(2,1)S(1)} %pad_maximum_fusion.1), channel_id=1, source_target_pairs={{0,2},{1,3},{2,0},{3,1},{4,6},{5,7},{6,4},{7,5},{8,10},{9,11},{10,... | collective-permute-start | bytes 921608 | tf_op jit(solution)/shard_map/ppermute | solution.py:903
  17.2 22.3 %collective-permute-start.1 = (bf16[24,3072]{1,0:T(8,128)(2,1)S(1)}, bf16[24,3072]{1,0:T(8,128)(2,1)S(1)}, u32[]{:S(2)}, u32[]{:S(2)}) collective-permute-start(bf16[24,3072]{1,0:T(8,128)(2,1)S(1)} %convert_element_type.118), channel_id=1, source_target_pairs={{0,16},{1,17},{2,18},{3,19},{4,20},{5,21},{6,22},{7,23},{8,24},{9,... | collective-permute-start | bytes 442376 | tf_op jit(solution)/shard_map/ppermute | solution.py:903
  20.6 19.0 %collective-permute-start.6 = (bf16[96,768]{1,0:T(8,128)(2,1)S(1)}, bf16[96,768]{1,0:T(8,128)(2,1)S(1)}, u32[]{:S(2)}, u32[]{:S(2)}) collective-permute-start(bf16[96,768]{1,0:T(8,128)(2,1)S(1)} %convert_element_type.119), channel_id=1, source_target_pairs={{0,16},{1,17},{2,18},{3,19},{4,20},{5,21},{6,22},{7,23},{8,24},{9,... | collective-permute-start | bytes 442376 | tf_op jit(solution)/shard_map/ppermute | solution.py:903
  28.4 7.5 %collective-permute-start.4 = (bf16[2,24,3200]{2,1,0:T(8,128)(2,1)S(1)}, bf16[2,24,3200]{2,1,0:T(8,128)(2,1)S(1)}, u32[]{:S(2)}, u32[]{:S(2)}) collective-permute-start(bf16[2,24,3200]{2,1,0:T(8,128)(2,1)S(1)} %collective-permute-done.3), channel_id=1, source_target_pairs={{0,4},{1,5},{2,6},{3,7},{4,0},{5,1},{6,2},{7,3},{8,12},{9,13},{10,... | collective-permute-start | bytes 921608 | tf_op jit(solution)/shard_map/ppermute | solution.py:903
  36.1 15.5 %collective-permute-start.9 = (bf16[4,24,3200]{2,1,0:T(8,128)(2,1)S(1)}, bf16[4,24,3200]{2,1,0:T(8,128)(2,1)S(1)}, u32[]{:S(2)}, u32[]{:S(2)}) collective-permute-start(bf16[4,24,3200]{2,1,0:T(8,128)(2,1)S(1)} %constant_dynamic-update-slice_fusion.refs_2_), channel_id=1, source_target_pairs={{0,2},{1,3},{2,0},{3,1},{4,6},{5,7},{6,4},{7,5},{8,10},{9,11},{10,... | collective-permute-start | bytes 1843208 | tf_op jit(solution)/shard_map/ppermute | solution.py:903
  38.1 13.6 %collective-permute-start.8 = (bf16[4,24,3200]{2,1,0:T(8,128)(2,1)S(1)}, bf16[4,24,3200]{2,1,0:T(8,128)(2,1)S(1)}, u32[]{:S(2)}, u32[]{:S(2)}) collective-permute-start(bf16[4,24,3200]{2,1,0:T(8,128)(2,1)S(1)} %pad_maximum_fusion.refs_0_), channel_id=1, source_target_pairs={{0,4},{1,5},{2,6},{3,7},{4,0},{5,1},{6,2},{7,3},{8,12},{9,13},{10,... | collective-permute-start | bytes 1843208 | tf_op jit(solution)/shard_map/ppermute | solution.py:903
  39.6 8.7 %collective-permute-start.5 = (bf16[2,24,3072]{2,1,0:T(8,128)(2,1)S(1)}, bf16[2,24,3072]{2,1,0:T(8,128)(2,1)S(1)}, u32[]{:S(2)}, u32[]{:S(2)}) collective-permute-start(bf16[2,24,3072]{2,1,0:T(8,128)(2,1)S(1)} %pad_maximum_fusion.2.refs_0_), channel_id=1, source_target_pairs={{0,8},{1,9},{2,10},{3,11},{4,12},{5,13},{6,14},{7,15},{8,0},{9,1},... | collective-permute-start | bytes 884744 | tf_op jit(solution)/shard_map/ppermute | solution.py:903
  39.8 11.9 %collective-permute-start.7 = (bf16[2,96,768]{2,1,0:T(8,128)(2,1)S(1)}, bf16[2,96,768]{2,1,0:T(8,128)(2,1)}, u32[]{:S(2)}, u32[]{:S(2)}) collective-permute-start(bf16[2,96,768]{2,1,0:T(8,128)(2,1)S(1)} %pad_maximum_fusion.3.refs_0_), channel_id=1, source_target_pairs={{0,8},{1,9},{2,10},{3,11},{4,12},{5,13},{6,14},{7,15},{8,0},{9,1},... | collective-permute-start | bytes 884744 | tf_op jit(solution)/shard_map/ppermute | solution.py:903
  55.9 5.0 %collective-permute-start.10 = (bf16[16,24,3200]{2,1,0:T(8,128)(2,1)}, bf16[16,24,3200]{2,1,0:T(8,128)(2,1)S(1)}, u32[]{:S(2)}, u32[]{:S(2)}) collective-permute-start(bf16[16,24,3200]{2,1,0:T(8,128)(2,1)} %join.5.refs_0_), channel_id=1, source_target_pairs={{0,1},{1,0},{2,3},{3,2},{4,5},{5,4},{6,7},{7,6},{8,9},{9,8},{10,11... | collective-permute-start | bytes 7372808 | tf_op jit(solution)/shard_map/ppermute | solution.py:903
  56.9 20.4 %collective-permute-start.11 = (bf16[2,24,3072]{2,1,0:T(8,128)(2,1)S(1)}, bf16[2,24,3072]{2,1,0:T(8,128)(2,1)}, u32[]{:S(2)}, u32[]{:S(2)}) collective-permute-start(bf16[2,24,3072]{2,1,0:T(8,128)(2,1)S(1)} %pad_maximum_fusion.2.refs_0_), channel_id=1, source_target_pairs={{0,2},{1,3},{2,0},{3,1},{4,6},{5,7},{6,4},{7,5},{8,10},{9,11},{10,... | collective-permute-start | bytes 884744 | tf_op jit(solution)/shard_map/ppermute | solution.py:903
  57.2 16.2 %collective-permute-start.13 = (bf16[2,96,768]{2,1,0:T(8,128)(2,1)S(1)}, bf16[2,96,768]{2,1,0:T(8,128)(2,1)}, u32[]{:S(2)}, u32[]{:S(2)}) collective-permute-start(bf16[2,96,768]{2,1,0:T(8,128)(2,1)S(1)} %pad_maximum_fusion.3.refs_0_), channel_id=1, source_target_pairs={{0,2},{1,3},{2,0},{3,1},{4,6},{5,7},{6,4},{7,5},{8,10},{9,11},{10,... | collective-permute-start | bytes 884744 | tf_op jit(solution)/shard_map/ppermute | solution.py:903
  58.9 18.4 %collective-permute-start.12 = (bf16[2,24,3072]{2,1,0:T(8,128)(2,1)S(1)}, bf16[2,24,3072]{2,1,0:T(8,128)(2,1)}, u32[]{:S(2)}, u32[]{:S(2)}) collective-permute-start(bf16[2,24,3072]{2,1,0:T(8,128)(2,1)S(1)} %collective-permute-done.5.refs_2_), channel_id=1, source_target_pairs={{0,4},{1,5},{2,6},{3,7},{4,0},{5,1},{6,2},{7,3},{8,12},{9,13},{10,... | collective-permute-start | bytes 884744 | tf_op jit(solution)/shard_map/ppermute | solution.py:903
  59.4 14.8 %collective-permute-start.14 = (bf16[2,96,768]{2,1,0:T(8,128)(2,1)}, bf16[2,96,768]{2,1,0:T(8,128)(2,1)}, u32[]{:S(2)}, u32[]{:S(2)}) collective-permute-start(bf16[2,96,768]{2,1,0:T(8,128)(2,1)} %collective-permute-done.7.refs_2_), channel_id=1, source_target_pairs={{0,4},{1,5},{2,6},{3,7},{4,0},{5,1},{6,2},{7,3},{8,12},{9,13},{10,... | collective-permute-start | bytes 884744 | tf_op jit(solution)/shard_map/ppermute | solution.py:903
  76.3 17.9 %collective-permute-start.15 = (bf16[4,96,768]{2,1,0:T(8,128)(2,1)}, bf16[4,96,768]{2,1,0:T(8,128)(2,1)S(1)}, u32[]{:S(2)}, u32[]{:S(2)}) collective-permute-start(bf16[4,96,768]{2,1,0:T(8,128)(2,1)} %get-tuple-element.157.refs_0_), channel_id=1, source_target_pairs={{0,4},{1,5},{2,6},{3,7},{4,0},{5,1},{6,2},{7,3},{8,12},{9,13},{10,... | collective-permute-start | bytes 1769480 | tf_op jit(solution)/shard_map/ppermute | solution.py:903
  76.8 17.3 %collective-permute-start.16 = (bf16[4,96,768]{2,1,0:T(8,128)(2,1)}, bf16[4,96,768]{2,1,0:T(8,128)(2,1)S(1)}, u32[]{:S(2)}, u32[]{:S(2)}) collective-permute-start(bf16[4,96,768]{2,1,0:T(8,128)(2,1)} %get-tuple-element.158.refs_2_), channel_id=1, source_target_pairs={{0,2},{1,3},{2,0},{3,1},{4,6},{5,7},{6,4},{7,5},{8,10},{9,11},{10,... | collective-permute-start | bytes 1769480 | tf_op jit(solution)/shard_map/ppermute | solution.py:903
  79.3 24.5 %collective-permute-start.17 = (bf16[4,24,3072]{2,1,0:T(8,128)(2,1)}, bf16[4,24,3072]{2,1,0:T(8,128)(2,1)S(1)}, u32[]{:S(2)}, u32[]{:S(2)}) collective-permute-start(bf16[4,24,3072]{2,1,0:T(8,128)(2,1)} %get-tuple-element.153.refs_0_), channel_id=1, source_target_pairs={{0,4},{1,5},{2,6},{3,7},{4,0},{5,1},{6,2},{7,3},{8,12},{9,13},{10,... | collective-permute-start | bytes 1769480 | tf_op jit(solution)/shard_map/ppermute | solution.py:903
  80.8 23.2 %collective-permute-start.18 = (bf16[4,24,3072]{2,1,0:T(8,128)(2,1)}, bf16[4,24,3072]{2,1,0:T(8,128)(2,1)S(1)}, u32[]{:S(2)}, u32[]{:S(2)}) collective-permute-start(bf16[4,24,3072]{2,1,0:T(8,128)(2,1)} %get-tuple-element.154.refs_2_), channel_id=1, source_target_pairs={{0,2},{1,3},{2,0},{3,1},{4,6},{5,7},{6,4},{7,5},{8,10},{9,11},{10,... | collective-permute-start | bytes 1769480 | tf_op jit(solution)/shard_map/ppermute | solution.py:903
  97.7 10.3 %collective-permute-start.20 = (bf16[16,96,768]{2,1,0:T(8,128)(2,1)}, bf16[16,96,768]{2,1,0:T(8,128)(2,1)S(1)}, u32[]{:S(2)}, u32[]{:S(2)}) collective-permute-start(bf16[16,96,768]{2,1,0:T(8,128)(2,1)} %join.8), channel_id=1, source_target_pairs={{0,1},{1,0},{2,3},{3,2},{4,5},{5,4},{6,7},{7,6},{8,9},{9,8},{10,11... | collective-permute-start | bytes 7077896 | tf_op jit(solution)/shard_map/ppermute | solution.py:903
  107.5 5.0 %collective-permute-start.19 = (bf16[16,24,3072]{2,1,0:T(8,128)(2,1)}, bf16[16,24,3072]{2,1,0:T(8,128)(2,1)}, u32[]{:S(2)}, u32[]{:S(2)}) collective-permute-start(bf16[16,24,3072]{2,1,0:T(8,128)(2,1)} %join.9), channel_id=1, source_target_pairs={{0,1},{1,0},{2,3},{3,2},{4,5},{5,4},{6,7},{7,6},{8,9},{9,8},{10,11... | collective-permute-start | bytes 7077896 | tf_op jit(solution)/shard_map/ppermute | solution.py:903
  138.6 8.3 %collective-permute-start.22 = (bf16[16,24,3072]{2,1,0:T(8,128)(2,1)}, bf16[16,24,3072]{2,1,0:T(8,128)(2,1)}, u32[]{:S(2)}, u32[]{:S(2)}) collective-permute-start(bf16[16,24,3072]{2,1,0:T(8,128)(2,1)} %bitcast.125), channel_id=1, source_target_pairs={{0,1},{1,0},{2,3},{3,2},{4,5},{5,4},{6,7},{7,6},{8,9},{9,8},{10,11... | collective-permute-start | bytes 7077896 | tf_op jit(solution)/shard_map/ppermute | solution.py:903
  139.0 16.8 %collective-permute-start.21 = (bf16[16,96,768]{2,1,0:T(8,128)(2,1)}, bf16[16,96,768]{2,1,0:T(8,128)(2,1)S(1)}, u32[]{:S(2)}, u32[]{:S(2)}) collective-permute-start(bf16[16,96,768]{2,1,0:T(8,128)(2,1)} %get-tuple-element.173), channel_id=1, source_target_pairs={{0,1},{1,0},{2,3},{3,2},{4,5},{5,4},{6,7},{7,6},{8,9},{9,8},{10,11... | collective-permute-start | bytes 7077896 | tf_op jit(solution)/shard_map/ppermute | solution.py:903
  154.0 22.0 %collective-permute-start.25 = (bf16[4,24,3840]{2,1,0:T(8,128)(2,1)}, bf16[4,24,3840]{2,1,0:T(8,128)(2,1)S(1)}, u32[]{:S(2)}, u32[]{:S(2)}) collective-permute-start(bf16[4,24,3840]{2,1,0:T(8,128)(2,1)} %bitcast.128), channel_id=1, source_target_pairs={{0,2},{1,3},{2,0},{3,1},{4,6},{5,7},{6,4},{7,5},{8,10},{9,11},{10,... | collective-permute-start | bytes 2211848 | tf_op jit(solution)/shard_map/ppermute | solution.py:903
  154.4 21.6 %collective-permute-start.24 = (bf16[4,24,3840]{2,1,0:T(8,128)(2,1)}, bf16[4,24,3840]{2,1,0:T(8,128)(2,1)S(1)}, u32[]{:S(2)}, u32[]{:S(2)}) collective-permute-start(bf16[4,24,3840]{2,1,0:T(8,128)(2,1)} %bitcast.127), channel_id=1, source_target_pairs={{0,4},{1,5},{2,6},{3,7},{4,0},{5,1},{6,2},{7,3},{8,12},{9,13},{10,... | collective-permute-start | bytes 2211848 | tf_op jit(solution)/shard_map/ppermute | solution.py:903
  160.7 26.0 %collective-permute-start.29 = (bf16[4,96,768]{2,1,0:T(8,128)(2,1)}, bf16[4,96,768]{2,1,0:T(8,128)(2,1)S(1)}, u32[]{:S(2)}, u32[]{:S(2)}) collective-permute-start(bf16[4,96,768]{2,1,0:T(8,128)(2,1)} %bitcast.130), channel_id=1, source_target_pairs={{0,2},{1,3},{2,0},{3,1},{4,6},{5,7},{6,4},{7,5},{8,10},{9,11},{10,... | collective-permute-start | bytes 1769480 | tf_op jit(solution)/shard_map/ppermute | solution.py:903
  162.4 24.3 %collective-permute-start.28 = (bf16[4,96,768]{2,1,0:T(8,128)(2,1)}, bf16[4,96,768]{2,1,0:T(8,128)(2,1)}, u32[]{:S(2)}, u32[]{:S(2)}) collective-permute-start(bf16[4,96,768]{2,1,0:T(8,128)(2,1)} %bitcast.129), channel_id=1, source_target_pairs={{0,4},{1,5},{2,6},{3,7},{4,0},{5,1},{6,2},{7,3},{8,12},{9,13},{10,... | collective-permute-start | bytes 1769480 | tf_op jit(solution)/shard_map/ppermute | solution.py:903
  179.8 13.9 %collective-permute-start.27 = (bf16[2,24,3840]{2,1,0:T(8,128)(2,1)}, bf16[2,24,3840]{2,1,0:T(8,128)(2,1)S(1)}, u32[]{:S(2)}, u32[]{:S(2)}) collective-permute-start(bf16[2,24,3840]{2,1,0:T(8,128)(2,1)} %bitcast.135), channel_id=1, source_target_pairs={{0,4},{1,5},{2,6},{3,7},{4,0},{5,1},{6,2},{7,3},{8,12},{9,13},{10,... | collective-permute-start | bytes 1105928 | tf_op jit(solution)/shard_map/ppermute | solution.py:903
  181.3 12.4 %collective-permute-start.26 = (bf16[2,24,3840]{2,1,0:T(8,128)(2,1)}, bf16[2,24,3840]{2,1,0:T(8,128)(2,1)S(1)}, u32[]{:S(2)}, u32[]{:S(2)}) collective-permute-start(bf16[2,24,3840]{2,1,0:T(8,128)(2,1)} %bitcast.134), channel_id=1, source_target_pairs={{0,2},{1,3},{2,0},{3,1},{4,6},{5,7},{6,4},{7,5},{8,10},{9,11},{10,... | collective-permute-start | bytes 1105928 | tf_op jit(solution)/shard_map/ppermute | solution.py:903
  186.7 18.9 %collective-permute-start.30 = (bf16[16,24,2304]{2,1,0:T(8,128)(2,1)}, bf16[16,24,2304]{2,1,0:T(8,128)(2,1)S(1)}, u32[]{:S(2)}, u32[]{:S(2)}) collective-permute-start(bf16[16,24,2304]{2,1,0:T(8,128)(2,1)} %bitcast.126), channel_id=1, source_target_pairs={{0,1},{1,0},{2,3},{3,2},{4,5},{5,4},{6,7},{7,6},{8,9},{9,8},{10,11... | collective-permute-start | bytes 5308424 | tf_op jit(solution)/shard_map/ppermute | solution.py:903
  190.0 15.5 %collective-permute-start.32 = (bf16[2,96,768]{2,1,0:T(8,128)(2,1)}, bf16[2,96,768]{2,1,0:T(8,128)(2,1)S(1)}, u32[]{:S(2)}, u32[]{:S(2)}) collective-permute-start(bf16[2,96,768]{2,1,0:T(8,128)(2,1)} %bitcast.138), channel_id=1, source_target_pairs={{0,4},{1,5},{2,6},{3,7},{4,0},{5,1},{6,2},{7,3},{8,12},{9,13},{10,... | collective-permute-start | bytes 884744 | tf_op jit(solution)/shard_map/ppermute | solution.py:903
  191.0 14.6 %collective-permute-start.31 = (bf16[2,96,768]{2,1,0:T(8,128)(2,1)}, bf16[2,96,768]{2,1,0:T(8,128)(2,1)S(1)}, u32[]{:S(2)}, u32[]{:S(2)}) collective-permute-start(bf16[2,96,768]{2,1,0:T(8,128)(2,1)} %bitcast.137), channel_id=1, source_target_pairs={{0,2},{1,3},{2,0},{3,1},{4,6},{5,7},{6,4},{7,5},{8,10},{9,11},{10,... | collective-permute-start | bytes 884744 | tf_op jit(solution)/shard_map/ppermute | solution.py:903
  196.8 20.6 %collective-permute-start.34 = (bf16[2,24,3840]{2,1,0:T(8,128)(2,1)}, bf16[2,24,3840]{2,1,0:T(8,128)(2,1)S(1)}, u32[]{:S(2)}, u32[]{:S(2)}) collective-permute-start(bf16[2,24,3840]{2,1,0:T(8,128)(2,1)} %bitcast.133), channel_id=1, source_target_pairs={{0,8},{1,9},{2,10},{3,11},{4,12},{5,13},{6,14},{7,15},{8,0},{9,1},... | collective-permute-start | bytes 1105928 | tf_op jit(solution)/shard_map/ppermute | solution.py:903
  209.9 13.3 %collective-permute-start.37 = (bf16[4,24,2304]{2,1,0:T(8,128)(2,1)}, bf16[4,24,2304]{2,1,0:T(8,128)(2,1)S(1)}, u32[]{:S(2)}, u32[]{:S(2)}) collective-permute-start(bf16[4,24,2304]{2,1,0:T(8,128)(2,1)} %bitcast.132), channel_id=1, source_target_pairs={{0,2},{1,3},{2,0},{3,1},{4,6},{5,7},{6,4},{7,5},{8,10},{9,11},{10,... | collective-permute-start | bytes 1327112 | tf_op jit(solution)/shard_map/ppermute | solution.py:903
  211.6 11.6 %collective-permute-start.36 = (bf16[4,24,2304]{2,1,0:T(8,128)(2,1)}, bf16[4,24,2304]{2,1,0:T(8,128)(2,1)S(1)}, u32[]{:S(2)}, u32[]{:S(2)}) collective-permute-start(bf16[4,24,2304]{2,1,0:T(8,128)(2,1)} %bitcast.131), channel_id=1, source_target_pairs={{0,4},{1,5},{2,6},{3,7},{4,0},{5,1},{6,2},{7,3},{8,12},{9,13},{10,... | collective-permute-start | bytes 1327112 | tf_op jit(solution)/shard_map/ppermute | solution.py:903
  213.5 3.9 %collective-permute-start.33 = (f32[112,128]{1,0:T(8,128)S(1)}, f32[112,128]{1,0:T(8,128)S(1)}, u32[]{:S(2)}, u32[]{:S(2)}) collective-permute-start(f32[112,128]{1,0:T(8,128)S(1)} %copy-done.30), channel_id=1, source_target_pairs={{0,1},{1,0},{2,3},{3,2},{4,5},{5,4},{6,7},{7,6},{8,9},{9,8},{10,11... | collective-permute-start | bytes 172040 | tf_op jit(solution)/shard_map/ppermute | solution.py:903
  215.7 18.0 %collective-permute-start.39 = (bf16[2,96,768]{2,1,0:T(8,128)(2,1)}, bf16[2,96,768]{2,1,0:T(8,128)(2,1)S(1)}, u32[]{:S(2)}, u32[]{:S(2)}) collective-permute-start(bf16[2,96,768]{2,1,0:T(8,128)(2,1)} %bitcast.136), channel_id=1, source_target_pairs={{0,8},{1,9},{2,10},{3,11},{4,12},{5,13},{6,14},{7,15},{8,0},{9,1},... | collective-permute-start | bytes 884744 | tf_op jit(solution)/shard_map/ppermute | solution.py:903
  217.5 13.0 %collective-permute-start.35 = (f32[112,128]{1,0:T(8,128)S(1)}, f32[112,128]{1,0:T(8,128)S(1)}, u32[]{:S(2)}, u32[]{:S(2)}) collective-permute-start(f32[112,128]{1,0:T(8,128)S(1)} %add.81), channel_id=1, source_target_pairs={{0,8},{1,9},{2,10},{3,11},{4,12},{5,13},{6,14},{7,15},{8,0},{9,1},... | collective-permute-start | bytes 172040 | tf_op jit(solution)/shard_map/ppermute | solution.py:903
  217.9 28.0 %collective-permute-start.41 = (bf16[24,3840]{1,0:T(8,128)(2,1)S(1)}, bf16[24,3840]{1,0:T(8,128)(2,1)S(1)}, u32[]{:S(2)}, u32[]{:S(2)}) collective-permute-start(bf16[24,3840]{1,0:T(8,128)(2,1)S(1)} %fusion.3), channel_id=1, source_target_pairs={{0,16},{1,17},{2,18},{3,19},{4,20},{5,21},{6,22},{7,23},{8,24},{9,... | collective-permute-start | bytes 552968 | tf_op jit(solution)/shard_map/ppermute | solution.py:903
  226.5 11.7 %collective-permute-start.43 = (bf16[2,24,2304]{2,1,0:T(8,128)(2,1)}, bf16[2,24,2304]{2,1,0:T(8,128)(2,1)S(1)}, u32[]{:S(2)}, u32[]{:S(2)}) collective-permute-start(bf16[2,24,2304]{2,1,0:T(8,128)(2,1)} %bitcast.140), channel_id=1, source_target_pairs={{0,4},{1,5},{2,6},{3,7},{4,0},{5,1},{6,2},{7,3},{8,12},{9,13},{10,... | collective-permute-start | bytes 663560 | tf_op jit(solution)/shard_map/ppermute | solution.py:903
  226.8 11.4 %collective-permute-start.42 = (bf16[2,24,2304]{2,1,0:T(8,128)(2,1)}, bf16[2,24,2304]{2,1,0:T(8,128)(2,1)S(1)}, u32[]{:S(2)}, u32[]{:S(2)}) collective-permute-start(bf16[2,24,2304]{2,1,0:T(8,128)(2,1)} %bitcast.139), channel_id=1, source_target_pairs={{0,2},{1,3},{2,0},{3,1},{4,6},{5,7},{6,4},{7,5},{8,10},{9,11},{10,... | collective-permute-start | bytes 663560 | tf_op jit(solution)/shard_map/ppermute | solution.py:903
  230.5 7.3 %collective-permute-start.38 = (f32[112,128]{1,0:T(8,128)S(1)}, f32[112,128]{1,0:T(8,128)S(1)}, u32[]{:S(2)}, u32[]{:S(2)}) collective-permute-start(f32[112,128]{1,0:T(8,128)S(1)} %add.82), channel_id=1, source_target_pairs={{0,16},{1,17},{2,18},{3,19},{4,20},{5,21},{6,22},{7,23},{8,24},{9,... | collective-permute-start | bytes 172040 | tf_op jit(solution)/shard_map/ppermute | solution.py:903
  233.7 13.1 %collective-permute-start.48 = (bf16[96,768]{1,0:T(8,128)(2,1)S(1)}, bf16[96,768]{1,0:T(8,128)(2,1)S(1)}, u32[]{:S(2)}, u32[]{:S(2)}) collective-permute-start(bf16[96,768]{1,0:T(8,128)(2,1)S(1)} %fusion.5), channel_id=1, source_target_pairs={{0,16},{1,17},{2,18},{3,19},{4,20},{5,21},{6,22},{7,23},{8,24},{9,... | collective-permute-start | bytes 442376 | tf_op jit(solution)/shard_map/ppermute | solution.py:903
  237.8 8.6 %collective-permute-start.40 = (f32[112,128]{1,0:T(8,128)S(1)}, f32[112,128]{1,0:T(8,128)S(1)}, u32[]{:S(2)}, u32[]{:S(2)}) collective-permute-start(f32[112,128]{1,0:T(8,128)S(1)} %add.84), channel_id=1, source_target_pairs={{0,2},{1,3},{2,0},{3,1},{4,6},{5,7},{6,4},{7,5},{8,10},{9,11},{10,... | collective-permute-start | bytes 172040 | tf_op jit(solution)/shard_map/ppermute | solution.py:903
  239.4 13.5 %collective-permute-start.45 = (bf16[24,2304]{1,0:T(8,128)(2,1)S(1)}, bf16[24,2304]{1,0:T(8,128)(2,1)S(1)}, u32[]{:S(2)}, u32[]{:S(2)}) collective-permute-start(bf16[24,2304]{1,0:T(8,128)(2,1)S(1)} %fusion.9), channel_id=1, source_target_pairs={{0,16},{1,17},{2,18},{3,19},{4,20},{5,21},{6,22},{7,23},{8,24},{9,... | collective-permute-start | bytes 331784 | tf_op jit(solution)/shard_map/ppermute | solution.py:903
  241.2 11.7 %collective-permute-start.47 = (bf16[24,2304]{1,0:T(8,128)(2,1)S(1)}, bf16[24,2304]{1,0:T(8,128)(2,1)S(1)}, u32[]{:S(2)}, u32[]{:S(2)}) collective-permute-start(bf16[24,2304]{1,0:T(8,128)(2,1)S(1)} %get-tuple-element.260), channel_id=1, source_target_pairs={{0,24},{1,25},{2,26},{3,27},{4,28},{5,29},{6,30},{7,31},{8,16},{9,... | collective-permute-start | bytes 331784 | tf_op jit(solution)/shard_map/ppermute | solution.py:903
  245.9 7.0 %collective-permute-start.46 = (bf16[24,2304]{1,0:T(8,128)(2,1)S(1)}, bf16[24,2304]{1,0:T(8,128)(2,1)S(1)}, u32[]{:S(2)}, u32[]{:S(2)}) collective-permute-start(bf16[24,2304]{1,0:T(8,128)(2,1)S(1)} %get-tuple-element.261), channel_id=1, source_target_pairs={{0,8},{1,9},{2,10},{3,11},{4,12},{5,13},{6,14},{7,15},{8,0},{9,1},... | collective-permute-start | bytes 331784 | tf_op jit(solution)/shard_map/ppermute | solution.py:903
  246.5 4.2 %collective-permute-start.44 = (f32[112,128]{1,0:T(8,128)S(1)}, f32[112,128]{1,0:T(8,128)S(1)}, u32[]{:S(2)}, u32[]{:S(2)}) collective-permute-start(f32[112,128]{1,0:T(8,128)S(1)} %add.89), channel_id=1, source_target_pairs={{0,4},{1,5},{2,6},{3,7},{4,0},{5,1},{6,2},{7,3},{8,12},{9,13},{10,... | collective-permute-start | bytes 172040 | tf_op jit(solution)/shard_map/ppermute | solution.py:903
  (35 other events, 228.2 us)

commit v5 on v4

--- a/solution.py
+++ b/solution.py
@@ -333,7 +333,7 @@
     for block in copies:
         start_all(block)
     unit, _ = normalise(tokens_ref[...].astype(F32))
-    normed = ((unit * rows_ref[0:1, :] + rows_ref[1:2, :]) * live_ref[...]).astype(BF)
+    normed = ((unit * rows_ref[0:1, :] + rows_ref[1:2, :]) * live_ref[:, :1]).astype(BF)
     turned = dot_nn(normed, order_ref[...])
     normed = turned.astype(BF)
     turned_ref[...] = turned.T.astype(BF)
@@ -405,7 +405,7 @@
         kept_down_ref, sent_down_ref, *rest = rest
     else:
         grad_down_ref, *rest = rest
-    branch, total, w_up, w_down, staged, sem, up_sem, down_sem = rest
+    branch, actives, grads, w_up, w_down, staged, sem, up_sem, down_sem = rest
     step = pl.program_id(0)
     half = D // 2
 
@@ -418,14 +418,11 @@
         start_all(down_copies(down_pieces, owners, me_ref, w_down, down_sem))
         for index in range(1, STEPS):
             start_all(up_copies(index))
-        branch[...] = (out_grad_ref[...].astype(F32) * live_ref[...]).astype(BF)
-        grad_normed_ref[...] = jnp.zeros_like(grad_normed_ref)
-        total[...] = residual_ref[...] + rows_ref[3:4, :]
+        branch[...] = (out_grad_ref[...].astype(F32) * live_ref[:, :1]).astype(BF)
 
     wait_all(up_copies(step))
     at = pl.multiple_of(step * TILE, TILE)
-    weight_up = w_up[:, pl.ds(at, TILE)]
-    hidden = dot_nn(normed_ref[...], weight_up) + b_up_ref[...]
+    hidden = dot_nn(normed_ref[...], w_up[:, pl.ds(at, TILE)]) + b_up_ref[...]
     cdf = normal_cdf(hidden)
     active = (hidden * cdf).astype(BF)
     slope = cdf + hidden * normal_pdf(hidden)
@@ -435,21 +432,22 @@
     def _():
         wait_all(down_copies(down_pieces, owners, me_ref, w_down, down_sem))
 
-    weight_down = w_down[pl.ds(at, TILE), :]
-    grad_active = dot_nt(branch[...], weight_down)
-    total[...] += dot_nn(active, weight_down)
+    grad_active = dot_nt(branch[...], w_down[pl.ds(at, TILE), :])
     grad_hidden = (grad_active * slope).astype(BF)
     sent_ref[...] = dot_nn(turned_ref[half:, :], grad_hidden).astype(BF)
     kept_ref[...] = dot_nn(turned_ref[:half, :], grad_hidden).astype(BF)
-    grad_normed_ref[...] += dot_nt(grad_hidden, weight_up)
+    actives[:, pl.ds(at, TILE)] = active
+    grads[:, pl.ds(at, TILE)] = grad_hidden
     grad_b_ref[...] = jnp.sum(grad_hidden.astype(F32), axis=0, keepdims=True)
 
-    @pl.when(step == STEPS - 1)
-    def _():
-        output_ref[...] = (total[...] * live_ref[...]).astype(BF)
+    def finish_sums():
+        grad_normed_ref[...] = dot_nt(grads[...], w_up[...])
+        total = residual_ref[...] + rows_ref[3:4, :] + dot_nn(actives[...], w_down[...])
+        output_ref[...] = (total * live_ref[:, :1]).astype(BF)
 
     if not split_rows:
         grad_down_ref[...] = grad_down
+        pl.when(step == STEPS - 1)(finish_sums)
         return
 
     slot = lax.rem(step, 2)
@@ -478,6 +476,7 @@
 
     @pl.when(step == STEPS - 1)
     def _():
+        finish_sums()
         for last_slot in range(2):
             for block in range(blocks):
                 copy(last_slot, block, kept_down_ref, 0).wait()
@@ -494,7 +493,7 @@
     start_all(copies)
     grad = natural_order(grad_normed_ref[...], order_ref[...])
     unit, rstd = normalise(residual_ref[...])
-    grad_out = out_grad_ref[...].astype(F32) * live_ref[...]
+    grad_out = out_grad_ref[...].astype(F32) * live_ref[:, :1]
     grad_residual = grad_out + normalise_back(grad, unit, rstd, rows_ref[1:2, :])
     grad_residual_ref[...] = grad_residual
     grad_attn = grad_residual.astype(BF)
@@ -574,7 +573,7 @@
     results = pl.pallas_call(
         functools.partial(mlp_kernel, split_rows, owners),
         grid=(STEPS,),
-        in_specs=[SMEM, SMEM, whole(*wide), whole(D, rows), whole(rows, 1)]
+        in_specs=[SMEM, SMEM, whole(*wide), whole(D, rows), whole(rows, 128)]
         + [whole(*wide), whole(*wide), whole(4, D), column(1)]
         + [HBM] * (len(up_pieces) + len(down_pieces)),
         out_specs=[whole(*wide), whole(*wide), column(D // 2), column(D // 2), column(1)]
@@ -589,7 +588,8 @@
         + grad_shapes,
         scratch_shapes=[
             pltpu.VMEM(wide, BF),
-            pltpu.VMEM(wide, F32),
+            pltpu.VMEM((rows, FF), BF),
+            pltpu.VMEM((rows, FF), BF),
             pltpu.VMEM((D, FF), BF),
             pltpu.VMEM((FF, D), BF),
             pltpu.VMEM(staged, BF),
@@ -744,7 +744,7 @@
     wait_all(stores)
 
 
-def add_ranges(groups, outputs):
+def add_ranges(groups, outputs, cost):
     rows = groups[0][0][0].shape[1]
     flat = [side.reshape(-1, side.shape[-1]) for group in groups for pair in group for side in pair]
     widths = tuple(tuple(pair[0].shape[-1] for pair in group) for group in groups)
@@ -761,7 +761,7 @@
             pltpu.SemaphoreType.DMA((len(plan),)),
         ]
         + [pltpu.VMEM(shape, BF) for shape in shapes for _ in range(2)],
-        cost_estimate=QUICK,
+        cost_estimate=cost,
         compiler_params=pltpu.CompilerParams(vmem_limit_bytes=KERNEL_VMEM),
         name="add_ranges",
     )(*flat)
@@ -801,7 +801,7 @@
     @pl.when(step == 2)
     def _():
         unit, rstd = normalise(tokens_ref[...].astype(F32))
-        grad = natural_order(total[...], order_ref[...]) * live_ref[...]
+        grad = natural_order(total[...], order_ref[...]) * live_ref[:, :1]
         tokens_grad_ref[...] = (
             grad_residual_ref[...] + normalise_back(grad, unit, rstd, gain_ref[...])
         ).astype(BF)
@@ -843,7 +843,7 @@
         in_specs=[
             pl.BlockSpec((rows, D), lambda step: (0, step)),
             whole(rows, D),
-            whole(rows, 1),
+            whole(rows, 128),
             whole(1, D),
             whole(D, D),
             whole(rows, D),
@@ -860,7 +860,7 @@
             pltpu.VMEM((D, 3 * D), BF),
             pltpu.SemaphoreType.DMA((3, PIECES)),
         ],
-        cost_estimate=LONG,
+        cost_estimate=QUICK,
         compiler_params=pltpu.CompilerParams(vmem_limit_bytes=KERNEL_VMEM),
         name="first_norm_back",
     )(grad_qkv, tokens, live, gain, order, grad_residual, sums, b_up, tables, *pieces)
@@ -1039,7 +1039,7 @@
     return (left.astype(F32) + right.astype(F32)).astype(BF)
 
 
-def scatter_stages(parts, count, result, late=(), direct=False, inbox=None):
+def scatter_stages(parts, count, result, late=(), direct=False, inbox=None, costs=()):
     farthest, far, middle = hop_plan(count)
     blocks = count // 2
     half = blocks // 2
@@ -1052,10 +1052,13 @@
     arrived = after(arrived, deps)
     pairs = list(zip(kept, arrived)) + [(shape(k), shape(got)) for k, got in late]
 
+    costs = list(costs)
+
     def added(groups, outputs):
+        cost = costs.pop(0) if costs else QUICK
         rows = groups[0][0][0].shape[1]
         if all(lo * rows % 16 == 0 and hi * rows % 16 == 0 for o in outputs for _, lo, hi in o):
-            return add_ranges(groups, outputs)
+            return add_ranges(groups, outputs, cost)
         return [
             jnp.concatenate(
                 [
@@ -1108,7 +1111,7 @@
 def sum_stages(array, count, result):
     bits = count.bit_length() - 1
     deps = yield
-    for mask in [1 << bit for bit in [0, bits - 2, bits - 1] + list(range(1, bits - 2))]:
+    for mask in [1 << bit for bit in [bits - 2, bits - 1, 0] + list(range(1, bits - 2))]:
         (array,) = after([array], deps)
         got = hop(array, mask, count)
         deps = yield [array]
@@ -1169,7 +1172,7 @@
     shift = jnp.asarray(shift)
     order = order_matrix(me, count, shard_rows)
     table = table_lanes(rel_pos_h, rel_pos_w)
-    live = slot_mask(window_pos)
+    live = jnp.broadcast_to(slot_mask(window_pos), (tokens.shape[0], 128))
     inverse = np.argsort(np.array(sum_order(count)))
     places = jnp.take(jnp.asarray(inverse, jnp.int32), jnp.bitwise_xor(me, np.arange(count)))
     first.send(None)
@@ -1229,7 +1232,9 @@
     )
     late, got_up, got_down = [], [], []
     up = start(scatter_stages([(kept_up, sent_up)], count, own_up, late, inbox=got_up))
-    down = start(scatter_stages([down_parts], count, own_down, inbox=got_down))
+    down = start(
+        scatter_stages([down_parts], count, own_down, inbox=got_down, costs=(QUICK, LONG))
+    )
     sent = up.send(None)
     sent = down.send(sent)
     (grad_normed,) = after([grad_normed], sent)
@@ -1248,9 +1253,6 @@
     kept_qkv, sent_qkv = weight_grad(turned_one, grad_qkv)
     third_sum = start(scatter_stages([(kept_qkv, sent_qkv)], count, own_third, direct=True))
     sent = third_sum.send(None)
-    for _ in range(middle - 1):
-        sent = down.send([kept_qkv] + sent)
-    sent = up.send(sent)
     (grad_qkv,) = after([grad_qkv], sent)
     tokens_grad, small_sums = first_norm_back(
         grad_qkv,
@@ -1265,21 +1267,24 @@
         tables,
     )
     small_stages = start(sum_stages(small_sums, count, all_small))
-    sent = third_sum.send([small_sums] + got_down)
-    sent = small_stages.send(sent)
-    sent = down.send(sent)
+    sent = small_stages.send(None)
+    for _ in range(middle - 1):
+        sent = down.send([small_sums] + sent + got_up)
+    sent = third_sum.send(sent)
     sent = up.send(sent)
     (gated_tables,) = after([tables], sent)
     sent = [marker(gated_tables)]
     sent = small_stages.send(sent)
+    sent = down.send(sent)
     for _ in range(middle - 1):
         sent = third_sum.send(sent)
+    sent = up.send(sent)
+    sent = small_stages.send(sent)
+    sent = third_sum.send(sent)
     sent = small_stages.send(sent)
     sent = down.send(sent)
     sent = small_stages.send(sent)
-    sent = third_sum.send(sent)
     sent = up.send(sent)
-    sent = small_stages.send(sent)
     for stages in (down, up, third_sum, small_stages):
         finish(stages)
     own_qkv, own_proj = own_third[0], own_up[0][:, FF:]

time: 255 us -> 253 us (level)
  starting transfers between devices: 58 us -> 62.1 us
  waiting for transfers between devices: 40.5 us -> 36.8 us
    ppermute x49, starting transfers between devices: 58 us -> 62.1 us  [hop(): return lax.ppermute(array, 'fsdp', [(i, i ^ mask) for i in range(count)])]
    ppermute x49, waiting for transfers between devices: 40.5 us -> 36.8 us  [hop(): return lax.ppermute(array, 'fsdp', [(i, i ^ mask) for i in range(count)])]
    unnamed x70 -> x72, local copies, waits for them, and re-layouts: 13.1 us -> 12.1 us
  transfers between devices with their start and end apart: 49 -> 49, of which waited for: 13 -> 14; matrix products, arithmetic and copies ran while one was open for 7% -> 7% of each run, Pallas kernels for 36% -> 36%
where the time goes in v5:
time: 253 us; the launch traced here: 252 us
  Pallas kernels  119 us (47%)
  starting transfers between devices  62.1 us (25%)
  waiting for transfers between devices  36.8 us (15%)
  local copies, waits for them, and re-layouts  18.3 us (7%)
  other arithmetic  14.4 us (6%)
    ppermute x49, starting transfers between devices, hop(): return lax.ppermute(array, 'fsdp', [(i, i ^ mask) for i in range(count)])  62.1 us
    ppermute x49, waiting for transfers between devices, hop(): return lax.ppermute(array, 'fsdp', [(i, i ^ mask) for i in range(count)])  36.8 us
    pallas_call x1, Pallas kernels, mlp(): pl.pallas_call(functools.partial(mlp_kernel, split_rows, owners), grid=(S...  24.3 us
    pallas_call x8, Pallas kernels, add_ranges(): pl.pallas_call(functools.partial(add_kernel, widths, plan), in_specs=[HBM...  22.8 us
    pallas_call x1, Pallas kernels, attention_back(): pl.pallas_call(attn_bwd_kernel, grid=(PAIRS,), in_specs=columns + [pl.Blo...  13 us
    unnamed x72, local copies, waits for them, and re-layouts  12.1 us
    pallas_call x5, Pallas kernels, join(): pl.pallas_call(functools.partial(join_kernel, sizes), in_specs=[HBM] * le...  11.9 us
    pallas_call x1, Pallas kernels, attention(): pl.pallas_call(attn_fwd_kernel, grid=(PAIRS,), in_specs=columns + constan...  9.9 us
  transfers between devices with their start and end apart: 49, of which 14 were waited for; matrix products, arithmetic and copies ran while one was open for 7% of the time, Pallas kernels for 36%

profile of v5, /device:TPU:0, one launch (start us, length us, event | category | flops | bytes accessed | tf_op | source)
XLA Modules:
  0.0 251.6 jit_solution(16112017501810654387)
XLA Ops:
  3.5 4.1 %collective-permute-start = (bf16[24,3200]{1,0:T(8,128)(2,1)S(1)}, bf16[24,3200]{1,0:T(8,128)(2,1)S(1)}, u32[]{:S(2)}, u32[]{:S(2)}) collective-permute-start(bf16[24,3200]{1,0:T(8,128)(2,1)S(1)} %pad_maximum_fusion.4), channel_id=1, source_target_pairs={{0,16},{1,17},{2,18},{3,19},{4,20},{5,21},{6,22},{7,23},{8,24},{9,... | collective-permute-start | bytes 460808 | tf_op jit(solution)/shard_map/ppermute | solution.py:903
  17.2 3.4 %collective-permute-start.1 = (bf16[24,3072]{1,0:T(8,128)(2,1)S(1)}, bf16[24,3072]{1,0:T(8,128)(2,1)S(1)}, u32[]{:S(2)}, u32[]{:S(2)}) collective-permute-start(bf16[24,3072]{1,0:T(8,128)(2,1)S(1)} %convert_element_type.124), channel_id=1, source_target_pairs={{0,16},{1,17},{2,18},{3,19},{4,20},{5,21},{6,22},{7,23},{8,24},{9,... | collective-permute-start | bytes 442376 | tf_op jit(solution)/shard_map/ppermute | solution.py:903
  20.7 7.8 %collective-permute-done.3 = bf16[2,24,3200]{2,1,0:T(8,128)(2,1)S(1)} collective-permute-done((bf16[2,24,3200]{2,1,0:T(8,128)(2,1)S(1)}, bf16[2,24,3200]{2,1,0:T(8,128)(2,1)S(1)}, u32[]{:S(2)}, u32[]{:S(2)}) %collective-permute-start.3) | collective-permute-done | bytes 307232 | tf_op jit(solution)/shard_map/ppermute | solution.py:903
  29.8 6.2 %collective-permute-done.4 = bf16[2,24,3200]{2,1,0:T(8,128)(2,1)S(1)} collective-permute-done((bf16[2,24,3200]{2,1,0:T(8,128)(2,1)S(1)}, bf16[2,24,3200]{2,1,0:T(8,128)(2,1)S(1)}, u32[]{:S(2)}, u32[]{:S(2)}) %collective-permute-start.4) | collective-permute-done | bytes 307232 | tf_op jit(solution)/shard_map/ppermute | solution.py:903
  36.1 2.0 collective-permute-start.9
  39.8 2.1 collective-permute-start.7
  44.1 4.3 %collective-permute-done.5.refs_2_ = bf16[2,24,3072]{2,1,0:T(8,128)(2,1)S(1)} collective-permute-done((bf16[2,24,3072]{2,1,0:T(8,128)(2,1)S(1)}, bf16[2,24,3072]{2,1,0:T(8,128)(2,1)S(1)}, u32[]{:S(2)}, u32[]{:S(2)}) %collective-permute-start.5) | collective-permute-done | bytes 294944 | tf_op jit(solution)/shard_map/ppermute | solution.py:903
  48.4 3.3 %collective-permute-done.7.refs_2_ = bf16[2,96,768]{2,1,0:T(8,128)(2,1)} collective-permute-done((bf16[2,96,768]{2,1,0:T(8,128)(2,1)S(1)}, bf16[2,96,768]{2,1,0:T(8,128)(2,1)}, u32[]{:S(2)}, u32[]{:S(2)}) %collective-permute-start.7) | collective-permute-done | bytes 294944 | tf_op jit(solution)/shard_map/ppermute | solution.py:903
  52.7 2.6 %join.5.refs_0_ = bf16[16,24,3200]{2,1,0:T(8,128)(2,1)} custom-call(bf16[4,24,3200]{2,1,0:T(8,128)(2,1)} %copy-done.2, bf16[4,24,3200]{2,1,0:T(8,128)(2,1)} %copy-done.12, bf16[4,24,3200]{2,1,0:T(8,128)(2,1)} %copy-done.6, bf16[4,24,3200]{2,1,0:T(8,128)(2,1)} %copy-done.11), custom_call_target="tpu_custom_call" | custom-call | flops 1 | bytes 1 | tf_op jit(solution)/shard_map/join/pallas_call | solution.py:679
  55.9 1.7 collective-permute-start.13
  61.8 1.9 place.1
  66.3 6.5 %front.1 = (bf16[768,392]{1,0:T(8,128)(2,1)}, bf16[392,2304]{1,0:T(8,128)(2,1)}) custom-call(bf16[392,768]{1,0:T(8,128)(2,1)} %tokens_ref.4, f32[392,128]{1,0:T(8,128)} %broadcast_in_dim.33.live_ref.rest_2_, bf16[768,768]{1,0:T(8,128)(2,1)} %fusion.order_ref, f32[2,768]{1,0:T(2,128)} %pad_maximum_fusion.6.rows_ref, f32[1,2304]{1,0:T(1,128)} %reshape_reshape.11.b_qkv_ref, ...), custom_call_target="tpu_custom_call" | custom-call | flops 1 | bytes 1 | tf_op jit(solution)/shard_map/front/pallas_call | solution.py:355
  72.8 2.1 join.7
  77.4 2.0 join.6
  80.9 1.7 collective-permute-start.18
  82.6 9.9 %attention.1 = (bf16[392,768]{1,0:T(8,128)(2,1)}, f32[6,4,200,256]{3,2,1,0:T(8,128)}) custom-call(bf16[392,2304]{1,0:T(8,128)(2,1)} %get-tuple-element.158.q_ref.k_ref.v_ref, bf16[392,2304]{1,0:T(8,128)(2,1)} %get-tuple-element.158.q_ref.k_ref.v_ref, bf16[392,2304]{1,0:T(8,128)(2,1)} %get-tuple-element.158.q_ref.k_ref.v_ref, ...), custom_call_target="tpu_custom_call" | custom-call | flops 1 | bytes 1 | tf_op jit(solution)/shard_map/attention/pallas_call | solution.py:238
  95.2 2.5 %join.8 = bf16[16,96,768]{2,1,0:T(8,128)(2,1)} custom-call(bf16[4,96,768]{2,1,0:T(8,128)(2,1)} %get-tuple-element.156.refs_0_, bf16[4,96,768]{2,1,0:T(8,128)(2,1)} %copy-done.13, bf16[4,96,768]{2,1,0:T(8,128)(2,1)} %get-tuple-element.157.refs_2_, bf16[4,96,768]{2,1,0:T(8,128)(2,1)} %copy-done.15), custom_call_target="tpu_custom_call" | custom-call | flops 1 | bytes 1 | tf_op jit(solution)/shard_map/join/pallas_call | solution.py:679
  97.8 6.0 %project.1 = (f32[392,768]{1,0:T(8,128)}, bf16[392,768]{1,0:T(8,128)(2,1)}, bf16[768,392]{1,0:T(8,128)(2,1)}, bf16[392,768]{1,0:T(8,128)(2,1)}) custom-call(bf16[392,768]{1,0:T(8,128)(2,1)} %tokens_ref.4, bf16[392,768]{1,0:T(8,128)(2,1)} %get-tuple-element.162.values_ref, bf16[768,768]{1,0:T(8,128)(2,1)} %fusion.order_ref, ...), custom_call_target="tpu_custom_call" | custom-call | flops 1 | bytes 1 | tf_op jit(solution)/shard_map/project/pallas_call | solution.py:532
  104.9 2.6 %join.9 = bf16[16,24,3072]{2,1,0:T(8,128)(2,1)} custom-call(bf16[4,24,3072]{2,1,0:T(8,128)(2,1)} %get-tuple-element.152.refs_0_, bf16[4,24,3072]{2,1,0:T(8,128)(2,1)} %copy-done.14, bf16[4,24,3072]{2,1,0:T(8,128)(2,1)} %get-tuple-element.153.refs_2_, bf16[4,24,3072]{2,1,0:T(8,128)(2,1)} %copy-done.16), custom_call_target="tpu_custom_call" | custom-call | flops 1 | bytes 1 | tf_op jit(solution)/shard_map/join/pallas_call | solution.py:679
  108.1 4.5 %collective-permute-done.19 = bf16[16,24,3072]{2,1,0:T(8,128)(2,1)} collective-permute-done((bf16[16,24,3072]{2,1,0:T(8,128)(2,1)}, bf16[16,24,3072]{2,1,0:T(8,128)(2,1)}, u32[]{:S(2)}, u32[]{:S(2)}) %collective-permute-start.19) | collective-permute-done | bytes 2359328 | tf_op jit(solution)/shard_map/ppermute | solution.py:903
  112.6 24.3 %mlp.1 = (bf16[392,768]{1,0:T(8,128)(2,1)}, f32[392,768]{1,0:T(8,128)}, bf16[384,3072]{1,0:T(8,128)(2,1)}, bf16[384,3072]{1,0:T(8,128)(2,1)}, f32[1,3072]{1,0:T(...) custom-call(s32[32]{0:T(128)} %and_select_fusion.2.place_ref, s32[1]{0:T(128)} %bitcast.me_ref, ...), custom_call_target="tpu_custom_call" | custom-call | flops 1 | bytes 1 | tf_op jit(solution)/shard_map/mlp/pallas_call | solution.py:573
  137.5 7.3 %second_norm_back.1 = (f32[392,768]{1,0:T(8,128)}, bf16[392,768]{1,0:T(8,128)(2,1)}, bf16[384,768]{1,0:T(8,128)(2,1)}, bf16[384,768]{1,0:T(8,128)(2,1)}, f32[8,768]{1,0:T(8,128)}) custom-call(f32[392,768]{1,0:T(8,128)} %get-tuple-element.173.grad_normed_ref, f32[392,768]{1,0:T(8,128)} %get-tuple-element.165.rest_4_.residual_ref, ...), custom_call_target="tpu_custom_call" | custom-call | flops 1 | bytes 1 | tf_op jit(solution)/shard_map/second_norm_back/pallas_call | solution.py:622
  145.2 1.8 collective-permute-done.23.refs_3_
  147.9 4.4 %add_ranges.8 = (bf16[96,3840]{1,0:T(8,128)(2,1)}, bf16[96,3840]{1,0:T(8,128)(2,1)}, bf16[96,3840]{1,0:T(8,128)(2,1)}, bf16[96,3840]{1,0:T(8,128)(2,1)}) custom-call(bf16[384,3072]{1,0:T(8,128)(2,1)} %get-tuple-element.177.refs_0_, bf16[384,3072]{1,0:T(8,128)(2,1)} %bitcast.18.refs_1_, bf16[384,768]{1,0:T(8,128)(2,1)} %get-tuple-element.179.refs_2_, ...), custom_call_target="tpu_custom_call" | custom-call | flops 1 | bytes 1 | tf_op jit(solution)/shard_map/add_ranges/pallas_call | solution.py:754
  154.9 3.4 %add_ranges.9 = (bf16[384,768]{1,0:T(8,128)(2,1)}, bf16[384,768]{1,0:T(8,128)(2,1)}, bf16[384,768]{1,0:T(8,128)(2,1)}, bf16[384,768]{1,0:T(8,128)(2,1)}) custom-call(bf16[1536,768]{1,0:T(8,128)(2,1)} %bitcast.102, bf16[1536,768]{1,0:T(8,128)(2,1)} %bitcast.103), custom_call_target="tpu_custom_call" | custom-call | flops 1 | bytes 1 | tf_op jit(solution)/shard_map/add_ranges/pallas_call | solution.py:754
  158.3 1.7 collective-permute-start.31
  161.3 13.0 %attention_back.1 = (bf16[392,2304]{1,0:T(8,128)(2,1)}, f32[128,128]{1,0:T(8,128)}) custom-call(bf16[392,2304]{1,0:T(8,128)(2,1)} %get-tuple-element.158.q_ref.k_ref.v_ref, bf16[392,2304]{1,0:T(8,128)(2,1)} %get-tuple-element.158.q_ref.k_ref.v_ref, bf16[392,2304]{1,0:T(8,128)(2,1)} %get-tuple-element.158.q_ref.k_ref.v_ref, ...), custom_call_target="tpu_custom_call" | custom-call | flops 1 | bytes 1 | tf_op jit(solution)/shard_map/attention_back/pallas_call | solution.py:256
  175.4 2.7 %add_ranges.10 = (bf16[48,3840]{1,0:T(8,128)(2,1)}, bf16[48,3840]{1,0:T(8,128)(2,1)}, bf16[48,3840]{1,0:T(8,128)(2,1)}, bf16[48,3840]{1,0:T(8,128)(2,1)}) custom-call(bf16[96,3840]{1,0:T(8,128)(2,1)} %get-tuple-element.189.refs_0_, bf16[96,3840]{1,0:T(8,128)(2,1)} %bitcast.108, bf16[96,3840]{1,0:T(8,128)(2,1)} %get-tuple-element.191.refs_2_, ...), custom_call_target="tpu_custom_call" | custom-call | flops 1 | bytes 1 | tf_op jit(solution)/shard_map/add_ranges/pallas_call | solution.py:754
  179.3 5.0 %weight_grad.1 = (bf16[384,2304]{1,0:T(8,128)(2,1)}, bf16[384,2304]{1,0:T(8,128)(2,1)}) custom-call(bf16[768,392]{1,0:T(8,128)(2,1)} %get-tuple-element.149.turned_ref, bf16[392,2304]{1,0:T(8,128)(2,1)} %get-tuple-element.197.grad_ref), custom_call_target="tpu_custom_call" | custom-call | flops 1 | bytes 1 | tf_op jit(solution)/shard_map/weight_grad/pallas_call | solution.py:702
  184.3 8.4 %first_norm_back.1 = (bf16[392,768]{1,0:T(8,128)(2,1)}, f32[112,128]{1,0:T(8,128)}) custom-call(bf16[392,2304]{1,0:T(8,128)(2,1)} %get-tuple-element.197.grad_ref, bf16[392,768]{1,0:T(8,128)(2,1)} %tokens_ref.4, f32[392,128]{1,0:T(8,128)} %broadcast_in_dim.33.live_ref.rest_2_, f32[1,768]{1,0:T(1,128)} %copy-done.32, bf16[768,768]{1,0:T(8,128)(2,1)} %fusion.order_ref, ...), custom_call_target="tpu_custom_call" | custom-call | flops 1 | bytes 1 | tf_op jit(solution)/shard_map/first_norm_back/pallas_call | solution.py:840
  193.2 2.7 %add_ranges.11 = (bf16[192,768]{1,0:T(8,128)(2,1)}, bf16[192,768]{1,0:T(8,128)(2,1)}, bf16[192,768]{1,0:T(8,128)(2,1)}, bf16[192,768]{1,0:T(8,128)(2,1)}) custom-call(bf16[384,768]{1,0:T(8,128)(2,1)} %get-tuple-element.206.refs_0_, bf16[384,768]{1,0:T(8,128)(2,1)} %bitcast.29.refs_1_, bf16[384,768]{1,0:T(8,128)(2,1)} %get-tuple-element.208.refs_2_, ...), custom_call_target="tpu_custom_call" | custom-call | flops 99999997952 | bytes 1 | tf_op jit(solution)/shard_map/add_ranges/pallas_call | solution.py:754
  197.2 1.7 collective-permute-start.36
  200.1 2.9 %add_ranges.12 = (bf16[96,2304]{1,0:T(8,128)(2,1)}, bf16[96,2304]{1,0:T(8,128)(2,1)}, bf16[96,2304]{1,0:T(8,128)(2,1)}, bf16[96,2304]{1,0:T(8,128)(2,1)}) custom-call(bf16[384,2304]{1,0:T(8,128)(2,1)} %get-tuple-element.205.refs_0_, bf16[384,2304]{1,0:T(8,128)(2,1)} %bitcast.105), custom_call_target="tpu_custom_call" | custom-call | flops 1 | bytes 1 | tf_op jit(solution)/shard_map/add_ranges/pallas_call | solution.py:754
  203.1 2.2 add_ranges.13
  205.3 1.8 collective-permute-start.33
  208.3 4.0 %collective-permute-start.32 = (f32[112,128]{1,0:T(8,128)S(1)}, f32[112,128]{1,0:T(8,128)S(1)}, u32[]{:S(2)}, u32[]{:S(2)}) collective-permute-start(f32[112,128]{1,0:T(8,128)S(1)} %add.80), channel_id=1, source_target_pairs={{0,16},{1,17},{2,18},{3,19},{4,20},{5,21},{6,22},{7,23},{8,24},{9,... | collective-permute-start | bytes 172040 | tf_op jit(solution)/shard_map/ppermute | solution.py:903
  213.0 2.1 add_ranges.14
  215.0 1.8 collective-permute-start.42
  216.8 1.9 collective-permute-done.35
  219.7 2.4 add_ranges.15
  222.9 1.6 collective-permute-start.39
  224.6 4.0 %collective-permute-start.47 = (bf16[24,3840]{1,0:T(8,128)(2,1)S(1)}, bf16[24,3840]{1,0:T(8,128)(2,1)S(1)}, u32[]{:S(2)}, u32[]{:S(2)}) collective-permute-start(bf16[24,3840]{1,0:T(8,128)(2,1)S(1)} %fusion.3), channel_id=1, source_target_pairs={{0,16},{1,17},{2,18},{3,19},{4,20},{5,21},{6,22},{7,23},{8,24},{9,... | collective-permute-start | bytes 552968 | tf_op jit(solution)/shard_map/ppermute | solution.py:903
  230.2 4.0 %collective-permute-start.44 = (bf16[24,2304]{1,0:T(8,128)(2,1)S(1)}, bf16[24,2304]{1,0:T(8,128)(2,1)S(1)}, u32[]{:S(2)}, u32[]{:S(2)}) collective-permute-start(bf16[24,2304]{1,0:T(8,128)(2,1)S(1)} %fusion.9), channel_id=1, source_target_pairs={{0,16},{1,17},{2,18},{3,19},{4,20},{5,21},{6,22},{7,23},{8,24},{9,... | collective-permute-start | bytes 331784 | tf_op jit(solution)/shard_map/ppermute | solution.py:903
  235.9 1.7 collective-permute-start.41
  237.6 2.5 %collective-permute-done.41 = f32[112,128]{1,0:T(8,128)S(1)} collective-permute-done((f32[112,128]{1,0:T(8,128)S(1)}, f32[112,128]{1,0:T(8,128)S(1)}, u32[]{:S(2)}, u32[]{:S(2)}) %collective-permute-start.41) | collective-permute-done | bytes 57376 | tf_op jit(solution)/shard_map/ppermute | solution.py:903
  240.2 2.7 %collective-permute-start.48 = (bf16[96,768]{1,0:T(8,128)(2,1)S(1)}, bf16[96,768]{1,0:T(8,128)(2,1)S(1)}, u32[]{:S(2)}, u32[]{:S(2)}) collective-permute-start(bf16[96,768]{1,0:T(8,128)(2,1)S(1)} %fusion.5), channel_id=1, source_target_pairs={{0,16},{1,17},{2,18},{3,19},{4,20},{5,21},{6,22},{7,23},{8,24},{9,... | collective-permute-start | bytes 442376 | tf_op jit(solution)/shard_map/ppermute | solution.py:903
  247.8 1.5 own_small.1
  249.3 1.5 collective-permute-done.48
  (204 shorter events, 57.9 us)
Async XLA Ops:
  3.5 11.4 %collective-permute-start = (bf16[24,3200]{1,0:T(8,128)(2,1)S(1)}, bf16[24,3200]{1,0:T(8,128)(2,1)S(1)}, u32[]{:S(2)}, u32[]{:S(2)}) collective-permute-start(bf16[24,3200]{1,0:T(8,128)(2,1)S(1)} %pad_maximum_fusion.4), channel_id=1, source_target_pairs={{0,16},{1,17},{2,18},{3,19},{4,20},{5,21},{6,22},{7,23},{8,24},{9,... | collective-permute-start | bytes 460808 | tf_op jit(solution)/shard_map/ppermute | solution.py:903
  14.9 13.6 %collective-permute-start.3 = (bf16[2,24,3200]{2,1,0:T(8,128)(2,1)S(1)}, bf16[2,24,3200]{2,1,0:T(8,128)(2,1)S(1)}, u32[]{:S(2)}, u32[]{:S(2)}) collective-permute-start(bf16[2,24,3200]{2,1,0:T(8,128)(2,1)S(1)} %pad_maximum_fusion.1), channel_id=1, source_target_pairs={{0,8},{1,9},{2,10},{3,11},{4,12},{5,13},{6,14},{7,15},{8,0},{9,1},... | collective-permute-start | bytes 921608 | tf_op jit(solution)/shard_map/ppermute | solution.py:903
  15.8 14.0 %collective-permute-start.2 = (bf16[2,24,3200]{2,1,0:T(8,128)(2,1)S(1)}, bf16[2,24,3200]{2,1,0:T(8,128)(2,1)S(1)}, u32[]{:S(2)}, u32[]{:S(2)}) collective-permute-start(bf16[2,24,3200]{2,1,0:T(8,128)(2,1)S(1)} %pad_maximum_fusion.1), channel_id=1, source_target_pairs={{0,2},{1,3},{2,0},{3,1},{4,6},{5,7},{6,4},{7,5},{8,10},{9,11},{10,... | collective-permute-start | bytes 921608 | tf_op jit(solution)/shard_map/ppermute | solution.py:903
  17.2 22.3 %collective-permute-start.1 = (bf16[24,3072]{1,0:T(8,128)(2,1)S(1)}, bf16[24,3072]{1,0:T(8,128)(2,1)S(1)}, u32[]{:S(2)}, u32[]{:S(2)}) collective-permute-start(bf16[24,3072]{1,0:T(8,128)(2,1)S(1)} %convert_element_type.124), channel_id=1, source_target_pairs={{0,16},{1,17},{2,18},{3,19},{4,20},{5,21},{6,22},{7,23},{8,24},{9,... | collective-permute-start | bytes 442376 | tf_op jit(solution)/shard_map/ppermute | solution.py:903
  20.6 19.0 %collective-permute-start.6 = (bf16[96,768]{1,0:T(8,128)(2,1)S(1)}, bf16[96,768]{1,0:T(8,128)(2,1)S(1)}, u32[]{:S(2)}, u32[]{:S(2)}) collective-permute-start(bf16[96,768]{1,0:T(8,128)(2,1)S(1)} %convert_element_type.125), channel_id=1, source_target_pairs={{0,16},{1,17},{2,18},{3,19},{4,20},{5,21},{6,22},{7,23},{8,24},{9,... | collective-permute-start | bytes 442376 | tf_op jit(solution)/shard_map/ppermute | solution.py:903
  28.4 7.5 %collective-permute-start.4 = (bf16[2,24,3200]{2,1,0:T(8,128)(2,1)S(1)}, bf16[2,24,3200]{2,1,0:T(8,128)(2,1)S(1)}, u32[]{:S(2)}, u32[]{:S(2)}) collective-permute-start(bf16[2,24,3200]{2,1,0:T(8,128)(2,1)S(1)} %collective-permute-done.3), channel_id=1, source_target_pairs={{0,4},{1,5},{2,6},{3,7},{4,0},{5,1},{6,2},{7,3},{8,12},{9,13},{10,... | collective-permute-start | bytes 921608 | tf_op jit(solution)/shard_map/ppermute | solution.py:903
  36.1 15.5 %collective-permute-start.9 = (bf16[4,24,3200]{2,1,0:T(8,128)(2,1)S(1)}, bf16[4,24,3200]{2,1,0:T(8,128)(2,1)S(1)}, u32[]{:S(2)}, u32[]{:S(2)}) collective-permute-start(bf16[4,24,3200]{2,1,0:T(8,128)(2,1)S(1)} %constant_dynamic-update-slice_fusion.refs_2_), channel_id=1, source_target_pairs={{0,2},{1,3},{2,0},{3,1},{4,6},{5,7},{6,4},{7,5},{8,10},{9,11},{10,... | collective-permute-start | bytes 1843208 | tf_op jit(solution)/shard_map/ppermute | solution.py:903
  38.1 13.6 %collective-permute-start.8 = (bf16[4,24,3200]{2,1,0:T(8,128)(2,1)S(1)}, bf16[4,24,3200]{2,1,0:T(8,128)(2,1)S(1)}, u32[]{:S(2)}, u32[]{:S(2)}) collective-permute-start(bf16[4,24,3200]{2,1,0:T(8,128)(2,1)S(1)} %pad_maximum_fusion.refs_0_), channel_id=1, source_target_pairs={{0,4},{1,5},{2,6},{3,7},{4,0},{5,1},{6,2},{7,3},{8,12},{9,13},{10,... | collective-permute-start | bytes 1843208 | tf_op jit(solution)/shard_map/ppermute | solution.py:903
  39.6 8.7 %collective-permute-start.5 = (bf16[2,24,3072]{2,1,0:T(8,128)(2,1)S(1)}, bf16[2,24,3072]{2,1,0:T(8,128)(2,1)S(1)}, u32[]{:S(2)}, u32[]{:S(2)}) collective-permute-start(bf16[2,24,3072]{2,1,0:T(8,128)(2,1)S(1)} %pad_maximum_fusion.2.refs_0_), channel_id=1, source_target_pairs={{0,8},{1,9},{2,10},{3,11},{4,12},{5,13},{6,14},{7,15},{8,0},{9,1},... | collective-permute-start | bytes 884744 | tf_op jit(solution)/shard_map/ppermute | solution.py:903
  39.8 11.9 %collective-permute-start.7 = (bf16[2,96,768]{2,1,0:T(8,128)(2,1)S(1)}, bf16[2,96,768]{2,1,0:T(8,128)(2,1)}, u32[]{:S(2)}, u32[]{:S(2)}) collective-permute-start(bf16[2,96,768]{2,1,0:T(8,128)(2,1)S(1)} %pad_maximum_fusion.3.refs_0_), channel_id=1, source_target_pairs={{0,8},{1,9},{2,10},{3,11},{4,12},{5,13},{6,14},{7,15},{8,0},{9,1},... | collective-permute-start | bytes 884744 | tf_op jit(solution)/shard_map/ppermute | solution.py:903
  55.4 5.0 %collective-permute-start.10 = (bf16[16,24,3200]{2,1,0:T(8,128)(2,1)}, bf16[16,24,3200]{2,1,0:T(8,128)(2,1)S(1)}, u32[]{:S(2)}, u32[]{:S(2)}) collective-permute-start(bf16[16,24,3200]{2,1,0:T(8,128)(2,1)} %join.5.refs_0_), channel_id=1, source_target_pairs={{0,1},{1,0},{2,3},{3,2},{4,5},{5,4},{6,7},{7,6},{8,9},{9,8},{10,11... | collective-permute-start | bytes 7372808 | tf_op jit(solution)/shard_map/ppermute | solution.py:903
  55.5 20.5 %collective-permute-start.11 = (bf16[2,24,3072]{2,1,0:T(8,128)(2,1)S(1)}, bf16[2,24,3072]{2,1,0:T(8,128)(2,1)S(1)}, u32[]{:S(2)}, u32[]{:S(2)}) collective-permute-start(bf16[2,24,3072]{2,1,0:T(8,128)(2,1)S(1)} %pad_maximum_fusion.2.refs_0_), channel_id=1, source_target_pairs={{0,2},{1,3},{2,0},{3,1},{4,6},{5,7},{6,4},{7,5},{8,10},{9,11},{10,... | collective-permute-start | bytes 884744 | tf_op jit(solution)/shard_map/ppermute | solution.py:903
  55.9 16.9 %collective-permute-start.13 = (bf16[2,96,768]{2,1,0:T(8,128)(2,1)S(1)}, bf16[2,96,768]{2,1,0:T(8,128)(2,1)}, u32[]{:S(2)}, u32[]{:S(2)}) collective-permute-start(bf16[2,96,768]{2,1,0:T(8,128)(2,1)S(1)} %pad_maximum_fusion.3.refs_0_), channel_id=1, source_target_pairs={{0,2},{1,3},{2,0},{3,1},{4,6},{5,7},{6,4},{7,5},{8,10},{9,11},{10,... | collective-permute-start | bytes 884744 | tf_op jit(solution)/shard_map/ppermute | solution.py:903
  57.6 18.4 %collective-permute-start.12 = (bf16[2,24,3072]{2,1,0:T(8,128)(2,1)S(1)}, bf16[2,24,3072]{2,1,0:T(8,128)(2,1)S(1)}, u32[]{:S(2)}, u32[]{:S(2)}) collective-permute-start(bf16[2,24,3072]{2,1,0:T(8,128)(2,1)S(1)} %collective-permute-done.5.refs_2_), channel_id=1, source_target_pairs={{0,4},{1,5},{2,6},{3,7},{4,0},{5,1},{6,2},{7,3},{8,12},{9,13},{10,... | collective-permute-start | bytes 884744 | tf_op jit(solution)/shard_map/ppermute | solution.py:903
  58.1 14.7 %collective-permute-start.14 = (bf16[2,96,768]{2,1,0:T(8,128)(2,1)}, bf16[2,96,768]{2,1,0:T(8,128)(2,1)}, u32[]{:S(2)}, u32[]{:S(2)}) collective-permute-start(bf16[2,96,768]{2,1,0:T(8,128)(2,1)} %collective-permute-done.7.refs_2_), channel_id=1, source_target_pairs={{0,4},{1,5},{2,6},{3,7},{4,0},{5,1},{6,2},{7,3},{8,12},{9,13},{10,... | collective-permute-start | bytes 884744 | tf_op jit(solution)/shard_map/ppermute | solution.py:903
  74.9 19.3 %collective-permute-start.15 = (bf16[4,96,768]{2,1,0:T(8,128)(2,1)}, bf16[4,96,768]{2,1,0:T(8,128)(2,1)S(1)}, u32[]{:S(2)}, u32[]{:S(2)}) collective-permute-start(bf16[4,96,768]{2,1,0:T(8,128)(2,1)} %get-tuple-element.156.refs_0_), channel_id=1, source_target_pairs={{0,4},{1,5},{2,6},{3,7},{4,0},{5,1},{6,2},{7,3},{8,12},{9,13},{10,... | collective-permute-start | bytes 1769480 | tf_op jit(solution)/shard_map/ppermute | solution.py:903
  75.5 18.7 %collective-permute-start.16 = (bf16[4,96,768]{2,1,0:T(8,128)(2,1)}, bf16[4,96,768]{2,1,0:T(8,128)(2,1)S(1)}, u32[]{:S(2)}, u32[]{:S(2)}) collective-permute-start(bf16[4,96,768]{2,1,0:T(8,128)(2,1)} %get-tuple-element.157.refs_2_), channel_id=1, source_target_pairs={{0,2},{1,3},{2,0},{3,1},{4,6},{5,7},{6,4},{7,5},{8,10},{9,11},{10,... | collective-permute-start | bytes 1769480 | tf_op jit(solution)/shard_map/ppermute | solution.py:903
  79.4 24.5 %collective-permute-start.17 = (bf16[4,24,3072]{2,1,0:T(8,128)(2,1)}, bf16[4,24,3072]{2,1,0:T(8,128)(2,1)S(1)}, u32[]{:S(2)}, u32[]{:S(2)}) collective-permute-start(bf16[4,24,3072]{2,1,0:T(8,128)(2,1)} %get-tuple-element.152.refs_0_), channel_id=1, source_target_pairs={{0,4},{1,5},{2,6},{3,7},{4,0},{5,1},{6,2},{7,3},{8,12},{9,13},{10,... | collective-permute-start | bytes 1769480 | tf_op jit(solution)/shard_map/ppermute | solution.py:903
  80.9 23.0 %collective-permute-start.18 = (bf16[4,24,3072]{2,1,0:T(8,128)(2,1)}, bf16[4,24,3072]{2,1,0:T(8,128)(2,1)S(1)}, u32[]{:S(2)}, u32[]{:S(2)}) collective-permute-start(bf16[4,24,3072]{2,1,0:T(8,128)(2,1)} %get-tuple-element.153.refs_2_), channel_id=1, source_target_pairs={{0,2},{1,3},{2,0},{3,1},{4,6},{5,7},{6,4},{7,5},{8,10},{9,11},{10,... | collective-permute-start | bytes 1769480 | tf_op jit(solution)/shard_map/ppermute | solution.py:903
  97.8 10.3 %collective-permute-start.20 = (bf16[16,96,768]{2,1,0:T(8,128)(2,1)}, bf16[16,96,768]{2,1,0:T(8,128)(2,1)S(1)}, u32[]{:S(2)}, u32[]{:S(2)}) collective-permute-start(bf16[16,96,768]{2,1,0:T(8,128)(2,1)} %join.8), channel_id=1, source_target_pairs={{0,1},{1,0},{2,3},{3,2},{4,5},{5,4},{6,7},{7,6},{8,9},{9,8},{10,11... | collective-permute-start | bytes 7077896 | tf_op jit(solution)/shard_map/ppermute | solution.py:903
  107.5 5.1 %collective-permute-start.19 = (bf16[16,24,3072]{2,1,0:T(8,128)(2,1)}, bf16[16,24,3072]{2,1,0:T(8,128)(2,1)}, u32[]{:S(2)}, u32[]{:S(2)}) collective-permute-start(bf16[16,24,3072]{2,1,0:T(8,128)(2,1)} %join.9), channel_id=1, source_target_pairs={{0,1},{1,0},{2,3},{3,2},{4,5},{5,4},{6,7},{7,6},{8,9},{9,8},{10,11... | collective-permute-start | bytes 7077896 | tf_op jit(solution)/shard_map/ppermute | solution.py:903
  136.9 8.3 %collective-permute-start.22 = (bf16[16,24,3072]{2,1,0:T(8,128)(2,1)}, bf16[16,24,3072]{2,1,0:T(8,128)(2,1)}, u32[]{:S(2)}, u32[]{:S(2)}) collective-permute-start(bf16[16,24,3072]{2,1,0:T(8,128)(2,1)} %bitcast.124), channel_id=1, source_target_pairs={{0,1},{1,0},{2,3},{3,2},{4,5},{5,4},{6,7},{7,6},{8,9},{9,8},{10,11... | collective-permute-start | bytes 7077896 | tf_op jit(solution)/shard_map/ppermute | solution.py:903
  137.3 16.1 %collective-permute-start.21 = (bf16[16,96,768]{2,1,0:T(8,128)(2,1)}, bf16[16,96,768]{2,1,0:T(8,128)(2,1)S(1)}, u32[]{:S(2)}, u32[]{:S(2)}) collective-permute-start(bf16[16,96,768]{2,1,0:T(8,128)(2,1)} %get-tuple-element.172), channel_id=1, source_target_pairs={{0,1},{1,0},{2,3},{3,2},{4,5},{5,4},{6,7},{7,6},{8,9},{9,8},{10,11... | collective-permute-start | bytes 7077896 | tf_op jit(solution)/shard_map/ppermute | solution.py:903
  152.2 22.0 %collective-permute-start.25 = (bf16[4,24,3840]{2,1,0:T(8,128)(2,1)}, bf16[4,24,3840]{2,1,0:T(8,128)(2,1)S(1)}, u32[]{:S(2)}, u32[]{:S(2)}) collective-permute-start(bf16[4,24,3840]{2,1,0:T(8,128)(2,1)} %bitcast.127), channel_id=1, source_target_pairs={{0,2},{1,3},{2,0},{3,1},{4,6},{5,7},{6,4},{7,5},{8,10},{9,11},{10,... | collective-permute-start | bytes 2211848 | tf_op jit(solution)/shard_map/ppermute | solution.py:903
  152.7 21.6 %collective-permute-start.24 = (bf16[4,24,3840]{2,1,0:T(8,128)(2,1)}, bf16[4,24,3840]{2,1,0:T(8,128)(2,1)S(1)}, u32[]{:S(2)}, u32[]{:S(2)}) collective-permute-start(bf16[4,24,3840]{2,1,0:T(8,128)(2,1)} %bitcast.126), channel_id=1, source_target_pairs={{0,4},{1,5},{2,6},{3,7},{4,0},{5,1},{6,2},{7,3},{8,12},{9,13},{10,... | collective-permute-start | bytes 2211848 | tf_op jit(solution)/shard_map/ppermute | solution.py:903
  158.3 34.5 %collective-permute-start.31 = (bf16[4,96,768]{2,1,0:T(8,128)(2,1)}, bf16[4,96,768]{2,1,0:T(8,128)(2,1)}, u32[]{:S(2)}, u32[]{:S(2)}) collective-permute-start(bf16[4,96,768]{2,1,0:T(8,128)(2,1)} %bitcast.129), channel_id=1, source_target_pairs={{0,2},{1,3},{2,0},{3,1},{4,6},{5,7},{6,4},{7,5},{8,10},{9,11},{10,... | collective-permute-start | bytes 1769480 | tf_op jit(solution)/shard_map/ppermute | solution.py:903
  160.1 33.1 %collective-permute-start.30 = (bf16[4,96,768]{2,1,0:T(8,128)(2,1)}, bf16[4,96,768]{2,1,0:T(8,128)(2,1)}, u32[]{:S(2)}, u32[]{:S(2)}) collective-permute-start(bf16[4,96,768]{2,1,0:T(8,128)(2,1)} %bitcast.128), channel_id=1, source_target_pairs={{0,4},{1,5},{2,6},{3,7},{4,0},{5,1},{6,2},{7,3},{8,12},{9,13},{10,... | collective-permute-start | bytes 1769480 | tf_op jit(solution)/shard_map/ppermute | solution.py:903
  178.1 15.1 %collective-permute-start.28 = (bf16[2,24,3840]{2,1,0:T(8,128)(2,1)}, bf16[2,24,3840]{2,1,0:T(8,128)(2,1)S(1)}, u32[]{:S(2)}, u32[]{:S(2)}) collective-permute-start(bf16[2,24,3840]{2,1,0:T(8,128)(2,1)} %bitcast.134), channel_id=1, source_target_pairs={{0,4},{1,5},{2,6},{3,7},{4,0},{5,1},{6,2},{7,3},{8,12},{9,13},{10,... | collective-permute-start | bytes 1105928 | tf_op jit(solution)/shard_map/ppermute | solution.py:903
  178.9 14.2 %collective-permute-start.27 = (bf16[2,24,3840]{2,1,0:T(8,128)(2,1)}, bf16[2,24,3840]{2,1,0:T(8,128)(2,1)S(1)}, u32[]{:S(2)}, u32[]{:S(2)}) collective-permute-start(bf16[2,24,3840]{2,1,0:T(8,128)(2,1)} %bitcast.133), channel_id=1, source_target_pairs={{0,2},{1,3},{2,0},{3,1},{4,6},{5,7},{6,4},{7,5},{8,10},{9,11},{10,... | collective-permute-start | bytes 1105928 | tf_op jit(solution)/shard_map/ppermute | solution.py:903
  184.3 14.6 %collective-permute-start.29 = (bf16[16,24,2304]{2,1,0:T(8,128)(2,1)}, bf16[16,24,2304]{2,1,0:T(8,128)(2,1)S(1)}, u32[]{:S(2)}, u32[]{:S(2)}) collective-permute-start(bf16[16,24,2304]{2,1,0:T(8,128)(2,1)} %bitcast.125), channel_id=1, source_target_pairs={{0,1},{1,0},{2,3},{3,2},{4,5},{5,4},{6,7},{7,6},{8,9},{9,8},{10,11... | collective-permute-start | bytes 5308424 | tf_op jit(solution)/shard_map/ppermute | solution.py:903
  192.8 14.7 %collective-permute-start.26 = (f32[112,128]{1,0:T(8,128)}, f32[112,128]{1,0:T(8,128)S(1)}, u32[]{:S(2)}, u32[]{:S(2)}) collective-permute-start(f32[112,128]{1,0:T(8,128)} %get-tuple-element.203), channel_id=1, source_target_pairs={{0,8},{1,9},{2,10},{3,11},{4,12},{5,13},{6,14},{7,15},{8,0},{9,1},... | collective-permute-start | bytes 172040 | tf_op jit(solution)/shard_map/ppermute | solution.py:903
  195.9 12.3 %collective-permute-start.37 = (bf16[2,96,768]{2,1,0:T(8,128)(2,1)}, bf16[2,96,768]{2,1,0:T(8,128)(2,1)S(1)}, u32[]{:S(2)}, u32[]{:S(2)}) collective-permute-start(bf16[2,96,768]{2,1,0:T(8,128)(2,1)} %bitcast.137), channel_id=1, source_target_pairs={{0,4},{1,5},{2,6},{3,7},{4,0},{5,1},{6,2},{7,3},{8,12},{9,13},{10,... | collective-permute-start | bytes 884744 | tf_op jit(solution)/shard_map/ppermute | solution.py:903
  197.2 15.0 %collective-permute-start.36 = (bf16[2,96,768]{2,1,0:T(8,128)(2,1)}, bf16[2,96,768]{2,1,0:T(8,128)(2,1)S(1)}, u32[]{:S(2)}, u32[]{:S(2)}) collective-permute-start(bf16[2,96,768]{2,1,0:T(8,128)(2,1)} %bitcast.136), channel_id=1, source_target_pairs={{0,2},{1,3},{2,0},{3,1},{4,6},{5,7},{6,4},{7,5},{8,10},{9,11},{10,... | collective-permute-start | bytes 884744 | tf_op jit(solution)/shard_map/ppermute | solution.py:903
  205.3 19.2 %collective-permute-start.33 = (bf16[2,24,3840]{2,1,0:T(8,128)(2,1)}, bf16[2,24,3840]{2,1,0:T(8,128)(2,1)S(1)}, u32[]{:S(2)}, u32[]{:S(2)}) collective-permute-start(bf16[2,24,3840]{2,1,0:T(8,128)(2,1)} %bitcast.132), channel_id=1, source_target_pairs={{0,8},{1,9},{2,10},{3,11},{4,12},{5,13},{6,14},{7,15},{8,0},{9,1},... | collective-permute-start | bytes 1105928 | tf_op jit(solution)/shard_map/ppermute | solution.py:903
  207.1 11.6 %collective-permute-start.35 = (bf16[4,24,2304]{2,1,0:T(8,128)(2,1)}, bf16[4,24,2304]{2,1,0:T(8,128)(2,1)S(1)}, u32[]{:S(2)}, u32[]{:S(2)}) collective-permute-start(bf16[4,24,2304]{2,1,0:T(8,128)(2,1)} %bitcast.131), channel_id=1, source_target_pairs={{0,2},{1,3},{2,0},{3,1},{4,6},{5,7},{6,4},{7,5},{8,10},{9,11},{10,... | collective-permute-start | bytes 1327112 | tf_op jit(solution)/shard_map/ppermute | solution.py:903
  207.5 11.4 %collective-permute-start.34 = (bf16[4,24,2304]{2,1,0:T(8,128)(2,1)}, bf16[4,24,2304]{2,1,0:T(8,128)(2,1)S(1)}, u32[]{:S(2)}, u32[]{:S(2)}) collective-permute-start(bf16[4,24,2304]{2,1,0:T(8,128)(2,1)} %bitcast.130), channel_id=1, source_target_pairs={{0,4},{1,5},{2,6},{3,7},{4,0},{5,1},{6,2},{7,3},{8,12},{9,13},{10,... | collective-permute-start | bytes 1327112 | tf_op jit(solution)/shard_map/ppermute | solution.py:903
  208.3 20.4 %collective-permute-start.32 = (f32[112,128]{1,0:T(8,128)S(1)}, f32[112,128]{1,0:T(8,128)S(1)}, u32[]{:S(2)}, u32[]{:S(2)}) collective-permute-start(f32[112,128]{1,0:T(8,128)S(1)} %add.80), channel_id=1, source_target_pairs={{0,16},{1,17},{2,18},{3,19},{4,20},{5,21},{6,22},{7,23},{8,24},{9,... | collective-permute-start | bytes 172040 | tf_op jit(solution)/shard_map/ppermute | solution.py:903
  215.0 20.9 %collective-permute-start.42 = (bf16[2,96,768]{2,1,0:T(8,128)(2,1)}, bf16[2,96,768]{2,1,0:T(8,128)(2,1)S(1)}, u32[]{:S(2)}, u32[]{:S(2)}) collective-permute-start(bf16[2,96,768]{2,1,0:T(8,128)(2,1)} %bitcast.135), channel_id=1, source_target_pairs={{0,8},{1,9},{2,10},{3,11},{4,12},{5,13},{6,14},{7,15},{8,0},{9,1},... | collective-permute-start | bytes 884744 | tf_op jit(solution)/shard_map/ppermute | solution.py:903
  222.1 6.6 %collective-permute-start.40 = (bf16[2,24,2304]{2,1,0:T(8,128)(2,1)}, bf16[2,24,2304]{2,1,0:T(8,128)(2,1)S(1)}, u32[]{:S(2)}, u32[]{:S(2)}) collective-permute-start(bf16[2,24,2304]{2,1,0:T(8,128)(2,1)} %bitcast.139), channel_id=1, source_target_pairs={{0,4},{1,5},{2,6},{3,7},{4,0},{5,1},{6,2},{7,3},{8,12},{9,13},{10,... | collective-permute-start | bytes 663560 | tf_op jit(solution)/shard_map/ppermute | solution.py:903
  222.9 6.1 %collective-permute-start.39 = (bf16[2,24,2304]{2,1,0:T(8,128)(2,1)}, bf16[2,24,2304]{2,1,0:T(8,128)(2,1)S(1)}, u32[]{:S(2)}, u32[]{:S(2)}) collective-permute-start(bf16[2,24,2304]{2,1,0:T(8,128)(2,1)} %bitcast.138), channel_id=1, source_target_pairs={{0,2},{1,3},{2,0},{3,1},{4,6},{5,7},{6,4},{7,5},{8,10},{9,11},{10,... | collective-permute-start | bytes 663560 | tf_op jit(solution)/shard_map/ppermute | solution.py:903
  224.6 18.3 %collective-permute-start.47 = (bf16[24,3840]{1,0:T(8,128)(2,1)S(1)}, bf16[24,3840]{1,0:T(8,128)(2,1)S(1)}, u32[]{:S(2)}, u32[]{:S(2)}) collective-permute-start(bf16[24,3840]{1,0:T(8,128)(2,1)S(1)} %fusion.3), channel_id=1, source_target_pairs={{0,16},{1,17},{2,18},{3,19},{4,20},{5,21},{6,22},{7,23},{8,24},{9,... | collective-permute-start | bytes 552968 | tf_op jit(solution)/shard_map/ppermute | solution.py:903
  228.6 6.8 %collective-permute-start.38 = (f32[112,128]{1,0:T(8,128)S(1)}, f32[112,128]{1,0:T(8,128)S(1)}, u32[]{:S(2)}, u32[]{:S(2)}) collective-permute-start(f32[112,128]{1,0:T(8,128)S(1)} %add.82), channel_id=1, source_target_pairs={{0,1},{1,0},{2,3},{3,2},{4,5},{5,4},{6,7},{7,6},{8,9},{9,8},{10,11... | collective-permute-start | bytes 172040 | tf_op jit(solution)/shard_map/ppermute | solution.py:903
  230.2 15.5 %collective-permute-start.44 = (bf16[24,2304]{1,0:T(8,128)(2,1)S(1)}, bf16[24,2304]{1,0:T(8,128)(2,1)S(1)}, u32[]{:S(2)}, u32[]{:S(2)}) collective-permute-start(bf16[24,2304]{1,0:T(8,128)(2,1)S(1)} %fusion.9), channel_id=1, source_target_pairs={{0,16},{1,17},{2,18},{3,19},{4,20},{5,21},{6,22},{7,23},{8,24},{9,... | collective-permute-start | bytes 331784 | tf_op jit(solution)/shard_map/ppermute | solution.py:903
  234.2 11.4 %collective-permute-start.46 = (bf16[24,2304]{1,0:T(8,128)(2,1)S(1)}, bf16[24,2304]{1,0:T(8,128)(2,1)S(1)}, u32[]{:S(2)}, u32[]{:S(2)}) collective-permute-start(bf16[24,2304]{1,0:T(8,128)(2,1)S(1)} %get-tuple-element.258), channel_id=1, source_target_pairs={{0,24},{1,25},{2,26},{3,27},{4,28},{5,29},{6,30},{7,31},{8,16},{9,... | collective-permute-start | bytes 331784 | tf_op jit(solution)/shard_map/ppermute | solution.py:903
  235.4 10.2 %collective-permute-start.45 = (bf16[24,2304]{1,0:T(8,128)(2,1)S(1)}, bf16[24,2304]{1,0:T(8,128)(2,1)S(1)}, u32[]{:S(2)}, u32[]{:S(2)}) collective-permute-start(bf16[24,2304]{1,0:T(8,128)(2,1)S(1)} %get-tuple-element.259), channel_id=1, source_target_pairs={{0,8},{1,9},{2,10},{3,11},{4,12},{5,13},{6,14},{7,15},{8,0},{9,1},... | collective-permute-start | bytes 331784 | tf_op jit(solution)/shard_map/ppermute | solution.py:903
  235.9 4.2 %collective-permute-start.41 = (f32[112,128]{1,0:T(8,128)S(1)}, f32[112,128]{1,0:T(8,128)S(1)}, u32[]{:S(2)}, u32[]{:S(2)}) collective-permute-start(f32[112,128]{1,0:T(8,128)S(1)} %add.85), channel_id=1, source_target_pairs={{0,2},{1,3},{2,0},{3,1},{4,6},{5,7},{6,4},{7,5},{8,10},{9,11},{10,... | collective-permute-start | bytes 172040 | tf_op jit(solution)/shard_map/ppermute | solution.py:903
  240.2 10.7 %collective-permute-start.48 = (bf16[96,768]{1,0:T(8,128)(2,1)S(1)}, bf16[96,768]{1,0:T(8,128)(2,1)S(1)}, u32[]{:S(2)}, u32[]{:S(2)}) collective-permute-start(bf16[96,768]{1,0:T(8,128)(2,1)S(1)} %fusion.5), channel_id=1, source_target_pairs={{0,16},{1,17},{2,18},{3,19},{4,20},{5,21},{6,22},{7,23},{8,24},{9,... | collective-permute-start | bytes 442376 | tf_op jit(solution)/shard_map/ppermute | solution.py:903
  242.9 4.2 %collective-permute-start.43 = (f32[112,128]{1,0:T(8,128)S(1)}, f32[112,128]{1,0:T(8,128)S(1)}, u32[]{:S(2)}, u32[]{:S(2)}) collective-permute-start(f32[112,128]{1,0:T(8,128)S(1)} %add.87), channel_id=1, source_target_pairs={{0,4},{1,5},{2,6},{3,7},{4,0},{5,1},{6,2},{7,3},{8,12},{9,13},{10,... | collective-permute-start | bytes 172040 | tf_op jit(solution)/shard_map/ppermute | solution.py:903
  (36 other events, 222.0 us)

commit v6 on v5

--- a/solution.py
+++ b/solution.py
@@ -126,7 +126,7 @@
         rows = pl.ds(192 * win, BLOCK)
         queries = pad_rows(q_ref[rows, :].astype(F32) * SCALE).T
         k = k_ref[rows, :].astype(F32)
-        v = v_ref[rows, :]
+        v = v_ref[rows, :].astype(F32)
         rel = dot_nn(table_ref[...], queries.astype(BF))
         onehot = onehot_ref[win].astype(F32)
         by_row = bit_masks(shift_ref[win, :8], 24)
@@ -149,8 +149,9 @@
             expon = jnp.exp(scores - jnp.max(scores, axis=0, keepdims=True))
             probs = expon * (1.0 / jnp.sum(expon, axis=0, keepdims=True))
             probs_ref[0, 2 * win + head] = probs
-            halves.append(dot_tn(v, probs.astype(BF)))
-        both = jnp.concatenate((halves[0][:HEAD_DIM], halves[1][HEAD_DIM:]), axis=0).T[:BLOCK]
+            halves.append(probs)
+        values = jnp.concatenate((jnp.where(low, v, 0.0), jnp.where(low, 0.0, v)), axis=0)
+        both = dot_tn(values.astype(BF), jnp.concatenate(halves, axis=0).astype(BF)).T[:BLOCK]
         mixed.append(jnp.where(row_valid(win), both, 0.0))
     mixed_ref[...] = merge_windows(*mixed).astype(BF)
 
@@ -178,43 +179,44 @@
     table_total = jnp.zeros((128, 128), F32)
     for win in range(2):
         rows = pl.ds(192 * win, BLOCK)
-        q = pad_rows(q_ref[rows, :].astype(F32) * SCALE).astype(BF)
+        q = pad_rows(q_ref[rows, :].astype(F32) * SCALE)
         k = k_ref[rows, :].astype(F32)
         v = v_ref[rows, :]
         grad = pad_rows(jnp.where(row_valid(win), grad_ref[rows, :].astype(F32), 0.0))
-        grad_low = grad.astype(BF)
         wide_low = lax.broadcasted_iota(jnp.int32, (LANES, 128), 1) < 64
+
+        def by_head(values):
+            return jnp.concatenate(
+                (jnp.where(wide_low, values, 0.0), jnp.where(wide_low, 0.0, values)), axis=0
+            ).astype(BF)
+
+        grads, queries = by_head(grad), by_head(q)
+        q = q.astype(BF)
         onehot = onehot_ref[win].astype(F32)
         by_row = bit_masks(shift_ref[win, :8], 24)
         by_col = bit_masks(shift_ref[win, 8:], 24)
-        by_query, by_key, by_value, rel = [], [], [], []
+        probs = jnp.concatenate((probs_ref[0, 2 * win], probs_ref[0, 2 * win + 1]), axis=1)
+        grad_probs = dot_nt(v, grads)
+        row_dot = jnp.sum(probs * grad_probs, axis=0, keepdims=True)
+        grad_scores = (probs * (grad_probs - row_dot)).astype(BF)
+        parts[2].append(dot_nn(probs.astype(BF), grads))
+        parts[1].append(dot_nn(grad_scores, queries))
+        by_query, rel = [], []
         for head in range(2):
-            if head == 0:
-                right = jnp.where(low, k, onehot).astype(BF)
-                grad_own = jnp.where(wide_low, grad, 0.0).astype(BF)
-            else:
-                right = jnp.where(low, onehot, k).astype(BF)
-                grad_own = jnp.where(wide_low, 0.0, grad).astype(BF)
-            probs = probs_ref[0, 2 * win + head]
-            grad_probs = dot_nt(v, grad_own)
-            row_dot = jnp.sum(probs * grad_probs, axis=0, keepdims=True)
-            grad_scores = (probs * (grad_probs - row_dot)).astype(BF)
-            by_value.append(dot_nn(probs.astype(BF), grad_low))
-            by_key.append(dot_nn(grad_scores, q))
-            back = dot_tn(right, grad_scores)
+            right = (jnp.where(low, k, onehot) if head == 0 else jnp.where(low, onehot, k)).astype(BF)
+            back = dot_tn(right, grad_scores[:, head * LANES : (head + 1) * LANES])
             own, base = (back[:64], 64) if head == 0 else (back[64:], 0)
             by_query.append(own)
             rel.append(unskew(back[base : base + 16], by_row))
             rel.append(unskew(back[base + 32 : base + 48], by_col))
         rel = jnp.concatenate((rel[2], rel[3], rel[0], rel[1]), axis=0)
-        rel_top = rel.astype(BF)
-        rel_rest = (rel - rel_top.astype(F32)).astype(BF)
+        rel_top = rel.astype(BF).astype(F32)
+        rel = jnp.concatenate((rel_top, rel - rel_top), axis=0).astype(BF)
         table = table_ref[...]
-        from_rel = dot_tn(table, rel_top) + dot_tn(table, rel_rest)
-        table_total += dot_nn(rel_top, q) + dot_nn(rel_rest, q)
+        from_rel = dot_tn(jnp.concatenate((table, table), axis=0), rel)
+        table_parts = dot_nn(rel, q)
+        table_total += table_parts[:128] + table_parts[128:]
         parts[0].append((jnp.concatenate(by_query, axis=0) + from_rel).T[:BLOCK] * SCALE)
-        parts[1].append(jnp.where(low, by_key[0], by_key[1]))
-        parts[2].append(jnp.where(low, by_value[0], by_value[1]))
     for block in range(3):
         at = pl.multiple_of(block * D + pair * 128, 128)
         grad_qkv_ref[:, pl.ds(at, 128)] = merge_windows(*parts[block]).astype(BF)
@@ -434,8 +436,9 @@
 
     grad_active = dot_nt(branch[...], w_down[pl.ds(at, TILE), :])
     grad_hidden = (grad_active * slope).astype(BF)
-    sent_ref[...] = dot_nn(turned_ref[half:, :], grad_hidden).astype(BF)
-    kept_ref[...] = dot_nn(turned_ref[:half, :], grad_hidden).astype(BF)
+    grad_up = dot_nn(turned_ref[...], grad_hidden).astype(BF)
+    kept_ref[...] = grad_up[:half]
+    sent_ref[...] = grad_up[half:]
     actives[:, pl.ds(at, TILE)] = active
     grads[:, pl.ds(at, TILE)] = grad_hidden
     grad_b_ref[...] = jnp.sum(grad_hidden.astype(F32), axis=0, keepdims=True)
@@ -510,9 +513,10 @@
 
 
 def natural_order(values, order):
-    top = values.astype(BF)
-    rest = (values - top.astype(F32)).astype(BF)
-    return dot_nt(top, order) + dot_nt(rest, order)
+    top = values.astype(BF).astype(F32)
+    rows = values.shape[0]
+    both = dot_nt(jnp.concatenate((top, values - top), axis=0).astype(BF), order)
+    return both[:rows] + both[rows:]
 
 
 TILE = 768
@@ -691,9 +695,9 @@
 
 
 def weight_kernel(turned_ref, grad_ref, kept_ref, sent_ref):
-    half = D // 2
-    sent_ref[...] = dot_nn(turned_ref[half:, :], grad_ref[...]).astype(BF)
-    kept_ref[...] = dot_nn(turned_ref[:half, :], grad_ref[...]).astype(BF)
+    total = dot_nn(turned_ref[...], grad_ref[...]).astype(BF)
+    kept_ref[...] = total[: D // 2]
+    sent_ref[...] = total[D // 2 :]
 
 
 def weight_grad(turned, grad):

time: 253 us -> 251 us (level)
  Pallas kernels: 119 us -> 116 us
  transfers between devices with their start and end apart: 49 -> 49, of which waited for: 14 -> 16; matrix products, arithmetic and copies ran while one was open for 7% -> 7% of each run, Pallas kernels for 36% -> 36%
where the time goes in v6:
time: 251 us; the launch traced here: 250 us
  Pallas kernels  116 us (46%)
  starting transfers between devices  61.2 us (24%)
  waiting for transfers between devices  39.3 us (16%)
  local copies, waits for them, and re-layouts  17.9 us (7%)
  other arithmetic  14.4 us (6%)
    ppermute x49, starting transfers between devices, hop(): return lax.ppermute(array, 'fsdp', [(i, i ^ mask) for i in range(count)])  61.2 us
    ppermute x49, waiting for transfers between devices, hop(): return lax.ppermute(array, 'fsdp', [(i, i ^ mask) for i in range(count)])  39.3 us
    pallas_call x1, Pallas kernels, mlp(): pl.pallas_call(functools.partial(mlp_kernel, split_rows, owners), grid=(S...  24.3 us
    pallas_call x8, Pallas kernels, add_ranges(): pl.pallas_call(functools.partial(add_kernel, widths, plan), in_specs=[HBM...  22.8 us
    pallas_call x5, Pallas kernels, join(): pl.pallas_call(functools.partial(join_kernel, sizes), in_specs=[HBM] * le...  11.9 us
    unnamed x72, local copies, waits for them, and re-layouts  11.7 us
    pallas_call x1, Pallas kernels, attention_back(): pl.pallas_call(attn_bwd_kernel, grid=(PAIRS,), in_specs=columns + [pl.Blo...  10.8 us
    pallas_call x1, Pallas kernels, attention(): pl.pallas_call(attn_fwd_kernel, grid=(PAIRS,), in_specs=columns + constan...  9 us
  transfers between devices with their start and end apart: 49, of which 16 were waited for; matrix products, arithmetic and copies ran while one was open for 7% of the time, Pallas kernels for 36%

profile of v6, /device:TPU:0, one launch (start us, length us, event | category | flops | bytes accessed | tf_op | source)
XLA Modules:
  0.0 250.1 jit_solution(14402543166110457461)
XLA Ops:
  3.5 4.1 %collective-permute-start = (bf16[24,3200]{1,0:T(8,128)(2,1)S(1)}, bf16[24,3200]{1,0:T(8,128)(2,1)S(1)}, u32[]{:S(2)}, u32[]{:S(2)}) collective-permute-start(bf16[24,3200]{1,0:T(8,128)(2,1)S(1)} %pad_maximum_fusion.4), channel_id=1, source_target_pairs={{0,16},{1,17},{2,18},{3,19},{4,20},{5,21},{6,22},{7,23},{8,24},{9,... | collective-permute-start | bytes 460808 | tf_op jit(solution)/shard_map/ppermute | solution.py:907
  17.2 3.4 %collective-permute-start.1 = (bf16[24,3072]{1,0:T(8,128)(2,1)S(1)}, bf16[24,3072]{1,0:T(8,128)(2,1)S(1)}, u32[]{:S(2)}, u32[]{:S(2)}) collective-permute-start(bf16[24,3072]{1,0:T(8,128)(2,1)S(1)} %convert_element_type.124), channel_id=1, source_target_pairs={{0,16},{1,17},{2,18},{3,19},{4,20},{5,21},{6,22},{7,23},{8,24},{9,... | collective-permute-start | bytes 442376 | tf_op jit(solution)/shard_map/ppermute | solution.py:907
  20.7 7.8 %collective-permute-done.3 = bf16[2,24,3200]{2,1,0:T(8,128)(2,1)S(1)} collective-permute-done((bf16[2,24,3200]{2,1,0:T(8,128)(2,1)S(1)}, bf16[2,24,3200]{2,1,0:T(8,128)(2,1)S(1)}, u32[]{:S(2)}, u32[]{:S(2)}) %collective-permute-start.3) | collective-permute-done | bytes 307232 | tf_op jit(solution)/shard_map/ppermute | solution.py:907
  29.8 6.2 %collective-permute-done.4 = bf16[2,24,3200]{2,1,0:T(8,128)(2,1)S(1)} collective-permute-done((bf16[2,24,3200]{2,1,0:T(8,128)(2,1)S(1)}, bf16[2,24,3200]{2,1,0:T(8,128)(2,1)S(1)}, u32[]{:S(2)}, u32[]{:S(2)}) %collective-permute-start.4) | collective-permute-done | bytes 307232 | tf_op jit(solution)/shard_map/ppermute | solution.py:907
  36.1 2.0 collective-permute-start.9
  38.1 1.5 collective-permute-start.8
  39.8 2.1 collective-permute-start.7
  44.1 4.3 %collective-permute-done.5.refs_2_ = bf16[2,24,3072]{2,1,0:T(8,128)(2,1)S(1)} collective-permute-done((bf16[2,24,3072]{2,1,0:T(8,128)(2,1)S(1)}, bf16[2,24,3072]{2,1,0:T(8,128)(2,1)S(1)}, u32[]{:S(2)}, u32[]{:S(2)}) %collective-permute-start.5) | collective-permute-done | bytes 294944 | tf_op jit(solution)/shard_map/ppermute | solution.py:907
  48.4 3.3 %collective-permute-done.7.refs_2_ = bf16[2,96,768]{2,1,0:T(8,128)(2,1)} collective-permute-done((bf16[2,96,768]{2,1,0:T(8,128)(2,1)S(1)}, bf16[2,96,768]{2,1,0:T(8,128)(2,1)}, u32[]{:S(2)}, u32[]{:S(2)}) %collective-permute-start.7) | collective-permute-done | bytes 294944 | tf_op jit(solution)/shard_map/ppermute | solution.py:907
  52.7 2.6 %join.5.refs_0_ = bf16[16,24,3200]{2,1,0:T(8,128)(2,1)} custom-call(bf16[4,24,3200]{2,1,0:T(8,128)(2,1)} %copy-done.2, bf16[4,24,3200]{2,1,0:T(8,128)(2,1)} %copy-done.12, bf16[4,24,3200]{2,1,0:T(8,128)(2,1)} %copy-done.6, bf16[4,24,3200]{2,1,0:T(8,128)(2,1)} %copy-done.11), custom_call_target="tpu_custom_call" | custom-call | flops 1 | bytes 1 | tf_op jit(solution)/shard_map/join/pallas_call | solution.py:683
  55.9 1.7 collective-permute-start.13
  61.8 1.9 place.1
  66.3 6.5 %front.1 = (bf16[768,392]{1,0:T(8,128)(2,1)}, bf16[392,2304]{1,0:T(8,128)(2,1)}) custom-call(bf16[392,768]{1,0:T(8,128)(2,1)} %tokens_ref.4, f32[392,128]{1,0:T(8,128)} %broadcast_in_dim.33.live_ref.rest_2_, bf16[768,768]{1,0:T(8,128)(2,1)} %fusion.order_ref, f32[2,768]{1,0:T(2,128)} %pad_maximum_fusion.6.rows_ref, f32[1,2304]{1,0:T(1,128)} %reshape_reshape.11.b_qkv_ref, ...), custom_call_target="tpu_custom_call" | custom-call | flops 1 | bytes 1 | tf_op jit(solution)/shard_map/front/pallas_call | solution.py:357
  72.8 2.1 join.7
  77.4 2.0 join.6
  79.4 1.5 collective-permute-start.17
  80.9 1.7 collective-permute-start.18
  82.6 9.0 %attention.1 = (bf16[392,768]{1,0:T(8,128)(2,1)}, f32[6,4,200,256]{3,2,1,0:T(8,128)}) custom-call(bf16[392,2304]{1,0:T(8,128)(2,1)} %get-tuple-element.158.q_ref.k_ref.v_ref, bf16[392,2304]{1,0:T(8,128)(2,1)} %get-tuple-element.158.q_ref.k_ref.v_ref, bf16[392,2304]{1,0:T(8,128)(2,1)} %get-tuple-element.158.q_ref.k_ref.v_ref, ...), custom_call_target="tpu_custom_call" | custom-call | flops 1 | bytes 1 | tf_op jit(solution)/shard_map/attention/pallas_call | solution.py:240
  94.3 2.5 %join.8 = bf16[16,96,768]{2,1,0:T(8,128)(2,1)} custom-call(bf16[4,96,768]{2,1,0:T(8,128)(2,1)} %get-tuple-element.156.refs_0_, bf16[4,96,768]{2,1,0:T(8,128)(2,1)} %copy-done.13, bf16[4,96,768]{2,1,0:T(8,128)(2,1)} %get-tuple-element.157.refs_2_, bf16[4,96,768]{2,1,0:T(8,128)(2,1)} %copy-done.15), custom_call_target="tpu_custom_call" | custom-call | flops 1 | bytes 1 | tf_op jit(solution)/shard_map/join/pallas_call | solution.py:683
  96.9 6.0 %project.1 = (f32[392,768]{1,0:T(8,128)}, bf16[392,768]{1,0:T(8,128)(2,1)}, bf16[768,392]{1,0:T(8,128)(2,1)}, bf16[392,768]{1,0:T(8,128)(2,1)}) custom-call(bf16[392,768]{1,0:T(8,128)(2,1)} %tokens_ref.4, bf16[392,768]{1,0:T(8,128)(2,1)} %get-tuple-element.162.values_ref, bf16[768,768]{1,0:T(8,128)(2,1)} %fusion.order_ref, ...), custom_call_target="tpu_custom_call" | custom-call | flops 1 | bytes 1 | tf_op jit(solution)/shard_map/project/pallas_call | solution.py:536
  104.3 2.6 %join.9 = bf16[16,24,3072]{2,1,0:T(8,128)(2,1)} custom-call(bf16[4,24,3072]{2,1,0:T(8,128)(2,1)} %get-tuple-element.152.refs_0_, bf16[4,24,3072]{2,1,0:T(8,128)(2,1)} %copy-done.14, bf16[4,24,3072]{2,1,0:T(8,128)(2,1)} %get-tuple-element.153.refs_2_, bf16[4,24,3072]{2,1,0:T(8,128)(2,1)} %copy-done.16), custom_call_target="tpu_custom_call" | custom-call | flops 1 | bytes 1 | tf_op jit(solution)/shard_map/join/pallas_call | solution.py:683
  107.2 4.7 %collective-permute-done.19 = bf16[16,24,3072]{2,1,0:T(8,128)(2,1)} collective-permute-done((bf16[16,24,3072]{2,1,0:T(8,128)(2,1)}, bf16[16,24,3072]{2,1,0:T(8,128)(2,1)}, u32[]{:S(2)}, u32[]{:S(2)}) %collective-permute-start.19) | collective-permute-done | bytes 2359328 | tf_op jit(solution)/shard_map/ppermute | solution.py:907
  111.9 24.3 %mlp.1 = (bf16[392,768]{1,0:T(8,128)(2,1)}, f32[392,768]{1,0:T(8,128)}, bf16[384,3072]{1,0:T(8,128)(2,1)}, bf16[384,3072]{1,0:T(8,128)(2,1)}, f32[1,3072]{1,0:T(...) custom-call(s32[32]{0:T(128)} %and_select_fusion.2.place_ref, s32[1]{0:T(128)} %bitcast.me_ref, ...), custom_call_target="tpu_custom_call" | custom-call | flops 1 | bytes 1 | tf_op jit(solution)/shard_map/mlp/pallas_call | solution.py:577
  136.8 7.3 %second_norm_back.1 = (f32[392,768]{1,0:T(8,128)}, bf16[392,768]{1,0:T(8,128)(2,1)}, bf16[384,768]{1,0:T(8,128)(2,1)}, bf16[384,768]{1,0:T(8,128)(2,1)}, f32[8,768]{1,0:T(8,128)}) custom-call(f32[392,768]{1,0:T(8,128)} %get-tuple-element.173.grad_normed_ref, f32[392,768]{1,0:T(8,128)} %get-tuple-element.165.rest_4_.residual_ref, ...), custom_call_target="tpu_custom_call" | custom-call | flops 1 | bytes 1 | tf_op jit(solution)/shard_map/second_norm_back/pallas_call | solution.py:626
  144.3 2.0 collective-permute-done.23.refs_3_
  147.2 4.4 %add_ranges.8 = (bf16[96,3840]{1,0:T(8,128)(2,1)}, bf16[96,3840]{1,0:T(8,128)(2,1)}, bf16[96,3840]{1,0:T(8,128)(2,1)}, bf16[96,3840]{1,0:T(8,128)(2,1)}) custom-call(bf16[384,3072]{1,0:T(8,128)(2,1)} %get-tuple-element.177.refs_0_, bf16[384,3072]{1,0:T(8,128)(2,1)} %bitcast.18.refs_1_, bf16[384,768]{1,0:T(8,128)(2,1)} %get-tuple-element.179.refs_2_, ...), custom_call_target="tpu_custom_call" | custom-call | flops 1 | bytes 1 | tf_op jit(solution)/shard_map/add_ranges/pallas_call | solution.py:758
  154.9 3.4 %add_ranges.9 = (bf16[384,768]{1,0:T(8,128)(2,1)}, bf16[384,768]{1,0:T(8,128)(2,1)}, bf16[384,768]{1,0:T(8,128)(2,1)}, bf16[384,768]{1,0:T(8,128)(2,1)}) custom-call(bf16[1536,768]{1,0:T(8,128)(2,1)} %bitcast.102, bf16[1536,768]{1,0:T(8,128)(2,1)} %bitcast.103), custom_call_target="tpu_custom_call" | custom-call | flops 1 | bytes 1 | tf_op jit(solution)/shard_map/add_ranges/pallas_call | solution.py:758
  158.3 1.7 collective-permute-start.31
  160.6 10.8 %attention_back.1 = (bf16[392,2304]{1,0:T(8,128)(2,1)}, f32[128,128]{1,0:T(8,128)}) custom-call(bf16[392,2304]{1,0:T(8,128)(2,1)} %get-tuple-element.158.q_ref.k_ref.v_ref, bf16[392,2304]{1,0:T(8,128)(2,1)} %get-tuple-element.158.q_ref.k_ref.v_ref, bf16[392,2304]{1,0:T(8,128)(2,1)} %get-tuple-element.158.q_ref.k_ref.v_ref, ...), custom_call_target="tpu_custom_call" | custom-call | flops 1 | bytes 1 | tf_op jit(solution)/shard_map/attention_back/pallas_call | solution.py:258
  172.5 2.7 %add_ranges.10 = (bf16[48,3840]{1,0:T(8,128)(2,1)}, bf16[48,3840]{1,0:T(8,128)(2,1)}, bf16[48,3840]{1,0:T(8,128)(2,1)}, bf16[48,3840]{1,0:T(8,128)(2,1)}) custom-call(bf16[96,3840]{1,0:T(8,128)(2,1)} %get-tuple-element.189.refs_0_, bf16[96,3840]{1,0:T(8,128)(2,1)} %bitcast.108, bf16[96,3840]{1,0:T(8,128)(2,1)} %get-tuple-element.191.refs_2_, ...), custom_call_target="tpu_custom_call" | custom-call | flops 1 | bytes 1 | tf_op jit(solution)/shard_map/add_ranges/pallas_call | solution.py:758
  175.2 1.6 collective-permute-start.28
  176.8 1.6 collective-permute-start.27
  178.3 5.2 %weight_grad.1 = (bf16[384,2304]{1,0:T(8,128)(2,1)}, bf16[384,2304]{1,0:T(8,128)(2,1)}) custom-call(bf16[768,392]{1,0:T(8,128)(2,1)} %get-tuple-element.149.turned_ref, bf16[392,2304]{1,0:T(8,128)(2,1)} %get-tuple-element.197.grad_ref), custom_call_target="tpu_custom_call" | custom-call | flops 1 | bytes 1 | tf_op jit(solution)/shard_map/weight_grad/pallas_call | solution.py:706
  183.6 8.6 %first_norm_back.1 = (bf16[392,768]{1,0:T(8,128)(2,1)}, f32[112,128]{1,0:T(8,128)}) custom-call(bf16[392,2304]{1,0:T(8,128)(2,1)} %get-tuple-element.197.grad_ref, bf16[392,768]{1,0:T(8,128)(2,1)} %tokens_ref.4, f32[392,128]{1,0:T(8,128)} %broadcast_in_dim.33.live_ref.rest_2_, f32[1,768]{1,0:T(1,128)} %copy-done.32, bf16[768,768]{1,0:T(8,128)(2,1)} %fusion.order_ref, ...), custom_call_target="tpu_custom_call" | custom-call | flops 1 | bytes 1 | tf_op jit(solution)/shard_map/first_norm_back/pallas_call | solution.py:844
  192.6 2.7 %add_ranges.11 = (bf16[192,768]{1,0:T(8,128)(2,1)}, bf16[192,768]{1,0:T(8,128)(2,1)}, bf16[192,768]{1,0:T(8,128)(2,1)}, bf16[192,768]{1,0:T(8,128)(2,1)}) custom-call(bf16[384,768]{1,0:T(8,128)(2,1)} %get-tuple-element.206.refs_0_, bf16[384,768]{1,0:T(8,128)(2,1)} %bitcast.29.refs_1_, bf16[384,768]{1,0:T(8,128)(2,1)} %get-tuple-element.208.refs_2_, ...), custom_call_target="tpu_custom_call" | custom-call | flops 99999997952 | bytes 1 | tf_op jit(solution)/shard_map/add_ranges/pallas_call | solution.py:758
  198.2 2.9 %add_ranges.12 = (bf16[96,2304]{1,0:T(8,128)(2,1)}, bf16[96,2304]{1,0:T(8,128)(2,1)}, bf16[96,2304]{1,0:T(8,128)(2,1)}, bf16[96,2304]{1,0:T(8,128)(2,1)}) custom-call(bf16[384,2304]{1,0:T(8,128)(2,1)} %get-tuple-element.205.refs_0_, bf16[384,2304]{1,0:T(8,128)(2,1)} %bitcast.105), custom_call_target="tpu_custom_call" | custom-call | flops 1 | bytes 1 | tf_op jit(solution)/shard_map/add_ranges/pallas_call | solution.py:758
  201.1 2.2 add_ranges.13
  204.6 1.6 collective-permute-start.35
  207.7 4.0 %collective-permute-start.32 = (f32[112,128]{1,0:T(8,128)S(1)}, f32[112,128]{1,0:T(8,128)S(1)}, u32[]{:S(2)}, u32[]{:S(2)}) collective-permute-start(f32[112,128]{1,0:T(8,128)S(1)} %add.80), channel_id=1, source_target_pairs={{0,16},{1,17},{2,18},{3,19},{4,20},{5,21},{6,22},{7,23},{8,24},{9,... | collective-permute-start | bytes 172040 | tf_op jit(solution)/shard_map/ppermute | solution.py:907
  212.4 2.1 add_ranges.14
  214.4 1.8 collective-permute-start.42
  218.3 2.4 add_ranges.15
  220.7 1.6 collective-permute-start.40
  222.8 4.0 %collective-permute-start.47 = (bf16[24,3840]{1,0:T(8,128)(2,1)S(1)}, bf16[24,3840]{1,0:T(8,128)(2,1)S(1)}, u32[]{:S(2)}, u32[]{:S(2)}) collective-permute-start(bf16[24,3840]{1,0:T(8,128)(2,1)S(1)} %fusion.3), channel_id=1, source_target_pairs={{0,16},{1,17},{2,18},{3,19},{4,20},{5,21},{6,22},{7,23},{8,24},{9,... | collective-permute-start | bytes 552968 | tf_op jit(solution)/shard_map/ppermute | solution.py:907
  229.5 4.0 %collective-permute-start.44 = (bf16[24,2304]{1,0:T(8,128)(2,1)S(1)}, bf16[24,2304]{1,0:T(8,128)(2,1)S(1)}, u32[]{:S(2)}, u32[]{:S(2)}) collective-permute-start(bf16[24,2304]{1,0:T(8,128)(2,1)S(1)} %fusion.9), channel_id=1, source_target_pairs={{0,16},{1,17},{2,18},{3,19},{4,20},{5,21},{6,22},{7,23},{8,24},{9,... | collective-permute-start | bytes 331784 | tf_op jit(solution)/shard_map/ppermute | solution.py:907
  235.8 3.7 %collective-permute-done.41 = f32[112,128]{1,0:T(8,128)S(1)} collective-permute-done((f32[112,128]{1,0:T(8,128)S(1)}, f32[112,128]{1,0:T(8,128)S(1)}, u32[]{:S(2)}, u32[]{:S(2)}) %collective-permute-start.41) | collective-permute-done | bytes 57376 | tf_op jit(solution)/shard_map/ppermute | solution.py:907
  239.5 2.7 %collective-permute-start.48 = (bf16[96,768]{1,0:T(8,128)(2,1)S(1)}, bf16[96,768]{1,0:T(8,128)(2,1)S(1)}, u32[]{:S(2)}, u32[]{:S(2)}) collective-permute-start(bf16[96,768]{1,0:T(8,128)(2,1)S(1)} %fusion.5), channel_id=1, source_target_pairs={{0,16},{1,17},{2,18},{3,19},{4,20},{5,21},{6,22},{7,23},{8,24},{9,... | collective-permute-start | bytes 442376 | tf_op jit(solution)/shard_map/ppermute | solution.py:907
  247.1 1.5 own_small.1
  (204 shorter events, 58.4 us)
Async XLA Ops:
  3.5 11.4 %collective-permute-start = (bf16[24,3200]{1,0:T(8,128)(2,1)S(1)}, bf16[24,3200]{1,0:T(8,128)(2,1)S(1)}, u32[]{:S(2)}, u32[]{:S(2)}) collective-permute-start(bf16[24,3200]{1,0:T(8,128)(2,1)S(1)} %pad_maximum_fusion.4), channel_id=1, source_target_pairs={{0,16},{1,17},{2,18},{3,19},{4,20},{5,21},{6,22},{7,23},{8,24},{9,... | collective-permute-start | bytes 460808 | tf_op jit(solution)/shard_map/ppermute | solution.py:907
  14.9 13.6 %collective-permute-start.3 = (bf16[2,24,3200]{2,1,0:T(8,128)(2,1)S(1)}, bf16[2,24,3200]{2,1,0:T(8,128)(2,1)S(1)}, u32[]{:S(2)}, u32[]{:S(2)}) collective-permute-start(bf16[2,24,3200]{2,1,0:T(8,128)(2,1)S(1)} %pad_maximum_fusion.1), channel_id=1, source_target_pairs={{0,8},{1,9},{2,10},{3,11},{4,12},{5,13},{6,14},{7,15},{8,0},{9,1},... | collective-permute-start | bytes 921608 | tf_op jit(solution)/shard_map/ppermute | solution.py:907
  15.8 14.0 %collective-permute-start.2 = (bf16[2,24,3200]{2,1,0:T(8,128)(2,1)S(1)}, bf16[2,24,3200]{2,1,0:T(8,128)(2,1)S(1)}, u32[]{:S(2)}, u32[]{:S(2)}) collective-permute-start(bf16[2,24,3200]{2,1,0:T(8,128)(2,1)S(1)} %pad_maximum_fusion.1), channel_id=1, source_target_pairs={{0,2},{1,3},{2,0},{3,1},{4,6},{5,7},{6,4},{7,5},{8,10},{9,11},{10,... | collective-permute-start | bytes 921608 | tf_op jit(solution)/shard_map/ppermute | solution.py:907
  17.2 22.3 %collective-permute-start.1 = (bf16[24,3072]{1,0:T(8,128)(2,1)S(1)}, bf16[24,3072]{1,0:T(8,128)(2,1)S(1)}, u32[]{:S(2)}, u32[]{:S(2)}) collective-permute-start(bf16[24,3072]{1,0:T(8,128)(2,1)S(1)} %convert_element_type.124), channel_id=1, source_target_pairs={{0,16},{1,17},{2,18},{3,19},{4,20},{5,21},{6,22},{7,23},{8,24},{9,... | collective-permute-start | bytes 442376 | tf_op jit(solution)/shard_map/ppermute | solution.py:907
  20.6 19.0 %collective-permute-start.6 = (bf16[96,768]{1,0:T(8,128)(2,1)S(1)}, bf16[96,768]{1,0:T(8,128)(2,1)S(1)}, u32[]{:S(2)}, u32[]{:S(2)}) collective-permute-start(bf16[96,768]{1,0:T(8,128)(2,1)S(1)} %convert_element_type.125), channel_id=1, source_target_pairs={{0,16},{1,17},{2,18},{3,19},{4,20},{5,21},{6,22},{7,23},{8,24},{9,... | collective-permute-start | bytes 442376 | tf_op jit(solution)/shard_map/ppermute | solution.py:907
  28.4 7.5 %collective-permute-start.4 = (bf16[2,24,3200]{2,1,0:T(8,128)(2,1)S(1)}, bf16[2,24,3200]{2,1,0:T(8,128)(2,1)S(1)}, u32[]{:S(2)}, u32[]{:S(2)}) collective-permute-start(bf16[2,24,3200]{2,1,0:T(8,128)(2,1)S(1)} %collective-permute-done.3), channel_id=1, source_target_pairs={{0,4},{1,5},{2,6},{3,7},{4,0},{5,1},{6,2},{7,3},{8,12},{9,13},{10,... | collective-permute-start | bytes 921608 | tf_op jit(solution)/shard_map/ppermute | solution.py:907
  36.1 15.5 %collective-permute-start.9 = (bf16[4,24,3200]{2,1,0:T(8,128)(2,1)S(1)}, bf16[4,24,3200]{2,1,0:T(8,128)(2,1)S(1)}, u32[]{:S(2)}, u32[]{:S(2)}) collective-permute-start(bf16[4,24,3200]{2,1,0:T(8,128)(2,1)S(1)} %constant_dynamic-update-slice_fusion.refs_2_), channel_id=1, source_target_pairs={{0,2},{1,3},{2,0},{3,1},{4,6},{5,7},{6,4},{7,5},{8,10},{9,11},{10,... | collective-permute-start | bytes 1843208 | tf_op jit(solution)/shard_map/ppermute | solution.py:907
  38.1 13.6 %collective-permute-start.8 = (bf16[4,24,3200]{2,1,0:T(8,128)(2,1)S(1)}, bf16[4,24,3200]{2,1,0:T(8,128)(2,1)S(1)}, u32[]{:S(2)}, u32[]{:S(2)}) collective-permute-start(bf16[4,24,3200]{2,1,0:T(8,128)(2,1)S(1)} %pad_maximum_fusion.refs_0_), channel_id=1, source_target_pairs={{0,4},{1,5},{2,6},{3,7},{4,0},{5,1},{6,2},{7,3},{8,12},{9,13},{10,... | collective-permute-start | bytes 1843208 | tf_op jit(solution)/shard_map/ppermute | solution.py:907
  39.6 8.7 %collective-permute-start.5 = (bf16[2,24,3072]{2,1,0:T(8,128)(2,1)S(1)}, bf16[2,24,3072]{2,1,0:T(8,128)(2,1)S(1)}, u32[]{:S(2)}, u32[]{:S(2)}) collective-permute-start(bf16[2,24,3072]{2,1,0:T(8,128)(2,1)S(1)} %pad_maximum_fusion.2.refs_0_), channel_id=1, source_target_pairs={{0,8},{1,9},{2,10},{3,11},{4,12},{5,13},{6,14},{7,15},{8,0},{9,1},... | collective-permute-start | bytes 884744 | tf_op jit(solution)/shard_map/ppermute | solution.py:907
  39.8 11.9 %collective-permute-start.7 = (bf16[2,96,768]{2,1,0:T(8,128)(2,1)S(1)}, bf16[2,96,768]{2,1,0:T(8,128)(2,1)}, u32[]{:S(2)}, u32[]{:S(2)}) collective-permute-start(bf16[2,96,768]{2,1,0:T(8,128)(2,1)S(1)} %pad_maximum_fusion.3.refs_0_), channel_id=1, source_target_pairs={{0,8},{1,9},{2,10},{3,11},{4,12},{5,13},{6,14},{7,15},{8,0},{9,1},... | collective-permute-start | bytes 884744 | tf_op jit(solution)/shard_map/ppermute | solution.py:907
  55.4 5.0 %collective-permute-start.10 = (bf16[16,24,3200]{2,1,0:T(8,128)(2,1)}, bf16[16,24,3200]{2,1,0:T(8,128)(2,1)S(1)}, u32[]{:S(2)}, u32[]{:S(2)}) collective-permute-start(bf16[16,24,3200]{2,1,0:T(8,128)(2,1)} %join.5.refs_0_), channel_id=1, source_target_pairs={{0,1},{1,0},{2,3},{3,2},{4,5},{5,4},{6,7},{7,6},{8,9},{9,8},{10,11... | collective-permute-start | bytes 7372808 | tf_op jit(solution)/shard_map/ppermute | solution.py:907
  55.5 20.5 %collective-permute-start.11 = (bf16[2,24,3072]{2,1,0:T(8,128)(2,1)S(1)}, bf16[2,24,3072]{2,1,0:T(8,128)(2,1)S(1)}, u32[]{:S(2)}, u32[]{:S(2)}) collective-permute-start(bf16[2,24,3072]{2,1,0:T(8,128)(2,1)S(1)} %pad_maximum_fusion.2.refs_0_), channel_id=1, source_target_pairs={{0,2},{1,3},{2,0},{3,1},{4,6},{5,7},{6,4},{7,5},{8,10},{9,11},{10,... | collective-permute-start | bytes 884744 | tf_op jit(solution)/shard_map/ppermute | solution.py:907
  55.9 16.9 %collective-permute-start.13 = (bf16[2,96,768]{2,1,0:T(8,128)(2,1)S(1)}, bf16[2,96,768]{2,1,0:T(8,128)(2,1)}, u32[]{:S(2)}, u32[]{:S(2)}) collective-permute-start(bf16[2,96,768]{2,1,0:T(8,128)(2,1)S(1)} %pad_maximum_fusion.3.refs_0_), channel_id=1, source_target_pairs={{0,2},{1,3},{2,0},{3,1},{4,6},{5,7},{6,4},{7,5},{8,10},{9,11},{10,... | collective-permute-start | bytes 884744 | tf_op jit(solution)/shard_map/ppermute | solution.py:907
  57.6 18.4 %collective-permute-start.12 = (bf16[2,24,3072]{2,1,0:T(8,128)(2,1)S(1)}, bf16[2,24,3072]{2,1,0:T(8,128)(2,1)S(1)}, u32[]{:S(2)}, u32[]{:S(2)}) collective-permute-start(bf16[2,24,3072]{2,1,0:T(8,128)(2,1)S(1)} %collective-permute-done.5.refs_2_), channel_id=1, source_target_pairs={{0,4},{1,5},{2,6},{3,7},{4,0},{5,1},{6,2},{7,3},{8,12},{9,13},{10,... | collective-permute-start | bytes 884744 | tf_op jit(solution)/shard_map/ppermute | solution.py:907
  58.1 14.7 %collective-permute-start.14 = (bf16[2,96,768]{2,1,0:T(8,128)(2,1)}, bf16[2,96,768]{2,1,0:T(8,128)(2,1)}, u32[]{:S(2)}, u32[]{:S(2)}) collective-permute-start(bf16[2,96,768]{2,1,0:T(8,128)(2,1)} %collective-permute-done.7.refs_2_), channel_id=1, source_target_pairs={{0,4},{1,5},{2,6},{3,7},{4,0},{5,1},{6,2},{7,3},{8,12},{9,13},{10,... | collective-permute-start | bytes 884744 | tf_op jit(solution)/shard_map/ppermute | solution.py:907
  74.9 18.4 %collective-permute-start.15 = (bf16[4,96,768]{2,1,0:T(8,128)(2,1)}, bf16[4,96,768]{2,1,0:T(8,128)(2,1)S(1)}, u32[]{:S(2)}, u32[]{:S(2)}) collective-permute-start(bf16[4,96,768]{2,1,0:T(8,128)(2,1)} %get-tuple-element.156.refs_0_), channel_id=1, source_target_pairs={{0,4},{1,5},{2,6},{3,7},{4,0},{5,1},{6,2},{7,3},{8,12},{9,13},{10,... | collective-permute-start | bytes 1769480 | tf_op jit(solution)/shard_map/ppermute | solution.py:907
  75.5 17.8 %collective-permute-start.16 = (bf16[4,96,768]{2,1,0:T(8,128)(2,1)}, bf16[4,96,768]{2,1,0:T(8,128)(2,1)S(1)}, u32[]{:S(2)}, u32[]{:S(2)}) collective-permute-start(bf16[4,96,768]{2,1,0:T(8,128)(2,1)} %get-tuple-element.157.refs_2_), channel_id=1, source_target_pairs={{0,2},{1,3},{2,0},{3,1},{4,6},{5,7},{6,4},{7,5},{8,10},{9,11},{10,... | collective-permute-start | bytes 1769480 | tf_op jit(solution)/shard_map/ppermute | solution.py:907
  79.4 23.8 %collective-permute-start.17 = (bf16[4,24,3072]{2,1,0:T(8,128)(2,1)}, bf16[4,24,3072]{2,1,0:T(8,128)(2,1)S(1)}, u32[]{:S(2)}, u32[]{:S(2)}) collective-permute-start(bf16[4,24,3072]{2,1,0:T(8,128)(2,1)} %get-tuple-element.152.refs_0_), channel_id=1, source_target_pairs={{0,4},{1,5},{2,6},{3,7},{4,0},{5,1},{6,2},{7,3},{8,12},{9,13},{10,... | collective-permute-start | bytes 1769480 | tf_op jit(solution)/shard_map/ppermute | solution.py:907
  80.9 22.5 %collective-permute-start.18 = (bf16[4,24,3072]{2,1,0:T(8,128)(2,1)}, bf16[4,24,3072]{2,1,0:T(8,128)(2,1)S(1)}, u32[]{:S(2)}, u32[]{:S(2)}) collective-permute-start(bf16[4,24,3072]{2,1,0:T(8,128)(2,1)} %get-tuple-element.153.refs_2_), channel_id=1, source_target_pairs={{0,2},{1,3},{2,0},{3,1},{4,6},{5,7},{6,4},{7,5},{8,10},{9,11},{10,... | collective-permute-start | bytes 1769480 | tf_op jit(solution)/shard_map/ppermute | solution.py:907
  96.9 10.3 %collective-permute-start.20 = (bf16[16,96,768]{2,1,0:T(8,128)(2,1)}, bf16[16,96,768]{2,1,0:T(8,128)(2,1)S(1)}, u32[]{:S(2)}, u32[]{:S(2)}) collective-permute-start(bf16[16,96,768]{2,1,0:T(8,128)(2,1)} %join.8), channel_id=1, source_target_pairs={{0,1},{1,0},{2,3},{3,2},{4,5},{5,4},{6,7},{7,6},{8,9},{9,8},{10,11... | collective-permute-start | bytes 7077896 | tf_op jit(solution)/shard_map/ppermute | solution.py:907
  106.9 4.9 %collective-permute-start.19 = (bf16[16,24,3072]{2,1,0:T(8,128)(2,1)}, bf16[16,24,3072]{2,1,0:T(8,128)(2,1)}, u32[]{:S(2)}, u32[]{:S(2)}) collective-permute-start(bf16[16,24,3072]{2,1,0:T(8,128)(2,1)} %join.9), channel_id=1, source_target_pairs={{0,1},{1,0},{2,3},{3,2},{4,5},{5,4},{6,7},{7,6},{8,9},{9,8},{10,11... | collective-permute-start | bytes 7077896 | tf_op jit(solution)/shard_map/ppermute | solution.py:907
  136.2 8.1 %collective-permute-start.22 = (bf16[16,24,3072]{2,1,0:T(8,128)(2,1)}, bf16[16,24,3072]{2,1,0:T(8,128)(2,1)}, u32[]{:S(2)}, u32[]{:S(2)}) collective-permute-start(bf16[16,24,3072]{2,1,0:T(8,128)(2,1)} %bitcast.124), channel_id=1, source_target_pairs={{0,1},{1,0},{2,3},{3,2},{4,5},{5,4},{6,7},{7,6},{8,9},{9,8},{10,11... | collective-permute-start | bytes 7077896 | tf_op jit(solution)/shard_map/ppermute | solution.py:907
  136.4 17.0 %collective-permute-start.21 = (bf16[16,96,768]{2,1,0:T(8,128)(2,1)}, bf16[16,96,768]{2,1,0:T(8,128)(2,1)S(1)}, u32[]{:S(2)}, u32[]{:S(2)}) collective-permute-start(bf16[16,96,768]{2,1,0:T(8,128)(2,1)} %get-tuple-element.172), channel_id=1, source_target_pairs={{0,1},{1,0},{2,3},{3,2},{4,5},{5,4},{6,7},{7,6},{8,9},{9,8},{10,11... | collective-permute-start | bytes 7077896 | tf_op jit(solution)/shard_map/ppermute | solution.py:907
  151.5 19.9 %collective-permute-start.25 = (bf16[4,24,3840]{2,1,0:T(8,128)(2,1)}, bf16[4,24,3840]{2,1,0:T(8,128)(2,1)S(1)}, u32[]{:S(2)}, u32[]{:S(2)}) collective-permute-start(bf16[4,24,3840]{2,1,0:T(8,128)(2,1)} %bitcast.127), channel_id=1, source_target_pairs={{0,2},{1,3},{2,0},{3,1},{4,6},{5,7},{6,4},{7,5},{8,10},{9,11},{10,... | collective-permute-start | bytes 2211848 | tf_op jit(solution)/shard_map/ppermute | solution.py:907
  152.0 19.6 %collective-permute-start.24 = (bf16[4,24,3840]{2,1,0:T(8,128)(2,1)}, bf16[4,24,3840]{2,1,0:T(8,128)(2,1)S(1)}, u32[]{:S(2)}, u32[]{:S(2)}) collective-permute-start(bf16[4,24,3840]{2,1,0:T(8,128)(2,1)} %bitcast.126), channel_id=1, source_target_pairs={{0,4},{1,5},{2,6},{3,7},{4,0},{5,1},{6,2},{7,3},{8,12},{9,13},{10,... | collective-permute-start | bytes 2211848 | tf_op jit(solution)/shard_map/ppermute | solution.py:907
  158.3 33.9 %collective-permute-start.31 = (bf16[4,96,768]{2,1,0:T(8,128)(2,1)}, bf16[4,96,768]{2,1,0:T(8,128)(2,1)}, u32[]{:S(2)}, u32[]{:S(2)}) collective-permute-start(bf16[4,96,768]{2,1,0:T(8,128)(2,1)} %bitcast.129), channel_id=1, source_target_pairs={{0,2},{1,3},{2,0},{3,1},{4,6},{5,7},{6,4},{7,5},{8,10},{9,11},{10,... | collective-permute-start | bytes 1769480 | tf_op jit(solution)/shard_map/ppermute | solution.py:907
  160.0 32.5 %collective-permute-start.30 = (bf16[4,96,768]{2,1,0:T(8,128)(2,1)}, bf16[4,96,768]{2,1,0:T(8,128)(2,1)}, u32[]{:S(2)}, u32[]{:S(2)}) collective-permute-start(bf16[4,96,768]{2,1,0:T(8,128)(2,1)} %bitcast.128), channel_id=1, source_target_pairs={{0,4},{1,5},{2,6},{3,7},{4,0},{5,1},{6,2},{7,3},{8,12},{9,13},{10,... | collective-permute-start | bytes 1769480 | tf_op jit(solution)/shard_map/ppermute | solution.py:907
  175.2 17.3 %collective-permute-start.28 = (bf16[2,24,3840]{2,1,0:T(8,128)(2,1)}, bf16[2,24,3840]{2,1,0:T(8,128)(2,1)S(1)}, u32[]{:S(2)}, u32[]{:S(2)}) collective-permute-start(bf16[2,24,3840]{2,1,0:T(8,128)(2,1)} %bitcast.134), channel_id=1, source_target_pairs={{0,4},{1,5},{2,6},{3,7},{4,0},{5,1},{6,2},{7,3},{8,12},{9,13},{10,... | collective-permute-start | bytes 1105928 | tf_op jit(solution)/shard_map/ppermute | solution.py:907
  176.8 15.8 %collective-permute-start.27 = (bf16[2,24,3840]{2,1,0:T(8,128)(2,1)}, bf16[2,24,3840]{2,1,0:T(8,128)(2,1)S(1)}, u32[]{:S(2)}, u32[]{:S(2)}) collective-permute-start(bf16[2,24,3840]{2,1,0:T(8,128)(2,1)} %bitcast.133), channel_id=1, source_target_pairs={{0,2},{1,3},{2,0},{3,1},{4,6},{5,7},{6,4},{7,5},{8,10},{9,11},{10,... | collective-permute-start | bytes 1105928 | tf_op jit(solution)/shard_map/ppermute | solution.py:907
  183.6 13.4 %collective-permute-start.29 = (bf16[16,24,2304]{2,1,0:T(8,128)(2,1)}, bf16[16,24,2304]{2,1,0:T(8,128)(2,1)S(1)}, u32[]{:S(2)}, u32[]{:S(2)}) collective-permute-start(bf16[16,24,2304]{2,1,0:T(8,128)(2,1)} %bitcast.125), channel_id=1, source_target_pairs={{0,1},{1,0},{2,3},{3,2},{4,5},{5,4},{6,7},{7,6},{8,9},{9,8},{10,11... | collective-permute-start | bytes 5308424 | tf_op jit(solution)/shard_map/ppermute | solution.py:907
  192.2 13.9 %collective-permute-start.26 = (f32[112,128]{1,0:T(8,128)}, f32[112,128]{1,0:T(8,128)S(1)}, u32[]{:S(2)}, u32[]{:S(2)}) collective-permute-start(f32[112,128]{1,0:T(8,128)} %get-tuple-element.203), channel_id=1, source_target_pairs={{0,8},{1,9},{2,10},{3,11},{4,12},{5,13},{6,14},{7,15},{8,0},{9,1},... | collective-permute-start | bytes 172040 | tf_op jit(solution)/shard_map/ppermute | solution.py:907
  195.3 12.3 %collective-permute-start.37 = (bf16[2,96,768]{2,1,0:T(8,128)(2,1)}, bf16[2,96,768]{2,1,0:T(8,128)(2,1)S(1)}, u32[]{:S(2)}, u32[]{:S(2)}) collective-permute-start(bf16[2,96,768]{2,1,0:T(8,128)(2,1)} %bitcast.137), channel_id=1, source_target_pairs={{0,4},{1,5},{2,6},{3,7},{4,0},{5,1},{6,2},{7,3},{8,12},{9,13},{10,... | collective-permute-start | bytes 884744 | tf_op jit(solution)/shard_map/ppermute | solution.py:907
  195.9 15.7 %collective-permute-start.36 = (bf16[2,96,768]{2,1,0:T(8,128)(2,1)}, bf16[2,96,768]{2,1,0:T(8,128)(2,1)S(1)}, u32[]{:S(2)}, u32[]{:S(2)}) collective-permute-start(bf16[2,96,768]{2,1,0:T(8,128)(2,1)} %bitcast.136), channel_id=1, source_target_pairs={{0,2},{1,3},{2,0},{3,1},{4,6},{5,7},{6,4},{7,5},{8,10},{9,11},{10,... | collective-permute-start | bytes 884744 | tf_op jit(solution)/shard_map/ppermute | solution.py:907
  203.3 19.4 %collective-permute-start.33 = (bf16[2,24,3840]{2,1,0:T(8,128)(2,1)}, bf16[2,24,3840]{2,1,0:T(8,128)(2,1)S(1)}, u32[]{:S(2)}, u32[]{:S(2)}) collective-permute-start(bf16[2,24,3840]{2,1,0:T(8,128)(2,1)} %bitcast.132), channel_id=1, source_target_pairs={{0,8},{1,9},{2,10},{3,11},{4,12},{5,13},{6,14},{7,15},{8,0},{9,1},... | collective-permute-start | bytes 1105928 | tf_op jit(solution)/shard_map/ppermute | solution.py:907
  204.6 11.7 %collective-permute-start.35 = (bf16[4,24,2304]{2,1,0:T(8,128)(2,1)}, bf16[4,24,2304]{2,1,0:T(8,128)(2,1)S(1)}, u32[]{:S(2)}, u32[]{:S(2)}) collective-permute-start(bf16[4,24,2304]{2,1,0:T(8,128)(2,1)} %bitcast.131), channel_id=1, source_target_pairs={{0,2},{1,3},{2,0},{3,1},{4,6},{5,7},{6,4},{7,5},{8,10},{9,11},{10,... | collective-permute-start | bytes 1327112 | tf_op jit(solution)/shard_map/ppermute | solution.py:907
  206.1 11.4 %collective-permute-start.34 = (bf16[4,24,2304]{2,1,0:T(8,128)(2,1)}, bf16[4,24,2304]{2,1,0:T(8,128)(2,1)S(1)}, u32[]{:S(2)}, u32[]{:S(2)}) collective-permute-start(bf16[4,24,2304]{2,1,0:T(8,128)(2,1)} %bitcast.130), channel_id=1, source_target_pairs={{0,4},{1,5},{2,6},{3,7},{4,0},{5,1},{6,2},{7,3},{8,12},{9,13},{10,... | collective-permute-start | bytes 1327112 | tf_op jit(solution)/shard_map/ppermute | solution.py:907
  207.7 19.2 %collective-permute-start.32 = (f32[112,128]{1,0:T(8,128)S(1)}, f32[112,128]{1,0:T(8,128)S(1)}, u32[]{:S(2)}, u32[]{:S(2)}) collective-permute-start(f32[112,128]{1,0:T(8,128)S(1)} %add.80), channel_id=1, source_target_pairs={{0,16},{1,17},{2,18},{3,19},{4,20},{5,21},{6,22},{7,23},{8,24},{9,... | collective-permute-start | bytes 172040 | tf_op jit(solution)/shard_map/ppermute | solution.py:907
  214.4 20.8 %collective-permute-start.42 = (bf16[2,96,768]{2,1,0:T(8,128)(2,1)}, bf16[2,96,768]{2,1,0:T(8,128)(2,1)S(1)}, u32[]{:S(2)}, u32[]{:S(2)}) collective-permute-start(bf16[2,96,768]{2,1,0:T(8,128)(2,1)} %bitcast.135), channel_id=1, source_target_pairs={{0,8},{1,9},{2,10},{3,11},{4,12},{5,13},{6,14},{7,15},{8,0},{9,1},... | collective-permute-start | bytes 884744 | tf_op jit(solution)/shard_map/ppermute | solution.py:907
  220.7 6.2 %collective-permute-start.40 = (bf16[2,24,2304]{2,1,0:T(8,128)(2,1)}, bf16[2,24,2304]{2,1,0:T(8,128)(2,1)S(1)}, u32[]{:S(2)}, u32[]{:S(2)}) collective-permute-start(bf16[2,24,2304]{2,1,0:T(8,128)(2,1)} %bitcast.139), channel_id=1, source_target_pairs={{0,4},{1,5},{2,6},{3,7},{4,0},{5,1},{6,2},{7,3},{8,12},{9,13},{10,... | collective-permute-start | bytes 663560 | tf_op jit(solution)/shard_map/ppermute | solution.py:907
  222.3 6.1 %collective-permute-start.39 = (bf16[2,24,2304]{2,1,0:T(8,128)(2,1)}, bf16[2,24,2304]{2,1,0:T(8,128)(2,1)S(1)}, u32[]{:S(2)}, u32[]{:S(2)}) collective-permute-start(bf16[2,24,2304]{2,1,0:T(8,128)(2,1)} %bitcast.138), channel_id=1, source_target_pairs={{0,2},{1,3},{2,0},{3,1},{4,6},{5,7},{6,4},{7,5},{8,10},{9,11},{10,... | collective-permute-start | bytes 663560 | tf_op jit(solution)/shard_map/ppermute | solution.py:907
  222.8 19.4 %collective-permute-start.47 = (bf16[24,3840]{1,0:T(8,128)(2,1)S(1)}, bf16[24,3840]{1,0:T(8,128)(2,1)S(1)}, u32[]{:S(2)}, u32[]{:S(2)}) collective-permute-start(bf16[24,3840]{1,0:T(8,128)(2,1)S(1)} %fusion.3), channel_id=1, source_target_pairs={{0,16},{1,17},{2,18},{3,19},{4,20},{5,21},{6,22},{7,23},{8,24},{9,... | collective-permute-start | bytes 552968 | tf_op jit(solution)/shard_map/ppermute | solution.py:907
  226.8 7.9 %collective-permute-start.38 = (f32[112,128]{1,0:T(8,128)S(1)}, f32[112,128]{1,0:T(8,128)S(1)}, u32[]{:S(2)}, u32[]{:S(2)}) collective-permute-start(f32[112,128]{1,0:T(8,128)S(1)} %add.82), channel_id=1, source_target_pairs={{0,1},{1,0},{2,3},{3,2},{4,5},{5,4},{6,7},{7,6},{8,9},{9,8},{10,11... | collective-permute-start | bytes 172040 | tf_op jit(solution)/shard_map/ppermute | solution.py:907
  229.5 14.7 %collective-permute-start.44 = (bf16[24,2304]{1,0:T(8,128)(2,1)S(1)}, bf16[24,2304]{1,0:T(8,128)(2,1)S(1)}, u32[]{:S(2)}, u32[]{:S(2)}) collective-permute-start(bf16[24,2304]{1,0:T(8,128)(2,1)S(1)} %fusion.9), channel_id=1, source_target_pairs={{0,16},{1,17},{2,18},{3,19},{4,20},{5,21},{6,22},{7,23},{8,24},{9,... | collective-permute-start | bytes 331784 | tf_op jit(solution)/shard_map/ppermute | solution.py:907
  233.6 10.7 %collective-permute-start.46 = (bf16[24,2304]{1,0:T(8,128)(2,1)S(1)}, bf16[24,2304]{1,0:T(8,128)(2,1)S(1)}, u32[]{:S(2)}, u32[]{:S(2)}) collective-permute-start(bf16[24,2304]{1,0:T(8,128)(2,1)S(1)} %get-tuple-element.258), channel_id=1, source_target_pairs={{0,24},{1,25},{2,26},{3,27},{4,28},{5,29},{6,30},{7,31},{8,16},{9,... | collective-permute-start | bytes 331784 | tf_op jit(solution)/shard_map/ppermute | solution.py:907
  234.7 9.5 %collective-permute-start.45 = (bf16[24,2304]{1,0:T(8,128)(2,1)S(1)}, bf16[24,2304]{1,0:T(8,128)(2,1)S(1)}, u32[]{:S(2)}, u32[]{:S(2)}) collective-permute-start(bf16[24,2304]{1,0:T(8,128)(2,1)S(1)} %get-tuple-element.259), channel_id=1, source_target_pairs={{0,8},{1,9},{2,10},{3,11},{4,12},{5,13},{6,14},{7,15},{8,0},{9,1},... | collective-permute-start | bytes 331784 | tf_op jit(solution)/shard_map/ppermute | solution.py:907
  235.2 4.2 %collective-permute-start.41 = (f32[112,128]{1,0:T(8,128)S(1)}, f32[112,128]{1,0:T(8,128)S(1)}, u32[]{:S(2)}, u32[]{:S(2)}) collective-permute-start(f32[112,128]{1,0:T(8,128)S(1)} %add.85), channel_id=1, source_target_pairs={{0,2},{1,3},{2,0},{3,1},{4,6},{5,7},{6,4},{7,5},{8,10},{9,11},{10,... | collective-permute-start | bytes 172040 | tf_op jit(solution)/shard_map/ppermute | solution.py:907
  239.5 9.8 %collective-permute-start.48 = (bf16[96,768]{1,0:T(8,128)(2,1)S(1)}, bf16[96,768]{1,0:T(8,128)(2,1)S(1)}, u32[]{:S(2)}, u32[]{:S(2)}) collective-permute-start(bf16[96,768]{1,0:T(8,128)(2,1)S(1)} %fusion.5), channel_id=1, source_target_pairs={{0,16},{1,17},{2,18},{3,19},{4,20},{5,21},{6,22},{7,23},{8,24},{9,... | collective-permute-start | bytes 442376 | tf_op jit(solution)/shard_map/ppermute | solution.py:907
  242.2 4.2 %collective-permute-start.43 = (f32[112,128]{1,0:T(8,128)S(1)}, f32[112,128]{1,0:T(8,128)S(1)}, u32[]{:S(2)}, u32[]{:S(2)}) collective-permute-start(f32[112,128]{1,0:T(8,128)S(1)} %add.87), channel_id=1, source_target_pairs={{0,4},{1,5},{2,6},{3,7},{4,0},{5,1},{6,2},{7,3},{8,12},{9,13},{10,... | collective-permute-start | bytes 172040 | tf_op jit(solution)/shard_map/ppermute | solution.py:907
  (36 other events, 224.1 us)

commit v7 on v6

--- a/solution.py
+++ b/solution.py
@@ -1246,17 +1246,16 @@
         grad_normed, residual, ordered_mixed, live, out_grad, order, vectors, first_pieces
     )
     late.append((kept_proj, hop(sent_proj, 1, count)))
-    sent = up.send([grad_mixed])
-    sent = down.send(sent)
+    sent = down.send([grad_mixed])
+    sent = up.send(sent)
     (grad_mixed,) = after([grad_mixed], sent)
     grad_qkv, tables = attention_back(qkv, grad_mixed, probs, table, onehot, shift)
-    sent = [grad_qkv]
+    kept_qkv, sent_qkv = weight_grad(turned_one, grad_qkv)
+    third_sum = start(scatter_stages([(kept_qkv, sent_qkv)], count, own_third, direct=True))
+    third_sum.send(None)
+    sent = [kept_qkv]
     for _ in range(middle - 1):
         sent = up.send(sent)
-    (grad_qkv,) = after([grad_qkv], sent)
-    kept_qkv, sent_qkv = weight_grad(turned_one, grad_qkv)
-    third_sum = start(scatter_stages([(kept_qkv, sent_qkv)], count, own_third, direct=True))
-    sent = third_sum.send(None)
     (grad_qkv,) = after([grad_qkv], sent)
     tokens_grad, small_sums = first_norm_back(
         grad_qkv,
@@ -1273,8 +1272,8 @@
     small_stages = start(sum_stages(small_sums, count, all_small))
     sent = small_stages.send(None)
     for _ in range(middle - 1):
-        sent = down.send([small_sums] + sent + got_up)
-    sent = third_sum.send(sent)
+        sent = down.send([small_sums] + sent)
+    sent = third_sum.send(sent + got_up)
     sent = up.send(sent)
     (gated_tables,) = after([tables], sent)
     sent = [marker(gated_tables)]

time: 251 us -> 249 us (level)
  waiting for transfers between devices: 39.3 us -> 33.7 us
  starting transfers between devices: 61.2 us -> 63.8 us
    ppermute x49, waiting for transfers between devices: 39.3 us -> 33.7 us  [hop(): return lax.ppermute(array, 'fsdp', [(i, i ^ mask) for i in range(count)])]
    ppermute x49, starting transfers between devices: 61.2 us -> 63.8 us  [hop(): return lax.ppermute(array, 'fsdp', [(i, i ^ mask) for i in range(count)])]
    unnamed x72 -> x74, local copies, waits for them, and re-layouts: 11.7 us -> 12.2 us
  transfers between devices with their start and end apart: 49 -> 49, of which waited for: 16 -> 14; matrix products, arithmetic and copies ran while one was open for 7% -> 7% of each run, Pallas kernels for 36% -> 34%
where the time goes in v7:
time: 249 us; the launch traced here: 247 us
  Pallas kernels  116 us (47%)
  starting transfers between devices  63.8 us (26%)
  waiting for transfers between devices  33.7 us (14%)
  local copies, waits for them, and re-layouts  18.4 us (7%)
  other arithmetic  14.4 us (6%)
    ppermute x49, starting transfers between devices, hop(): return lax.ppermute(array, 'fsdp', [(i, i ^ mask) for i in range(count)])  63.8 us
    ppermute x49, waiting for transfers between devices, hop(): return lax.ppermute(array, 'fsdp', [(i, i ^ mask) for i in range(count)])  33.7 us
    pallas_call x1, Pallas kernels, mlp(): pl.pallas_call(functools.partial(mlp_kernel, split_rows, owners), grid=(S...  24.3 us
    pallas_call x8, Pallas kernels, add_ranges(): pl.pallas_call(functools.partial(add_kernel, widths, plan), in_specs=[HBM...  22.6 us
    unnamed x74, local copies, waits for them, and re-layouts  12.2 us
    pallas_call x5, Pallas kernels, join(): pl.pallas_call(functools.partial(join_kernel, sizes), in_specs=[HBM] * le...  11.9 us
    pallas_call x1, Pallas kernels, attention_back(): pl.pallas_call(attn_bwd_kernel, grid=(PAIRS,), in_specs=columns + [pl.Blo...  10.8 us
    pallas_call x1, Pallas kernels, attention(): pl.pallas_call(attn_fwd_kernel, grid=(PAIRS,), in_specs=columns + constan...  9 us
  transfers between devices with their start and end apart: 49, of which 14 were waited for; matrix products, arithmetic and copies ran while one was open for 7% of the time, Pallas kernels for 34%

profile of v7, /device:TPU:0, one launch (start us, length us, event | category | flops | bytes accessed | tf_op | source)
XLA Modules:
  0.0 247.3 jit_solution(6585909720876175931)
XLA Ops:
  3.5 4.1 %collective-permute-start = (bf16[24,3200]{1,0:T(8,128)(2,1)S(1)}, bf16[24,3200]{1,0:T(8,128)(2,1)S(1)}, u32[]{:S(2)}, u32[]{:S(2)}) collective-permute-start(bf16[24,3200]{1,0:T(8,128)(2,1)S(1)} %pad_maximum_fusion.4), channel_id=1, source_target_pairs={{0,16},{1,17},{2,18},{3,19},{4,20},{5,21},{6,22},{7,23},{8,24},{9,... | collective-permute-start | bytes 460808 | tf_op jit(solution)/shard_map/ppermute | solution.py:907
  15.8 1.5 collective-permute-start.2
  17.2 3.4 %collective-permute-start.1 = (bf16[24,3072]{1,0:T(8,128)(2,1)S(1)}, bf16[24,3072]{1,0:T(8,128)(2,1)S(1)}, u32[]{:S(2)}, u32[]{:S(2)}) collective-permute-start(bf16[24,3072]{1,0:T(8,128)(2,1)S(1)} %convert_element_type.124), channel_id=1, source_target_pairs={{0,16},{1,17},{2,18},{3,19},{4,20},{5,21},{6,22},{7,23},{8,24},{9,... | collective-permute-start | bytes 442376 | tf_op jit(solution)/shard_map/ppermute | solution.py:907
  20.7 7.8 %collective-permute-done.3 = bf16[2,24,3200]{2,1,0:T(8,128)(2,1)S(1)} collective-permute-done((bf16[2,24,3200]{2,1,0:T(8,128)(2,1)S(1)}, bf16[2,24,3200]{2,1,0:T(8,128)(2,1)S(1)}, u32[]{:S(2)}, u32[]{:S(2)}) %collective-permute-start.3) | collective-permute-done | bytes 307232 | tf_op jit(solution)/shard_map/ppermute | solution.py:907
  29.8 6.2 %collective-permute-done.4 = bf16[2,24,3200]{2,1,0:T(8,128)(2,1)S(1)} collective-permute-done((bf16[2,24,3200]{2,1,0:T(8,128)(2,1)S(1)}, bf16[2,24,3200]{2,1,0:T(8,128)(2,1)S(1)}, u32[]{:S(2)}, u32[]{:S(2)}) %collective-permute-start.4) | collective-permute-done | bytes 307232 | tf_op jit(solution)/shard_map/ppermute | solution.py:907
  36.1 2.0 collective-permute-start.9
  38.1 1.5 collective-permute-start.8
  39.8 2.1 collective-permute-start.7
  44.1 4.3 %collective-permute-done.5.refs_2_ = bf16[2,24,3072]{2,1,0:T(8,128)(2,1)S(1)} collective-permute-done((bf16[2,24,3072]{2,1,0:T(8,128)(2,1)S(1)}, bf16[2,24,3072]{2,1,0:T(8,128)(2,1)S(1)}, u32[]{:S(2)}, u32[]{:S(2)}) %collective-permute-start.5) | collective-permute-done | bytes 294944 | tf_op jit(solution)/shard_map/ppermute | solution.py:907
  48.4 3.3 %collective-permute-done.7.refs_2_ = bf16[2,96,768]{2,1,0:T(8,128)(2,1)} collective-permute-done((bf16[2,96,768]{2,1,0:T(8,128)(2,1)S(1)}, bf16[2,96,768]{2,1,0:T(8,128)(2,1)}, u32[]{:S(2)}, u32[]{:S(2)}) %collective-permute-start.7) | collective-permute-done | bytes 294944 | tf_op jit(solution)/shard_map/ppermute | solution.py:907
  52.7 2.6 %join.5.refs_0_ = bf16[16,24,3200]{2,1,0:T(8,128)(2,1)} custom-call(bf16[4,24,3200]{2,1,0:T(8,128)(2,1)} %copy-done.2, bf16[4,24,3200]{2,1,0:T(8,128)(2,1)} %copy-done.12, bf16[4,24,3200]{2,1,0:T(8,128)(2,1)} %copy-done.6, bf16[4,24,3200]{2,1,0:T(8,128)(2,1)} %copy-done.11), custom_call_target="tpu_custom_call" | custom-call | flops 1 | bytes 1 | tf_op jit(solution)/shard_map/join/pallas_call | solution.py:683
  55.9 1.7 collective-permute-start.13
  58.1 1.5 collective-permute-start.14
  61.8 1.9 place.1
  66.3 6.5 %front.1 = (bf16[768,392]{1,0:T(8,128)(2,1)}, bf16[392,2304]{1,0:T(8,128)(2,1)}) custom-call(bf16[392,768]{1,0:T(8,128)(2,1)} %tokens_ref.4, f32[392,128]{1,0:T(8,128)} %broadcast_in_dim.33.live_ref.rest_2_, bf16[768,768]{1,0:T(8,128)(2,1)} %fusion.order_ref, f32[2,768]{1,0:T(2,128)} %pad_maximum_fusion.6.rows_ref, f32[1,2304]{1,0:T(1,128)} %reshape_reshape.11.b_qkv_ref, ...), custom_call_target="tpu_custom_call" | custom-call | flops 1 | bytes 1 | tf_op jit(solution)/shard_map/front/pallas_call | solution.py:357
  72.8 2.1 join.7
  77.3 2.0 join.6
  79.4 1.5 collective-permute-start.17
  80.9 1.7 collective-permute-start.18
  82.6 9.0 %attention.1 = (bf16[392,768]{1,0:T(8,128)(2,1)}, f32[6,4,200,256]{3,2,1,0:T(8,128)}) custom-call(bf16[392,2304]{1,0:T(8,128)(2,1)} %get-tuple-element.157.q_ref.k_ref.v_ref, bf16[392,2304]{1,0:T(8,128)(2,1)} %get-tuple-element.157.q_ref.k_ref.v_ref, bf16[392,2304]{1,0:T(8,128)(2,1)} %get-tuple-element.157.q_ref.k_ref.v_ref, ...), custom_call_target="tpu_custom_call" | custom-call | flops 1 | bytes 1 | tf_op jit(solution)/shard_map/attention/pallas_call | solution.py:240
  94.3 2.6 %join.8 = bf16[16,96,768]{2,1,0:T(8,128)(2,1)} custom-call(bf16[4,96,768]{2,1,0:T(8,128)(2,1)} %get-tuple-element.155.refs_0_, bf16[4,96,768]{2,1,0:T(8,128)(2,1)} %copy-done.13, bf16[4,96,768]{2,1,0:T(8,128)(2,1)} %get-tuple-element.156.refs_2_, bf16[4,96,768]{2,1,0:T(8,128)(2,1)} %copy-done.15), custom_call_target="tpu_custom_call" | custom-call | flops 1 | bytes 1 | tf_op jit(solution)/shard_map/join/pallas_call | solution.py:683
  97.0 6.0 %project.1 = (f32[392,768]{1,0:T(8,128)}, bf16[392,768]{1,0:T(8,128)(2,1)}, bf16[768,392]{1,0:T(8,128)(2,1)}, bf16[392,768]{1,0:T(8,128)(2,1)}) custom-call(bf16[392,768]{1,0:T(8,128)(2,1)} %tokens_ref.4, bf16[392,768]{1,0:T(8,128)(2,1)} %get-tuple-element.161.values_ref, bf16[768,768]{1,0:T(8,128)(2,1)} %fusion.order_ref, ...), custom_call_target="tpu_custom_call" | custom-call | flops 1 | bytes 1 | tf_op jit(solution)/shard_map/project/pallas_call | solution.py:536
  104.3 2.6 %join.9 = bf16[16,24,3072]{2,1,0:T(8,128)(2,1)} custom-call(bf16[4,24,3072]{2,1,0:T(8,128)(2,1)} %get-tuple-element.151.refs_0_, bf16[4,24,3072]{2,1,0:T(8,128)(2,1)} %copy-done.14, bf16[4,24,3072]{2,1,0:T(8,128)(2,1)} %get-tuple-element.152.refs_2_, bf16[4,24,3072]{2,1,0:T(8,128)(2,1)} %copy-done.16), custom_call_target="tpu_custom_call" | custom-call | flops 1 | bytes 1 | tf_op jit(solution)/shard_map/join/pallas_call | solution.py:683
  107.2 4.6 %collective-permute-done.19 = bf16[16,24,3072]{2,1,0:T(8,128)(2,1)} collective-permute-done((bf16[16,24,3072]{2,1,0:T(8,128)(2,1)}, bf16[16,24,3072]{2,1,0:T(8,128)(2,1)}, u32[]{:S(2)}, u32[]{:S(2)}) %collective-permute-start.19) | collective-permute-done | bytes 2359328 | tf_op jit(solution)/shard_map/ppermute | solution.py:907
  111.8 24.3 %mlp.1 = (bf16[392,768]{1,0:T(8,128)(2,1)}, f32[392,768]{1,0:T(8,128)}, bf16[384,3072]{1,0:T(8,128)(2,1)}, bf16[384,3072]{1,0:T(8,128)(2,1)}, f32[1,3072]{1,0:T(...) custom-call(s32[32]{0:T(128)} %and_select_fusion.2.place_ref, s32[1]{0:T(128)} %bitcast.me_ref, ...), custom_call_target="tpu_custom_call" | custom-call | flops 1 | bytes 1 | tf_op jit(solution)/shard_map/mlp/pallas_call | solution.py:577
  136.7 7.3 %second_norm_back.1 = (f32[392,768]{1,0:T(8,128)}, bf16[392,768]{1,0:T(8,128)(2,1)}, bf16[384,768]{1,0:T(8,128)(2,1)}, bf16[384,768]{1,0:T(8,128)(2,1)}, f32[8,768]{1,0:T(8,128)}) custom-call(f32[392,768]{1,0:T(8,128)} %get-tuple-element.172.grad_normed_ref, f32[392,768]{1,0:T(8,128)} %get-tuple-element.164.rest_4_.residual_ref, ...), custom_call_target="tpu_custom_call" | custom-call | flops 1 | bytes 1 | tf_op jit(solution)/shard_map/second_norm_back/pallas_call | solution.py:626
  145.8 3.4 %add_ranges.8 = (bf16[384,768]{1,0:T(8,128)(2,1)}, bf16[384,768]{1,0:T(8,128)(2,1)}, bf16[384,768]{1,0:T(8,128)(2,1)}, bf16[384,768]{1,0:T(8,128)(2,1)}) custom-call(bf16[1536,768]{1,0:T(8,128)(2,1)} %bitcast.102, bf16[1536,768]{1,0:T(8,128)(2,1)} %bitcast.103), custom_call_target="tpu_custom_call" | custom-call | flops 1 | bytes 1 | tf_op jit(solution)/shard_map/add_ranges/pallas_call | solution.py:758
  150.1 4.4 %add_ranges.9 = (bf16[96,3840]{1,0:T(8,128)(2,1)}, bf16[96,3840]{1,0:T(8,128)(2,1)}, bf16[96,3840]{1,0:T(8,128)(2,1)}, bf16[96,3840]{1,0:T(8,128)(2,1)}) custom-call(bf16[384,3072]{1,0:T(8,128)(2,1)} %get-tuple-element.175.refs_0_, bf16[384,3072]{1,0:T(8,128)(2,1)} %bitcast.21.refs_1_, bf16[384,768]{1,0:T(8,128)(2,1)} %get-tuple-element.181.refs_2_, ...), custom_call_target="tpu_custom_call" | custom-call | flops 1 | bytes 1 | tf_op jit(solution)/shard_map/add_ranges/pallas_call | solution.py:758
  156.4 1.7 collective-permute-start.31
  158.7 10.8 %attention_back.1 = (bf16[392,2304]{1,0:T(8,128)(2,1)}, f32[128,128]{1,0:T(8,128)}) custom-call(bf16[392,2304]{1,0:T(8,128)(2,1)} %get-tuple-element.157.q_ref.k_ref.v_ref, bf16[392,2304]{1,0:T(8,128)(2,1)} %get-tuple-element.157.q_ref.k_ref.v_ref, bf16[392,2304]{1,0:T(8,128)(2,1)} %get-tuple-element.157.q_ref.k_ref.v_ref, ...), custom_call_target="tpu_custom_call" | custom-call | flops 1 | bytes 1 | tf_op jit(solution)/shard_map/attention_back/pallas_call | solution.py:258
  169.5 5.2 %weight_grad.1 = (bf16[384,2304]{1,0:T(8,128)(2,1)}, bf16[384,2304]{1,0:T(8,128)(2,1)}) custom-call(bf16[768,392]{1,0:T(8,128)(2,1)} %get-tuple-element.148.turned_ref, bf16[392,2304]{1,0:T(8,128)(2,1)} %get-tuple-element.195.grad_ref), custom_call_target="tpu_custom_call" | custom-call | flops 1 | bytes 1 | tf_op jit(solution)/shard_map/weight_grad/pallas_call | solution.py:706
  175.9 2.7 %add_ranges.10 = (bf16[48,3840]{1,0:T(8,128)(2,1)}, bf16[48,3840]{1,0:T(8,128)(2,1)}, bf16[48,3840]{1,0:T(8,128)(2,1)}, bf16[48,3840]{1,0:T(8,128)(2,1)}) custom-call(bf16[96,3840]{1,0:T(8,128)(2,1)} %get-tuple-element.188.refs_0_, bf16[96,3840]{1,0:T(8,128)(2,1)} %bitcast.108, bf16[96,3840]{1,0:T(8,128)(2,1)} %get-tuple-element.191.refs_2_, ...), custom_call_target="tpu_custom_call" | custom-call | flops 1 | bytes 1 | tf_op jit(solution)/shard_map/add_ranges/pallas_call | solution.py:758
  181.3 8.6 %first_norm_back.1 = (bf16[392,768]{1,0:T(8,128)(2,1)}, f32[112,128]{1,0:T(8,128)}) custom-call(bf16[392,2304]{1,0:T(8,128)(2,1)} %get-tuple-element.195.grad_ref, bf16[392,768]{1,0:T(8,128)(2,1)} %tokens_ref.4, f32[392,128]{1,0:T(8,128)} %broadcast_in_dim.33.live_ref.rest_2_, f32[1,768]{1,0:T(1,128)} %copy-done.32, bf16[768,768]{1,0:T(8,128)(2,1)} %fusion.order_ref, ...), custom_call_target="tpu_custom_call" | custom-call | flops 1 | bytes 1 | tf_op jit(solution)/shard_map/first_norm_back/pallas_call | solution.py:844
  190.2 2.5 %add_ranges.11 = (bf16[192,768]{1,0:T(8,128)(2,1)}, bf16[192,768]{1,0:T(8,128)(2,1)}, bf16[192,768]{1,0:T(8,128)(2,1)}, bf16[192,768]{1,0:T(8,128)(2,1)}) custom-call(bf16[384,768]{1,0:T(8,128)(2,1)} %get-tuple-element.204.refs_0_, bf16[384,768]{1,0:T(8,128)(2,1)} %bitcast.29.refs_1_, bf16[384,768]{1,0:T(8,128)(2,1)} %get-tuple-element.206.refs_2_, ...), custom_call_target="tpu_custom_call" | custom-call | flops 99999997952 | bytes 1 | tf_op jit(solution)/shard_map/add_ranges/pallas_call | solution.py:758
  194.1 1.6 collective-permute-start.36
  197.0 2.9 %add_ranges.12 = (bf16[96,2304]{1,0:T(8,128)(2,1)}, bf16[96,2304]{1,0:T(8,128)(2,1)}, bf16[96,2304]{1,0:T(8,128)(2,1)}, bf16[96,2304]{1,0:T(8,128)(2,1)}) custom-call(bf16[384,2304]{1,0:T(8,128)(2,1)} %get-tuple-element.189.refs_0_, bf16[384,2304]{1,0:T(8,128)(2,1)} %bitcast.105), custom_call_target="tpu_custom_call" | custom-call | flops 1 | bytes 1 | tf_op jit(solution)/shard_map/add_ranges/pallas_call | solution.py:758
  200.0 2.2 add_ranges.13
  205.2 5.2 %collective-permute-start.32 = (f32[112,128]{1,0:T(8,128)S(1)}, f32[112,128]{1,0:T(8,128)S(1)}, u32[]{:S(2)}, u32[]{:S(2)}) collective-permute-start(f32[112,128]{1,0:T(8,128)S(1)} %add.80), channel_id=1, source_target_pairs={{0,16},{1,17},{2,18},{3,19},{4,20},{5,21},{6,22},{7,23},{8,24},{9,... | collective-permute-start | bytes 172040 | tf_op jit(solution)/shard_map/ppermute | solution.py:907
  211.1 2.1 add_ranges.14
  214.6 2.4 add_ranges.15
  218.5 1.6 collective-permute-start.39
  220.2 5.3 %collective-permute-start.47 = (bf16[24,3840]{1,0:T(8,128)(2,1)S(1)}, bf16[24,3840]{1,0:T(8,128)(2,1)S(1)}, u32[]{:S(2)}, u32[]{:S(2)}) collective-permute-start(bf16[24,3840]{1,0:T(8,128)(2,1)S(1)} %fusion.3), channel_id=1, source_target_pairs={{0,16},{1,17},{2,18},{3,19},{4,20},{5,21},{6,22},{7,23},{8,24},{9,... | collective-permute-start | bytes 552968 | tf_op jit(solution)/shard_map/ppermute | solution.py:907
  226.7 4.4 %collective-permute-start.44 = (bf16[24,2304]{1,0:T(8,128)(2,1)S(1)}, bf16[24,2304]{1,0:T(8,128)(2,1)S(1)}, u32[]{:S(2)}, u32[]{:S(2)}) collective-permute-start(bf16[24,2304]{1,0:T(8,128)(2,1)S(1)} %fusion.9), channel_id=1, source_target_pairs={{0,16},{1,17},{2,18},{3,19},{4,20},{5,21},{6,22},{7,23},{8,24},{9,... | collective-permute-start | bytes 331784 | tf_op jit(solution)/shard_map/ppermute | solution.py:907
  231.8 1.7 collective-permute-start.41
  233.5 2.5 %collective-permute-done.41 = f32[112,128]{1,0:T(8,128)S(1)} collective-permute-done((f32[112,128]{1,0:T(8,128)S(1)}, f32[112,128]{1,0:T(8,128)S(1)}, u32[]{:S(2)}, u32[]{:S(2)}) %collective-permute-start.41) | collective-permute-done | bytes 57376 | tf_op jit(solution)/shard_map/ppermute | solution.py:907
  236.0 3.7 %collective-permute-start.48 = (bf16[96,768]{1,0:T(8,128)(2,1)S(1)}, bf16[96,768]{1,0:T(8,128)(2,1)S(1)}, u32[]{:S(2)}, u32[]{:S(2)}) collective-permute-start(bf16[96,768]{1,0:T(8,128)(2,1)S(1)} %fusion.5), channel_id=1, source_target_pairs={{0,16},{1,17},{2,18},{3,19},{4,20},{5,21},{6,22},{7,23},{8,24},{9,... | collective-permute-start | bytes 442376 | tf_op jit(solution)/shard_map/ppermute | solution.py:907
  242.4 1.6 collective-permute-done.43
  244.6 1.5 own_small.1
  (206 shorter events, 53.9 us)
Async XLA Ops:
  3.5 11.4 %collective-permute-start = (bf16[24,3200]{1,0:T(8,128)(2,1)S(1)}, bf16[24,3200]{1,0:T(8,128)(2,1)S(1)}, u32[]{:S(2)}, u32[]{:S(2)}) collective-permute-start(bf16[24,3200]{1,0:T(8,128)(2,1)S(1)} %pad_maximum_fusion.4), channel_id=1, source_target_pairs={{0,16},{1,17},{2,18},{3,19},{4,20},{5,21},{6,22},{7,23},{8,24},{9,... | collective-permute-start | bytes 460808 | tf_op jit(solution)/shard_map/ppermute | solution.py:907
  14.9 13.6 %collective-permute-start.3 = (bf16[2,24,3200]{2,1,0:T(8,128)(2,1)S(1)}, bf16[2,24,3200]{2,1,0:T(8,128)(2,1)S(1)}, u32[]{:S(2)}, u32[]{:S(2)}) collective-permute-start(bf16[2,24,3200]{2,1,0:T(8,128)(2,1)S(1)} %pad_maximum_fusion.1), channel_id=1, source_target_pairs={{0,8},{1,9},{2,10},{3,11},{4,12},{5,13},{6,14},{7,15},{8,0},{9,1},... | collective-permute-start | bytes 921608 | tf_op jit(solution)/shard_map/ppermute | solution.py:907
  15.8 14.0 %collective-permute-start.2 = (bf16[2,24,3200]{2,1,0:T(8,128)(2,1)S(1)}, bf16[2,24,3200]{2,1,0:T(8,128)(2,1)S(1)}, u32[]{:S(2)}, u32[]{:S(2)}) collective-permute-start(bf16[2,24,3200]{2,1,0:T(8,128)(2,1)S(1)} %pad_maximum_fusion.1), channel_id=1, source_target_pairs={{0,2},{1,3},{2,0},{3,1},{4,6},{5,7},{6,4},{7,5},{8,10},{9,11},{10,... | collective-permute-start | bytes 921608 | tf_op jit(solution)/shard_map/ppermute | solution.py:907
  17.2 22.3 %collective-permute-start.1 = (bf16[24,3072]{1,0:T(8,128)(2,1)S(1)}, bf16[24,3072]{1,0:T(8,128)(2,1)S(1)}, u32[]{:S(2)}, u32[]{:S(2)}) collective-permute-start(bf16[24,3072]{1,0:T(8,128)(2,1)S(1)} %convert_element_type.124), channel_id=1, source_target_pairs={{0,16},{1,17},{2,18},{3,19},{4,20},{5,21},{6,22},{7,23},{8,24},{9,... | collective-permute-start | bytes 442376 | tf_op jit(solution)/shard_map/ppermute | solution.py:907
  20.6 19.0 %collective-permute-start.6 = (bf16[96,768]{1,0:T(8,128)(2,1)S(1)}, bf16[96,768]{1,0:T(8,128)(2,1)S(1)}, u32[]{:S(2)}, u32[]{:S(2)}) collective-permute-start(bf16[96,768]{1,0:T(8,128)(2,1)S(1)} %convert_element_type.125), channel_id=1, source_target_pairs={{0,16},{1,17},{2,18},{3,19},{4,20},{5,21},{6,22},{7,23},{8,24},{9,... | collective-permute-start | bytes 442376 | tf_op jit(solution)/shard_map/ppermute | solution.py:907
  28.4 7.5 %collective-permute-start.4 = (bf16[2,24,3200]{2,1,0:T(8,128)(2,1)S(1)}, bf16[2,24,3200]{2,1,0:T(8,128)(2,1)S(1)}, u32[]{:S(2)}, u32[]{:S(2)}) collective-permute-start(bf16[2,24,3200]{2,1,0:T(8,128)(2,1)S(1)} %collective-permute-done.3), channel_id=1, source_target_pairs={{0,4},{1,5},{2,6},{3,7},{4,0},{5,1},{6,2},{7,3},{8,12},{9,13},{10,... | collective-permute-start | bytes 921608 | tf_op jit(solution)/shard_map/ppermute | solution.py:907
  36.1 15.5 %collective-permute-start.9 = (bf16[4,24,3200]{2,1,0:T(8,128)(2,1)S(1)}, bf16[4,24,3200]{2,1,0:T(8,128)(2,1)S(1)}, u32[]{:S(2)}, u32[]{:S(2)}) collective-permute-start(bf16[4,24,3200]{2,1,0:T(8,128)(2,1)S(1)} %constant_dynamic-update-slice_fusion.refs_2_), channel_id=1, source_target_pairs={{0,2},{1,3},{2,0},{3,1},{4,6},{5,7},{6,4},{7,5},{8,10},{9,11},{10,... | collective-permute-start | bytes 1843208 | tf_op jit(solution)/shard_map/ppermute | solution.py:907
  38.1 13.6 %collective-permute-start.8 = (bf16[4,24,3200]{2,1,0:T(8,128)(2,1)S(1)}, bf16[4,24,3200]{2,1,0:T(8,128)(2,1)S(1)}, u32[]{:S(2)}, u32[]{:S(2)}) collective-permute-start(bf16[4,24,3200]{2,1,0:T(8,128)(2,1)S(1)} %pad_maximum_fusion.refs_0_), channel_id=1, source_target_pairs={{0,4},{1,5},{2,6},{3,7},{4,0},{5,1},{6,2},{7,3},{8,12},{9,13},{10,... | collective-permute-start | bytes 1843208 | tf_op jit(solution)/shard_map/ppermute | solution.py:907
  39.6 8.7 %collective-permute-start.5 = (bf16[2,24,3072]{2,1,0:T(8,128)(2,1)S(1)}, bf16[2,24,3072]{2,1,0:T(8,128)(2,1)S(1)}, u32[]{:S(2)}, u32[]{:S(2)}) collective-permute-start(bf16[2,24,3072]{2,1,0:T(8,128)(2,1)S(1)} %pad_maximum_fusion.2.refs_0_), channel_id=1, source_target_pairs={{0,8},{1,9},{2,10},{3,11},{4,12},{5,13},{6,14},{7,15},{8,0},{9,1},... | collective-permute-start | bytes 884744 | tf_op jit(solution)/shard_map/ppermute | solution.py:907
  39.8 11.9 %collective-permute-start.7 = (bf16[2,96,768]{2,1,0:T(8,128)(2,1)S(1)}, bf16[2,96,768]{2,1,0:T(8,128)(2,1)}, u32[]{:S(2)}, u32[]{:S(2)}) collective-permute-start(bf16[2,96,768]{2,1,0:T(8,128)(2,1)S(1)} %pad_maximum_fusion.3.refs_0_), channel_id=1, source_target_pairs={{0,8},{1,9},{2,10},{3,11},{4,12},{5,13},{6,14},{7,15},{8,0},{9,1},... | collective-permute-start | bytes 884744 | tf_op jit(solution)/shard_map/ppermute | solution.py:907
  55.4 5.0 %collective-permute-start.10 = (bf16[16,24,3200]{2,1,0:T(8,128)(2,1)}, bf16[16,24,3200]{2,1,0:T(8,128)(2,1)S(1)}, u32[]{:S(2)}, u32[]{:S(2)}) collective-permute-start(bf16[16,24,3200]{2,1,0:T(8,128)(2,1)} %join.5.refs_0_), channel_id=1, source_target_pairs={{0,1},{1,0},{2,3},{3,2},{4,5},{5,4},{6,7},{7,6},{8,9},{9,8},{10,11... | collective-permute-start | bytes 7372808 | tf_op jit(solution)/shard_map/ppermute | solution.py:907
  55.4 20.5 %collective-permute-start.11 = (bf16[2,24,3072]{2,1,0:T(8,128)(2,1)S(1)}, bf16[2,24,3072]{2,1,0:T(8,128)(2,1)S(1)}, u32[]{:S(2)}, u32[]{:S(2)}) collective-permute-start(bf16[2,24,3072]{2,1,0:T(8,128)(2,1)S(1)} %pad_maximum_fusion.2.refs_0_), channel_id=1, source_target_pairs={{0,2},{1,3},{2,0},{3,1},{4,6},{5,7},{6,4},{7,5},{8,10},{9,11},{10,... | collective-permute-start | bytes 884744 | tf_op jit(solution)/shard_map/ppermute | solution.py:907
  55.9 16.9 %collective-permute-start.13 = (bf16[2,96,768]{2,1,0:T(8,128)(2,1)S(1)}, bf16[2,96,768]{2,1,0:T(8,128)(2,1)}, u32[]{:S(2)}, u32[]{:S(2)}) collective-permute-start(bf16[2,96,768]{2,1,0:T(8,128)(2,1)S(1)} %pad_maximum_fusion.3.refs_0_), channel_id=1, source_target_pairs={{0,2},{1,3},{2,0},{3,1},{4,6},{5,7},{6,4},{7,5},{8,10},{9,11},{10,... | collective-permute-start | bytes 884744 | tf_op jit(solution)/shard_map/ppermute | solution.py:907
  57.5 18.4 %collective-permute-start.12 = (bf16[2,24,3072]{2,1,0:T(8,128)(2,1)S(1)}, bf16[2,24,3072]{2,1,0:T(8,128)(2,1)S(1)}, u32[]{:S(2)}, u32[]{:S(2)}) collective-permute-start(bf16[2,24,3072]{2,1,0:T(8,128)(2,1)S(1)} %collective-permute-done.5.refs_2_), channel_id=1, source_target_pairs={{0,4},{1,5},{2,6},{3,7},{4,0},{5,1},{6,2},{7,3},{8,12},{9,13},{10,... | collective-permute-start | bytes 884744 | tf_op jit(solution)/shard_map/ppermute | solution.py:907
  58.1 14.7 %collective-permute-start.14 = (bf16[2,96,768]{2,1,0:T(8,128)(2,1)}, bf16[2,96,768]{2,1,0:T(8,128)(2,1)}, u32[]{:S(2)}, u32[]{:S(2)}) collective-permute-start(bf16[2,96,768]{2,1,0:T(8,128)(2,1)} %collective-permute-done.7.refs_2_), channel_id=1, source_target_pairs={{0,4},{1,5},{2,6},{3,7},{4,0},{5,1},{6,2},{7,3},{8,12},{9,13},{10,... | collective-permute-start | bytes 884744 | tf_op jit(solution)/shard_map/ppermute | solution.py:907
  74.9 18.4 %collective-permute-start.15 = (bf16[4,96,768]{2,1,0:T(8,128)(2,1)}, bf16[4,96,768]{2,1,0:T(8,128)(2,1)S(1)}, u32[]{:S(2)}, u32[]{:S(2)}) collective-permute-start(bf16[4,96,768]{2,1,0:T(8,128)(2,1)} %get-tuple-element.155.refs_0_), channel_id=1, source_target_pairs={{0,4},{1,5},{2,6},{3,7},{4,0},{5,1},{6,2},{7,3},{8,12},{9,13},{10,... | collective-permute-start | bytes 1769480 | tf_op jit(solution)/shard_map/ppermute | solution.py:907
  75.5 17.8 %collective-permute-start.16 = (bf16[4,96,768]{2,1,0:T(8,128)(2,1)}, bf16[4,96,768]{2,1,0:T(8,128)(2,1)S(1)}, u32[]{:S(2)}, u32[]{:S(2)}) collective-permute-start(bf16[4,96,768]{2,1,0:T(8,128)(2,1)} %get-tuple-element.156.refs_2_), channel_id=1, source_target_pairs={{0,2},{1,3},{2,0},{3,1},{4,6},{5,7},{6,4},{7,5},{8,10},{9,11},{10,... | collective-permute-start | bytes 1769480 | tf_op jit(solution)/shard_map/ppermute | solution.py:907
  79.4 23.8 %collective-permute-start.17 = (bf16[4,24,3072]{2,1,0:T(8,128)(2,1)}, bf16[4,24,3072]{2,1,0:T(8,128)(2,1)S(1)}, u32[]{:S(2)}, u32[]{:S(2)}) collective-permute-start(bf16[4,24,3072]{2,1,0:T(8,128)(2,1)} %get-tuple-element.151.refs_0_), channel_id=1, source_target_pairs={{0,4},{1,5},{2,6},{3,7},{4,0},{5,1},{6,2},{7,3},{8,12},{9,13},{10,... | collective-permute-start | bytes 1769480 | tf_op jit(solution)/shard_map/ppermute | solution.py:907
  80.9 22.5 %collective-permute-start.18 = (bf16[4,24,3072]{2,1,0:T(8,128)(2,1)}, bf16[4,24,3072]{2,1,0:T(8,128)(2,1)S(1)}, u32[]{:S(2)}, u32[]{:S(2)}) collective-permute-start(bf16[4,24,3072]{2,1,0:T(8,128)(2,1)} %get-tuple-element.152.refs_2_), channel_id=1, source_target_pairs={{0,2},{1,3},{2,0},{3,1},{4,6},{5,7},{6,4},{7,5},{8,10},{9,11},{10,... | collective-permute-start | bytes 1769480 | tf_op jit(solution)/shard_map/ppermute | solution.py:907
  96.9 10.3 %collective-permute-start.20 = (bf16[16,96,768]{2,1,0:T(8,128)(2,1)}, bf16[16,96,768]{2,1,0:T(8,128)(2,1)S(1)}, u32[]{:S(2)}, u32[]{:S(2)}) collective-permute-start(bf16[16,96,768]{2,1,0:T(8,128)(2,1)} %join.8), channel_id=1, source_target_pairs={{0,1},{1,0},{2,3},{3,2},{4,5},{5,4},{6,7},{7,6},{8,9},{9,8},{10,11... | collective-permute-start | bytes 7077896 | tf_op jit(solution)/shard_map/ppermute | solution.py:907
  106.9 4.9 %collective-permute-start.19 = (bf16[16,24,3072]{2,1,0:T(8,128)(2,1)}, bf16[16,24,3072]{2,1,0:T(8,128)(2,1)}, u32[]{:S(2)}, u32[]{:S(2)}) collective-permute-start(bf16[16,24,3072]{2,1,0:T(8,128)(2,1)} %join.9), channel_id=1, source_target_pairs={{0,1},{1,0},{2,3},{3,2},{4,5},{5,4},{6,7},{7,6},{8,9},{9,8},{10,11... | collective-permute-start | bytes 7077896 | tf_op jit(solution)/shard_map/ppermute | solution.py:907
  136.1 8.2 %collective-permute-start.22 = (bf16[16,96,768]{2,1,0:T(8,128)(2,1)}, bf16[16,96,768]{2,1,0:T(8,128)(2,1)S(1)}, u32[]{:S(2)}, u32[]{:S(2)}) collective-permute-start(bf16[16,96,768]{2,1,0:T(8,128)(2,1)} %get-tuple-element.171), channel_id=1, source_target_pairs={{0,1},{1,0},{2,3},{3,2},{4,5},{5,4},{6,7},{7,6},{8,9},{9,8},{10,11... | collective-permute-start | bytes 7077896 | tf_op jit(solution)/shard_map/ppermute | solution.py:907
  136.5 12.8 %collective-permute-start.21 = (bf16[16,24,3072]{2,1,0:T(8,128)(2,1)}, bf16[16,24,3072]{2,1,0:T(8,128)(2,1)}, u32[]{:S(2)}, u32[]{:S(2)}) collective-permute-start(bf16[16,24,3072]{2,1,0:T(8,128)(2,1)} %bitcast.124), channel_id=1, source_target_pairs={{0,1},{1,0},{2,3},{3,2},{4,5},{5,4},{6,7},{7,6},{8,9},{9,8},{10,11... | collective-permute-start | bytes 7077896 | tf_op jit(solution)/shard_map/ppermute | solution.py:907
  144.0 5.2 %collective-permute-start.23 = (bf16[384,768]{1,0:T(8,128)(2,1)}, bf16[384,768]{1,0:T(8,128)(2,1)S(1)}, u32[]{:S(2)}, u32[]{:S(2)}) collective-permute-start(bf16[384,768]{1,0:T(8,128)(2,1)} %get-tuple-element.182), channel_id=1, source_target_pairs={{0,1},{1,0},{2,3},{3,2},{4,5},{5,4},{6,7},{7,6},{8,9},{9,8},{10,11... | collective-permute-start | bytes 1769480 | tf_op jit(solution)/shard_map/ppermute | solution.py:907
  154.5 20.2 %collective-permute-start.25 = (bf16[4,24,3840]{2,1,0:T(8,128)(2,1)}, bf16[4,24,3840]{2,1,0:T(8,128)(2,1)S(1)}, u32[]{:S(2)}, u32[]{:S(2)}) collective-permute-start(bf16[4,24,3840]{2,1,0:T(8,128)(2,1)} %bitcast.127), channel_id=1, source_target_pairs={{0,2},{1,3},{2,0},{3,1},{4,6},{5,7},{6,4},{7,5},{8,10},{9,11},{10,... | collective-permute-start | bytes 2211848 | tf_op jit(solution)/shard_map/ppermute | solution.py:907
  155.0 19.8 %collective-permute-start.24 = (bf16[4,24,3840]{2,1,0:T(8,128)(2,1)}, bf16[4,24,3840]{2,1,0:T(8,128)(2,1)S(1)}, u32[]{:S(2)}, u32[]{:S(2)}) collective-permute-start(bf16[4,24,3840]{2,1,0:T(8,128)(2,1)} %bitcast.126), channel_id=1, source_target_pairs={{0,4},{1,5},{2,6},{3,7},{4,0},{5,1},{6,2},{7,3},{8,12},{9,13},{10,... | collective-permute-start | bytes 2211848 | tf_op jit(solution)/shard_map/ppermute | solution.py:907
  156.4 33.5 %collective-permute-start.31 = (bf16[4,96,768]{2,1,0:T(8,128)(2,1)}, bf16[4,96,768]{2,1,0:T(8,128)(2,1)}, u32[]{:S(2)}, u32[]{:S(2)}) collective-permute-start(bf16[4,96,768]{2,1,0:T(8,128)(2,1)} %bitcast.20), channel_id=1, source_target_pairs={{0,2},{1,3},{2,0},{3,1},{4,6},{5,7},{6,4},{7,5},{8,10},{9,11},{10,... | collective-permute-start | bytes 1769480 | tf_op jit(solution)/shard_map/ppermute | solution.py:907
  158.1 32.2 %collective-permute-start.30 = (bf16[4,96,768]{2,1,0:T(8,128)(2,1)S(1)}, bf16[4,96,768]{2,1,0:T(8,128)(2,1)}, u32[]{:S(2)}, u32[]{:S(2)}) collective-permute-start(bf16[4,96,768]{2,1,0:T(8,128)(2,1)S(1)} %bitcast.128), channel_id=1, source_target_pairs={{0,4},{1,5},{2,6},{3,7},{4,0},{5,1},{6,2},{7,3},{8,12},{9,13},{10,... | collective-permute-start | bytes 1769480 | tf_op jit(solution)/shard_map/ppermute | solution.py:907
  174.7 21.0 %collective-permute-start.29 = (bf16[16,24,2304]{2,1,0:T(8,128)(2,1)}, bf16[16,24,2304]{2,1,0:T(8,128)(2,1)S(1)}, u32[]{:S(2)}, u32[]{:S(2)}) collective-permute-start(bf16[16,24,2304]{2,1,0:T(8,128)(2,1)} %bitcast.125), channel_id=1, source_target_pairs={{0,1},{1,0},{2,3},{3,2},{4,5},{5,4},{6,7},{7,6},{8,9},{9,8},{10,11... | collective-permute-start | bytes 5308424 | tf_op jit(solution)/shard_map/ppermute | solution.py:907
  178.6 15.5 %collective-permute-start.28 = (bf16[2,24,3840]{2,1,0:T(8,128)(2,1)}, bf16[2,24,3840]{2,1,0:T(8,128)(2,1)S(1)}, u32[]{:S(2)}, u32[]{:S(2)}) collective-permute-start(bf16[2,24,3840]{2,1,0:T(8,128)(2,1)} %bitcast.133), channel_id=1, source_target_pairs={{0,4},{1,5},{2,6},{3,7},{4,0},{5,1},{6,2},{7,3},{8,12},{9,13},{10,... | collective-permute-start | bytes 1105928 | tf_op jit(solution)/shard_map/ppermute | solution.py:907
  180.1 15.6 %collective-permute-start.27 = (bf16[2,24,3840]{2,1,0:T(8,128)(2,1)}, bf16[2,24,3840]{2,1,0:T(8,128)(2,1)S(1)}, u32[]{:S(2)}, u32[]{:S(2)}) collective-permute-start(bf16[2,24,3840]{2,1,0:T(8,128)(2,1)} %bitcast.132), channel_id=1, source_target_pairs={{0,2},{1,3},{2,0},{3,1},{4,6},{5,7},{6,4},{7,5},{8,10},{9,11},{10,... | collective-permute-start | bytes 1105928 | tf_op jit(solution)/shard_map/ppermute | solution.py:907
  189.9 13.8 %collective-permute-start.26 = (f32[112,128]{1,0:T(8,128)}, f32[112,128]{1,0:T(8,128)S(1)}, u32[]{:S(2)}, u32[]{:S(2)}) collective-permute-start(f32[112,128]{1,0:T(8,128)} %get-tuple-element.201), channel_id=1, source_target_pairs={{0,8},{1,9},{2,10},{3,11},{4,12},{5,13},{6,14},{7,15},{8,0},{9,1},... | collective-permute-start | bytes 172040 | tf_op jit(solution)/shard_map/ppermute | solution.py:907
  192.7 12.4 %collective-permute-start.37 = (bf16[2,96,768]{2,1,0:T(8,128)(2,1)}, bf16[2,96,768]{2,1,0:T(8,128)(2,1)S(1)}, u32[]{:S(2)}, u32[]{:S(2)}) collective-permute-start(bf16[2,96,768]{2,1,0:T(8,128)(2,1)} %bitcast.136), channel_id=1, source_target_pairs={{0,4},{1,5},{2,6},{3,7},{4,0},{5,1},{6,2},{7,3},{8,12},{9,13},{10,... | collective-permute-start | bytes 884744 | tf_op jit(solution)/shard_map/ppermute | solution.py:907
  194.1 16.2 %collective-permute-start.36 = (bf16[2,96,768]{2,1,0:T(8,128)(2,1)}, bf16[2,96,768]{2,1,0:T(8,128)(2,1)S(1)}, u32[]{:S(2)}, u32[]{:S(2)}) collective-permute-start(bf16[2,96,768]{2,1,0:T(8,128)(2,1)} %bitcast.135), channel_id=1, source_target_pairs={{0,2},{1,3},{2,0},{3,1},{4,6},{5,7},{6,4},{7,5},{8,10},{9,11},{10,... | collective-permute-start | bytes 884744 | tf_op jit(solution)/shard_map/ppermute | solution.py:907
  202.2 17.9 %collective-permute-start.33 = (bf16[2,24,3840]{2,1,0:T(8,128)(2,1)}, bf16[2,24,3840]{2,1,0:T(8,128)(2,1)S(1)}, u32[]{:S(2)}, u32[]{:S(2)}) collective-permute-start(bf16[2,24,3840]{2,1,0:T(8,128)(2,1)} %bitcast.131), channel_id=1, source_target_pairs={{0,8},{1,9},{2,10},{3,11},{4,12},{5,13},{6,14},{7,15},{8,0},{9,1},... | collective-permute-start | bytes 1105928 | tf_op jit(solution)/shard_map/ppermute | solution.py:907
  202.6 11.2 %collective-permute-start.35 = (bf16[4,24,2304]{2,1,0:T(8,128)(2,1)}, bf16[4,24,2304]{2,1,0:T(8,128)(2,1)S(1)}, u32[]{:S(2)}, u32[]{:S(2)}) collective-permute-start(bf16[4,24,2304]{2,1,0:T(8,128)(2,1)} %bitcast.130), channel_id=1, source_target_pairs={{0,2},{1,3},{2,0},{3,1},{4,6},{5,7},{6,4},{7,5},{8,10},{9,11},{10,... | collective-permute-start | bytes 1327112 | tf_op jit(solution)/shard_map/ppermute | solution.py:907
  203.7 10.1 %collective-permute-start.34 = (bf16[4,24,2304]{2,1,0:T(8,128)(2,1)}, bf16[4,24,2304]{2,1,0:T(8,128)(2,1)S(1)}, u32[]{:S(2)}, u32[]{:S(2)}) collective-permute-start(bf16[4,24,2304]{2,1,0:T(8,128)(2,1)} %bitcast.129), channel_id=1, source_target_pairs={{0,4},{1,5},{2,6},{3,7},{4,0},{5,1},{6,2},{7,3},{8,12},{9,13},{10,... | collective-permute-start | bytes 1327112 | tf_op jit(solution)/shard_map/ppermute | solution.py:907
  205.2 20.3 %collective-permute-start.32 = (f32[112,128]{1,0:T(8,128)S(1)}, f32[112,128]{1,0:T(8,128)S(1)}, u32[]{:S(2)}, u32[]{:S(2)}) collective-permute-start(f32[112,128]{1,0:T(8,128)S(1)} %add.80), channel_id=1, source_target_pairs={{0,16},{1,17},{2,18},{3,19},{4,20},{5,21},{6,22},{7,23},{8,24},{9,... | collective-permute-start | bytes 172040 | tf_op jit(solution)/shard_map/ppermute | solution.py:907
  213.1 18.6 %collective-permute-start.42 = (bf16[2,96,768]{2,1,0:T(8,128)(2,1)}, bf16[2,96,768]{2,1,0:T(8,128)(2,1)S(1)}, u32[]{:S(2)}, u32[]{:S(2)}) collective-permute-start(bf16[2,96,768]{2,1,0:T(8,128)(2,1)} %bitcast.134), channel_id=1, source_target_pairs={{0,8},{1,9},{2,10},{3,11},{4,12},{5,13},{6,14},{7,15},{8,0},{9,1},... | collective-permute-start | bytes 884744 | tf_op jit(solution)/shard_map/ppermute | solution.py:907
  217.0 8.6 %collective-permute-start.40 = (bf16[2,24,2304]{2,1,0:T(8,128)(2,1)}, bf16[2,24,2304]{2,1,0:T(8,128)(2,1)S(1)}, u32[]{:S(2)}, u32[]{:S(2)}) collective-permute-start(bf16[2,24,2304]{2,1,0:T(8,128)(2,1)} %bitcast.138), channel_id=1, source_target_pairs={{0,4},{1,5},{2,6},{3,7},{4,0},{5,1},{6,2},{7,3},{8,12},{9,13},{10,... | collective-permute-start | bytes 663560 | tf_op jit(solution)/shard_map/ppermute | solution.py:907
  218.5 7.1 %collective-permute-start.39 = (bf16[2,24,2304]{2,1,0:T(8,128)(2,1)}, bf16[2,24,2304]{2,1,0:T(8,128)(2,1)S(1)}, u32[]{:S(2)}, u32[]{:S(2)}) collective-permute-start(bf16[2,24,2304]{2,1,0:T(8,128)(2,1)} %bitcast.137), channel_id=1, source_target_pairs={{0,2},{1,3},{2,0},{3,1},{4,6},{5,7},{6,4},{7,5},{8,10},{9,11},{10,... | collective-permute-start | bytes 663560 | tf_op jit(solution)/shard_map/ppermute | solution.py:907
  220.2 19.6 %collective-permute-start.47 = (bf16[24,3840]{1,0:T(8,128)(2,1)S(1)}, bf16[24,3840]{1,0:T(8,128)(2,1)S(1)}, u32[]{:S(2)}, u32[]{:S(2)}) collective-permute-start(bf16[24,3840]{1,0:T(8,128)(2,1)S(1)} %fusion.3), channel_id=1, source_target_pairs={{0,16},{1,17},{2,18},{3,19},{4,20},{5,21},{6,22},{7,23},{8,24},{9,... | collective-permute-start | bytes 552968 | tf_op jit(solution)/shard_map/ppermute | solution.py:907
  225.5 5.6 %collective-permute-start.38 = (f32[112,128]{1,0:T(8,128)S(1)}, f32[112,128]{1,0:T(8,128)S(1)}, u32[]{:S(2)}, u32[]{:S(2)}) collective-permute-start(f32[112,128]{1,0:T(8,128)S(1)} %add.82), channel_id=1, source_target_pairs={{0,1},{1,0},{2,3},{3,2},{4,5},{5,4},{6,7},{7,6},{8,9},{9,8},{10,11... | collective-permute-start | bytes 172040 | tf_op jit(solution)/shard_map/ppermute | solution.py:907
  226.7 15.0 %collective-permute-start.44 = (bf16[24,2304]{1,0:T(8,128)(2,1)S(1)}, bf16[24,2304]{1,0:T(8,128)(2,1)S(1)}, u32[]{:S(2)}, u32[]{:S(2)}) collective-permute-start(bf16[24,2304]{1,0:T(8,128)(2,1)S(1)} %fusion.9), channel_id=1, source_target_pairs={{0,16},{1,17},{2,18},{3,19},{4,20},{5,21},{6,22},{7,23},{8,24},{9,... | collective-permute-start | bytes 331784 | tf_op jit(solution)/shard_map/ppermute | solution.py:907
  231.1 10.6 %collective-permute-start.46 = (bf16[24,2304]{1,0:T(8,128)(2,1)S(1)}, bf16[24,2304]{1,0:T(8,128)(2,1)S(1)}, u32[]{:S(2)}, u32[]{:S(2)}) collective-permute-start(bf16[24,2304]{1,0:T(8,128)(2,1)S(1)} %get-tuple-element.256), channel_id=1, source_target_pairs={{0,24},{1,25},{2,26},{3,27},{4,28},{5,29},{6,30},{7,31},{8,16},{9,... | collective-permute-start | bytes 331784 | tf_op jit(solution)/shard_map/ppermute | solution.py:907
  231.1 10.6 %collective-permute-start.45 = (bf16[24,2304]{1,0:T(8,128)(2,1)S(1)}, bf16[24,2304]{1,0:T(8,128)(2,1)S(1)}, u32[]{:S(2)}, u32[]{:S(2)}) collective-permute-start(bf16[24,2304]{1,0:T(8,128)(2,1)S(1)} %get-tuple-element.257), channel_id=1, source_target_pairs={{0,8},{1,9},{2,10},{3,11},{4,12},{5,13},{6,14},{7,15},{8,0},{9,1},... | collective-permute-start | bytes 331784 | tf_op jit(solution)/shard_map/ppermute | solution.py:907
  231.8 4.2 %collective-permute-start.41 = (f32[112,128]{1,0:T(8,128)S(1)}, f32[112,128]{1,0:T(8,128)S(1)}, u32[]{:S(2)}, u32[]{:S(2)}) collective-permute-start(f32[112,128]{1,0:T(8,128)S(1)} %add.85), channel_id=1, source_target_pairs={{0,2},{1,3},{2,0},{3,1},{4,6},{5,7},{6,4},{7,5},{8,10},{9,11},{10,... | collective-permute-start | bytes 172040 | tf_op jit(solution)/shard_map/ppermute | solution.py:907
  236.0 10.6 %collective-permute-start.48 = (bf16[96,768]{1,0:T(8,128)(2,1)S(1)}, bf16[96,768]{1,0:T(8,128)(2,1)S(1)}, u32[]{:S(2)}, u32[]{:S(2)}) collective-permute-start(bf16[96,768]{1,0:T(8,128)(2,1)S(1)} %fusion.5), channel_id=1, source_target_pairs={{0,16},{1,17},{2,18},{3,19},{4,20},{5,21},{6,22},{7,23},{8,24},{9,... | collective-permute-start | bytes 442376 | tf_op jit(solution)/shard_map/ppermute | solution.py:907
  (37 other events, 238.9 us)

commit v8 on v7

--- a/solution.py
+++ b/solution.py
@@ -490,11 +490,25 @@
 ):
     pieces, rest = rest[:PIECES], rest[PIECES:]
     grad_residual_ref, grad_mixed_ref, *rest = rest
-    kept_proj_ref, sent_proj_ref, sums_ref, w_proj, sem = rest
+    kept_proj_ref, sent_proj_ref, sums_ref, w_proj, sem, *rest = rest
+    residual_here, mixed_here, out_grad_here, side_sem = rest
     half = D // 2
+    sides = [
+        pltpu.make_async_copy(source, here, side_sem.at[index])
+        for index, (source, here) in enumerate(
+            (
+                (residual_ref, residual_here),
+                (out_grad_ref, out_grad_here),
+                (mixed_ref, mixed_here),
+            )
+        )
+    ]
+    start_all(sides)
     copies = copy_rows(pieces, (3 * D, D), w_proj, 0, sem)
     start_all(copies)
     grad = natural_order(grad_normed_ref[...], order_ref[...])
+    wait_all(sides)
+    residual_ref, out_grad_ref, mixed_ref = residual_here, out_grad_here, mixed_here
     unit, rstd = normalise(residual_ref[...])
     grad_out = out_grad_ref[...].astype(F32) * live_ref[:, :1]
     grad_residual = grad_out + normalise_back(grad, unit, rstd, rows_ref[1:2, :])
@@ -625,7 +639,7 @@
     rows = residual.shape[0]
     return pl.pallas_call(
         second_norm_kernel,
-        in_specs=[VMEM] * 7 + [HBM] * PIECES,
+        in_specs=[VMEM, HBM, HBM, VMEM, HBM, VMEM, VMEM] + [HBM] * PIECES,
         out_specs=[VMEM] * 5,
         out_shape=[
             struct((rows, D), F32),
@@ -634,7 +648,14 @@
             struct((D // 2, D), BF),
             struct((8, D), F32),
         ],
-        scratch_shapes=[pltpu.VMEM((D, D), BF), pltpu.SemaphoreType.DMA((PIECES,))],
+        scratch_shapes=[
+            pltpu.VMEM((D, D), BF),
+            pltpu.SemaphoreType.DMA((PIECES,)),
+            pltpu.VMEM((rows, D), F32),
+            pltpu.VMEM((rows, D), BF),
+            pltpu.VMEM((rows, D), BF),
+            pltpu.SemaphoreType.DMA((3,)),
+        ],
         cost_estimate=QUICK,
         compiler_params=pltpu.CompilerParams(vmem_limit_bytes=KERNEL_VMEM),
         name="second_norm_back",

time: 249 us -> 249 us (level)
  no operation moved by 1% of the time
where the time goes in v8:
time: 249 us; the launch traced here: 248 us
  Pallas kernels  116 us (47%)
  starting transfers between devices  63.8 us (26%)
  waiting for transfers between devices  33.7 us (14%)
  local copies, waits for them, and re-layouts  18.4 us (7%)
  other arithmetic  14.4 us (6%)
    ppermute x49, starting transfers between devices, hop(): return lax.ppermute(array, 'fsdp', [(i, i ^ mask) for i in range(count)])  63.8 us
    ppermute x49, waiting for transfers between devices, hop(): return lax.ppermute(array, 'fsdp', [(i, i ^ mask) for i in range(count)])  33.7 us
    pallas_call x1, Pallas kernels, mlp(): pl.pallas_call(functools.partial(mlp_kernel, split_rows, owners), grid=(S...  24.3 us
    pallas_call x8, Pallas kernels, add_ranges(): pl.pallas_call(functools.partial(add_kernel, widths, plan), in_specs=[HBM...  22.6 us
    unnamed x74, local copies, waits for them, and re-layouts  12.2 us
    pallas_call x5, Pallas kernels, join(): pl.pallas_call(functools.partial(join_kernel, sizes), in_specs=[HBM] * le...  11.9 us
    pallas_call x1, Pallas kernels, attention_back(): pl.pallas_call(attn_bwd_kernel, grid=(PAIRS,), in_specs=columns + [pl.Blo...  10.9 us
    pallas_call x1, Pallas kernels, attention(): pl.pallas_call(attn_fwd_kernel, grid=(PAIRS,), in_specs=columns + constan...  9 us
  transfers between devices with their start and end apart: 49, of which 14 were waited for; matrix products, arithmetic and copies ran while one was open for 7% of the time, Pallas kernels for 34%

profile of v8, /device:TPU:0, one launch (start us, length us, event | category | flops | bytes accessed | tf_op | source)
XLA Modules:
  0.0 247.6 jit_solution(12795782616527453)
XLA Ops:
  3.5 4.1 %collective-permute-start = (bf16[24,3200]{1,0:T(8,128)(2,1)S(1)}, bf16[24,3200]{1,0:T(8,128)(2,1)S(1)}, u32[]{:S(2)}, u32[]{:S(2)}) collective-permute-start(bf16[24,3200]{1,0:T(8,128)(2,1)S(1)} %pad_maximum_fusion.4), channel_id=1, source_target_pairs={{0,16},{1,17},{2,18},{3,19},{4,20},{5,21},{6,22},{7,23},{8,24},{9,... | collective-permute-start | bytes 460808 | tf_op jit(solution)/shard_map/ppermute | solution.py:928
  15.8 1.5 collective-permute-start.2
  17.2 3.4 %collective-permute-start.1 = (bf16[24,3072]{1,0:T(8,128)(2,1)S(1)}, bf16[24,3072]{1,0:T(8,128)(2,1)S(1)}, u32[]{:S(2)}, u32[]{:S(2)}) collective-permute-start(bf16[24,3072]{1,0:T(8,128)(2,1)S(1)} %convert_element_type.124), channel_id=1, source_target_pairs={{0,16},{1,17},{2,18},{3,19},{4,20},{5,21},{6,22},{7,23},{8,24},{9,... | collective-permute-start | bytes 442376 | tf_op jit(solution)/shard_map/ppermute | solution.py:928
  20.7 7.8 %collective-permute-done.3 = bf16[2,24,3200]{2,1,0:T(8,128)(2,1)S(1)} collective-permute-done((bf16[2,24,3200]{2,1,0:T(8,128)(2,1)S(1)}, bf16[2,24,3200]{2,1,0:T(8,128)(2,1)S(1)}, u32[]{:S(2)}, u32[]{:S(2)}) %collective-permute-start.3) | collective-permute-done | bytes 307232 | tf_op jit(solution)/shard_map/ppermute | solution.py:928
  29.8 6.2 %collective-permute-done.4 = bf16[2,24,3200]{2,1,0:T(8,128)(2,1)S(1)} collective-permute-done((bf16[2,24,3200]{2,1,0:T(8,128)(2,1)S(1)}, bf16[2,24,3200]{2,1,0:T(8,128)(2,1)S(1)}, u32[]{:S(2)}, u32[]{:S(2)}) %collective-permute-start.4) | collective-permute-done | bytes 307232 | tf_op jit(solution)/shard_map/ppermute | solution.py:928
  36.1 2.0 collective-permute-start.9
  38.1 1.5 collective-permute-start.8
  39.8 2.1 collective-permute-start.7
  44.1 4.3 %collective-permute-done.5.refs_2_ = bf16[2,24,3072]{2,1,0:T(8,128)(2,1)S(1)} collective-permute-done((bf16[2,24,3072]{2,1,0:T(8,128)(2,1)S(1)}, bf16[2,24,3072]{2,1,0:T(8,128)(2,1)S(1)}, u32[]{:S(2)}, u32[]{:S(2)}) %collective-permute-start.5) | collective-permute-done | bytes 294944 | tf_op jit(solution)/shard_map/ppermute | solution.py:928
  48.4 3.3 %collective-permute-done.7.refs_2_ = bf16[2,96,768]{2,1,0:T(8,128)(2,1)} collective-permute-done((bf16[2,96,768]{2,1,0:T(8,128)(2,1)S(1)}, bf16[2,96,768]{2,1,0:T(8,128)(2,1)}, u32[]{:S(2)}, u32[]{:S(2)}) %collective-permute-start.7) | collective-permute-done | bytes 294944 | tf_op jit(solution)/shard_map/ppermute | solution.py:928
  52.7 2.6 %join.5.refs_0_ = bf16[16,24,3200]{2,1,0:T(8,128)(2,1)} custom-call(bf16[4,24,3200]{2,1,0:T(8,128)(2,1)} %copy-done.2, bf16[4,24,3200]{2,1,0:T(8,128)(2,1)} %copy-done.12, bf16[4,24,3200]{2,1,0:T(8,128)(2,1)} %copy-done.6, bf16[4,24,3200]{2,1,0:T(8,128)(2,1)} %copy-done.11), custom_call_target="tpu_custom_call" | custom-call | flops 1 | bytes 1 | tf_op jit(solution)/shard_map/join/pallas_call | solution.py:704
  55.9 1.7 collective-permute-start.13
  58.1 1.5 collective-permute-start.14
  61.8 1.9 place.1
  66.3 6.5 %front.1 = (bf16[768,392]{1,0:T(8,128)(2,1)}, bf16[392,2304]{1,0:T(8,128)(2,1)}) custom-call(bf16[392,768]{1,0:T(8,128)(2,1)} %tokens_ref.4, f32[392,128]{1,0:T(8,128)} %broadcast_in_dim.33.live_ref.rest_2_, bf16[768,768]{1,0:T(8,128)(2,1)} %fusion.order_ref, f32[2,768]{1,0:T(2,128)} %pad_maximum_fusion.6.rows_ref, f32[1,2304]{1,0:T(1,128)} %reshape_reshape.11.b_qkv_ref, ...), custom_call_target="tpu_custom_call" | custom-call | flops 1 | bytes 1 | tf_op jit(solution)/shard_map/front/pallas_call | solution.py:357
  72.8 2.1 join.7
  77.3 2.0 join.6
  79.4 1.5 collective-permute-start.17
  80.9 1.7 collective-permute-start.18
  82.6 9.0 %attention.1 = (bf16[392,768]{1,0:T(8,128)(2,1)}, f32[6,4,200,256]{3,2,1,0:T(8,128)}) custom-call(bf16[392,2304]{1,0:T(8,128)(2,1)} %get-tuple-element.157.q_ref.k_ref.v_ref, bf16[392,2304]{1,0:T(8,128)(2,1)} %get-tuple-element.157.q_ref.k_ref.v_ref, bf16[392,2304]{1,0:T(8,128)(2,1)} %get-tuple-element.157.q_ref.k_ref.v_ref, ...), custom_call_target="tpu_custom_call" | custom-call | flops 1 | bytes 1 | tf_op jit(solution)/shard_map/attention/pallas_call | solution.py:240
  94.3 2.6 %join.8 = bf16[16,96,768]{2,1,0:T(8,128)(2,1)} custom-call(bf16[4,96,768]{2,1,0:T(8,128)(2,1)} %get-tuple-element.155.refs_0_, bf16[4,96,768]{2,1,0:T(8,128)(2,1)} %copy-done.13, bf16[4,96,768]{2,1,0:T(8,128)(2,1)} %get-tuple-element.156.refs_2_, bf16[4,96,768]{2,1,0:T(8,128)(2,1)} %copy-done.15), custom_call_target="tpu_custom_call" | custom-call | flops 1 | bytes 1 | tf_op jit(solution)/shard_map/join/pallas_call | solution.py:704
  97.0 6.0 %project.1 = (f32[392,768]{1,0:T(8,128)}, bf16[392,768]{1,0:T(8,128)(2,1)}, bf16[768,392]{1,0:T(8,128)(2,1)}, bf16[392,768]{1,0:T(8,128)(2,1)}) custom-call(bf16[392,768]{1,0:T(8,128)(2,1)} %tokens_ref.4, bf16[392,768]{1,0:T(8,128)(2,1)} %get-tuple-element.161.values_ref, bf16[768,768]{1,0:T(8,128)(2,1)} %fusion.order_ref, ...), custom_call_target="tpu_custom_call" | custom-call | flops 1 | bytes 1 | tf_op jit(solution)/shard_map/project/pallas_call | solution.py:550
  104.3 2.6 %join.9 = bf16[16,24,3072]{2,1,0:T(8,128)(2,1)} custom-call(bf16[4,24,3072]{2,1,0:T(8,128)(2,1)} %get-tuple-element.151.refs_0_, bf16[4,24,3072]{2,1,0:T(8,128)(2,1)} %copy-done.14, bf16[4,24,3072]{2,1,0:T(8,128)(2,1)} %get-tuple-element.152.refs_2_, bf16[4,24,3072]{2,1,0:T(8,128)(2,1)} %copy-done.16), custom_call_target="tpu_custom_call" | custom-call | flops 1 | bytes 1 | tf_op jit(solution)/shard_map/join/pallas_call | solution.py:704
  107.2 4.6 %collective-permute-done.19 = bf16[16,24,3072]{2,1,0:T(8,128)(2,1)} collective-permute-done((bf16[16,24,3072]{2,1,0:T(8,128)(2,1)}, bf16[16,24,3072]{2,1,0:T(8,128)(2,1)}, u32[]{:S(2)}, u32[]{:S(2)}) %collective-permute-start.19) | collective-permute-done | bytes 2359328 | tf_op jit(solution)/shard_map/ppermute | solution.py:928
  111.8 24.3 %mlp.1 = (bf16[392,768]{1,0:T(8,128)(2,1)}, f32[392,768]{1,0:T(8,128)}, bf16[384,3072]{1,0:T(8,128)(2,1)}, bf16[384,3072]{1,0:T(8,128)(2,1)}, f32[1,3072]{1,0:T(...) custom-call(s32[32]{0:T(128)} %and_select_fusion.2.place_ref, s32[1]{0:T(128)} %bitcast.me_ref, ...), custom_call_target="tpu_custom_call" | custom-call | flops 1 | bytes 1 | tf_op jit(solution)/shard_map/mlp/pallas_call | solution.py:591
  136.7 7.6 %second_norm_back.1 = (f32[392,768]{1,0:T(8,128)}, bf16[392,768]{1,0:T(8,128)(2,1)}, bf16[384,768]{1,0:T(8,128)(2,1)}, bf16[384,768]{1,0:T(8,128)(2,1)}, f32[8,768]{1,0:T(8,128)}) custom-call(f32[392,768]{1,0:T(8,128)} %get-tuple-element.172.grad_normed_ref, f32[392,768]{1,0:T(8,128)} %get-tuple-element.164.rest_4_.residual_ref, ...), custom_call_target="tpu_custom_call" | custom-call | flops 1 | bytes 1 | tf_op jit(solution)/shard_map/second_norm_back/pallas_call | solution.py:640
  146.1 3.4 %add_ranges.8 = (bf16[384,768]{1,0:T(8,128)(2,1)}, bf16[384,768]{1,0:T(8,128)(2,1)}, bf16[384,768]{1,0:T(8,128)(2,1)}, bf16[384,768]{1,0:T(8,128)(2,1)}) custom-call(bf16[1536,768]{1,0:T(8,128)(2,1)} %bitcast.102, bf16[1536,768]{1,0:T(8,128)(2,1)} %bitcast.103), custom_call_target="tpu_custom_call" | custom-call | flops 1 | bytes 1 | tf_op jit(solution)/shard_map/add_ranges/pallas_call | solution.py:779
  150.4 4.4 %add_ranges.9 = (bf16[96,3840]{1,0:T(8,128)(2,1)}, bf16[96,3840]{1,0:T(8,128)(2,1)}, bf16[96,3840]{1,0:T(8,128)(2,1)}, bf16[96,3840]{1,0:T(8,128)(2,1)}) custom-call(bf16[384,3072]{1,0:T(8,128)(2,1)} %get-tuple-element.175.refs_0_, bf16[384,3072]{1,0:T(8,128)(2,1)} %bitcast.21.refs_1_, bf16[384,768]{1,0:T(8,128)(2,1)} %get-tuple-element.181.refs_2_, ...), custom_call_target="tpu_custom_call" | custom-call | flops 1 | bytes 1 | tf_op jit(solution)/shard_map/add_ranges/pallas_call | solution.py:779
  156.7 1.7 collective-permute-start.31
  158.9 10.9 %attention_back.1 = (bf16[392,2304]{1,0:T(8,128)(2,1)}, f32[128,128]{1,0:T(8,128)}) custom-call(bf16[392,2304]{1,0:T(8,128)(2,1)} %get-tuple-element.157.q_ref.k_ref.v_ref, bf16[392,2304]{1,0:T(8,128)(2,1)} %get-tuple-element.157.q_ref.k_ref.v_ref, bf16[392,2304]{1,0:T(8,128)(2,1)} %get-tuple-element.157.q_ref.k_ref.v_ref, ...), custom_call_target="tpu_custom_call" | custom-call | flops 1 | bytes 1 | tf_op jit(solution)/shard_map/attention_back/pallas_call | solution.py:258
  169.8 5.2 %weight_grad.1 = (bf16[384,2304]{1,0:T(8,128)(2,1)}, bf16[384,2304]{1,0:T(8,128)(2,1)}) custom-call(bf16[768,392]{1,0:T(8,128)(2,1)} %get-tuple-element.148.turned_ref, bf16[392,2304]{1,0:T(8,128)(2,1)} %get-tuple-element.195.grad_ref), custom_call_target="tpu_custom_call" | custom-call | flops 1 | bytes 1 | tf_op jit(solution)/shard_map/weight_grad/pallas_call | solution.py:727
  176.2 2.7 %add_ranges.10 = (bf16[48,3840]{1,0:T(8,128)(2,1)}, bf16[48,3840]{1,0:T(8,128)(2,1)}, bf16[48,3840]{1,0:T(8,128)(2,1)}, bf16[48,3840]{1,0:T(8,128)(2,1)}) custom-call(bf16[96,3840]{1,0:T(8,128)(2,1)} %get-tuple-element.188.refs_0_, bf16[96,3840]{1,0:T(8,128)(2,1)} %bitcast.108, bf16[96,3840]{1,0:T(8,128)(2,1)} %get-tuple-element.191.refs_2_, ...), custom_call_target="tpu_custom_call" | custom-call | flops 1 | bytes 1 | tf_op jit(solution)/shard_map/add_ranges/pallas_call | solution.py:779
  181.6 8.6 %first_norm_back.1 = (bf16[392,768]{1,0:T(8,128)(2,1)}, f32[112,128]{1,0:T(8,128)}) custom-call(bf16[392,2304]{1,0:T(8,128)(2,1)} %get-tuple-element.195.grad_ref, bf16[392,768]{1,0:T(8,128)(2,1)} %tokens_ref.4, f32[392,128]{1,0:T(8,128)} %broadcast_in_dim.33.live_ref.rest_2_, f32[1,768]{1,0:T(1,128)} %copy-done.32, bf16[768,768]{1,0:T(8,128)(2,1)} %fusion.order_ref, ...), custom_call_target="tpu_custom_call" | custom-call | flops 1 | bytes 1 | tf_op jit(solution)/shard_map/first_norm_back/pallas_call | solution.py:865
  190.5 2.5 %add_ranges.11 = (bf16[192,768]{1,0:T(8,128)(2,1)}, bf16[192,768]{1,0:T(8,128)(2,1)}, bf16[192,768]{1,0:T(8,128)(2,1)}, bf16[192,768]{1,0:T(8,128)(2,1)}) custom-call(bf16[384,768]{1,0:T(8,128)(2,1)} %get-tuple-element.204.refs_0_, bf16[384,768]{1,0:T(8,128)(2,1)} %bitcast.29.refs_1_, bf16[384,768]{1,0:T(8,128)(2,1)} %get-tuple-element.206.refs_2_, ...), custom_call_target="tpu_custom_call" | custom-call | flops 99999997952 | bytes 1 | tf_op jit(solution)/shard_map/add_ranges/pallas_call | solution.py:779
  194.4 1.6 collective-permute-start.36
  197.3 2.9 %add_ranges.12 = (bf16[96,2304]{1,0:T(8,128)(2,1)}, bf16[96,2304]{1,0:T(8,128)(2,1)}, bf16[96,2304]{1,0:T(8,128)(2,1)}, bf16[96,2304]{1,0:T(8,128)(2,1)}) custom-call(bf16[384,2304]{1,0:T(8,128)(2,1)} %get-tuple-element.189.refs_0_, bf16[384,2304]{1,0:T(8,128)(2,1)} %bitcast.105), custom_call_target="tpu_custom_call" | custom-call | flops 1 | bytes 1 | tf_op jit(solution)/shard_map/add_ranges/pallas_call | solution.py:779
  200.3 2.2 add_ranges.13
  205.4 5.2 %collective-permute-start.32 = (f32[112,128]{1,0:T(8,128)S(1)}, f32[112,128]{1,0:T(8,128)S(1)}, u32[]{:S(2)}, u32[]{:S(2)}) collective-permute-start(f32[112,128]{1,0:T(8,128)S(1)} %add.80), channel_id=1, source_target_pairs={{0,16},{1,17},{2,18},{3,19},{4,20},{5,21},{6,22},{7,23},{8,24},{9,... | collective-permute-start | bytes 172040 | tf_op jit(solution)/shard_map/ppermute | solution.py:928
  211.3 2.1 add_ranges.14
  214.9 2.4 add_ranges.15
  218.8 1.6 collective-permute-start.39
  220.4 5.3 %collective-permute-start.47 = (bf16[24,3840]{1,0:T(8,128)(2,1)S(1)}, bf16[24,3840]{1,0:T(8,128)(2,1)S(1)}, u32[]{:S(2)}, u32[]{:S(2)}) collective-permute-start(bf16[24,3840]{1,0:T(8,128)(2,1)S(1)} %fusion.3), channel_id=1, source_target_pairs={{0,16},{1,17},{2,18},{3,19},{4,20},{5,21},{6,22},{7,23},{8,24},{9,... | collective-permute-start | bytes 552968 | tf_op jit(solution)/shard_map/ppermute | solution.py:928
  227.0 4.4 %collective-permute-start.44 = (bf16[24,2304]{1,0:T(8,128)(2,1)S(1)}, bf16[24,2304]{1,0:T(8,128)(2,1)S(1)}, u32[]{:S(2)}, u32[]{:S(2)}) collective-permute-start(bf16[24,2304]{1,0:T(8,128)(2,1)S(1)} %fusion.9), channel_id=1, source_target_pairs={{0,16},{1,17},{2,18},{3,19},{4,20},{5,21},{6,22},{7,23},{8,24},{9,... | collective-permute-start | bytes 331784 | tf_op jit(solution)/shard_map/ppermute | solution.py:928
  232.0 1.7 collective-permute-start.41
  233.8 2.5 %collective-permute-done.41 = f32[112,128]{1,0:T(8,128)S(1)} collective-permute-done((f32[112,128]{1,0:T(8,128)S(1)}, f32[112,128]{1,0:T(8,128)S(1)}, u32[]{:S(2)}, u32[]{:S(2)}) %collective-permute-start.41) | collective-permute-done | bytes 57376 | tf_op jit(solution)/shard_map/ppermute | solution.py:928
  236.3 3.7 %collective-permute-start.48 = (bf16[96,768]{1,0:T(8,128)(2,1)S(1)}, bf16[96,768]{1,0:T(8,128)(2,1)S(1)}, u32[]{:S(2)}, u32[]{:S(2)}) collective-permute-start(bf16[96,768]{1,0:T(8,128)(2,1)S(1)} %fusion.5), channel_id=1, source_target_pairs={{0,16},{1,17},{2,18},{3,19},{4,20},{5,21},{6,22},{7,23},{8,24},{9,... | collective-permute-start | bytes 442376 | tf_op jit(solution)/shard_map/ppermute | solution.py:928
  242.7 1.6 collective-permute-done.43
  244.9 1.5 own_small.1
  (206 shorter events, 53.9 us)
Async XLA Ops:
  3.5 11.4 %collective-permute-start = (bf16[24,3200]{1,0:T(8,128)(2,1)S(1)}, bf16[24,3200]{1,0:T(8,128)(2,1)S(1)}, u32[]{:S(2)}, u32[]{:S(2)}) collective-permute-start(bf16[24,3200]{1,0:T(8,128)(2,1)S(1)} %pad_maximum_fusion.4), channel_id=1, source_target_pairs={{0,16},{1,17},{2,18},{3,19},{4,20},{5,21},{6,22},{7,23},{8,24},{9,... | collective-permute-start | bytes 460808 | tf_op jit(solution)/shard_map/ppermute | solution.py:928
  14.9 13.6 %collective-permute-start.3 = (bf16[2,24,3200]{2,1,0:T(8,128)(2,1)S(1)}, bf16[2,24,3200]{2,1,0:T(8,128)(2,1)S(1)}, u32[]{:S(2)}, u32[]{:S(2)}) collective-permute-start(bf16[2,24,3200]{2,1,0:T(8,128)(2,1)S(1)} %pad_maximum_fusion.1), channel_id=1, source_target_pairs={{0,8},{1,9},{2,10},{3,11},{4,12},{5,13},{6,14},{7,15},{8,0},{9,1},... | collective-permute-start | bytes 921608 | tf_op jit(solution)/shard_map/ppermute | solution.py:928
  15.8 14.0 %collective-permute-start.2 = (bf16[2,24,3200]{2,1,0:T(8,128)(2,1)S(1)}, bf16[2,24,3200]{2,1,0:T(8,128)(2,1)S(1)}, u32[]{:S(2)}, u32[]{:S(2)}) collective-permute-start(bf16[2,24,3200]{2,1,0:T(8,128)(2,1)S(1)} %pad_maximum_fusion.1), channel_id=1, source_target_pairs={{0,2},{1,3},{2,0},{3,1},{4,6},{5,7},{6,4},{7,5},{8,10},{9,11},{10,... | collective-permute-start | bytes 921608 | tf_op jit(solution)/shard_map/ppermute | solution.py:928
  17.2 22.3 %collective-permute-start.1 = (bf16[24,3072]{1,0:T(8,128)(2,1)S(1)}, bf16[24,3072]{1,0:T(8,128)(2,1)S(1)}, u32[]{:S(2)}, u32[]{:S(2)}) collective-permute-start(bf16[24,3072]{1,0:T(8,128)(2,1)S(1)} %convert_element_type.124), channel_id=1, source_target_pairs={{0,16},{1,17},{2,18},{3,19},{4,20},{5,21},{6,22},{7,23},{8,24},{9,... | collective-permute-start | bytes 442376 | tf_op jit(solution)/shard_map/ppermute | solution.py:928
  20.6 19.0 %collective-permute-start.6 = (bf16[96,768]{1,0:T(8,128)(2,1)S(1)}, bf16[96,768]{1,0:T(8,128)(2,1)S(1)}, u32[]{:S(2)}, u32[]{:S(2)}) collective-permute-start(bf16[96,768]{1,0:T(8,128)(2,1)S(1)} %convert_element_type.125), channel_id=1, source_target_pairs={{0,16},{1,17},{2,18},{3,19},{4,20},{5,21},{6,22},{7,23},{8,24},{9,... | collective-permute-start | bytes 442376 | tf_op jit(solution)/shard_map/ppermute | solution.py:928
  28.4 7.5 %collective-permute-start.4 = (bf16[2,24,3200]{2,1,0:T(8,128)(2,1)S(1)}, bf16[2,24,3200]{2,1,0:T(8,128)(2,1)S(1)}, u32[]{:S(2)}, u32[]{:S(2)}) collective-permute-start(bf16[2,24,3200]{2,1,0:T(8,128)(2,1)S(1)} %collective-permute-done.3), channel_id=1, source_target_pairs={{0,4},{1,5},{2,6},{3,7},{4,0},{5,1},{6,2},{7,3},{8,12},{9,13},{10,... | collective-permute-start | bytes 921608 | tf_op jit(solution)/shard_map/ppermute | solution.py:928
  36.1 15.5 %collective-permute-start.9 = (bf16[4,24,3200]{2,1,0:T(8,128)(2,1)S(1)}, bf16[4,24,3200]{2,1,0:T(8,128)(2,1)S(1)}, u32[]{:S(2)}, u32[]{:S(2)}) collective-permute-start(bf16[4,24,3200]{2,1,0:T(8,128)(2,1)S(1)} %constant_dynamic-update-slice_fusion.refs_2_), channel_id=1, source_target_pairs={{0,2},{1,3},{2,0},{3,1},{4,6},{5,7},{6,4},{7,5},{8,10},{9,11},{10,... | collective-permute-start | bytes 1843208 | tf_op jit(solution)/shard_map/ppermute | solution.py:928
  38.1 13.6 %collective-permute-start.8 = (bf16[4,24,3200]{2,1,0:T(8,128)(2,1)S(1)}, bf16[4,24,3200]{2,1,0:T(8,128)(2,1)S(1)}, u32[]{:S(2)}, u32[]{:S(2)}) collective-permute-start(bf16[4,24,3200]{2,1,0:T(8,128)(2,1)S(1)} %pad_maximum_fusion.refs_0_), channel_id=1, source_target_pairs={{0,4},{1,5},{2,6},{3,7},{4,0},{5,1},{6,2},{7,3},{8,12},{9,13},{10,... | collective-permute-start | bytes 1843208 | tf_op jit(solution)/shard_map/ppermute | solution.py:928
  39.6 8.7 %collective-permute-start.5 = (bf16[2,24,3072]{2,1,0:T(8,128)(2,1)S(1)}, bf16[2,24,3072]{2,1,0:T(8,128)(2,1)S(1)}, u32[]{:S(2)}, u32[]{:S(2)}) collective-permute-start(bf16[2,24,3072]{2,1,0:T(8,128)(2,1)S(1)} %pad_maximum_fusion.2.refs_0_), channel_id=1, source_target_pairs={{0,8},{1,9},{2,10},{3,11},{4,12},{5,13},{6,14},{7,15},{8,0},{9,1},... | collective-permute-start | bytes 884744 | tf_op jit(solution)/shard_map/ppermute | solution.py:928
  39.8 11.9 %collective-permute-start.7 = (bf16[2,96,768]{2,1,0:T(8,128)(2,1)S(1)}, bf16[2,96,768]{2,1,0:T(8,128)(2,1)}, u32[]{:S(2)}, u32[]{:S(2)}) collective-permute-start(bf16[2,96,768]{2,1,0:T(8,128)(2,1)S(1)} %pad_maximum_fusion.3.refs_0_), channel_id=1, source_target_pairs={{0,8},{1,9},{2,10},{3,11},{4,12},{5,13},{6,14},{7,15},{8,0},{9,1},... | collective-permute-start | bytes 884744 | tf_op jit(solution)/shard_map/ppermute | solution.py:928
  55.4 5.0 %collective-permute-start.10 = (bf16[16,24,3200]{2,1,0:T(8,128)(2,1)}, bf16[16,24,3200]{2,1,0:T(8,128)(2,1)S(1)}, u32[]{:S(2)}, u32[]{:S(2)}) collective-permute-start(bf16[16,24,3200]{2,1,0:T(8,128)(2,1)} %join.5.refs_0_), channel_id=1, source_target_pairs={{0,1},{1,0},{2,3},{3,2},{4,5},{5,4},{6,7},{7,6},{8,9},{9,8},{10,11... | collective-permute-start | bytes 7372808 | tf_op jit(solution)/shard_map/ppermute | solution.py:928
  55.4 20.5 %collective-permute-start.11 = (bf16[2,24,3072]{2,1,0:T(8,128)(2,1)S(1)}, bf16[2,24,3072]{2,1,0:T(8,128)(2,1)S(1)}, u32[]{:S(2)}, u32[]{:S(2)}) collective-permute-start(bf16[2,24,3072]{2,1,0:T(8,128)(2,1)S(1)} %pad_maximum_fusion.2.refs_0_), channel_id=1, source_target_pairs={{0,2},{1,3},{2,0},{3,1},{4,6},{5,7},{6,4},{7,5},{8,10},{9,11},{10,... | collective-permute-start | bytes 884744 | tf_op jit(solution)/shard_map/ppermute | solution.py:928
  55.9 16.9 %collective-permute-start.13 = (bf16[2,96,768]{2,1,0:T(8,128)(2,1)S(1)}, bf16[2,96,768]{2,1,0:T(8,128)(2,1)}, u32[]{:S(2)}, u32[]{:S(2)}) collective-permute-start(bf16[2,96,768]{2,1,0:T(8,128)(2,1)S(1)} %pad_maximum_fusion.3.refs_0_), channel_id=1, source_target_pairs={{0,2},{1,3},{2,0},{3,1},{4,6},{5,7},{6,4},{7,5},{8,10},{9,11},{10,... | collective-permute-start | bytes 884744 | tf_op jit(solution)/shard_map/ppermute | solution.py:928
  57.5 18.4 %collective-permute-start.12 = (bf16[2,24,3072]{2,1,0:T(8,128)(2,1)S(1)}, bf16[2,24,3072]{2,1,0:T(8,128)(2,1)S(1)}, u32[]{:S(2)}, u32[]{:S(2)}) collective-permute-start(bf16[2,24,3072]{2,1,0:T(8,128)(2,1)S(1)} %collective-permute-done.5.refs_2_), channel_id=1, source_target_pairs={{0,4},{1,5},{2,6},{3,7},{4,0},{5,1},{6,2},{7,3},{8,12},{9,13},{10,... | collective-permute-start | bytes 884744 | tf_op jit(solution)/shard_map/ppermute | solution.py:928
  58.1 14.7 %collective-permute-start.14 = (bf16[2,96,768]{2,1,0:T(8,128)(2,1)}, bf16[2,96,768]{2,1,0:T(8,128)(2,1)}, u32[]{:S(2)}, u32[]{:S(2)}) collective-permute-start(bf16[2,96,768]{2,1,0:T(8,128)(2,1)} %collective-permute-done.7.refs_2_), channel_id=1, source_target_pairs={{0,4},{1,5},{2,6},{3,7},{4,0},{5,1},{6,2},{7,3},{8,12},{9,13},{10,... | collective-permute-start | bytes 884744 | tf_op jit(solution)/shard_map/ppermute | solution.py:928
  74.9 18.4 %collective-permute-start.15 = (bf16[4,96,768]{2,1,0:T(8,128)(2,1)}, bf16[4,96,768]{2,1,0:T(8,128)(2,1)S(1)}, u32[]{:S(2)}, u32[]{:S(2)}) collective-permute-start(bf16[4,96,768]{2,1,0:T(8,128)(2,1)} %get-tuple-element.155.refs_0_), channel_id=1, source_target_pairs={{0,4},{1,5},{2,6},{3,7},{4,0},{5,1},{6,2},{7,3},{8,12},{9,13},{10,... | collective-permute-start | bytes 1769480 | tf_op jit(solution)/shard_map/ppermute | solution.py:928
  75.5 17.8 %collective-permute-start.16 = (bf16[4,96,768]{2,1,0:T(8,128)(2,1)}, bf16[4,96,768]{2,1,0:T(8,128)(2,1)S(1)}, u32[]{:S(2)}, u32[]{:S(2)}) collective-permute-start(bf16[4,96,768]{2,1,0:T(8,128)(2,1)} %get-tuple-element.156.refs_2_), channel_id=1, source_target_pairs={{0,2},{1,3},{2,0},{3,1},{4,6},{5,7},{6,4},{7,5},{8,10},{9,11},{10,... | collective-permute-start | bytes 1769480 | tf_op jit(solution)/shard_map/ppermute | solution.py:928
  79.4 23.8 %collective-permute-start.17 = (bf16[4,24,3072]{2,1,0:T(8,128)(2,1)}, bf16[4,24,3072]{2,1,0:T(8,128)(2,1)S(1)}, u32[]{:S(2)}, u32[]{:S(2)}) collective-permute-start(bf16[4,24,3072]{2,1,0:T(8,128)(2,1)} %get-tuple-element.151.refs_0_), channel_id=1, source_target_pairs={{0,4},{1,5},{2,6},{3,7},{4,0},{5,1},{6,2},{7,3},{8,12},{9,13},{10,... | collective-permute-start | bytes 1769480 | tf_op jit(solution)/shard_map/ppermute | solution.py:928
  80.9 22.5 %collective-permute-start.18 = (bf16[4,24,3072]{2,1,0:T(8,128)(2,1)}, bf16[4,24,3072]{2,1,0:T(8,128)(2,1)S(1)}, u32[]{:S(2)}, u32[]{:S(2)}) collective-permute-start(bf16[4,24,3072]{2,1,0:T(8,128)(2,1)} %get-tuple-element.152.refs_2_), channel_id=1, source_target_pairs={{0,2},{1,3},{2,0},{3,1},{4,6},{5,7},{6,4},{7,5},{8,10},{9,11},{10,... | collective-permute-start | bytes 1769480 | tf_op jit(solution)/shard_map/ppermute | solution.py:928
  96.9 10.3 %collective-permute-start.20 = (bf16[16,96,768]{2,1,0:T(8,128)(2,1)}, bf16[16,96,768]{2,1,0:T(8,128)(2,1)S(1)}, u32[]{:S(2)}, u32[]{:S(2)}) collective-permute-start(bf16[16,96,768]{2,1,0:T(8,128)(2,1)} %join.8), channel_id=1, source_target_pairs={{0,1},{1,0},{2,3},{3,2},{4,5},{5,4},{6,7},{7,6},{8,9},{9,8},{10,11... | collective-permute-start | bytes 7077896 | tf_op jit(solution)/shard_map/ppermute | solution.py:928
  106.9 4.9 %collective-permute-start.19 = (bf16[16,24,3072]{2,1,0:T(8,128)(2,1)}, bf16[16,24,3072]{2,1,0:T(8,128)(2,1)}, u32[]{:S(2)}, u32[]{:S(2)}) collective-permute-start(bf16[16,24,3072]{2,1,0:T(8,128)(2,1)} %join.9), channel_id=1, source_target_pairs={{0,1},{1,0},{2,3},{3,2},{4,5},{5,4},{6,7},{7,6},{8,9},{9,8},{10,11... | collective-permute-start | bytes 7077896 | tf_op jit(solution)/shard_map/ppermute | solution.py:928
  136.1 8.5 %collective-permute-start.22 = (bf16[16,96,768]{2,1,0:T(8,128)(2,1)}, bf16[16,96,768]{2,1,0:T(8,128)(2,1)S(1)}, u32[]{:S(2)}, u32[]{:S(2)}) collective-permute-start(bf16[16,96,768]{2,1,0:T(8,128)(2,1)} %get-tuple-element.171), channel_id=1, source_target_pairs={{0,1},{1,0},{2,3},{3,2},{4,5},{5,4},{6,7},{7,6},{8,9},{9,8},{10,11... | collective-permute-start | bytes 7077896 | tf_op jit(solution)/shard_map/ppermute | solution.py:928
  136.5 13.1 %collective-permute-start.21 = (bf16[16,24,3072]{2,1,0:T(8,128)(2,1)}, bf16[16,24,3072]{2,1,0:T(8,128)(2,1)}, u32[]{:S(2)}, u32[]{:S(2)}) collective-permute-start(bf16[16,24,3072]{2,1,0:T(8,128)(2,1)} %bitcast.124), channel_id=1, source_target_pairs={{0,1},{1,0},{2,3},{3,2},{4,5},{5,4},{6,7},{7,6},{8,9},{9,8},{10,11... | collective-permute-start | bytes 7077896 | tf_op jit(solution)/shard_map/ppermute | solution.py:928
  144.3 5.2 %collective-permute-start.23 = (bf16[384,768]{1,0:T(8,128)(2,1)}, bf16[384,768]{1,0:T(8,128)(2,1)S(1)}, u32[]{:S(2)}, u32[]{:S(2)}) collective-permute-start(bf16[384,768]{1,0:T(8,128)(2,1)} %get-tuple-element.182), channel_id=1, source_target_pairs={{0,1},{1,0},{2,3},{3,2},{4,5},{5,4},{6,7},{7,6},{8,9},{9,8},{10,11... | collective-permute-start | bytes 1769480 | tf_op jit(solution)/shard_map/ppermute | solution.py:928
  154.8 20.2 %collective-permute-start.25 = (bf16[4,24,3840]{2,1,0:T(8,128)(2,1)}, bf16[4,24,3840]{2,1,0:T(8,128)(2,1)S(1)}, u32[]{:S(2)}, u32[]{:S(2)}) collective-permute-start(bf16[4,24,3840]{2,1,0:T(8,128)(2,1)} %bitcast.127), channel_id=1, source_target_pairs={{0,2},{1,3},{2,0},{3,1},{4,6},{5,7},{6,4},{7,5},{8,10},{9,11},{10,... | collective-permute-start | bytes 2211848 | tf_op jit(solution)/shard_map/ppermute | solution.py:928
  155.2 19.8 %collective-permute-start.24 = (bf16[4,24,3840]{2,1,0:T(8,128)(2,1)}, bf16[4,24,3840]{2,1,0:T(8,128)(2,1)S(1)}, u32[]{:S(2)}, u32[]{:S(2)}) collective-permute-start(bf16[4,24,3840]{2,1,0:T(8,128)(2,1)} %bitcast.126), channel_id=1, source_target_pairs={{0,4},{1,5},{2,6},{3,7},{4,0},{5,1},{6,2},{7,3},{8,12},{9,13},{10,... | collective-permute-start | bytes 2211848 | tf_op jit(solution)/shard_map/ppermute | solution.py:928
  156.7 33.5 %collective-permute-start.31 = (bf16[4,96,768]{2,1,0:T(8,128)(2,1)}, bf16[4,96,768]{2,1,0:T(8,128)(2,1)}, u32[]{:S(2)}, u32[]{:S(2)}) collective-permute-start(bf16[4,96,768]{2,1,0:T(8,128)(2,1)} %bitcast.20), channel_id=1, source_target_pairs={{0,2},{1,3},{2,0},{3,1},{4,6},{5,7},{6,4},{7,5},{8,10},{9,11},{10,... | collective-permute-start | bytes 1769480 | tf_op jit(solution)/shard_map/ppermute | solution.py:928
  158.3 32.2 %collective-permute-start.30 = (bf16[4,96,768]{2,1,0:T(8,128)(2,1)S(1)}, bf16[4,96,768]{2,1,0:T(8,128)(2,1)}, u32[]{:S(2)}, u32[]{:S(2)}) collective-permute-start(bf16[4,96,768]{2,1,0:T(8,128)(2,1)S(1)} %bitcast.128), channel_id=1, source_target_pairs={{0,4},{1,5},{2,6},{3,7},{4,0},{5,1},{6,2},{7,3},{8,12},{9,13},{10,... | collective-permute-start | bytes 1769480 | tf_op jit(solution)/shard_map/ppermute | solution.py:928
  175.0 21.0 %collective-permute-start.29 = (bf16[16,24,2304]{2,1,0:T(8,128)(2,1)}, bf16[16,24,2304]{2,1,0:T(8,128)(2,1)S(1)}, u32[]{:S(2)}, u32[]{:S(2)}) collective-permute-start(bf16[16,24,2304]{2,1,0:T(8,128)(2,1)} %bitcast.125), channel_id=1, source_target_pairs={{0,1},{1,0},{2,3},{3,2},{4,5},{5,4},{6,7},{7,6},{8,9},{9,8},{10,11... | collective-permute-start | bytes 5308424 | tf_op jit(solution)/shard_map/ppermute | solution.py:928
  178.9 15.5 %collective-permute-start.28 = (bf16[2,24,3840]{2,1,0:T(8,128)(2,1)}, bf16[2,24,3840]{2,1,0:T(8,128)(2,1)S(1)}, u32[]{:S(2)}, u32[]{:S(2)}) collective-permute-start(bf16[2,24,3840]{2,1,0:T(8,128)(2,1)} %bitcast.133), channel_id=1, source_target_pairs={{0,4},{1,5},{2,6},{3,7},{4,0},{5,1},{6,2},{7,3},{8,12},{9,13},{10,... | collective-permute-start | bytes 1105928 | tf_op jit(solution)/shard_map/ppermute | solution.py:928
  180.4 15.6 %collective-permute-start.27 = (bf16[2,24,3840]{2,1,0:T(8,128)(2,1)}, bf16[2,24,3840]{2,1,0:T(8,128)(2,1)S(1)}, u32[]{:S(2)}, u32[]{:S(2)}) collective-permute-start(bf16[2,24,3840]{2,1,0:T(8,128)(2,1)} %bitcast.132), channel_id=1, source_target_pairs={{0,2},{1,3},{2,0},{3,1},{4,6},{5,7},{6,4},{7,5},{8,10},{9,11},{10,... | collective-permute-start | bytes 1105928 | tf_op jit(solution)/shard_map/ppermute | solution.py:928
  190.1 13.8 %collective-permute-start.26 = (f32[112,128]{1,0:T(8,128)}, f32[112,128]{1,0:T(8,128)S(1)}, u32[]{:S(2)}, u32[]{:S(2)}) collective-permute-start(f32[112,128]{1,0:T(8,128)} %get-tuple-element.201), channel_id=1, source_target_pairs={{0,8},{1,9},{2,10},{3,11},{4,12},{5,13},{6,14},{7,15},{8,0},{9,1},... | collective-permute-start | bytes 172040 | tf_op jit(solution)/shard_map/ppermute | solution.py:928
  193.0 12.4 %collective-permute-start.37 = (bf16[2,96,768]{2,1,0:T(8,128)(2,1)}, bf16[2,96,768]{2,1,0:T(8,128)(2,1)S(1)}, u32[]{:S(2)}, u32[]{:S(2)}) collective-permute-start(bf16[2,96,768]{2,1,0:T(8,128)(2,1)} %bitcast.136), channel_id=1, source_target_pairs={{0,4},{1,5},{2,6},{3,7},{4,0},{5,1},{6,2},{7,3},{8,12},{9,13},{10,... | collective-permute-start | bytes 884744 | tf_op jit(solution)/shard_map/ppermute | solution.py:928
  194.4 16.2 %collective-permute-start.36 = (bf16[2,96,768]{2,1,0:T(8,128)(2,1)}, bf16[2,96,768]{2,1,0:T(8,128)(2,1)S(1)}, u32[]{:S(2)}, u32[]{:S(2)}) collective-permute-start(bf16[2,96,768]{2,1,0:T(8,128)(2,1)} %bitcast.135), channel_id=1, source_target_pairs={{0,2},{1,3},{2,0},{3,1},{4,6},{5,7},{6,4},{7,5},{8,10},{9,11},{10,... | collective-permute-start | bytes 884744 | tf_op jit(solution)/shard_map/ppermute | solution.py:928
  202.5 17.9 %collective-permute-start.33 = (bf16[2,24,3840]{2,1,0:T(8,128)(2,1)}, bf16[2,24,3840]{2,1,0:T(8,128)(2,1)S(1)}, u32[]{:S(2)}, u32[]{:S(2)}) collective-permute-start(bf16[2,24,3840]{2,1,0:T(8,128)(2,1)} %bitcast.131), channel_id=1, source_target_pairs={{0,8},{1,9},{2,10},{3,11},{4,12},{5,13},{6,14},{7,15},{8,0},{9,1},... | collective-permute-start | bytes 1105928 | tf_op jit(solution)/shard_map/ppermute | solution.py:928
  202.9 11.1 %collective-permute-start.35 = (bf16[4,24,2304]{2,1,0:T(8,128)(2,1)}, bf16[4,24,2304]{2,1,0:T(8,128)(2,1)S(1)}, u32[]{:S(2)}, u32[]{:S(2)}) collective-permute-start(bf16[4,24,2304]{2,1,0:T(8,128)(2,1)} %bitcast.130), channel_id=1, source_target_pairs={{0,2},{1,3},{2,0},{3,1},{4,6},{5,7},{6,4},{7,5},{8,10},{9,11},{10,... | collective-permute-start | bytes 1327112 | tf_op jit(solution)/shard_map/ppermute | solution.py:928
  204.0 10.1 %collective-permute-start.34 = (bf16[4,24,2304]{2,1,0:T(8,128)(2,1)}, bf16[4,24,2304]{2,1,0:T(8,128)(2,1)S(1)}, u32[]{:S(2)}, u32[]{:S(2)}) collective-permute-start(bf16[4,24,2304]{2,1,0:T(8,128)(2,1)} %bitcast.129), channel_id=1, source_target_pairs={{0,4},{1,5},{2,6},{3,7},{4,0},{5,1},{6,2},{7,3},{8,12},{9,13},{10,... | collective-permute-start | bytes 1327112 | tf_op jit(solution)/shard_map/ppermute | solution.py:928
  205.4 20.3 %collective-permute-start.32 = (f32[112,128]{1,0:T(8,128)S(1)}, f32[112,128]{1,0:T(8,128)S(1)}, u32[]{:S(2)}, u32[]{:S(2)}) collective-permute-start(f32[112,128]{1,0:T(8,128)S(1)} %add.80), channel_id=1, source_target_pairs={{0,16},{1,17},{2,18},{3,19},{4,20},{5,21},{6,22},{7,23},{8,24},{9,... | collective-permute-start | bytes 172040 | tf_op jit(solution)/shard_map/ppermute | solution.py:928
  213.4 18.6 %collective-permute-start.42 = (bf16[2,96,768]{2,1,0:T(8,128)(2,1)}, bf16[2,96,768]{2,1,0:T(8,128)(2,1)S(1)}, u32[]{:S(2)}, u32[]{:S(2)}) collective-permute-start(bf16[2,96,768]{2,1,0:T(8,128)(2,1)} %bitcast.134), channel_id=1, source_target_pairs={{0,8},{1,9},{2,10},{3,11},{4,12},{5,13},{6,14},{7,15},{8,0},{9,1},... | collective-permute-start | bytes 884744 | tf_op jit(solution)/shard_map/ppermute | solution.py:928
  217.3 8.6 %collective-permute-start.40 = (bf16[2,24,2304]{2,1,0:T(8,128)(2,1)}, bf16[2,24,2304]{2,1,0:T(8,128)(2,1)S(1)}, u32[]{:S(2)}, u32[]{:S(2)}) collective-permute-start(bf16[2,24,2304]{2,1,0:T(8,128)(2,1)} %bitcast.138), channel_id=1, source_target_pairs={{0,4},{1,5},{2,6},{3,7},{4,0},{5,1},{6,2},{7,3},{8,12},{9,13},{10,... | collective-permute-start | bytes 663560 | tf_op jit(solution)/shard_map/ppermute | solution.py:928
  218.8 7.1 %collective-permute-start.39 = (bf16[2,24,2304]{2,1,0:T(8,128)(2,1)}, bf16[2,24,2304]{2,1,0:T(8,128)(2,1)S(1)}, u32[]{:S(2)}, u32[]{:S(2)}) collective-permute-start(bf16[2,24,2304]{2,1,0:T(8,128)(2,1)} %bitcast.137), channel_id=1, source_target_pairs={{0,2},{1,3},{2,0},{3,1},{4,6},{5,7},{6,4},{7,5},{8,10},{9,11},{10,... | collective-permute-start | bytes 663560 | tf_op jit(solution)/shard_map/ppermute | solution.py:928
  220.4 19.6 %collective-permute-start.47 = (bf16[24,3840]{1,0:T(8,128)(2,1)S(1)}, bf16[24,3840]{1,0:T(8,128)(2,1)S(1)}, u32[]{:S(2)}, u32[]{:S(2)}) collective-permute-start(bf16[24,3840]{1,0:T(8,128)(2,1)S(1)} %fusion.3), channel_id=1, source_target_pairs={{0,16},{1,17},{2,18},{3,19},{4,20},{5,21},{6,22},{7,23},{8,24},{9,... | collective-permute-start | bytes 552968 | tf_op jit(solution)/shard_map/ppermute | solution.py:928
  225.8 5.6 %collective-permute-start.38 = (f32[112,128]{1,0:T(8,128)S(1)}, f32[112,128]{1,0:T(8,128)S(1)}, u32[]{:S(2)}, u32[]{:S(2)}) collective-permute-start(f32[112,128]{1,0:T(8,128)S(1)} %add.82), channel_id=1, source_target_pairs={{0,1},{1,0},{2,3},{3,2},{4,5},{5,4},{6,7},{7,6},{8,9},{9,8},{10,11... | collective-permute-start | bytes 172040 | tf_op jit(solution)/shard_map/ppermute | solution.py:928
  227.0 15.0 %collective-permute-start.44 = (bf16[24,2304]{1,0:T(8,128)(2,1)S(1)}, bf16[24,2304]{1,0:T(8,128)(2,1)S(1)}, u32[]{:S(2)}, u32[]{:S(2)}) collective-permute-start(bf16[24,2304]{1,0:T(8,128)(2,1)S(1)} %fusion.9), channel_id=1, source_target_pairs={{0,16},{1,17},{2,18},{3,19},{4,20},{5,21},{6,22},{7,23},{8,24},{9,... | collective-permute-start | bytes 331784 | tf_op jit(solution)/shard_map/ppermute | solution.py:928
  231.4 10.6 %collective-permute-start.46 = (bf16[24,2304]{1,0:T(8,128)(2,1)S(1)}, bf16[24,2304]{1,0:T(8,128)(2,1)S(1)}, u32[]{:S(2)}, u32[]{:S(2)}) collective-permute-start(bf16[24,2304]{1,0:T(8,128)(2,1)S(1)} %get-tuple-element.256), channel_id=1, source_target_pairs={{0,24},{1,25},{2,26},{3,27},{4,28},{5,29},{6,30},{7,31},{8,16},{9,... | collective-permute-start | bytes 331784 | tf_op jit(solution)/shard_map/ppermute | solution.py:928
  231.4 10.6 %collective-permute-start.45 = (bf16[24,2304]{1,0:T(8,128)(2,1)S(1)}, bf16[24,2304]{1,0:T(8,128)(2,1)S(1)}, u32[]{:S(2)}, u32[]{:S(2)}) collective-permute-start(bf16[24,2304]{1,0:T(8,128)(2,1)S(1)} %get-tuple-element.257), channel_id=1, source_target_pairs={{0,8},{1,9},{2,10},{3,11},{4,12},{5,13},{6,14},{7,15},{8,0},{9,1},... | collective-permute-start | bytes 331784 | tf_op jit(solution)/shard_map/ppermute | solution.py:928
  236.3 10.6 %collective-permute-start.48 = (bf16[96,768]{1,0:T(8,128)(2,1)S(1)}, bf16[96,768]{1,0:T(8,128)(2,1)S(1)}, u32[]{:S(2)}, u32[]{:S(2)}) collective-permute-start(bf16[96,768]{1,0:T(8,128)(2,1)S(1)} %fusion.5), channel_id=1, source_target_pairs={{0,16},{1,17},{2,18},{3,19},{4,20},{5,21},{6,22},{7,23},{8,24},{9,... | collective-permute-start | bytes 442376 | tf_op jit(solution)/shard_map/ppermute | solution.py:928
  240.0 4.2 %collective-permute-start.43 = (f32[112,128]{1,0:T(8,128)S(1)}, f32[112,128]{1,0:T(8,128)S(1)}, u32[]{:S(2)}, u32[]{:S(2)}) collective-permute-start(f32[112,128]{1,0:T(8,128)S(1)} %add.87), channel_id=1, source_target_pairs={{0,4},{1,5},{2,6},{3,7},{4,0},{5,1},{6,2},{7,3},{8,12},{9,13},{10,... | collective-permute-start | bytes 172040 | tf_op jit(solution)/shard_map/ppermute | solution.py:928
  (37 other events, 238.9 us)
